TPU v7x, 256 devices: a whole 4x4x8 slice. The times are simulated.
256 devices in a mesh: dp: 32 (over y, x, core), tensor: 8 (over z).
Axes of the slice: x: 4, y: 4, z: 8, core: 2. Of those that a mesh axis runs over, the one named last changes fastest.
Arguments:
- qkv: bfloat16 [4, 2560, 3, 4096], P(None, 'dp', None, 'tensor'), may hold values from -6 to 6
- fir_buffer: bfloat16 [2560, 3, 2, 4096], P('dp', None, None, 'tensor'), may hold values from -6 to 6
- fir_taps: float32 [3, 3, 4096], P(None, None, 'tensor'), may hold values from -3 to 3
- modal_state: float32 [2560, 16, 4096], P('dp', None, 'tensor'), may hold values from -6 to 6
- poles: float32 [16, 4096], P(None, 'tensor'), may hold values from 0.5 to 0.999
- residues: float32 [16, 4096], P(None, 'tensor'), may hold values from -1.5 to 1.5
- skip: float32 [4096], P('tensor'), may hold values from -3 to 3
- out_weight: bfloat16 [4096, 4096], P('tensor')
- norm_gain: float32 [4096], P('tensor'), may hold values from 0.25 to 1.75
- finished: int32 [3, 2560], P(None, 'dp'), may hold values 0 or 1
- dest_group: int32 [3, 2560], P(None, 'dp'), may hold values from 0 to 31, as said below
Outputs:
- mixed: bfloat16 [4, 2560, 4096], P(None, 'dp', 'tensor')
- final_state: float32 [2560, 16, 4096], P('dp', None, 'tensor')
- final_lagged: bfloat16 [2560, 3, 2, 4096], P('dp', None, None, 'tensor')
Inputs may be any that keep to these rules, and one draw needn't show every extreme that they name: `dest_group`: for each migration, the slots s < 64 of every group form bands of 2 slots; all rows of band b of group g go to group (g + k_b) mod 32, where k_b is the same for every group and takes each value of 0 to 31 for exactly one band. Rows in later slots stay. So each group sends exactly 2 rows to every group and the moves are a permutation of the rows.
All inputs are finite; a program needn't handle non-finite values. No bound on the sum of `finished` on one device may be relied on, other than what follows from the above.
Results may differ from a plain program's by a relative error of at most 0.0048.
Values may be sent and summed in bfloat16 or wider, within the bound.
No kernel may reach another device: no remote copies, remote signals or barrier semaphores. Data moves between devices by JAX's collectives and lax.ppermute only.
A program may use at most 64 MiB of HBM per device.

v0:
```python
import jax
import jax.numpy as jnp
from jax import lax
from jax.sharding import PartitionSpec as P

STEPS = 4
CAP = 2


def migrate(state_now, lagged, dropped, plan_row):
    alive = (1 - dropped).astype(jnp.float32)
    state_now = state_now * alive[:, None, None]
    lagged = lagged * alive.astype(jnp.bfloat16)[:, None, None, None]
    groups = lax.axis_size("dp")
    own_group = lax.axis_index("dp")
    band_rows = groups * CAP
    group_ids = jnp.arange(groups, dtype=jnp.int32)
    band_target = plan_row[0:band_rows:CAP]
    picked = (band_target[None, :] == group_ids[:, None]).astype(jnp.int32)
    band_for = jnp.sum(picked * group_ids[None, :], axis=1)
    state_bands = state_now[:band_rows].reshape((groups, CAP) + state_now.shape[1:])
    lag_bands = lagged[:band_rows].reshape((groups, CAP) + lagged.shape[1:])
    got_state = lax.all_to_all(state_bands[band_for], "dp", split_axis=0, concat_axis=0, tiled=True)
    got_lag = lax.all_to_all(lag_bands[band_for], "dp", split_axis=0, concat_axis=0, tiled=True)
    band_shift = (band_target - own_group + groups) % groups
    source = (own_group - band_shift + groups) % groups
    new_state = got_state[source].reshape((band_rows,) + state_now.shape[1:])
    new_lag = got_lag[source].reshape((band_rows,) + lagged.shape[1:])
    state_now = jnp.concatenate([new_state, state_now[band_rows:]], axis=0)
    lagged = jnp.concatenate([new_lag, lagged[band_rows:]], axis=0)
    return (state_now, lagged)


def per_device(
    qkv,
    fir_buffer,
    fir_taps,
    modal_state,
    poles,
    residues,
    skip,
    out_weight,
    norm_gain,
    finished,
    dest_group,
):
    state_now = modal_state
    lagged = fir_buffer
    own_cols = norm_gain.shape[0]
    results = []
    for turn_index in range(STEPS):
        incoming = qkv[turn_index]
        filtered = fir_taps[None, :, 0, :] * incoming.astype(jnp.float32)
        filtered = filtered + fir_taps[None, :, 1, :] * lagged[:, :, 0, :].astype(jnp.float32)
        filtered = filtered + fir_taps[None, :, 2, :] * lagged[:, :, 1, :].astype(jnp.float32)
        lagged = jnp.stack([incoming, lagged[:, :, 0, :]], axis=2)
        product = filtered[:, 1] * filtered[:, 2]
        state_now = poles[None] * state_now + product[:, None, :]
        modal_out = jnp.sum(residues[None] * state_now, axis=1) + skip[None] * product
        gated_out = (filtered[:, 0] * modal_out).astype(jnp.bfloat16)
        partial_out = jnp.dot(gated_out, out_weight, preferred_element_type=jnp.float32)
        summed = lax.psum(partial_out, "tensor")
        mean_square = jnp.mean(summed * summed, axis=1)
        own_part = lax.dynamic_slice_in_dim(
            summed, lax.axis_index("tensor") * own_cols, own_cols, 1
        )
        norm_scale = lax.rsqrt(mean_square + 1e-05)
        results.append((own_part * norm_scale[:, None] * norm_gain[None]).astype(jnp.bfloat16))
        if turn_index < STEPS - 1:
            state_now, lagged = migrate(
                state_now, lagged, finished[turn_index], dest_group[turn_index]
            )
    return (jnp.stack(results), state_now, lagged)


def solution(mesh):
    return jax.shard_map(
        per_device,
        mesh=mesh,
        in_specs=(
            P(None, "dp", None, "tensor"),
            P("dp", None, None, "tensor"),
            P(None, None, "tensor"),
            P("dp", None, "tensor"),
            P(None, "tensor"),
            P(None, "tensor"),
            P("tensor"),
            P("tensor", None),
            P("tensor"),
            P(None, "dp"),
            P(None, "dp"),
        ),
        out_specs=(P(None, "dp", "tensor"), P("dp", None, "tensor"), P("dp", None, None, "tensor")),
        check_vma=False,
    )
```

profile of v0, /device:TPU:1, one launch (start us, length us, event | category | flops | bytes accessed | tf_op | source)
XLA Modules:
  0.0 345.8 jit_solution(7720512047077642710)
XLA Ops:
  7.2 1.3 slice_bitcast_fusion.8
  9.5 1.4 convert_bitcast_fusion
  12.9 2.2 slice_bitcast_fusion
  15.8 1.9 fusion.12
  18.8 3.3 gather_fusion
  22.1 8.6 %all-to-all-start = ((bf16[32,2,3,2,512]{4,1,2,3,0:T(2,128)(2,1)}), bf16[32,2,3,2,512]{4,1,2,3,0:T(2,128)(2,1)}, u32[]{:S(2)}, u32[]{:S(2)}) async-start(bf16[32,2,3,2,512]{4,1,2,3,0:T(2,128)(2,1)} %gather_fusion), calls=%async_computation | async-start | bytes 786432 | tf_op jit(solution)/shard_map/all_to_all | solution.py:24
  32.8 1.5 copy-done.4
  34.4 2.2 gather_fusion.2
  36.6 4.4 %all-to-all-done = bf16[32,2,3,2,512]{4,1,2,3,0:T(2,128)(2,1)} async-done(((bf16[32,2,3,2,512]{4,1,2,3,0:T(2,128)(2,1)}), bf16[32,2,3,2,512]{4,1,2,3,0:T(2,128)(2,1)}, u32[]{:S(2)}, u32[]{:S(2)}) %all-to-all-start) | async-done | bytes 393248 | tf_op jit(solution)/shard_map/all_to_all | solution.py:24
  41.0 4.0 %all-to-all-start.1 = ((f32[32,2,16,512]{3,2,1,0:T(8,128)}), f32[32,2,16,512]{3,2,1,0:T(8,128)S(1)}, u32[]{:S(2)}, u32[]{:S(2)}) async-start(f32[32,2,16,512]{3,2,1,0:T(8,128)} %gather_fusion.2), calls=%async_computation.1 | async-start | bytes 4194304 | tf_op jit(solution)/shard_map/all_to_all | solution.py:23
  46.2 3.1 gather_fusion.1
  51.5 1.3 fusion.10
  55.6 1.9 reshape.191
  57.5 3.1 gather_fusion.4
  60.6 12.4 %all-to-all-done.1 = f32[32,2,16,512]{3,2,1,0:T(8,128)S(1)} async-done(((f32[32,2,16,512]{3,2,1,0:T(8,128)}), f32[32,2,16,512]{3,2,1,0:T(8,128)S(1)}, u32[]{:S(2)}, u32[]{:S(2)}) %all-to-all-start.1) | async-done | bytes 2097184 | tf_op jit(solution)/shard_map/all_to_all | solution.py:23
  73.0 6.5 %all-to-all-start.2 = ((bf16[32,2,3,2,512]{4,1,2,3,0:T(2,128)(2,1)}), bf16[32,2,3,2,512]{4,1,2,3,0:T(2,128)(2,1)}, u32[]{:S(2)}, u32[]{:S(2)}) async-start(bf16[32,2,3,2,512]{4,1,2,3,0:T(2,128)(2,1)} %gather_fusion.4), calls=%async_computation.2 | async-start | bytes 786432 | tf_op jit(solution)/shard_map/all_to_all | solution.py:24
  79.6 2.3 gather_fusion.3
  82.2 1.5 copy-done.2
  83.7 1.5 slice.246
  85.2 3.6 %gather_fusion.6 = f32[32,2,16,512]{3,2,1,0:T(8,128)} fusion(f32[32,2,16,512]{3,2,1,0:T(8,128)} %bitcast.167, s32[1024]{0:T(1024)S(1)} %pad_clamp_fusion.3), kind=kCustom, calls=%fused_computation.6 | custom fusion | bytes 4194432 | tf_op jit(solution)/shard_map/gather | solution.py:23
  89.9 6.5 %all-to-all-start.3 = ((f32[32,2,16,512]{3,2,1,0:T(8,128)}), f32[32,2,16,512]{3,2,1,0:T(8,128)}, u32[]{:S(2)}, u32[]{:S(2)}) async-start(f32[32,2,16,512]{3,2,1,0:T(8,128)} %gather_fusion.6), calls=%async_computation.3 | async-start | bytes 4194304 | tf_op jit(solution)/shard_map/all_to_all | solution.py:23
  96.7 1.5 slice.242
  98.3 3.1 gather_fusion.5
  101.3 1.3 copy.34
  103.5 1.3 fusion.8
  107.8 1.9 reshape.195
  109.7 3.1 gather_fusion.8
  112.8 11.5 %all-to-all-done.3 = f32[32,2,16,512]{3,2,1,0:T(8,128)} async-done(((f32[32,2,16,512]{3,2,1,0:T(8,128)}), f32[32,2,16,512]{3,2,1,0:T(8,128)}, u32[]{:S(2)}, u32[]{:S(2)}) %all-to-all-start.3) | async-done | bytes 2097184 | tf_op jit(solution)/shard_map/all_to_all | solution.py:23
  124.3 6.7 %all-to-all-start.4 = ((bf16[32,2,3,2,512]{4,1,2,3,0:T(2,128)(2,1)}), bf16[32,2,3,2,512]{4,1,2,3,0:T(2,128)(2,1)}, u32[]{:S(2)}, u32[]{:S(2)}) async-start(bf16[32,2,3,2,512]{4,1,2,3,0:T(2,128)(2,1)} %gather_fusion.8), calls=%async_computation.4 | async-start | bytes 786432 | tf_op jit(solution)/shard_map/all_to_all | solution.py:24
  132.8 3.8 %gather_fusion.7 = f32[32,2,16,512]{3,2,1,0:T(8,128)} fusion(f32[32,2,16,512]{3,2,1,0:T(8,128)} %all-to-all-done.3, s32[1024]{0:T(1024)S(1)} %pad_clamp_fusion.2), kind=kCustom, calls=%fused_computation.7 | custom fusion | bytes 4194432 | tf_op jit(solution)/shard_map/gather | solution.py:27
  136.6 1.9 fusion.4
  138.6 1.5 copy-done.3
  140.1 1.6 slice.255
  141.6 3.6 %gather_fusion.10 = f32[32,2,16,512]{3,2,1,0:T(8,128)} fusion(f32[32,2,16,512]{3,2,1,0:T(8,128)} %bitcast.168, s32[1024]{0:T(1024)S(1)} %pad_clamp_fusion.1), kind=kCustom, calls=%fused_computation.10 | custom fusion | bytes 4194432 | tf_op jit(solution)/shard_map/gather | solution.py:23
  145.3 7.7 %all-to-all-start.5 = ((f32[32,2,16,512]{3,2,1,0:T(8,128)}), f32[32,2,16,512]{3,2,1,0:T(8,128)}, u32[]{:S(2)}, u32[]{:S(2)}) async-start(f32[32,2,16,512]{3,2,1,0:T(8,128)} %gather_fusion.10), calls=%async_computation.5 | async-start | bytes 4194304 | tf_op jit(solution)/shard_map/all_to_all | solution.py:23
  153.0 3.1 gather_fusion.9
  158.3 2.0 fusion.6
  161.8 19.0 %all-to-all-done.5 = f32[32,2,16,512]{3,2,1,0:T(8,128)} async-done(((f32[32,2,16,512]{3,2,1,0:T(8,128)}), f32[32,2,16,512]{3,2,1,0:T(8,128)}, u32[]{:S(2)}, u32[]{:S(2)}) %all-to-all-start.5) | async-done | bytes 2097184 | tf_op jit(solution)/shard_map/all_to_all | solution.py:23
  180.8 3.7 %gather_fusion.11 = f32[32,2,16,512]{3,2,1,0:T(8,128)} fusion(f32[32,2,16,512]{3,2,1,0:T(8,128)} %all-to-all-done.5, s32[1024]{0:T(1024)} %copy-done.25), kind=kCustom, calls=%fused_computation.11 | custom fusion | bytes 4194432 | tf_op jit(solution)/shard_map/gather | solution.py:27
  184.6 6.8 %multiply_reduce_fusion.3 = (f32[80,512]{1,0:T(8,128)S(1)}, f32[80,512]{1,0:T(8,128)S(1)}, f32[80,512]{1,0:T(8,128)S(1)}, f32[80,512]{1,0:T(8,128)S(1)}, f32[80,16,512]{2,1,0:T(8,128)}) fusion(f32[80,16,512]{2,1,0:T(8,128)} %param.14, f32[80,512]{1,0:T(8,128)S(1)} %fusion.29, f32[16,512]{1,0:T(8,128)S(1)} %copy-done.20, f32[16,512]{1,0:T(8,128)S(1)} %copy-done.23, ...), kind=kLoop, calls=%fused_computation.21 | loop fusion | flops 12288000 | bytes 14483456 | tf_op jit(solution)/shard_map/reduce_sum | solution.py:59
  191.4 2.9 fusion.36
  194.3 2.9 fusion.38
  197.2 2.9 fusion.40
  200.1 2.9 fusion.42
  204.1 1.3 copy.36
  205.4 128.0 %all-reduce.3.cloned.1.call-done = (f32[80,4096]{1,0:T(8,128)}, f32[80,4096]{1,0:T(8,128)}, f32[80,4096]{1,0:T(8,128)}, f32[80,4096]{1,0:T(8,128)}) async-done(((f32[80,4096]{1,0:T(8,128)}, f32[80,4096]{1,0:T(8,128)}, f32[80,4096]{1,0:T(8,128)}, f32[80,4096]{1,0:T(8,128)}), (f32[80,4096]{1,0:T(8,128)}, f32[80,4096]{1,0:T(8,128)}, f32[80,4096]{1,0:T(8,128)}, ...) | async-done | bytes 5242896 | tf_op jit(solution)/shard_map/psum | solution.py:62
  333.4 1.6 multiply_reduce_fusion.4
  335.1 1.5 multiply_reduce_fusion.5
  (132 shorter events, 27.6 us)
Async XLA Ops:
  7.2 8.0 %copy-start.14 = (bf16[80,3,2,512]{3,2,1,0:T(2,128)(2,1)S(1)}, bf16[80,3,2,512]{3,2,1,0:T(2,128)(2,1)}, u32[]{:S(2)}) copy-start(bf16[80,3,2,512]{3,2,1,0:T(2,128)(2,1)} %param.12) | copy-start | bytes 1474564
  8.6 2.8 copy-start.35
  8.7 0.6 copy-start.33
  15.8 2.0 copy-start.21
  17.7 14.0 %copy-start.1 = (f32[80,16,512]{2,1,0:T(8,128)S(1)}, f32[80,16,512]{2,1,0:T(8,128)}, u32[]{:S(2)}) copy-start(f32[80,16,512]{2,1,0:T(8,128)} %param.14) | copy-start | bytes 7864324
  17.7 14.0 %copy-start.20 = (f32[16,512]{1,0:T(8,128)S(1)}, f32[16,512]{1,0:T(8,128)}, u32[]{:S(2)}) copy-start(f32[16,512]{1,0:T(8,128)} %param.15) | copy-start | bytes 98308
  17.9 27.2 %copy-start.13 = (bf16[80,3,2,512]{3,0,1,2:T(8,128)(2,1)}, bf16[80,3,2,512]{3,0,1,2:T(8,128)(2,1)S(1)}, u32[]{:S(2)}) copy-start(bf16[80,3,2,512]{3,0,1,2:T(8,128)(2,1)S(1)} %maximum_multiply_fusion.3) | copy-start | bytes 1474564
  22.1 18.9 %all-to-all-start = ((bf16[32,2,3,2,512]{4,1,2,3,0:T(2,128)(2,1)}), bf16[32,2,3,2,512]{4,1,2,3,0:T(2,128)(2,1)}, u32[]{:S(2)}, u32[]{:S(2)}) async-start(bf16[32,2,3,2,512]{4,1,2,3,0:T(2,128)(2,1)} %gather_fusion), calls=%async_computation | async-start | bytes 786432 | tf_op jit(solution)/shard_map/all_to_all | solution.py:24
  32.8 1.5 copy-start.4
  36.6 9.6 %copy-start.36 = (s32[32]{0:T(128)S(1)}, s32[32]{0:T(128)}, u32[]{:S(2)}) copy-start(s32[32]{0:T(128)} %copy-done.35) | copy-start | bytes 388
  36.6 9.6 %copy-start.31 = (s32[32]{0:T(128)S(1)}, s32[32]{0:T(128)}, u32[]{:S(2)}) copy-start(s32[32]{0:T(128)} %get-tuple-element.51) | copy-start | bytes 388
  41.0 32.0 %all-to-all-start.1 = ((f32[32,2,16,512]{3,2,1,0:T(8,128)}), f32[32,2,16,512]{3,2,1,0:T(8,128)S(1)}, u32[]{:S(2)}, u32[]{:S(2)}) async-start(f32[32,2,16,512]{3,2,1,0:T(8,128)} %gather_fusion.2), calls=%async_computation.1 | async-start | bytes 4194304 | tf_op jit(solution)/shard_map/all_to_all | solution.py:23
  45.0 6.5 %copy-start.22 = (f32[3,512]{1,0:T(4,128)S(1)}, f32[3,512]{1,0:T(4,128)}, u32[]{:S(2)}) copy-start(f32[3,512]{1,0:T(4,128)} %copy-done.21) | copy-start | bytes 18436
  45.0 7.7 %copy-start.27 = (bf16[80]{0:T(256)(128)(2,1)S(1)}, bf16[80]{0:T(256)(128)(2,1)}, u32[]{:S(2)}) copy-start(bf16[80]{0:T(256)(128)(2,1)} %get-tuple-element.41) | copy-start | bytes 484
  45.0 6.4 %slice-start.2 = ((bf16[80,3,2,512]{3,0,1,2:T(8,128)(2,1)}), bf16[16,3,2,512]{3,0,1,2:T(8,128)(2,1)S(1)}, s32[]{:S(2)}) async-start(bf16[80,3,2,512]{3,0,1,2:T(8,128)(2,1)} %copy-done.13), calls=%async_computation.9 | async-start | bytes 196608 | tf_op jit(solution)/shard_map/slice | solution.py:30
  52.7 29.1 %copy-start.8 = (f32[80,3,512]{2,0,1:T(8,128)}, f32[80,3,512]{2,0,1:T(8,128)S(1)}, u32[]{:S(2)}) copy-start(f32[80,3,512]{2,0,1:T(8,128)S(1)} %get-tuple-element.20) | copy-start | bytes 1474564
  54.0 0.8 copy-start.10
  60.6 21.3 %copy-start.30 = (f32[80]{0:T(128)S(1)}, f32[80]{0:T(128)}, u32[]{:S(2)}) copy-start(f32[80]{0:T(128)} %get-tuple-element.44) | copy-start | bytes 964
  73.0 6.6 %copy-start.5 = (f32[32,2,16,512]{3,2,1,0:T(8,128)}, f32[32,2,16,512]{3,2,1,0:T(8,128)S(1)}, u32[]{:S(2)}) copy-start(f32[32,2,16,512]{3,2,1,0:T(8,128)S(1)} %all-to-all-done.1) | copy-start | bytes 6291460
  73.0 16.9 %all-to-all-start.2 = ((bf16[32,2,3,2,512]{4,1,2,3,0:T(2,128)(2,1)}), bf16[32,2,3,2,512]{4,1,2,3,0:T(2,128)(2,1)}, u32[]{:S(2)}, u32[]{:S(2)}) async-start(bf16[32,2,3,2,512]{4,1,2,3,0:T(2,128)(2,1)} %gather_fusion.4), calls=%async_computation.2 | async-start | bytes 786432 | tf_op jit(solution)/shard_map/all_to_all | solution.py:24
  82.2 1.5 copy-start.2
  88.8 7.6 %copy-start.32 = (s32[80]{0:T(128)S(1)}, s32[80]{0:T(128)}, u32[]{:S(2)}) copy-start(s32[80]{0:T(128)} %get-tuple-element.45) | copy-start | bytes 964
  88.8 7.9 %copy-start.34 = (s32[32]{0:T(128)S(1)}, s32[32]{0:T(128)}, u32[]{:S(2)}) copy-start(s32[32]{0:T(128)} %copy-done.33) | copy-start | bytes 388
  89.9 34.4 %all-to-all-start.3 = ((f32[32,2,16,512]{3,2,1,0:T(8,128)}), f32[32,2,16,512]{3,2,1,0:T(8,128)}, u32[]{:S(2)}, u32[]{:S(2)}) async-start(f32[32,2,16,512]{3,2,1,0:T(8,128)} %gather_fusion.6), calls=%async_computation.3 | async-start | bytes 4194304 | tf_op jit(solution)/shard_map/all_to_all | solution.py:23
  96.4 8.5 %copy-start.26 = (bf16[80]{0:T(256)(128)(2,1)S(1)}, bf16[80]{0:T(256)(128)(2,1)}, u32[]{:S(2)}) copy-start(bf16[80]{0:T(256)(128)(2,1)} %get-tuple-element.40) | copy-start | bytes 484
  104.9 26.2 %copy-start.9 = (f32[80,3,512]{2,0,1:T(8,128)}, f32[80,3,512]{2,0,1:T(8,128)S(1)}, u32[]{:S(2)}) copy-start(f32[80,3,512]{2,0,1:T(8,128)S(1)} %get-tuple-element.18) | copy-start | bytes 1474564
  106.1 0.8 copy-start.11
  124.3 21.0 %all-to-all-start.4 = ((bf16[32,2,3,2,512]{4,1,2,3,0:T(2,128)(2,1)}), bf16[32,2,3,2,512]{4,1,2,3,0:T(2,128)(2,1)}, u32[]{:S(2)}, u32[]{:S(2)}) async-start(bf16[32,2,3,2,512]{4,1,2,3,0:T(2,128)(2,1)} %gather_fusion.8), calls=%async_computation.4 | async-start | bytes 786432 | tf_op jit(solution)/shard_map/all_to_all | solution.py:24
  131.7 4.9 %copy-start.29 = (f32[80]{0:T(128)S(1)}, f32[80]{0:T(128)}, u32[]{:S(2)}) copy-start(f32[80]{0:T(128)} %get-tuple-element.39) | copy-start | bytes 964
  132.8 5.7 %copy-start.6 = (f32[16,16,512]{2,1,0:T(8,128)}, f32[16,16,512]{2,1,0:T(8,128)S(1)}, u32[]{:S(2)}) copy-start(f32[16,16,512]{2,1,0:T(8,128)S(1)} %slice.247) | copy-start | bytes 1572868
  138.6 1.5 copy-start.3
  145.3 13.1 %slice-start.1 = ((bf16[80,3,2,512]{3,0,1,2:T(8,128)(2,1)}), bf16[16,3,2,512]{3,0,1,2:T(8,128)(2,1)S(1)}, s32[]{:S(2)}) async-start(bf16[80,3,2,512]{3,0,1,2:T(8,128)(2,1)} %copy-done.11), calls=%async_computation.8 | async-start | bytes 196608 | tf_op jit(solution)/shard_map/slice | solution.py:30
  145.3 35.6 %all-to-all-start.5 = ((f32[32,2,16,512]{3,2,1,0:T(8,128)}), f32[32,2,16,512]{3,2,1,0:T(8,128)}, u32[]{:S(2)}, u32[]{:S(2)}) async-start(f32[32,2,16,512]{3,2,1,0:T(8,128)} %gather_fusion.10), calls=%async_computation.5 | async-start | bytes 4194304 | tf_op jit(solution)/shard_map/all_to_all | solution.py:23
  152.9 180.5 %all-reduce.3.cloned.1.call-start = ((), (), s32[]{:S(2)}) async-start(), calls=%async_computation.6 | async-start | bytes 10485760 | tf_op jit(solution)/shard_map/psum | solution.py:62
  153.0 7.3 %copy-start.25 = (s32[1024]{0:T(1024)}, s32[1024]{0:T(1024)S(1)}, u32[]{:S(2)}) copy-start(s32[1024]{0:T(1024)S(1)} %pad_clamp_fusion) | copy-start | bytes 12292
  160.3 0.8 copy-start.12
  161.8 22.8 %slice-start = ((f32[80,16,512]{2,1,0:T(8,128)}), f32[16,16,512]{2,1,0:T(8,128)S(1)}, s32[]{:S(2)}) async-start(f32[80,16,512]{2,1,0:T(8,128)} %copy-done.3), calls=%async_computation.7 | async-start | bytes 1048576 | tf_op jit(solution)/shard_map/slice | solution.py:29
  161.8 22.8 %copy-start.23 = (f32[16,512]{1,0:T(8,128)S(1)}, f32[16,512]{1,0:T(8,128)}, u32[]{:S(2)}) copy-start(f32[16,512]{1,0:T(8,128)} %param.16) | copy-start | bytes 98308
  184.6 6.8 %copy-start = (bf16[512,4096]{1,0:T(8,128)(2,1)S(1)}, bf16[512,4096]{1,0:T(8,128)(2,1)}, u32[]{:S(2)}) copy-start(bf16[512,4096]{1,0:T(8,128)(2,1)} %param.18) | copy-start | bytes 12582916
  184.6 6.8 %copy-start.24 = (f32[512]{0:T(512)S(1)}, f32[512]{0:T(512)}, u32[]{:S(2)}) copy-start(f32[512]{0:T(512)} %param.17) | copy-start | bytes 6148
  194.3 2.9 copy-start.7
  197.2 2.9 copy-start.17
  203.0 0.9 copy-start.18
  203.0 1.1 copy-start.19
  333.4 3.2 copy-start.15
  333.4 3.4 copy-start.16
  333.4 3.6 %copy-start.28 = (f32[512]{0:T(512)S(1)}, f32[512]{0:T(512)}, u32[]{:S(2)}) copy-start(f32[512]{0:T(512)} %param.19) | copy-start | bytes 6148
Sparse Core Ops, SparseCore 0:
  203.1 130.2 all-reduce.2
where the time goes:
time: 348 us; the launch traced here: 346 us
  waiting for transfers between devices  176 us (51%)
  local copies, waits for them, and re-layouts  73.2 us (21%)
  starting transfers between devices  40.2 us (12%)
  other arithmetic  30 us (9%)
  between operations  14.6 us (4%)
  matrix products  11.5 us (3%)
    psum x1, waiting for transfers between devices, per_device(): summed = lax.psum(partial_out, 'tensor')  128 us
    all_to_all x3, waiting for transfers between devices, migrate(): lax.all_to_all(state_bands[band_for], 'dp', split_axis=0, concat_axis=0,...  42.8 us
    all_to_all x3, starting transfers between devices, migrate(): lax.all_to_all(lag_bands[band_for], 'dp', split_axis=0, concat_axis=0, ti...  21.9 us
    all_to_all x3, starting transfers between devices, migrate(): lax.all_to_all(state_bands[band_for], 'dp', split_axis=0, concat_axis=0,...  18.3 us
    gather x6, local copies, waits for them, and re-layouts, migrate(): new_lag = got_lag[source].reshape((band_rows,) + lagged.shape[1:])  13 us
    dot_general x4, matrix products, per_device(): jnp.dot(gated_out, out_weight, preferred_element_type=jnp.float32)  11.5 us
    unnamed x77, local copies, waits for them, and re-layouts  9.89 us
    gather x3, local copies, waits for them, and re-layouts, migrate(): new_state = got_state[source].reshape((band_rows,) + state_now.shape[1:])  9.82 us
  transfers between devices with their start and end apart: 7, of which 6 were waited for; matrix products, arithmetic and copies ran while one was open for 19% of the time, Pallas kernels for 0%

commit v1 on v0

v1 whole, which is shorter than its diff:
```python
import jax
import jax.numpy as jnp
from jax import lax
from jax.experimental import pallas as pl
from jax.experimental.pallas import tpu as pltpu
from jax.sharding import PartitionSpec as P

CAP = 2
MODES = 16
KINDS = 16
F32, BF16 = jnp.float32, jnp.bfloat16


def dot(a, b):
    return jnp.dot(a, b, preferred_element_type=F32)


def wide(x, width):
    return jnp.concatenate([x] * (width // x.shape[-1]), axis=-1)


def home_kernel(qkv, fir, taps, state, poles, residues, skip, alive, packed, gated, stay_state, y_rows):
    block = pl.program_id(0)
    rows, width = 16, qkv.shape[-1]
    alive0 = wide(alive[0], width)
    q0 = [qkv[0, j].astype(F32) for j in range(3)]
    l0 = [fir[j, 0].astype(F32) for j in range(3)]
    f = [
        taps[j, 0:1] * q0[j] + taps[j, 1:2] * l0[j] + taps[j, 2:3] * fir[j, 1].astype(F32)
        for j in range(3)
    ]
    product = f[1] * f[2]
    modes = []
    for r in range(rows):
        s = poles[...] * state[r] + product[r : r + 1]
        y_rows[r : r + 1] = jnp.sum(residues[...] * s, axis=0, keepdims=True)
        modes.append(s * alive0[r : r + 1])
    gated[pl.ds(block * rows, rows)] = (f[0] * (y_rows[...] + skip[...] * product)).astype(BF16)

    @pl.when(block < 4)
    def _():
        for pair in range(rows // 2):
            both = jnp.concatenate([modes[2 * pair], modes[2 * pair + 1]], axis=0)
            packed[pair, 0 : 2 * MODES] = both.astype(BF16)
        sent = [(x * alive0).astype(BF16) for x in q0 + l0]
        sent += [qkv[t, j] for t in range(1, 4) for j in range(3)]
        ends = wide(alive[1], width // 2), wide(alive[2], width // 2)
        sent.append(jnp.concatenate(ends, axis=-1).astype(BF16))
        stacked = jnp.concatenate(sent, axis=0)
        n = KINDS * rows
        r = lax.broadcasted_iota(jnp.int32, (n, n), 0)
        c = lax.broadcasted_iota(jnp.int32, (n, n), 1)
        source = ((r >> 1) & 15) * rows + (r >> 5) * 2 + (r & 1)
        order = jnp.where(c == source, 1.0, 0.0).astype(BF16)
        moved = dot(order, stacked).reshape(rows // 2, 2 * KINDS, width)
        packed[:, 2 * MODES :] = moved.astype(BF16)

    @pl.when(block == 4)
    def _():
        for r in range(rows):
            stay_state[r] = modes[r]
        lag0, lag1 = [x * alive0 for x in q0], [x * alive0 for x in l0]
        for t in range(1, 4):
            q = [qkv[t, j].astype(F32) for j in range(3)]
            g = [
                taps[j, 0:1] * q[j] + taps[j, 1:2] * lag0[j] + taps[j, 2:3] * lag1[j]
                for j in range(3)
            ]
            prod = g[1] * g[2]
            live = wide(alive[t], width) if t < 3 else None
            for r in range(rows):
                s = poles[...] * stay_state[r] + prod[r : r + 1]
                y_rows[r : r + 1] = jnp.sum(residues[...] * s, axis=0, keepdims=True)
                stay_state[r] = s * live[r : r + 1] if t < 3 else s
            gated[64 + t * rows : 80 + t * rows] = (
                g[0] * (y_rows[...] + skip[...] * prod)
            ).astype(BF16)
            if t < 3:
                lag0, lag1 = [x * live for x in q], [x * live for x in lag0]


def band_kernel(
    turns, got, taps, poles, residues, skip, sent, gated, lags, inputs, live, heads, products, y_rows
):
    groups, _, width = got.shape
    rows = 2 * groups
    kinds = got[:, 2 * MODES :].reshape(groups * 2 * KINDS, width)

    def taken(first, count, turn):
        shape = (count * rows, groups * 2 * KINDS)
        r = lax.broadcasted_iota(jnp.int32, shape, 0)
        c = lax.broadcasted_iota(jnp.int32, shape, 1)
        group = (((r & (rows - 1)) >> 1) + turn) & (groups - 1)
        source = group * (2 * KINDS) + (first + r // rows) * 2 + (r & 1)
        order = jnp.where(c == source, 1.0, 0.0).astype(BF16)
        return dot(order, kinds).reshape(count, rows, width)

    lags[...] = taken(0, 6, 0)
    for t in range(3):
        inputs[t] = taken(6 + 3 * t, 3, turns[t])
    half = width // 2
    live[0] = wide(taken(15, 1, turns[0])[0, :, :half], width)
    live[1] = wide(taken(15, 1, turns[1])[0, :, half:], width)

    @pl.loop(0, rows // 8)
    def _(i):
        at = pl.ds(pl.multiple_of(i * 8, 8), 8)
        lag0 = [lags[j, at] for j in range(3)]
        lag1 = [lags[3 + j, at] for j in range(3)]
        for t in range(3):
            q = [inputs[t, j, at] for j in range(3)]
            f = [
                taps[j, 0:1] * q[j] + taps[j, 1:2] * lag0[j] + taps[j, 2:3] * lag1[j]
                for j in range(3)
            ]
            heads[t, at] = f[0]
            products[t, at] = f[1] * f[2]
            if t < 2:
                on = live[t, at]
                lag0, lag1 = [x * on for x in q], [x * on for x in lag0]
                if t == 1:
                    for j in range(3):
                        lags[j, at] = lag0[j]

    shape = (groups * 16, 3 * rows)
    r = lax.broadcasted_iota(jnp.int32, shape, 0)
    c = lax.broadcasted_iota(jnp.int32, shape, 1)
    group = ((r >> 4) - turns[2] + groups) & (groups - 1)
    source = ((r & 15) >> 1) * rows + group * 2 + (r & 1)
    order = jnp.where((c == source) & ((r & 15) < 6), 1.0, 0.0).astype(BF16)
    last = lags[0:3].reshape(3 * rows, width).astype(BF16)
    sent[:, 2 * MODES :] = dot(order, last).reshape(groups, 16, width).astype(BF16)

    @pl.loop(0, groups)
    def _(g):
        final = []
        for side in range(2):
            row = pl.ds(g * 2 + side, 1)
            s = got[g, side * MODES : (side + 1) * MODES].astype(F32)
            for t in range(3):
                product = products[t, row]
                s = poles[...] * s + product
                y = jnp.sum(residues[...] * s, axis=0, keepdims=True)
                there = ((g + turns[t]) & (groups - 1)) * 2 + side
                y_rows[t, pl.ds(there, 1)] = heads[t, row] * (y + skip[...] * product)
                if t < 2:
                    s = s * live[t, row]
            final.append(s)
        end = (g + turns[2]) & (groups - 1)
        sent[end, 0 : 2 * MODES] = jnp.concatenate(final, axis=0).astype(BF16)

    gated[...] = y_rows[...].astype(BF16)


def whole(shape):
    return pl.BlockSpec(shape, lambda *_: (0,) * len(shape))


def ring_sums(part, own_cols):
    n = lax.axis_size("tensor")
    me = lax.axis_index("tensor")

    def piece(away):
        return lax.dynamic_slice_in_dim(part, ((me + away) % n) * own_cols, own_cols, 1)

    right = left = None
    for away in range(n // 2, 0, -1):
        held = [right, left]
        for side, step in enumerate((1, -1)):
            if step == -1 and away > (n - 1) // 2:
                continue
            mine = piece(step * away)
            held[side] = (mine if held[side] is None else mine + held[side].astype(F32)).astype(BF16)
        held = [
            x if x is None else lax.ppermute(x, "tensor", [(i, (i + step) % n) for i in range(n)])
            for x, step in zip(held, (1, -1))
        ]
        right, left = lax.optimization_barrier(tuple(held))
    total = piece(0) + right.astype(F32)
    return total if left is None else total + left.astype(F32)


def normed(part, gain):
    n = lax.axis_size("tensor")
    own = ring_sums(part, gain.shape[0])
    mine = jnp.sum(own * own, axis=1)
    squares = mine
    for away in range(1, n):
        squares = squares + lax.ppermute(mine, "tensor", [(i, (i + away) % n) for i in range(n)])
    scale = lax.rsqrt(squares / (n * gain.shape[0]) + 1e-05)
    return (own * scale[:, None] * gain[None]).astype(BF16)


def per_device(
    qkv,
    fir_buffer,
    fir_taps,
    modal_state,
    poles,
    residues,
    skip,
    out_weight,
    norm_gain,
    finished,
    dest_group,
):
    groups = lax.axis_size("dp")
    own_group = lax.axis_index("dp")
    slots, width = modal_state.shape[0], modal_state.shape[2]
    moving = groups * CAP
    qkv_kinds = jnp.transpose(qkv, (0, 2, 1, 3))
    fir_kinds = jnp.transpose(fir_buffer, (1, 2, 0, 3))
    alive = jnp.broadcast_to((1 - finished).astype(F32)[:, :, None], (3, slots, 128))
    skip_row = skip[None]
    shifts = lax.dynamic_slice_in_dim(dest_group, own_group * CAP, 1, 1)[:, 0] - own_group + groups
    turns = jnp.cumsum(shifts).astype(jnp.int32) % groups

    params = pltpu.CompilerParams(vmem_limit_bytes=32 * 1024 * 1024)
    packed, gated_home, stay_state = pl.pallas_call(
        home_kernel,
        grid=(slots // 16,),
        in_specs=[
            pl.BlockSpec((4, 3, 16, width), lambda i: (0, 0, i, 0)),
            pl.BlockSpec((3, 2, 16, width), lambda i: (0, 0, i, 0)),
            whole((3, 3, width)),
            pl.BlockSpec((16, MODES, width), lambda i: (i, 0, 0)),
            whole((MODES, width)),
            whole((MODES, width)),
            whole((1, width)),
            pl.BlockSpec((3, 16, 128), lambda i: (0, i, 0)),
        ],
        out_specs=[
            pl.BlockSpec((8, 2 * MODES + 2 * KINDS, width), lambda i: (jnp.minimum(i, 3), 0, 0)),
            whole((slots + 48, width)),
            whole((16, MODES, width)),
        ],
        out_shape=[
            jax.ShapeDtypeStruct((groups, 2 * MODES + 2 * KINDS, width), BF16),
            jax.ShapeDtypeStruct((slots + 48, width), BF16),
            jax.ShapeDtypeStruct((16, MODES, width), F32),
        ],
        scratch_shapes=[pltpu.VMEM((16, width), F32)],
        compiler_params=params,
        name="home_rows",
    )(qkv_kinds, fir_kinds, fir_taps, modal_state, poles, residues, skip_row, alive)

    got = lax.all_to_all(packed, "dp", split_axis=0, concat_axis=0, tiled=True)
    mixed_home = normed(dot(gated_home, out_weight), norm_gain)
    got, mixed_home = lax.optimization_barrier((got, mixed_home))

    sent, gated_band = pl.pallas_call(
        band_kernel,
        in_specs=[pl.BlockSpec(memory_space=pltpu.SMEM)]
        + [pl.BlockSpec(memory_space=pltpu.VMEM)] * 5,
        out_specs=[pl.BlockSpec(memory_space=pltpu.VMEM)] * 2,
        out_shape=[
            jax.ShapeDtypeStruct((groups, 2 * MODES + 16, width), BF16),
            jax.ShapeDtypeStruct((3, moving, width), BF16),
        ],
        scratch_shapes=[
            pltpu.VMEM((6, moving, width), F32),
            pltpu.VMEM((3, 3, moving, width), F32),
            pltpu.VMEM((2, moving, width), F32),
            pltpu.VMEM((3, moving, width), F32),
            pltpu.VMEM((3, moving, width), F32),
            pltpu.VMEM((3, moving, width), F32),
        ],
        compiler_params=params,
        name="band_rows",
    )(turns, got, fir_taps, poles, residues, skip_row)

    back = lax.all_to_all(sent, "dp", split_axis=0, concat_axis=0, tiled=True)
    mixed_band = normed(dot(gated_band.reshape(3 * moving, width), out_weight), norm_gain)
    own_cols = norm_gain.shape[0]
    back, mixed_band = lax.optimization_barrier((back, mixed_band))
    mixed_band = jnp.transpose(mixed_band.reshape(3, groups, CAP, own_cols), (1, 0, 2, 3))
    mixed_back = lax.all_to_all(mixed_band, "dp", split_axis=0, concat_axis=0, tiled=True)
    mixed_later = jnp.transpose(mixed_back, (1, 0, 2, 3)).reshape(3, moving, own_cols)
    mixed_stay = mixed_home[slots:].reshape(3, 16, own_cols)
    mixed = jnp.concatenate(
        [mixed_home[None, :slots], jnp.concatenate([mixed_later, mixed_stay], axis=1)], axis=0
    )

    moved_state = back[:, : 2 * MODES].reshape(moving, MODES, width).astype(F32)
    final_state = jnp.concatenate([moved_state, stay_state], axis=0)
    moved_lag = back[:, 2 * MODES : 2 * MODES + 6].reshape(groups, 3, CAP, width)
    moved_lag = jnp.transpose(moved_lag, (0, 2, 1, 3)).reshape(moving, 3, width)
    stay_alive = (1 - finished[2, moving:]).astype(BF16)[:, None, None]
    last_lag = jnp.concatenate([moved_lag, qkv[2, moving:] * stay_alive], axis=0)
    final_lagged = jnp.stack([qkv[3], last_lag], axis=2)
    return (mixed, final_state, final_lagged)


def solution(mesh):
    return jax.shard_map(
        per_device,
        mesh=mesh,
        in_specs=(
            P(None, "dp", None, "tensor"),
            P("dp", None, None, "tensor"),
            P(None, None, "tensor"),
            P("dp", None, "tensor"),
            P(None, "tensor"),
            P(None, "tensor"),
            P("tensor"),
            P("tensor", None),
            P("tensor"),
            P(None, "dp"),
            P(None, "dp"),
        ),
        out_specs=(P(None, "dp", "tensor"), P("dp", None, "tensor"), P("dp", None, None, "tensor")),
        check_vma=False,
    )
```

time: 348 us -> 154 us (0.44)
  waiting for transfers between devices: 176 us -> 40 us
  local copies, waits for them, and re-layouts: 73.2 us -> 12.9 us
  starting transfers between devices: 40.2 us -> 72.8 us
  other arithmetic: 30 us -> 14.5 us
  between operations: 14.6 us -> 1.2 us
  Pallas kernels: 0 us -> 7.6 us
  matrix products: 11.5 us -> 4.46 us
    psum x1 -> x0, waiting for transfers between devices: 128 us -> none  [per_device(): summed = lax.psum(partial_out, 'tensor')]
    all_to_all x6 -> x3, waiting for transfers between devices: 48.2 us -> 4.33 us  [the longest x1 4.33 us: per_device(): lax.all_to_all(mixed_band, 'dp', split_axis=0, concat_axis=0, tiled=True)]
    gather x15 -> x0, local copies, waits for them, and re-layouts: 41.7 us -> none  [the longest x6 13 us: migrate(): new_lag = got_lag[source].reshape((band_rows,) + lagged.shape[1:])]
    ppermute x0 -> x28, starting transfers between devices: none -> 37.9 us  [the longest x14 22.7 us: normed(): lax.ppermute(mine, 'tensor', [(i, (i + away) % n) for i in range(n)])]
    ppermute x0 -> x28, waiting for transfers between devices: none -> 35.6 us  [the longest x14 30.9 us: ring_sums(): lax.ppermute(x, 'tensor', [(i, (i + step) % n) for i in range(n)])]
    slice x20 -> x5, local copies, waits for them, and re-layouts: 10.5 us -> 0.17 us  [the longest x1 0.09 us: per_device(): moved_state = back[:, :2 * MODES].reshape(moving, MODES, width).astype(F32)]
    add x8 -> x1, other arithmetic: 8.9 us -> 0.07 us  [per_device(): lax.dynamic_slice_in_dim(dest_group, own_group * CAP, 1, 1)[:, 0]]
    reduce_sum x8 -> x2, other arithmetic: 10.7 us -> 2.24 us  [normed(): mine = jnp.sum(own * own, axis=1)]
  transfers between devices with their start and end apart: 7 -> 31, of which waited for: 6 -> 16; matrix products, arithmetic and copies ran while one was open for 19% -> 10% of each run, Pallas kernels for 0% -> 0%
where the time goes in v1:
time: 154 us; the launch traced here: 153 us
  starting transfers between devices  72.8 us (47%)
  waiting for transfers between devices  40 us (26%)
  other arithmetic  14.5 us (9%)
  local copies, waits for them, and re-layouts  12.9 us (8%)
  Pallas kernels  7.6 us (5%)
  matrix products  4.46 us (3%)
    ppermute x14, waiting for transfers between devices, ring_sums(): lax.ppermute(x, 'tensor', [(i, (i + step) % n) for i in range(n)])  30.9 us
    ppermute x14, starting transfers between devices, normed(): lax.ppermute(mine, 'tensor', [(i, (i + away) % n) for i in range(n)])  22.7 us
    all_to_all x1, starting transfers between devices, per_device(): back = lax.all_to_all(sent, 'dp', split_axis=0, concat_axis=0, tiled=True)  15.9 us
    ppermute x14, starting transfers between devices, ring_sums(): lax.ppermute(x, 'tensor', [(i, (i + step) % n) for i in range(n)])  15.3 us
    all_to_all x1, starting transfers between devices, per_device(): lax.all_to_all(mixed_band, 'dp', split_axis=0, concat_axis=0, tiled=True)  10.9 us
    unnamed x38, local copies, waits for them, and re-layouts  10.2 us
    all_to_all x1, starting transfers between devices, per_device(): got = lax.all_to_all(packed, 'dp', split_axis=0, concat_axis=0, tiled=True)  8.04 us
    pallas_call x1, Pallas kernels, per_device(): pl.pallas_call(band_kernel, in_specs=[pl.BlockSpec(memory_space=pltpu.SME...  4.8 us
  transfers between devices with their start and end apart: 31, of which 16 were waited for; matrix products, arithmetic and copies ran while one was open for 10% of the time, Pallas kernels for 0%

profile of v1, /device:TPU:1, one launch (start us, length us, event | category | flops | bytes accessed | tf_op | source)
XLA Modules:
  0.0 153.4 jit_solution(1837965471644677844)
XLA Ops:
  1.4 1.1 copy.38
  2.6 1.7 %copy-done = f32[80,16,512]{2,1,0:T(8,128)S(1)} copy-done((f32[80,16,512]{2,1,0:T(8,128)S(1)}, f32[80,16,512]{2,1,0:T(8,128)}, u32[]{:S(2)}) %copy-start) | copy-done | bytes 2621464
  4.3 1.2 copy-done.2
  8.4 2.8 %home_rows.1 = (bf16[32,64,512]{2,1,0:T(8,128)(2,1)S(1)}, bf16[128,512]{1,0:T(8,128)(2,1)S(1)}, f32[16,16,512]{2,1,0:T(8,128)S(1)}) custom-call(bf16[4,3,80,512]{3,2,1,0:T(8,128)(2,1)S(1)} %bitcast.33, bf16[3,2,80,512]{3,2,1,0:T(8,128)(2,1)S(1)} %bitcast.32, f32[3,3,512]{2,1,0:T(4,128)S(1)} %copy-done.8, f32[80,16,512]{2,1,0:T(8,128)S(1)} %copy-done, ...), custom_call_target="tpu_custom_call" | custom-call | tf_op jit(solution)/shard_map/home_rows/pallas_call | solution.py:219
  12.6 1.3 copy-done.14
  13.9 2.5 %collective-permute-start = (bf16[128,512]{1,0:T(8,128)(2,1)S(1)}, bf16[128,512]{1,0:T(8,128)(2,1)S(1)}, u32[]{:S(2)}, u32[]{:S(2)}) collective-permute-start(bf16[128,512]{1,0:T(8,128)(2,1)S(1)} %get-tuple-element.68), channel_id=1, source_target_pairs={{0,1},{1,2},{2,3},{3,4},{4,5},{5,6},{6,7},{7,0},{8,9},{9,10},{10,1... | collective-permute-start | bytes 393224 | tf_op jit(solution)/shard_map/ppermute | solution.py:175
  16.4 8.0 %all-to-all-start = ((bf16[32,64,512]{2,1,0:T(8,128)(2,1)}), bf16[32,64,512]{2,1,0:T(8,128)(2,1)S(1)}, u32[]{:S(2)}, u32[]{:S(2)}) async-start(bf16[32,64,512]{2,1,0:T(8,128)(2,1)} %copy-done.1), calls=%async_computation | async-start | bytes 4194304 | tf_op jit(solution)/shard_map/all_to_all | solution.py:247
  24.5 3.7 %collective-permute-start.2 = (bf16[128,512]{1,0:T(8,128)(2,1)S(1)}, bf16[128,512]{1,0:T(8,128)(2,1)S(1)}, u32[]{:S(2)}, u32[]{:S(2)}) collective-permute-start(bf16[128,512]{1,0:T(8,128)(2,1)S(1)} %get-tuple-element.67), channel_id=1, source_target_pairs={{0,7},{1,0},{2,1},{3,2},{4,3},{5,4},{6,5},{7,6},{8,15},{9,8},{10,9... | collective-permute-start | bytes 393224 | tf_op jit(solution)/shard_map/ppermute | solution.py:175
  29.3 1.5 %collective-permute-done.2 = bf16[128,512]{1,0:T(8,128)(2,1)S(1)} collective-permute-done((bf16[128,512]{1,0:T(8,128)(2,1)S(1)}, bf16[128,512]{1,0:T(8,128)(2,1)S(1)}, u32[]{:S(2)}, u32[]{:S(2)}) %collective-permute-start.2) | collective-permute-done | bytes 131104 | tf_op jit(solution)/shard_map/ppermute | solution.py:175
  30.9 4.2 %collective-permute-done.1 = bf16[128,512]{1,0:T(8,128)(2,1)S(1)} collective-permute-done((bf16[128,512]{1,0:T(8,128)(2,1)S(1)}, bf16[128,512]{1,0:T(8,128)(2,1)S(1)}, u32[]{:S(2)}, u32[]{:S(2)}) %collective-permute-start.1) | collective-permute-done | bytes 131104 | tf_op jit(solution)/shard_map/ppermute | solution.py:175
  35.1 1.1 add_convert_fusion.7
  37.7 2.6 %collective-permute-done.4 = bf16[128,512]{1,0:T(8,128)(2,1)S(1)} collective-permute-done((bf16[128,512]{1,0:T(8,128)(2,1)S(1)}, bf16[128,512]{1,0:T(8,128)(2,1)S(1)}, u32[]{:S(2)}, u32[]{:S(2)}) %collective-permute-start.4) | collective-permute-done | bytes 131104 | tf_op jit(solution)/shard_map/ppermute | solution.py:175
  40.4 1.7 %collective-permute-done.3 = bf16[128,512]{1,0:T(8,128)(2,1)S(1)} collective-permute-done((bf16[128,512]{1,0:T(8,128)(2,1)S(1)}, bf16[128,512]{1,0:T(8,128)(2,1)S(1)}, u32[]{:S(2)}, u32[]{:S(2)}) %collective-permute-start.3) | collective-permute-done | bytes 131104 | tf_op jit(solution)/shard_map/ppermute | solution.py:175
  42.1 1.1 add_convert_fusion.5
  43.3 1.5 collective-permute-start.5
  44.8 2.6 %collective-permute-done.6 = bf16[128,512]{1,0:T(8,128)(2,1)S(1)} collective-permute-done((bf16[128,512]{1,0:T(8,128)(2,1)S(1)}, bf16[128,512]{1,0:T(8,128)(2,1)S(1)}, u32[]{:S(2)}, u32[]{:S(2)}) %collective-permute-start.6) | collective-permute-done | bytes 131104 | tf_op jit(solution)/shard_map/ppermute | solution.py:175
  47.4 1.3 collective-permute-done.5
  48.7 1.1 multiply_reduce_fusion.1
  50.5 2.5 %collective-permute-start.12 = (f32[128]{0:T(128)S(1)}, f32[128]{0:T(128)S(1)}, u32[]{:S(2)}, u32[]{:S(2)}) collective-permute-start(f32[128]{0:T(128)S(1)} %multiply_reduce_fusion.1), channel_id=1, source_target_pairs={{0,6},{1,7},{2,0},{3,1},{4,2},{5,3},{6,4},{7,5},{8,14},{9,15},{10,... | collective-permute-start | bytes 1544 | tf_op jit(solution)/shard_map/ppermute | solution.py:189
  53.2 1.1 collective-permute-start.11
  54.3 3.3 %collective-permute-start.10 = (f32[128]{0:T(128)S(1)}, f32[128]{0:T(128)S(1)}, u32[]{:S(2)}, u32[]{:S(2)}) collective-permute-start(f32[128]{0:T(128)S(1)} %multiply_reduce_fusion.1), channel_id=1, source_target_pairs={{0,4},{1,5},{2,6},{3,7},{4,0},{5,1},{6,2},{7,3},{8,12},{9,13},{10,... | collective-permute-start | bytes 1544 | tf_op jit(solution)/shard_map/ppermute | solution.py:189
  58.1 2.9 %collective-permute-start.8 = (f32[128]{0:T(128)S(1)}, f32[128]{0:T(128)S(1)}, u32[]{:S(2)}, u32[]{:S(2)}) collective-permute-start(f32[128]{0:T(128)S(1)} %multiply_reduce_fusion.1), channel_id=1, source_target_pairs={{0,2},{1,3},{2,4},{3,5},{4,6},{5,7},{6,0},{7,1},{8,10},{9,11},{10,... | collective-permute-start | bytes 1544 | tf_op jit(solution)/shard_map/ppermute | solution.py:189
  60.9 1.4 collective-permute-start.7
  63.0 1.5 collective-permute-done.7
  64.6 1.0 multiply_convert_fusion.1
  65.7 4.8 %band_rows.1 = (bf16[32,48,512]{2,1,0:T(8,128)(2,1)S(1)}, bf16[3,64,512]{2,1,0:T(8,128)(2,1)S(1)}) custom-call(s32[3]{0:T(128)S(1)} %and_select_fusion.turns, bf16[32,64,512]{2,1,0:T(8,128)(2,1)S(1)} %all-to-all-done.got, f32[3,3,512]{2,1,0:T(4,128)S(1)} %copy-done.9, f32[16,512]{1,0:T(8,128)S(1)} %copy-done.5, f32[16,512]{1,0:T(8,128)S(1)} %copy-done.7, ...), custom_call_target="tpu_custom_call" | custom-call | tf_op jit(solution)/shard_map/band_rows/pallas_call | solution.py:251
  70.5 3.7 %fusion.4 = f32[192,4096]{1,0:T(8,128)S(1)} fusion(bf16[192,512]{1,0:T(8,128)(2,1)S(1)} %bitcast.34, bf16[512,4096]{1,0:T(8,128)(2,1)} %param.18), kind=kOutput, calls=%fused_computation.41 | convolution fusion | flops 805306368 | bytes 7536640 | tf_op jit(solution)/shard_map/dot_general | solution.py:15
  74.6 2.5 %collective-permute-start.16 = (bf16[192,512]{1,0:T(8,128)(2,1)S(1)}, bf16[192,512]{1,0:T(8,128)(2,1)S(1)}, u32[]{:S(2)}, u32[]{:S(2)}) collective-permute-start(bf16[192,512]{1,0:T(8,128)(2,1)S(1)} %get-tuple-element.61), channel_id=1, source_target_pairs={{0,7},{1,0},{2,1},{3,2},{4,3},{5,4},{6,5},{7,6},{8,15},{9,8},{10,9... | collective-permute-start | bytes 589832 | tf_op jit(solution)/shard_map/ppermute | solution.py:175
  77.1 3.1 %collective-permute-done.14 = bf16[192,512]{1,0:T(8,128)(2,1)S(1)} collective-permute-done((bf16[192,512]{1,0:T(8,128)(2,1)S(1)}, bf16[192,512]{1,0:T(8,128)(2,1)S(1)}, u32[]{:S(2)}, u32[]{:S(2)}) %collective-permute-start.14) | collective-permute-done | bytes 196640 | tf_op jit(solution)/shard_map/ppermute | solution.py:175
  80.3 7.9 %collective-permute-done.15 = bf16[192,512]{1,0:T(8,128)(2,1)S(1)} collective-permute-done((bf16[192,512]{1,0:T(8,128)(2,1)S(1)}, bf16[192,512]{1,0:T(8,128)(2,1)S(1)}, u32[]{:S(2)}, u32[]{:S(2)}) %collective-permute-start.15) | collective-permute-done | bytes 196640 | tf_op jit(solution)/shard_map/ppermute | solution.py:175
  88.4 1.5 collective-permute-start.17
  90.8 15.9 %all-to-all-start.1 = ((bf16[32,48,512]{2,1,0:T(8,128)(2,1)}), bf16[32,48,512]{2,1,0:T(8,128)(2,1)S(1)}, u32[]{:S(2)}, u32[]{:S(2)}) async-start(bf16[32,48,512]{2,1,0:T(8,128)(2,1)} %copy-done.3), calls=%async_computation.1 | async-start | bytes 3145728 | tf_op jit(solution)/shard_map/all_to_all | solution.py:272
  106.8 1.2 add_convert_fusion
  108.0 1.1 collective-permute-start.20
  110.3 4.0 %collective-permute-done.20 = bf16[192,512]{1,0:T(8,128)(2,1)S(1)} collective-permute-done((bf16[192,512]{1,0:T(8,128)(2,1)S(1)}, bf16[192,512]{1,0:T(8,128)(2,1)S(1)}, u32[]{:S(2)}, u32[]{:S(2)}) %collective-permute-start.20) | collective-permute-done | bytes 196640 | tf_op jit(solution)/shard_map/ppermute | solution.py:175
  114.4 1.9 %collective-permute-done.19 = bf16[192,512]{1,0:T(8,128)(2,1)S(1)} collective-permute-done((bf16[192,512]{1,0:T(8,128)(2,1)S(1)}, bf16[192,512]{1,0:T(8,128)(2,1)S(1)}, u32[]{:S(2)}, u32[]{:S(2)}) %collective-permute-start.19) | collective-permute-done | bytes 196640 | tf_op jit(solution)/shard_map/ppermute | solution.py:175
  116.3 1.2 multiply_reduce_fusion
  118.7 2.8 %collective-permute-start.25 = (f32[192]{0:T(256)S(1)}, f32[192]{0:T(256)S(1)}, u32[]{:S(2)}, u32[]{:S(2)}) collective-permute-start(f32[192]{0:T(256)S(1)} %multiply_reduce_fusion), channel_id=1, source_target_pairs={{0,5},{1,6},{2,7},{3,0},{4,1},{5,2},{6,3},{7,4},{8,13},{9,14},{10,... | collective-permute-start | bytes 2312 | tf_op jit(solution)/shard_map/ppermute | solution.py:189
  121.5 2.9 %collective-permute-start.24 = (f32[192]{0:T(256)S(1)}, f32[192]{0:T(256)S(1)}, u32[]{:S(2)}, u32[]{:S(2)}) collective-permute-start(f32[192]{0:T(256)S(1)} %multiply_reduce_fusion), channel_id=1, source_target_pairs={{0,4},{1,5},{2,6},{3,7},{4,0},{5,1},{6,2},{7,3},{8,12},{9,13},{10,... | collective-permute-start | bytes 2312 | tf_op jit(solution)/shard_map/ppermute | solution.py:189
  124.4 1.2 collective-permute-start.23
  125.6 2.0 %collective-permute-start.22 = (f32[192]{0:T(256)S(1)}, f32[192]{0:T(256)S(1)}, u32[]{:S(2)}, u32[]{:S(2)}) collective-permute-start(f32[192]{0:T(256)S(1)} %multiply_reduce_fusion), channel_id=1, source_target_pairs={{0,2},{1,3},{2,4},{3,5},{4,6},{5,7},{6,0},{7,1},{8,10},{9,11},{10,... | collective-permute-start | bytes 2312 | tf_op jit(solution)/shard_map/ppermute | solution.py:189
  127.6 1.1 collective-permute-start.21
  128.7 1.4 collective-permute-done.23
  131.2 1.1 multiply_convert_fusion
  133.2 10.9 %all-to-all-start.2 = ((bf16[32,3,2,512]{3,2,1,0:T(2,128)(2,1)}), bf16[32,3,2,512]{3,2,1,0:T(2,128)(2,1)S(1)}, u32[]{:S(2)}, u32[]{:S(2)}) async-start(bf16[32,3,2,512]{3,2,1,0:T(2,128)(2,1)} %bitcast.31), calls=%async_computation.2 | async-start | bytes 393216 | tf_op jit(solution)/shard_map/all_to_all | solution.py:277
  144.7 1.3 copy.35
  146.3 1.8 %pad_maximum_fusion = f32[80,16,512]{2,1,0:T(8,128)} fusion(f32[16,16,512]{2,1,0:T(8,128)S(1)} %get-tuple-element.44, f32[64,16,512]{2,1,0:T(8,128)S(1)} %convert.1), kind=kLoop, calls=%fused_computation | loop fusion | flops 655360 | bytes 5242880 | tf_op jit(solution)/shard_map/concatenate | solution.py:285
  148.1 4.3 %all-to-all-done.2 = bf16[32,3,2,512]{3,2,1,0:T(2,128)(2,1)S(1)} async-done(((bf16[32,3,2,512]{3,2,1,0:T(2,128)(2,1)}), bf16[32,3,2,512]{3,2,1,0:T(2,128)(2,1)S(1)}, u32[]{:S(2)}, u32[]{:S(2)}) %all-to-all-start.2) | async-done | bytes 196640 | tf_op jit(solution)/shard_map/all_to_all | solution.py:277
  (96 shorter events, 17.8 us)
Async XLA Ops:
  2.5 1.7 %copy-start = (f32[80,16,512]{2,1,0:T(8,128)S(1)}, f32[80,16,512]{2,1,0:T(8,128)}, u32[]{:S(2)}) copy-start(f32[80,16,512]{2,1,0:T(8,128)} %state.1) | copy-start | bytes 7864324
  4.3 1.2 copy-start.2
  5.5 0.8 copy-start.4
  6.3 0.8 copy-start.6
  8.4 2.8 %copy-start.12 = (bf16[512,4096]{1,0:T(8,128)(2,1)S(1)}, bf16[512,4096]{1,0:T(8,128)(2,1)}, u32[]{:S(2)}) copy-start(bf16[512,4096]{1,0:T(8,128)(2,1)} %param.18) | copy-start | bytes 12582916
  11.2 1.3 copy-start.1
  12.6 1.3 copy-start.14
  13.9 14.3 %collective-permute-start = (bf16[128,512]{1,0:T(8,128)(2,1)S(1)}, bf16[128,512]{1,0:T(8,128)(2,1)S(1)}, u32[]{:S(2)}, u32[]{:S(2)}) collective-permute-start(bf16[128,512]{1,0:T(8,128)(2,1)S(1)} %get-tuple-element.68), channel_id=1, source_target_pairs={{0,1},{1,2},{2,3},{3,4},{4,5},{5,6},{6,7},{7,0},{8,9},{9,10},{10,1... | collective-permute-start | bytes 393224 | tf_op jit(solution)/shard_map/ppermute | solution.py:175
  16.4 49.3 %all-to-all-start = ((bf16[32,64,512]{2,1,0:T(8,128)(2,1)}), bf16[32,64,512]{2,1,0:T(8,128)(2,1)S(1)}, u32[]{:S(2)}, u32[]{:S(2)}) async-start(bf16[32,64,512]{2,1,0:T(8,128)(2,1)} %copy-done.1), calls=%async_computation | async-start | bytes 4194304 | tf_op jit(solution)/shard_map/all_to_all | solution.py:247
  24.4 28.6 %copy-start.17 = (s32[3,80]{1,0:T(4,128)S(1)}, s32[3,80]{1,0:T(4,128)}, u32[]{:S(2)}) copy-start(s32[3,80]{1,0:T(4,128)} %param.21) | copy-start | bytes 2884
  24.4 40.1 %copy-start.16 = (f32[512]{0:T(512)S(1)}, f32[512]{0:T(512)}, u32[]{:S(2)}) copy-start(f32[512]{0:T(512)} %param.19) | copy-start | bytes 6148
  24.4 41.2 %copy-start.5 = (f32[16,512]{1,0:T(8,128)S(1)}, f32[16,512]{1,0:T(8,128)}, u32[]{:S(2)}) copy-start(f32[16,512]{1,0:T(8,128)} %poles.3) | copy-start | bytes 98308
  24.5 41.2 %copy-start.7 = (f32[16,512]{1,0:T(8,128)S(1)}, f32[16,512]{1,0:T(8,128)}, u32[]{:S(2)}) copy-start(f32[16,512]{1,0:T(8,128)} %residues.3) | copy-start | bytes 98308
  24.5 41.2 %copy-start.9 = (f32[3,3,512]{2,1,0:T(4,128)S(1)}, f32[3,3,512]{2,1,0:T(4,128)}, u32[]{:S(2)}) copy-start(f32[3,3,512]{2,1,0:T(4,128)} %taps.3) | copy-start | bytes 55300
  24.5 41.2 %copy-start.11 = (f32[512]{0:T(512)S(1)}, f32[512]{0:T(512)}, u32[]{:S(2)}) copy-start(f32[512]{0:T(512)} %param.17) | copy-start | bytes 6148
  24.5 6.4 %collective-permute-start.2 = (bf16[128,512]{1,0:T(8,128)(2,1)S(1)}, bf16[128,512]{1,0:T(8,128)(2,1)S(1)}, u32[]{:S(2)}, u32[]{:S(2)}) collective-permute-start(bf16[128,512]{1,0:T(8,128)(2,1)S(1)} %get-tuple-element.67), channel_id=1, source_target_pairs={{0,7},{1,0},{2,1},{3,2},{4,3},{5,4},{6,5},{7,6},{8,15},{9,8},{10,9... | collective-permute-start | bytes 393224 | tf_op jit(solution)/shard_map/ppermute | solution.py:175
  29.2 5.8 %collective-permute-start.1 = (bf16[128,512]{1,0:T(8,128)(2,1)S(1)}, bf16[128,512]{1,0:T(8,128)(2,1)S(1)}, u32[]{:S(2)}, u32[]{:S(2)}) collective-permute-start(bf16[128,512]{1,0:T(8,128)(2,1)S(1)} %add_convert_fusion.9), channel_id=1, source_target_pairs={{0,1},{1,2},{2,3},{3,4},{4,5},{5,6},{6,7},{7,0},{8,9},{9,10},{10,1... | collective-permute-start | bytes 393224 | tf_op jit(solution)/shard_map/ppermute | solution.py:175
  36.2 4.2 %collective-permute-start.4 = (bf16[128,512]{1,0:T(8,128)(2,1)S(1)}, bf16[128,512]{1,0:T(8,128)(2,1)S(1)}, u32[]{:S(2)}, u32[]{:S(2)}) collective-permute-start(bf16[128,512]{1,0:T(8,128)(2,1)S(1)} %get-tuple-element.65), channel_id=1, source_target_pairs={{0,7},{1,0},{2,1},{3,2},{4,3},{5,4},{6,5},{7,6},{8,15},{9,8},{10,9... | collective-permute-start | bytes 393224 | tf_op jit(solution)/shard_map/ppermute | solution.py:175
  36.8 5.3 %collective-permute-start.3 = (bf16[128,512]{1,0:T(8,128)(2,1)S(1)}, bf16[128,512]{1,0:T(8,128)(2,1)S(1)}, u32[]{:S(2)}, u32[]{:S(2)}) collective-permute-start(bf16[128,512]{1,0:T(8,128)(2,1)S(1)} %get-tuple-element.66), channel_id=1, source_target_pairs={{0,1},{1,2},{2,3},{3,4},{4,5},{5,6},{6,7},{7,0},{8,9},{9,10},{10,1... | collective-permute-start | bytes 393224 | tf_op jit(solution)/shard_map/ppermute | solution.py:175
  43.2 4.2 %collective-permute-start.6 = (bf16[128,512]{1,0:T(8,128)(2,1)S(1)}, bf16[128,512]{1,0:T(8,128)(2,1)S(1)}, u32[]{:S(2)}, u32[]{:S(2)}) collective-permute-start(bf16[128,512]{1,0:T(8,128)(2,1)S(1)} %get-tuple-element.63), channel_id=1, source_target_pairs={{0,7},{1,0},{2,1},{3,2},{4,3},{5,4},{6,5},{7,6},{8,15},{9,8},{10,9... | collective-permute-start | bytes 393224 | tf_op jit(solution)/shard_map/ppermute | solution.py:175
  43.3 5.4 %collective-permute-start.5 = (bf16[128,512]{1,0:T(8,128)(2,1)S(1)}, bf16[128,512]{1,0:T(8,128)(2,1)S(1)}, u32[]{:S(2)}, u32[]{:S(2)}) collective-permute-start(bf16[128,512]{1,0:T(8,128)(2,1)S(1)} %get-tuple-element.64), channel_id=1, source_target_pairs={{0,1},{1,2},{2,3},{3,4},{4,5},{5,6},{6,7},{7,0},{8,9},{9,10},{10,1... | collective-permute-start | bytes 393224 | tf_op jit(solution)/shard_map/ppermute | solution.py:175
  49.8 8.3 %collective-permute-start.13 = (f32[128]{0:T(128)S(1)}, f32[128]{0:T(128)S(1)}, u32[]{:S(2)}, u32[]{:S(2)}) collective-permute-start(f32[128]{0:T(128)S(1)} %multiply_reduce_fusion.1), channel_id=1, source_target_pairs={{0,7},{1,0},{2,1},{3,2},{4,3},{5,4},{6,5},{7,6},{8,15},{9,8},{10,9... | collective-permute-start | bytes 1544 | tf_op jit(solution)/shard_map/ppermute | solution.py:189
  50.5 10.5 %collective-permute-start.12 = (f32[128]{0:T(128)S(1)}, f32[128]{0:T(128)S(1)}, u32[]{:S(2)}, u32[]{:S(2)}) collective-permute-start(f32[128]{0:T(128)S(1)} %multiply_reduce_fusion.1), channel_id=1, source_target_pairs={{0,6},{1,7},{2,0},{3,1},{4,2},{5,3},{6,4},{7,5},{8,14},{9,15},{10,... | collective-permute-start | bytes 1544 | tf_op jit(solution)/shard_map/ppermute | solution.py:189
  53.2 9.1 %collective-permute-start.11 = (f32[128]{0:T(128)S(1)}, f32[128]{0:T(128)S(1)}, u32[]{:S(2)}, u32[]{:S(2)}) collective-permute-start(f32[128]{0:T(128)S(1)} %multiply_reduce_fusion.1), channel_id=1, source_target_pairs={{0,5},{1,6},{2,7},{3,0},{4,1},{5,2},{6,3},{7,4},{8,13},{9,14},{10,... | collective-permute-start | bytes 1544 | tf_op jit(solution)/shard_map/ppermute | solution.py:189
  54.3 8.0 %collective-permute-start.10 = (f32[128]{0:T(128)S(1)}, f32[128]{0:T(128)S(1)}, u32[]{:S(2)}, u32[]{:S(2)}) collective-permute-start(f32[128]{0:T(128)S(1)} %multiply_reduce_fusion.1), channel_id=1, source_target_pairs={{0,4},{1,5},{2,6},{3,7},{4,0},{5,1},{6,2},{7,3},{8,12},{9,13},{10,... | collective-permute-start | bytes 1544 | tf_op jit(solution)/shard_map/ppermute | solution.py:189
  57.6 5.4 %collective-permute-start.9 = (f32[128]{0:T(128)S(1)}, f32[128]{0:T(128)S(1)}, u32[]{:S(2)}, u32[]{:S(2)}) collective-permute-start(f32[128]{0:T(128)S(1)} %multiply_reduce_fusion.1), channel_id=1, source_target_pairs={{0,3},{1,4},{2,5},{3,6},{4,7},{5,0},{6,1},{7,2},{8,11},{9,12},{10,... | collective-permute-start | bytes 1544 | tf_op jit(solution)/shard_map/ppermute | solution.py:189
  58.1 5.0 %collective-permute-start.8 = (f32[128]{0:T(128)S(1)}, f32[128]{0:T(128)S(1)}, u32[]{:S(2)}, u32[]{:S(2)}) collective-permute-start(f32[128]{0:T(128)S(1)} %multiply_reduce_fusion.1), channel_id=1, source_target_pairs={{0,2},{1,3},{2,4},{3,5},{4,6},{5,7},{6,0},{7,1},{8,10},{9,11},{10,... | collective-permute-start | bytes 1544 | tf_op jit(solution)/shard_map/ppermute | solution.py:189
  60.9 3.6 %collective-permute-start.7 = (f32[128]{0:T(128)S(1)}, f32[128]{0:T(128)S(1)}, u32[]{:S(2)}, u32[]{:S(2)}) collective-permute-start(f32[128]{0:T(128)S(1)} %multiply_reduce_fusion.1), channel_id=1, source_target_pairs={{0,1},{1,2},{2,3},{3,4},{4,5},{5,6},{6,7},{7,0},{8,9},{9,10},{10,1... | collective-permute-start | bytes 1544 | tf_op jit(solution)/shard_map/ppermute | solution.py:189
  65.6 63.1 %copy-start.15 = (bf16[128,512]{1,0:T(8,128)(2,1)}, bf16[128,512]{1,0:T(8,128)(2,1)S(1)}, u32[]{:S(2)}) copy-start(bf16[128,512]{1,0:T(8,128)(2,1)S(1)} %multiply_convert_fusion.1) | copy-start | bytes 393220
  70.5 20.4 %copy-start.3 = (bf16[32,48,512]{2,1,0:T(8,128)(2,1)}, bf16[32,48,512]{2,1,0:T(8,128)(2,1)S(1)}, u32[]{:S(2)}) copy-start(bf16[32,48,512]{2,1,0:T(8,128)(2,1)S(1)} %get-tuple-element.34) | copy-start | bytes 4718596
  74.3 13.9 %copy-start.13 = (f32[192,4096]{1,0:T(8,128)}, f32[192,4096]{1,0:T(8,128)S(1)}, u32[]{:S(2)}) copy-start(f32[192,4096]{1,0:T(8,128)S(1)} %fusion.4) | copy-start | bytes 9437188
  74.3 5.8 %collective-permute-start.14 = (bf16[192,512]{1,0:T(8,128)(2,1)S(1)}, bf16[192,512]{1,0:T(8,128)(2,1)S(1)}, u32[]{:S(2)}, u32[]{:S(2)}) collective-permute-start(bf16[192,512]{1,0:T(8,128)(2,1)S(1)} %get-tuple-element.62), channel_id=1, source_target_pairs={{0,1},{1,2},{2,3},{3,4},{4,5},{5,6},{6,7},{7,0},{8,9},{9,10},{10,1... | collective-permute-start | bytes 589832 | tf_op jit(solution)/shard_map/ppermute | solution.py:175
  74.6 5.7 %collective-permute-start.16 = (bf16[192,512]{1,0:T(8,128)(2,1)S(1)}, bf16[192,512]{1,0:T(8,128)(2,1)S(1)}, u32[]{:S(2)}, u32[]{:S(2)}) collective-permute-start(bf16[192,512]{1,0:T(8,128)(2,1)S(1)} %get-tuple-element.61), channel_id=1, source_target_pairs={{0,7},{1,0},{2,1},{3,2},{4,3},{5,4},{6,5},{7,6},{8,15},{9,8},{10,9... | collective-permute-start | bytes 589832 | tf_op jit(solution)/shard_map/ppermute | solution.py:175
  80.2 8.0 %collective-permute-start.15 = (bf16[192,512]{1,0:T(8,128)(2,1)S(1)}, bf16[192,512]{1,0:T(8,128)(2,1)S(1)}, u32[]{:S(2)}, u32[]{:S(2)}) collective-permute-start(bf16[192,512]{1,0:T(8,128)(2,1)S(1)} %add_convert_fusion.4), channel_id=1, source_target_pairs={{0,1},{1,2},{2,3},{3,4},{4,5},{5,6},{6,7},{7,0},{8,9},{9,10},{10,1... | collective-permute-start | bytes 589832 | tf_op jit(solution)/shard_map/ppermute | solution.py:175
  88.3 18.4 %collective-permute-start.18 = (bf16[192,512]{1,0:T(8,128)(2,1)S(1)}, bf16[192,512]{1,0:T(8,128)(2,1)S(1)}, u32[]{:S(2)}, u32[]{:S(2)}) collective-permute-start(bf16[192,512]{1,0:T(8,128)(2,1)S(1)} %get-tuple-element.59), channel_id=1, source_target_pairs={{0,7},{1,0},{2,1},{3,2},{4,3},{5,4},{6,5},{7,6},{8,15},{9,8},{10,9... | collective-permute-start | bytes 589832 | tf_op jit(solution)/shard_map/ppermute | solution.py:175
  88.4 18.4 %collective-permute-start.17 = (bf16[192,512]{1,0:T(8,128)(2,1)S(1)}, bf16[192,512]{1,0:T(8,128)(2,1)S(1)}, u32[]{:S(2)}, u32[]{:S(2)}) collective-permute-start(bf16[192,512]{1,0:T(8,128)(2,1)S(1)} %get-tuple-element.60), channel_id=1, source_target_pairs={{0,1},{1,2},{2,3},{3,4},{4,5},{5,6},{6,7},{7,0},{8,9},{9,10},{10,1... | collective-permute-start | bytes 589832 | tf_op jit(solution)/shard_map/ppermute | solution.py:175
  90.8 41.5 %all-to-all-start.1 = ((bf16[32,48,512]{2,1,0:T(8,128)(2,1)}), bf16[32,48,512]{2,1,0:T(8,128)(2,1)S(1)}, u32[]{:S(2)}, u32[]{:S(2)}) async-start(bf16[32,48,512]{2,1,0:T(8,128)(2,1)} %copy-done.3), calls=%async_computation.1 | async-start | bytes 3145728 | tf_op jit(solution)/shard_map/all_to_all | solution.py:272
  108.0 6.3 %collective-permute-start.20 = (bf16[192,512]{1,0:T(8,128)(2,1)S(1)}, bf16[192,512]{1,0:T(8,128)(2,1)S(1)}, u32[]{:S(2)}, u32[]{:S(2)}) collective-permute-start(bf16[192,512]{1,0:T(8,128)(2,1)S(1)} %get-tuple-element.57), channel_id=1, source_target_pairs={{0,7},{1,0},{2,1},{3,2},{4,3},{5,4},{6,5},{7,6},{8,15},{9,8},{10,9... | collective-permute-start | bytes 589832 | tf_op jit(solution)/shard_map/ppermute | solution.py:175
  109.1 7.2 %collective-permute-start.19 = (bf16[192,512]{1,0:T(8,128)(2,1)S(1)}, bf16[192,512]{1,0:T(8,128)(2,1)S(1)}, u32[]{:S(2)}, u32[]{:S(2)}) collective-permute-start(bf16[192,512]{1,0:T(8,128)(2,1)S(1)} %get-tuple-element.58), channel_id=1, source_target_pairs={{0,1},{1,2},{2,3},{3,4},{4,5},{5,6},{6,7},{7,0},{8,9},{9,10},{10,1... | collective-permute-start | bytes 589832 | tf_op jit(solution)/shard_map/ppermute | solution.py:175
  117.5 8.2 %collective-permute-start.27 = (f32[192]{0:T(256)S(1)}, f32[192]{0:T(256)S(1)}, u32[]{:S(2)}, u32[]{:S(2)}) collective-permute-start(f32[192]{0:T(256)S(1)} %multiply_reduce_fusion), channel_id=1, source_target_pairs={{0,7},{1,0},{2,1},{3,2},{4,3},{5,4},{6,5},{7,6},{8,15},{9,8},{10,9... | collective-permute-start | bytes 2312 | tf_op jit(solution)/shard_map/ppermute | solution.py:189
  117.8 9.7 %collective-permute-start.26 = (f32[192]{0:T(256)S(1)}, f32[192]{0:T(256)S(1)}, u32[]{:S(2)}, u32[]{:S(2)}) collective-permute-start(f32[192]{0:T(256)S(1)} %multiply_reduce_fusion), channel_id=1, source_target_pairs={{0,6},{1,7},{2,0},{3,1},{4,2},{5,3},{6,4},{7,5},{8,14},{9,15},{10,... | collective-permute-start | bytes 2312 | tf_op jit(solution)/shard_map/ppermute | solution.py:189
  118.7 10.0 %collective-permute-start.25 = (f32[192]{0:T(256)S(1)}, f32[192]{0:T(256)S(1)}, u32[]{:S(2)}, u32[]{:S(2)}) collective-permute-start(f32[192]{0:T(256)S(1)} %multiply_reduce_fusion), channel_id=1, source_target_pairs={{0,5},{1,6},{2,7},{3,0},{4,1},{5,2},{6,3},{7,4},{8,13},{9,14},{10,... | collective-permute-start | bytes 2312 | tf_op jit(solution)/shard_map/ppermute | solution.py:189
  121.5 7.3 %collective-permute-start.24 = (f32[192]{0:T(256)S(1)}, f32[192]{0:T(256)S(1)}, u32[]{:S(2)}, u32[]{:S(2)}) collective-permute-start(f32[192]{0:T(256)S(1)} %multiply_reduce_fusion), channel_id=1, source_target_pairs={{0,4},{1,5},{2,6},{3,7},{4,0},{5,1},{6,2},{7,3},{8,12},{9,13},{10,... | collective-permute-start | bytes 2312 | tf_op jit(solution)/shard_map/ppermute | solution.py:189
  124.4 5.7 %collective-permute-start.23 = (f32[192]{0:T(256)S(1)}, f32[192]{0:T(256)S(1)}, u32[]{:S(2)}, u32[]{:S(2)}) collective-permute-start(f32[192]{0:T(256)S(1)} %multiply_reduce_fusion), channel_id=1, source_target_pairs={{0,3},{1,4},{2,5},{3,6},{4,7},{5,0},{6,1},{7,2},{8,11},{9,12},{10,... | collective-permute-start | bytes 2312 | tf_op jit(solution)/shard_map/ppermute | solution.py:189
  125.6 4.8 %collective-permute-start.22 = (f32[192]{0:T(256)S(1)}, f32[192]{0:T(256)S(1)}, u32[]{:S(2)}, u32[]{:S(2)}) collective-permute-start(f32[192]{0:T(256)S(1)} %multiply_reduce_fusion), channel_id=1, source_target_pairs={{0,2},{1,3},{2,4},{3,5},{4,6},{5,7},{6,0},{7,1},{8,10},{9,11},{10,... | collective-permute-start | bytes 2312 | tf_op jit(solution)/shard_map/ppermute | solution.py:189
  127.6 3.6 %collective-permute-start.21 = (f32[192]{0:T(256)S(1)}, f32[192]{0:T(256)S(1)}, u32[]{:S(2)}, u32[]{:S(2)}) collective-permute-start(f32[192]{0:T(256)S(1)} %multiply_reduce_fusion), channel_id=1, source_target_pairs={{0,1},{1,2},{2,3},{3,4},{4,5},{5,6},{6,7},{7,0},{8,9},{9,10},{10,1... | collective-permute-start | bytes 2312 | tf_op jit(solution)/shard_map/ppermute | solution.py:189
  133.2 19.2 %all-to-all-start.2 = ((bf16[32,3,2,512]{3,2,1,0:T(2,128)(2,1)}), bf16[32,3,2,512]{3,2,1,0:T(2,128)(2,1)S(1)}, u32[]{:S(2)}, u32[]{:S(2)}) async-start(bf16[32,3,2,512]{3,2,1,0:T(2,128)(2,1)} %bitcast.31), calls=%async_computation.2 | async-start | bytes 393216 | tf_op jit(solution)/shard_map/all_to_all | solution.py:277
  146.3 6.4 %slice-start = ((bf16[128,512]{1,0:T(8,128)(2,1)}), bf16[48,512]{1,0:T(8,128)(2,1)S(1)}, s32[]{:S(2)}) async-start(bf16[128,512]{1,0:T(8,128)(2,1)} %copy-done.15), calls=%async_computation.3 | async-start | bytes 98304 | tf_op jit(solution)/shard_map/slice | solution.py:279
  (2 other events, 1.4 us)

commit v2 on v1

--- a/solution.py
+++ b/solution.py
@@ -19,10 +19,19 @@
     return jnp.concatenate([x] * (width // x.shape[-1]), axis=-1)
 
 
-def home_kernel(qkv, fir, taps, state, poles, residues, skip, alive, packed, gated, stay_state, y_rows):
+def home_kernel(qkv, fir, taps, state, poles, residues, skip, finished, packed, gated, stay_state, y_rows):
     block = pl.program_id(0)
     rows, width = 16, qkv.shape[-1]
-    alive0 = wide(alive[0], width)
+    at = lax.broadcasted_iota(jnp.int32, (rows, finished.shape[1]), 0) + block * rows
+    own = at == lax.broadcasted_iota(jnp.int32, at.shape, 1)
+    alive = [
+        jnp.broadcast_to(
+            1.0 - jnp.sum(jnp.where(own, finished[t : t + 1].astype(F32), 0.0), axis=1, keepdims=True),
+            (rows, width),
+        )
+        for t in range(3)
+    ]
+    alive0 = alive[0]
     q0 = [qkv[0, j].astype(F32) for j in range(3)]
     l0 = [fir[j, 0].astype(F32) for j in range(3)]
     f = [
@@ -44,8 +53,8 @@
             packed[pair, 0 : 2 * MODES] = both.astype(BF16)
         sent = [(x * alive0).astype(BF16) for x in q0 + l0]
         sent += [qkv[t, j] for t in range(1, 4) for j in range(3)]
-        ends = wide(alive[1], width // 2), wide(alive[2], width // 2)
-        sent.append(jnp.concatenate(ends, axis=-1).astype(BF16))
+        half = width // 2
+        sent.append(jnp.concatenate([alive[1][:, :half], alive[2][:, :half]], axis=-1).astype(BF16))
         stacked = jnp.concatenate(sent, axis=0)
         n = KINDS * rows
         r = lax.broadcasted_iota(jnp.int32, (n, n), 0)
@@ -67,7 +76,7 @@
                 for j in range(3)
             ]
             prod = g[1] * g[2]
-            live = wide(alive[t], width) if t < 3 else None
+            live = alive[t] if t < 3 else None
             for r in range(rows):
                 s = poles[...] * stay_state[r] + prod[r : r + 1]
                 y_rows[r : r + 1] = jnp.sum(residues[...] * s, axis=0, keepdims=True)
@@ -156,39 +165,53 @@
     return pl.BlockSpec(shape, lambda *_: (0,) * len(shape))
 
 
-def ring_sums(part, own_cols):
+def swap(blocks):
+    return lax.all_to_all(blocks, "dp", split_axis=0, concat_axis=0, tiled=True)
+
+
+def ring_sums(gated, weight, block=None):
     n = lax.axis_size("tensor")
     me = lax.axis_index("tensor")
-
-    def piece(away):
-        return lax.dynamic_slice_in_dim(part, ((me + away) % n) * own_cols, own_cols, 1)
-
-    right = left = None
-    for away in range(n // 2, 0, -1):
-        held = [right, left]
-        for side, step in enumerate((1, -1)):
-            if step == -1 and away > (n - 1) // 2:
-                continue
-            mine = piece(step * away)
-            held[side] = (mine if held[side] is None else mine + held[side].astype(F32)).astype(BF16)
-        held = [
-            x if x is None else lax.ppermute(x, "tensor", [(i, (i + step) % n) for i in range(n)])
-            for x, step in zip(held, (1, -1))
-        ]
-        right, left = lax.optimization_barrier(tuple(held))
-    total = piece(0) + right.astype(F32)
-    return total if left is None else total + left.astype(F32)
-
-
-def normed(part, gain):
+    own_cols = weight.shape[1] // n
+    half = gated.shape[0] // 2
+
+    def piece(away, rows):
+        return dot(rows, lax.dynamic_slice_in_dim(weight, ((me + away) % n) * own_cols, own_cols, 1))
+
+    def pass_on(right, left):
+        right = lax.ppermute(right, "tensor", [(i, (i + 1) % n) for i in range(n)])
+        left = lax.ppermute(left, "tensor", [(i, (i - 1) % n) for i in range(n)])
+        return right, left
+
+    far = piece(n // 2, gated).astype(BF16)
+    right, left = pass_on(far[:half], far[half:])
+    ahead, behind = piece(n // 2 - 1, gated), piece(1 - n // 2, gated)
+    for away in range(n // 2 - 1, 0, -1):
+        right, left, gated, block = lax.optimization_barrier((right, left, gated, block))
+        if right.shape[0] == half:
+            if block is not None:
+                block = swap(block)
+            ahead = jnp.concatenate([ahead[:half] + right.astype(F32), ahead[half:]], axis=0)
+            behind = jnp.concatenate([behind[:half], behind[half:] + left.astype(F32)], axis=0)
+            swapped, block = block, None
+        else:
+            ahead, behind = ahead + right.astype(F32), behind + left.astype(F32)
+        right, left = pass_on(ahead.astype(BF16), behind.astype(BF16))
+        ahead = lax.optimization_barrier(piece(away - 1, gated))
+        behind = lax.optimization_barrier(piece(1 - away, gated)) if away > 1 else None
+    total = ahead + right.astype(F32) + left.astype(F32)
+    return total if swapped is None else lax.optimization_barrier((total, swapped))
+
+
+def row_scales(own):
     n = lax.axis_size("tensor")
-    own = ring_sums(part, gain.shape[0])
-    mine = jnp.sum(own * own, axis=1)
-    squares = mine
-    for away in range(1, n):
-        squares = squares + lax.ppermute(mine, "tensor", [(i, (i + away) % n) for i in range(n)])
-    scale = lax.rsqrt(squares / (n * gain.shape[0]) + 1e-05)
-    return (own * scale[:, None] * gain[None]).astype(BF16)
+    squares = jnp.concatenate([jnp.sum(x * x, axis=1) for x in own])
+    away = 1
+    while away < n:
+        pairs = [(i, (i + away) % n) for i in range(n)]
+        squares = squares + lax.ppermute(squares, "tensor", pairs)
+        away *= 2
+    return lax.rsqrt(squares / (n * own[0].shape[1]) + 1e-05)[:, None]
 
 
 def per_device(
@@ -210,12 +233,10 @@
     moving = groups * CAP
     qkv_kinds = jnp.transpose(qkv, (0, 2, 1, 3))
     fir_kinds = jnp.transpose(fir_buffer, (1, 2, 0, 3))
-    alive = jnp.broadcast_to((1 - finished).astype(F32)[:, :, None], (3, slots, 128))
     skip_row = skip[None]
     shifts = lax.dynamic_slice_in_dim(dest_group, own_group * CAP, 1, 1)[:, 0] - own_group + groups
     turns = jnp.cumsum(shifts).astype(jnp.int32) % groups
 
-    params = pltpu.CompilerParams(vmem_limit_bytes=32 * 1024 * 1024)
     packed, gated_home, stay_state = pl.pallas_call(
         home_kernel,
         grid=(slots // 16,),
@@ -227,7 +248,7 @@
             whole((MODES, width)),
             whole((MODES, width)),
             whole((1, width)),
-            pl.BlockSpec((3, 16, 128), lambda i: (0, i, 0)),
+            whole((3, slots)),
         ],
         out_specs=[
             pl.BlockSpec((8, 2 * MODES + 2 * KINDS, width), lambda i: (jnp.minimum(i, 3), 0, 0)),
@@ -240,13 +261,13 @@
             jax.ShapeDtypeStruct((16, MODES, width), F32),
         ],
         scratch_shapes=[pltpu.VMEM((16, width), F32)],
-        compiler_params=params,
+        compiler_params=pltpu.CompilerParams(vmem_limit_bytes=56 * 1024 * 1024),
         name="home_rows",
-    )(qkv_kinds, fir_kinds, fir_taps, modal_state, poles, residues, skip_row, alive)
-
-    got = lax.all_to_all(packed, "dp", split_axis=0, concat_axis=0, tiled=True)
-    mixed_home = normed(dot(gated_home, out_weight), norm_gain)
-    got, mixed_home = lax.optimization_barrier((got, mixed_home))
+    )(qkv_kinds, fir_kinds, fir_taps, modal_state, poles, residues, skip_row, finished)
+
+    got = swap(packed)
+    own_home = ring_sums(gated_home, out_weight)
+    got, own_home = lax.optimization_barrier((got, own_home))
 
     sent, gated_band = pl.pallas_call(
         band_kernel,
@@ -265,17 +286,18 @@
             pltpu.VMEM((3, moving, width), F32),
             pltpu.VMEM((3, moving, width), F32),
         ],
-        compiler_params=params,
+        compiler_params=pltpu.CompilerParams(vmem_limit_bytes=32 * 1024 * 1024),
         name="band_rows",
     )(turns, got, fir_taps, poles, residues, skip_row)
 
-    back = lax.all_to_all(sent, "dp", split_axis=0, concat_axis=0, tiled=True)
-    mixed_band = normed(dot(gated_band.reshape(3 * moving, width), out_weight), norm_gain)
+    own_band, back = ring_sums(gated_band.reshape(3 * moving, width), out_weight, sent)
+    scales = row_scales([own_band, own_home])
+    mixed_band = (own_band * scales[: 3 * moving] * norm_gain[None]).astype(BF16)
     own_cols = norm_gain.shape[0]
-    back, mixed_band = lax.optimization_barrier((back, mixed_band))
     mixed_band = jnp.transpose(mixed_band.reshape(3, groups, CAP, own_cols), (1, 0, 2, 3))
-    mixed_back = lax.all_to_all(mixed_band, "dp", split_axis=0, concat_axis=0, tiled=True)
+    mixed_back = swap(mixed_band)
     mixed_later = jnp.transpose(mixed_back, (1, 0, 2, 3)).reshape(3, moving, own_cols)
+    mixed_home = (own_home * scales[3 * moving :] * norm_gain[None]).astype(BF16)
     mixed_stay = mixed_home[slots:].reshape(3, 16, own_cols)
     mixed = jnp.concatenate(
         [mixed_home[None, :slots], jnp.concatenate([mixed_later, mixed_stay], axis=1)], axis=0

time: 154 us -> 146 us (0.948)
  matrix products: 4.46 us -> 21 us
  starting transfers between devices: 72.8 us -> 58.2 us
  local copies, waits for them, and re-layouts: 12.9 us -> 7.38 us
  other arithmetic: 14.5 us -> 9.48 us
  waiting for transfers between devices: 40 us -> 35.2 us
  Pallas kernels: 7.6 us -> 11.6 us
    dot_general x2 -> x16, matrix products: 4.46 us -> 21 us  [dot(): return jnp.dot(a, b, preferred_element_type=F32)]
    ppermute x28 -> x19, starting transfers between devices: 37.9 us -> 24.1 us  [the longest x8 16.8 us: pass_on(): left = lax.ppermute(left, 'tensor', [(i, (i - 1) % n) for i in range(n)])]
    ppermute x28 -> x19, waiting for transfers between devices: 35.6 us -> 27 us  [the longest x8 13.6 us: pass_on(): right = lax.ppermute(right, 'tensor', [(i, (i + 1) % n) for i in range(n)])]
    convert_element_type x9 -> x10, other arithmetic: 7.48 us -> 0.5 us  [the longest x8 0.3 us: ring_sums(): right, left = pass_on(ahead.astype(BF16), behind.astype(BF16))]
    unnamed x38 -> x26, local copies, waits for them, and re-layouts: 10.2 us -> 4.71 us
    all_to_all x3, waiting for transfers between devices: 4.33 us -> 8.24 us  [swap(): return lax.all_to_all(blocks, 'dp', split_axis=0, concat_axis=0, tiled=True)]
    pallas_call x1, Pallas kernels: 2.8 us -> 6.7 us  [per_device(): pl.pallas_call(home_kernel, grid=(slots // 16,), in_specs=[pl.BlockSpec((...]
    reduce_sum x2, other arithmetic: 2.24 us -> 0.22 us  [row_scales(): squares = jnp.concatenate([jnp.sum(x * x, axis=1) for x in own])]
  transfers between devices with their start and end apart: 31 -> 22, of which waited for: 16 -> 14; matrix products, arithmetic and copies ran while one was open for 10% -> 19% of each run, Pallas kernels for 0% -> 0%
where the time goes in v2:
time: 146 us; the launch traced here: 144 us
  starting transfers between devices  58.2 us (40%)
  waiting for transfers between devices  35.2 us (24%)
  matrix products  21 us (14%)
  Pallas kernels  11.6 us (8%)
  other arithmetic  9.48 us (6%)
  local copies, waits for them, and re-layouts  7.38 us (5%)
    all_to_all x3, starting transfers between devices, swap(): return lax.all_to_all(blocks, 'dp', split_axis=0, concat_axis=0, tiled=True)  34.1 us
    dot_general x16, matrix products, dot(): return jnp.dot(a, b, preferred_element_type=F32)  21 us
    ppermute x8, starting transfers between devices, pass_on(): left = lax.ppermute(left, 'tensor', [(i, (i - 1) % n) for i in range(n)])  16.8 us
    ppermute x8, waiting for transfers between devices, pass_on(): right = lax.ppermute(right, 'tensor', [(i, (i + 1) % n) for i in range(n)])  13.6 us
    all_to_all x3, waiting for transfers between devices, swap(): return lax.all_to_all(blocks, 'dp', split_axis=0, concat_axis=0, tiled=True)  8.24 us
    ppermute x3, waiting for transfers between devices, row_scales(): squares = squares + lax.ppermute(squares, 'tensor', pairs)  7.33 us
    pallas_call x1, Pallas kernels, per_device(): pl.pallas_call(home_kernel, grid=(slots // 16,), in_specs=[pl.BlockSpec((...  6.7 us
    ppermute x8, waiting for transfers between devices, pass_on(): left = lax.ppermute(left, 'tensor', [(i, (i - 1) % n) for i in range(n)])  6.06 us
  transfers between devices with their start and end apart: 22, of which 14 were waited for; matrix products, arithmetic and copies ran while one was open for 19% of the time, Pallas kernels for 0%

profile of v2, /device:TPU:1, one launch (start us, length us, event | category | flops | bytes accessed | tf_op | source)
XLA Modules:
  0.0 144.2 jit_solution(1640900840504823680)
XLA Ops:
  0.6 1.9 %copy.38 = bf16[80,3,2,512]{3,0,2,1:T(8,128)(2,1)} copy(bf16[80,3,2,512]{3,2,1,0:T(2,128)(2,1)} %param.12) | data formatting | bytes 983040 | tf_op args[1]
  2.5 6.7 %home_rows.1 = (bf16[32,64,512]{2,1,0:T(8,128)(2,1)}, bf16[128,512]{1,0:T(8,128)(2,1)}, f32[16,16,512]{2,1,0:T(8,128)}) custom-call(bf16[4,3,80,512]{3,2,1,0:T(8,128)(2,1)} %bitcast.56, bf16[3,2,80,512]{3,2,1,0:T(8,128)(2,1)} %bitcast.55, f32[3,3,512]{2,1,0:T(4,128)} %taps.3, f32[80,16,512]{2,1,0:T(8,128)} %state.1, f32[16,512]{1,0:T(8,128)} %poles.3, ...), custom_call_target="tpu_custom_call" | custom-call | tf_op jit(solution)/shard_map/home_rows/pallas_call | solution.py:240
  9.2 8.7 %all-to-all-start = ((bf16[32,64,512]{2,1,0:T(8,128)(2,1)}), bf16[32,64,512]{2,1,0:T(8,128)(2,1)S(1)}, u32[]{:S(2)}, u32[]{:S(2)}) async-start(bf16[32,64,512]{2,1,0:T(8,128)(2,1)} %get-tuple-element.31), calls=%async_computation | async-start | bytes 4194304 | tf_op jit(solution)/shard_map/all_to_all | solution.py:169
  18.0 1.3 convolution_convert_fusion.1
  19.3 5.7 %collective-permute-start.1 = (bf16[64,512]{1,0:T(8,128)(2,1)S(1)}, bf16[64,512]{1,0:T(8,128)(2,1)S(1)}, u32[]{:S(2)}, u32[]{:S(2)}) collective-permute-start(bf16[64,512]{1,0:T(8,128)(2,1)S(1)} %get-tuple-element.73), channel_id=1, source_target_pairs={{0,7},{1,0},{2,1},{3,2},{4,3},{5,4},{6,5},{7,6},{8,15},{9,8},{10,9... | collective-permute-start | bytes 196616 | tf_op jit(solution)/shard_map/ppermute | solution.py:183
  26.9 1.5 %bitcast_multiply_fusion = bf16[16,3,512]{2,0,1:T(8,128)(2,1)} fusion(bf16[4,80,3,512]{3,1,2,0:T(8,128)(2,1)} %param.11, bf16[16]{0:T(256)(128)(2,1)S(1)} %convert_bitcast_fusion), kind=kLoop, calls=%fused_computation.70 | loop fusion | flops 24576 | bytes 98336 | tf_op jit(solution)/shard_map/mul | solution.py:311
  28.4 1.3 fusion.18
  29.7 1.3 fusion.22
  31.2 2.7 %collective-permute-start.3 = (bf16[128,512]{1,0:T(8,128)(2,1)S(1)}, bf16[128,512]{1,0:T(8,128)(2,1)S(1)}, u32[]{:S(2)}, u32[]{:S(2)}) collective-permute-start(bf16[128,512]{1,0:T(8,128)(2,1)S(1)} %pad_maximum_fusion.5), channel_id=1, source_target_pairs={{0,7},{1,0},{2,1},{3,2},{4,3},{5,4},{6,5},{7,6},{8,15},{9,8},{10,9... | collective-permute-start | bytes 393224 | tf_op jit(solution)/shard_map/ppermute | solution.py:183
  34.1 1.3 fusion.14
  35.4 1.3 fusion.26
  36.7 2.7 %collective-permute-done.2 = bf16[128,512]{1,0:T(8,128)(2,1)S(1)} collective-permute-done((bf16[128,512]{1,0:T(8,128)(2,1)S(1)}, bf16[128,512]{1,0:T(8,128)(2,1)S(1)}, u32[]{:S(2)}, u32[]{:S(2)}) %collective-permute-start.2) | collective-permute-done | bytes 131104 | tf_op jit(solution)/shard_map/ppermute | solution.py:182
  39.4 1.3 fusion.2
  40.8 1.5 %collective-permute-start.4 = (bf16[128,512]{1,0:T(8,128)(2,1)S(1)}, bf16[128,512]{1,0:T(8,128)(2,1)S(1)}, u32[]{:S(2)}, u32[]{:S(2)}) collective-permute-start(bf16[128,512]{1,0:T(8,128)(2,1)S(1)} %add_convert_fusion.7), channel_id=1, source_target_pairs={{0,1},{1,2},{2,3},{3,4},{4,5},{5,6},{6,7},{7,0},{8,9},{9,10},{10,1... | collective-permute-start | bytes 393224 | tf_op jit(solution)/shard_map/ppermute | solution.py:182
  42.4 1.3 fusion.6
  43.6 1.0 collective-permute-done.5
  44.6 1.3 collective-permute-done.4
  46.3 2.5 %collective-permute-start.7 = (bf16[128,512]{1,0:T(8,128)(2,1)S(1)}, bf16[128,512]{1,0:T(8,128)(2,1)S(1)}, u32[]{:S(2)}, u32[]{:S(2)}) collective-permute-start(bf16[128,512]{1,0:T(8,128)(2,1)S(1)} %add_convert_fusion.4), channel_id=1, source_target_pairs={{0,7},{1,0},{2,1},{3,2},{4,3},{5,4},{6,5},{7,6},{8,15},{9,8},{10,9... | collective-permute-start | bytes 393224 | tf_op jit(solution)/shard_map/ppermute | solution.py:183
  48.8 1.3 fusion.10
  50.1 1.0 collective-permute-done.6
  51.2 4.9 %band_rows.1 = (bf16[32,48,512]{2,1,0:T(8,128)(2,1)S(1)}, bf16[3,64,512]{2,1,0:T(8,128)(2,1)S(1)}) custom-call(s32[3]{0:T(128)S(1)} %and_select_fusion.turns, bf16[32,64,512]{2,1,0:T(8,128)(2,1)S(1)} %all-to-all-done.got, f32[3,3,512]{2,1,0:T(4,128)S(1)} %copy-done.3, f32[16,512]{1,0:T(8,128)S(1)} %copy-done.1, f32[16,512]{1,0:T(8,128)S(1)} %copy-done.2, ...), custom_call_target="tpu_custom_call" | custom-call | tf_op jit(solution)/shard_map/band_rows/pallas_call | solution.py:272
  56.1 1.7 %convolution_convert_fusion = bf16[192,512]{1,0:T(8,128)(2,1)S(1)} fusion(bf16[192,512]{1,0:T(8,128)(2,1)S(1)} %bitcast.44, bf16[512,4096]{1,0:T(8,128)(2,1)} %param.18, s32[]{:T(128)S(6)} %select_n.93), kind=kOutput, calls=%fused_computation.1 | convolution fusion | flops 100761600 | bytes 917508 | tf_op jit(solution)/shard_map/dot_general | solution.py:15
  57.8 1.3 fusion.16
  59.1 1.3 fusion.20
  60.4 2.9 %collective-permute-start.9 = (bf16[96,512]{1,0:T(8,128)(2,1)S(1)}, bf16[96,512]{1,0:T(8,128)(2,1)S(1)}, u32[]{:S(2)}, u32[]{:S(2)}) collective-permute-start(bf16[96,512]{1,0:T(8,128)(2,1)S(1)} %get-tuple-element.71), channel_id=1, source_target_pairs={{0,7},{1,0},{2,1},{3,2},{4,3},{5,4},{6,5},{7,6},{8,15},{9,8},{10,9... | collective-permute-start | bytes 294920 | tf_op jit(solution)/shard_map/ppermute | solution.py:183
  63.4 1.5 %collective-permute-done.9 = bf16[96,512]{1,0:T(8,128)(2,1)S(1)} collective-permute-done((bf16[96,512]{1,0:T(8,128)(2,1)S(1)}, bf16[96,512]{1,0:T(8,128)(2,1)S(1)}, u32[]{:S(2)}, u32[]{:S(2)}) %collective-permute-start.9) | collective-permute-done | bytes 98336 | tf_op jit(solution)/shard_map/ppermute | solution.py:183
  64.9 3.0 %collective-permute-done.8 = bf16[96,512]{1,0:T(8,128)(2,1)S(1)} collective-permute-done((bf16[96,512]{1,0:T(8,128)(2,1)S(1)}, bf16[96,512]{1,0:T(8,128)(2,1)S(1)}, u32[]{:S(2)}, u32[]{:S(2)}) %collective-permute-start.8) | collective-permute-done | bytes 98336 | tf_op jit(solution)/shard_map/ppermute | solution.py:182
  68.6 13.1 %all-to-all-start.1 = ((bf16[32,48,512]{2,1,0:T(8,128)(2,1)}), bf16[32,48,512]{2,1,0:T(8,128)(2,1)S(1)}, u32[]{:S(2)}, u32[]{:S(2)}) async-start(bf16[32,48,512]{2,1,0:T(8,128)(2,1)} %copy-done), calls=%async_computation.1 | async-start | bytes 3145728 | tf_op jit(solution)/shard_map/all_to_all | solution.py:169
  83.7 1.5 %collective-permute-start.10 = (bf16[192,512]{1,0:T(8,128)(2,1)S(1)}, bf16[192,512]{1,0:T(8,128)(2,1)S(1)}, u32[]{:S(2)}, u32[]{:S(2)}) collective-permute-start(bf16[192,512]{1,0:T(8,128)(2,1)S(1)} %pad_maximum_fusion.2), channel_id=1, source_target_pairs={{0,1},{1,2},{2,3},{3,4},{4,5},{5,6},{6,7},{7,0},{8,9},{9,10},{10,1... | collective-permute-start | bytes 589832 | tf_op jit(solution)/shard_map/ppermute | solution.py:182
  85.2 1.3 fusion.12
  86.5 1.3 fusion.24
  87.8 1.2 collective-permute-done.11
  89.0 2.2 %collective-permute-done.10 = bf16[192,512]{1,0:T(8,128)(2,1)S(1)} collective-permute-done((bf16[192,512]{1,0:T(8,128)(2,1)S(1)}, bf16[192,512]{1,0:T(8,128)(2,1)S(1)}, u32[]{:S(2)}, u32[]{:S(2)}) %collective-permute-start.10) | collective-permute-done | bytes 196640 | tf_op jit(solution)/shard_map/ppermute | solution.py:182
  91.3 1.3 fusion
  92.7 1.5 %collective-permute-start.12 = (bf16[192,512]{1,0:T(8,128)(2,1)S(1)}, bf16[192,512]{1,0:T(8,128)(2,1)S(1)}, u32[]{:S(2)}, u32[]{:S(2)}) collective-permute-start(bf16[192,512]{1,0:T(8,128)(2,1)S(1)} %add_convert_fusion.3), channel_id=1, source_target_pairs={{0,1},{1,2},{2,3},{3,4},{4,5},{5,6},{6,7},{7,0},{8,9},{9,10},{10,1... | collective-permute-start | bytes 589832 | tf_op jit(solution)/shard_map/ppermute | solution.py:182
  94.3 1.3 fusion.4
  95.6 2.4 %collective-permute-done.13 = bf16[192,512]{1,0:T(8,128)(2,1)S(1)} collective-permute-done((bf16[192,512]{1,0:T(8,128)(2,1)S(1)}, bf16[192,512]{1,0:T(8,128)(2,1)S(1)}, u32[]{:S(2)}, u32[]{:S(2)}) %collective-permute-start.13) | collective-permute-done | bytes 196640 | tf_op jit(solution)/shard_map/ppermute | solution.py:183
  98.0 1.4 collective-permute-done.12
  99.6 2.7 %collective-permute-start.15 = (bf16[192,512]{1,0:T(8,128)(2,1)S(1)}, bf16[192,512]{1,0:T(8,128)(2,1)S(1)}, u32[]{:S(2)}, u32[]{:S(2)}) collective-permute-start(bf16[192,512]{1,0:T(8,128)(2,1)S(1)} %add_convert_fusion), channel_id=1, source_target_pairs={{0,7},{1,0},{2,1},{3,2},{4,3},{5,4},{6,5},{7,6},{8,15},{9,8},{10,9... | collective-permute-start | bytes 589832 | tf_op jit(solution)/shard_map/ppermute | solution.py:183
  102.3 1.3 fusion.8
  103.6 1.9 %collective-permute-done.14 = bf16[192,512]{1,0:T(8,128)(2,1)S(1)} collective-permute-done((bf16[192,512]{1,0:T(8,128)(2,1)S(1)}, bf16[192,512]{1,0:T(8,128)(2,1)S(1)}, u32[]{:S(2)}, u32[]{:S(2)}) %collective-permute-start.14) | collective-permute-done | bytes 196640 | tf_op jit(solution)/shard_map/ppermute | solution.py:182
  107.1 3.0 %pad_maximum_fusion = f32[80,16,512]{2,1,0:T(8,128)} fusion(f32[16,16,512]{2,1,0:T(8,128)} %get-tuple-element.58, f32[64,16,512]{2,1,0:T(8,128)S(1)} %convert.37), kind=kLoop, calls=%fused_computation | loop fusion | flops 655360 | bytes 5242880 | tf_op jit(solution)/shard_map/concatenate | solution.py:307
  111.5 3.6 %collective-permute-done.17 = f32[320]{0:T(512)S(1)} collective-permute-done((f32[320]{0:T(512)S(1)}, f32[320]{0:T(512)S(1)}, u32[]{:S(2)}, u32[]{:S(2)}) %collective-permute-start.17) | collective-permute-done | bytes 1312 | tf_op jit(solution)/shard_map/ppermute | solution.py:212
  115.1 1.3 collective-permute-start.18
  116.5 1.3 copy.35
  117.8 3.7 %collective-permute-done.18 = f32[320]{0:T(512)S(1)} collective-permute-done((f32[320]{0:T(512)S(1)}, f32[320]{0:T(512)S(1)}, u32[]{:S(2)}, u32[]{:S(2)}) %collective-permute-start.18) | collective-permute-done | bytes 1312 | tf_op jit(solution)/shard_map/ppermute | solution.py:212
  122.6 12.3 %all-to-all-start.2 = ((bf16[32,3,2,512]{3,2,1,0:T(2,128)(2,1)}), bf16[32,3,2,512]{3,2,1,0:T(2,128)(2,1)S(1)}, u32[]{:S(2)}, u32[]{:S(2)}) async-start(bf16[32,3,2,512]{3,2,1,0:T(2,128)(2,1)} %bitcast.43), calls=%async_computation.2 | async-start | bytes 393216 | tf_op jit(solution)/shard_map/all_to_all | solution.py:169
  135.0 8.2 %all-to-all-done.2 = bf16[32,3,2,512]{3,2,1,0:T(2,128)(2,1)S(1)} async-done(((bf16[32,3,2,512]{3,2,1,0:T(2,128)(2,1)}), bf16[32,3,2,512]{3,2,1,0:T(2,128)(2,1)S(1)}, u32[]{:S(2)}, u32[]{:S(2)}) %all-to-all-start.2) | async-done | bytes 196640 | tf_op jit(solution)/shard_map/all_to_all | solution.py:169
  (98 shorter events, 10.9 us)
Async XLA Ops:
  2.5 24.2 %copy-start.11 = (s32[3,80]{1,0:T(4,128)S(1)}, s32[3,80]{1,0:T(4,128)}, u32[]{:S(2)}) copy-start(s32[3,80]{1,0:T(4,128)} %param.21) | copy-start | bytes 2884
  9.2 8.8 %copy-start.5 = (bf16[128,512]{1,0:T(8,128)(2,1)S(1)}, bf16[128,512]{1,0:T(8,128)(2,1)}, u32[]{:S(2)}) copy-start(bf16[128,512]{1,0:T(8,128)(2,1)} %get-tuple-element.39) | copy-start | bytes 393220
  9.2 41.9 %all-to-all-start = ((bf16[32,64,512]{2,1,0:T(8,128)(2,1)}), bf16[32,64,512]{2,1,0:T(8,128)(2,1)S(1)}, u32[]{:S(2)}, u32[]{:S(2)}) async-start(bf16[32,64,512]{2,1,0:T(8,128)(2,1)} %get-tuple-element.31), calls=%async_computation | async-start | bytes 4194304 | tf_op jit(solution)/shard_map/all_to_all | solution.py:169
  19.3 11.8 %collective-permute-start.1 = (bf16[64,512]{1,0:T(8,128)(2,1)S(1)}, bf16[64,512]{1,0:T(8,128)(2,1)S(1)}, u32[]{:S(2)}, u32[]{:S(2)}) collective-permute-start(bf16[64,512]{1,0:T(8,128)(2,1)S(1)} %get-tuple-element.73), channel_id=1, source_target_pairs={{0,7},{1,0},{2,1},{3,2},{4,3},{5,4},{6,5},{7,6},{8,15},{9,8},{10,9... | collective-permute-start | bytes 196616 | tf_op jit(solution)/shard_map/ppermute | solution.py:183
  24.9 6.2 %collective-permute-start = (bf16[64,512]{1,0:T(8,128)(2,1)S(1)}, bf16[64,512]{1,0:T(8,128)(2,1)S(1)}, u32[]{:S(2)}, u32[]{:S(2)}) collective-permute-start(bf16[64,512]{1,0:T(8,128)(2,1)S(1)} %get-tuple-element.74), channel_id=1, source_target_pairs={{0,1},{1,2},{2,3},{3,4},{4,5},{5,6},{6,7},{7,0},{8,9},{9,10},{10,1... | collective-permute-start | bytes 196616 | tf_op jit(solution)/shard_map/ppermute | solution.py:182
  31.1 20.0 %copy-start.1 = (f32[16,512]{1,0:T(8,128)S(1)}, f32[16,512]{1,0:T(8,128)}, u32[]{:S(2)}) copy-start(f32[16,512]{1,0:T(8,128)} %poles.3) | copy-start | bytes 98308
  31.2 20.0 %copy-start.2 = (f32[16,512]{1,0:T(8,128)S(1)}, f32[16,512]{1,0:T(8,128)}, u32[]{:S(2)}) copy-start(f32[16,512]{1,0:T(8,128)} %residues.3) | copy-start | bytes 98308
  31.2 20.0 %copy-start.3 = (f32[3,3,512]{2,1,0:T(4,128)S(1)}, f32[3,3,512]{2,1,0:T(4,128)}, u32[]{:S(2)}) copy-start(f32[3,3,512]{2,1,0:T(4,128)} %taps.3) | copy-start | bytes 55300
  31.2 20.0 %copy-start.4 = (f32[512]{0:T(512)S(1)}, f32[512]{0:T(512)}, u32[]{:S(2)}) copy-start(f32[512]{0:T(512)} %param.17) | copy-start | bytes 6148
  31.2 5.4 %collective-permute-start.3 = (bf16[128,512]{1,0:T(8,128)(2,1)S(1)}, bf16[128,512]{1,0:T(8,128)(2,1)S(1)}, u32[]{:S(2)}, u32[]{:S(2)}) collective-permute-start(bf16[128,512]{1,0:T(8,128)(2,1)S(1)} %pad_maximum_fusion.5), channel_id=1, source_target_pairs={{0,7},{1,0},{2,1},{3,2},{4,3},{5,4},{6,5},{7,6},{8,15},{9,8},{10,9... | collective-permute-start | bytes 393224 | tf_op jit(solution)/shard_map/ppermute | solution.py:183
  34.0 5.4 %collective-permute-start.2 = (bf16[128,512]{1,0:T(8,128)(2,1)S(1)}, bf16[128,512]{1,0:T(8,128)(2,1)S(1)}, u32[]{:S(2)}, u32[]{:S(2)}) collective-permute-start(bf16[128,512]{1,0:T(8,128)(2,1)S(1)} %pad_maximum_fusion.4), channel_id=1, source_target_pairs={{0,1},{1,2},{2,3},{3,4},{4,5},{5,6},{6,7},{7,0},{8,9},{9,10},{10,1... | collective-permute-start | bytes 393224 | tf_op jit(solution)/shard_map/ppermute | solution.py:182
  40.7 3.9 %collective-permute-start.5 = (bf16[128,512]{1,0:T(8,128)(2,1)S(1)}, bf16[128,512]{1,0:T(8,128)(2,1)S(1)}, u32[]{:S(2)}, u32[]{:S(2)}) collective-permute-start(bf16[128,512]{1,0:T(8,128)(2,1)S(1)} %add_convert_fusion.6), channel_id=1, source_target_pairs={{0,7},{1,0},{2,1},{3,2},{4,3},{5,4},{6,5},{7,6},{8,15},{9,8},{10,9... | collective-permute-start | bytes 393224 | tf_op jit(solution)/shard_map/ppermute | solution.py:183
  40.8 5.1 %collective-permute-start.4 = (bf16[128,512]{1,0:T(8,128)(2,1)S(1)}, bf16[128,512]{1,0:T(8,128)(2,1)S(1)}, u32[]{:S(2)}, u32[]{:S(2)}) collective-permute-start(bf16[128,512]{1,0:T(8,128)(2,1)S(1)} %add_convert_fusion.7), channel_id=1, source_target_pairs={{0,1},{1,2},{2,3},{3,4},{4,5},{5,6},{6,7},{7,0},{8,9},{9,10},{10,1... | collective-permute-start | bytes 393224 | tf_op jit(solution)/shard_map/ppermute | solution.py:182
  46.0 5.1 %collective-permute-start.6 = (bf16[128,512]{1,0:T(8,128)(2,1)S(1)}, bf16[128,512]{1,0:T(8,128)(2,1)S(1)}, u32[]{:S(2)}, u32[]{:S(2)}) collective-permute-start(bf16[128,512]{1,0:T(8,128)(2,1)S(1)} %add_convert_fusion.5), channel_id=1, source_target_pairs={{0,1},{1,2},{2,3},{3,4},{4,5},{5,6},{6,7},{7,0},{8,9},{9,10},{10,1... | collective-permute-start | bytes 393224 | tf_op jit(solution)/shard_map/ppermute | solution.py:182
  46.3 4.8 %collective-permute-start.7 = (bf16[128,512]{1,0:T(8,128)(2,1)S(1)}, bf16[128,512]{1,0:T(8,128)(2,1)S(1)}, u32[]{:S(2)}, u32[]{:S(2)}) collective-permute-start(bf16[128,512]{1,0:T(8,128)(2,1)S(1)} %add_convert_fusion.4), channel_id=1, source_target_pairs={{0,7},{1,0},{2,1},{3,2},{4,3},{5,4},{6,5},{7,6},{8,15},{9,8},{10,9... | collective-permute-start | bytes 393224 | tf_op jit(solution)/shard_map/ppermute | solution.py:183
  56.0 11.9 %copy-start = (bf16[32,48,512]{2,1,0:T(8,128)(2,1)}, bf16[32,48,512]{2,1,0:T(8,128)(2,1)S(1)}, u32[]{:S(2)}) copy-start(bf16[32,48,512]{2,1,0:T(8,128)(2,1)S(1)} %get-tuple-element.55) | copy-start | bytes 4718596
  60.4 4.5 %collective-permute-start.9 = (bf16[96,512]{1,0:T(8,128)(2,1)S(1)}, bf16[96,512]{1,0:T(8,128)(2,1)S(1)}, u32[]{:S(2)}, u32[]{:S(2)}) collective-permute-start(bf16[96,512]{1,0:T(8,128)(2,1)S(1)} %get-tuple-element.71), channel_id=1, source_target_pairs={{0,7},{1,0},{2,1},{3,2},{4,3},{5,4},{6,5},{7,6},{8,15},{9,8},{10,9... | collective-permute-start | bytes 294920 | tf_op jit(solution)/shard_map/ppermute | solution.py:183
  63.3 4.7 %collective-permute-start.8 = (bf16[96,512]{1,0:T(8,128)(2,1)S(1)}, bf16[96,512]{1,0:T(8,128)(2,1)S(1)}, u32[]{:S(2)}, u32[]{:S(2)}) collective-permute-start(bf16[96,512]{1,0:T(8,128)(2,1)S(1)} %get-tuple-element.72), channel_id=1, source_target_pairs={{0,1},{1,2},{2,3},{3,4},{4,5},{5,6},{6,7},{7,0},{8,9},{9,10},{10,1... | collective-permute-start | bytes 294920 | tf_op jit(solution)/shard_map/ppermute | solution.py:182
  64.9 3.0 %copy-start.9 = (bf16[96,512]{1,0:T(8,128)(2,1)}, bf16[96,512]{1,0:T(8,128)(2,1)S(1)}, u32[]{:S(2)}) copy-start(bf16[96,512]{1,0:T(8,128)(2,1)S(1)} %collective-permute-done.9) | copy-start | bytes 294916
  68.0 0.6 copy-start.8
  68.6 36.9 %all-to-all-start.1 = ((bf16[32,48,512]{2,1,0:T(8,128)(2,1)}), bf16[32,48,512]{2,1,0:T(8,128)(2,1)S(1)}, u32[]{:S(2)}, u32[]{:S(2)}) async-start(bf16[32,48,512]{2,1,0:T(8,128)(2,1)} %copy-done), calls=%async_computation.1 | async-start | bytes 3145728 | tf_op jit(solution)/shard_map/all_to_all | solution.py:169
  82.7 6.3 %collective-permute-start.11 = (bf16[192,512]{1,0:T(8,128)(2,1)S(1)}, bf16[192,512]{1,0:T(8,128)(2,1)S(1)}, u32[]{:S(2)}, u32[]{:S(2)}) collective-permute-start(bf16[192,512]{1,0:T(8,128)(2,1)S(1)} %pad_maximum_fusion.3), channel_id=1, source_target_pairs={{0,7},{1,0},{2,1},{3,2},{4,3},{5,4},{6,5},{7,6},{8,15},{9,8},{10,9... | collective-permute-start | bytes 589832 | tf_op jit(solution)/shard_map/ppermute | solution.py:183
  83.7 7.5 %collective-permute-start.10 = (bf16[192,512]{1,0:T(8,128)(2,1)S(1)}, bf16[192,512]{1,0:T(8,128)(2,1)S(1)}, u32[]{:S(2)}, u32[]{:S(2)}) collective-permute-start(bf16[192,512]{1,0:T(8,128)(2,1)S(1)} %pad_maximum_fusion.2), channel_id=1, source_target_pairs={{0,1},{1,2},{2,3},{3,4},{4,5},{5,6},{6,7},{7,0},{8,9},{9,10},{10,1... | collective-permute-start | bytes 589832 | tf_op jit(solution)/shard_map/ppermute | solution.py:182
  92.6 5.4 %collective-permute-start.13 = (bf16[192,512]{1,0:T(8,128)(2,1)S(1)}, bf16[192,512]{1,0:T(8,128)(2,1)S(1)}, u32[]{:S(2)}, u32[]{:S(2)}) collective-permute-start(bf16[192,512]{1,0:T(8,128)(2,1)S(1)} %add_convert_fusion.2), channel_id=1, source_target_pairs={{0,7},{1,0},{2,1},{3,2},{4,3},{5,4},{6,5},{7,6},{8,15},{9,8},{10,9... | collective-permute-start | bytes 589832 | tf_op jit(solution)/shard_map/ppermute | solution.py:183
  92.7 6.6 %collective-permute-start.12 = (bf16[192,512]{1,0:T(8,128)(2,1)S(1)}, bf16[192,512]{1,0:T(8,128)(2,1)S(1)}, u32[]{:S(2)}, u32[]{:S(2)}) collective-permute-start(bf16[192,512]{1,0:T(8,128)(2,1)S(1)} %add_convert_fusion.3), channel_id=1, source_target_pairs={{0,1},{1,2},{2,3},{3,4},{4,5},{5,6},{6,7},{7,0},{8,9},{9,10},{10,1... | collective-permute-start | bytes 589832 | tf_op jit(solution)/shard_map/ppermute | solution.py:182
  99.4 6.1 %collective-permute-start.14 = (bf16[192,512]{1,0:T(8,128)(2,1)S(1)}, bf16[192,512]{1,0:T(8,128)(2,1)S(1)}, u32[]{:S(2)}, u32[]{:S(2)}) collective-permute-start(bf16[192,512]{1,0:T(8,128)(2,1)S(1)} %add_convert_fusion.1), channel_id=1, source_target_pairs={{0,1},{1,2},{2,3},{3,4},{4,5},{5,6},{6,7},{7,0},{8,9},{9,10},{10,1... | collective-permute-start | bytes 589832 | tf_op jit(solution)/shard_map/ppermute | solution.py:182
  99.6 5.9 %collective-permute-start.15 = (bf16[192,512]{1,0:T(8,128)(2,1)S(1)}, bf16[192,512]{1,0:T(8,128)(2,1)S(1)}, u32[]{:S(2)}, u32[]{:S(2)}) collective-permute-start(bf16[192,512]{1,0:T(8,128)(2,1)S(1)} %add_convert_fusion), channel_id=1, source_target_pairs={{0,7},{1,0},{2,1},{3,2},{4,3},{5,4},{6,5},{7,6},{8,15},{9,8},{10,9... | collective-permute-start | bytes 589832 | tf_op jit(solution)/shard_map/ppermute | solution.py:183
  105.6 1.2 copy-start.6
  105.8 4.7 %collective-permute-start.16 = (f32[320]{0:T(512)S(1)}, f32[320]{0:T(512)S(1)}, u32[]{:S(2)}, u32[]{:S(2)}) collective-permute-start(f32[320]{0:T(512)S(1)} %pad_maximum_fusion.6), channel_id=1, source_target_pairs={{0,1},{1,2},{2,3},{3,4},{4,5},{5,6},{6,7},{7,0},{8,9},{9,10},{10,1... | collective-permute-start | bytes 3848 | tf_op jit(solution)/shard_map/ppermute | solution.py:212
  106.8 3.3 %slice-start = ((bf16[32,48,512]{2,1,0:T(8,128)(2,1)}), bf16[32,6,512]{2,1,0:T(8,128)(2,1)S(1)}, s32[]{:S(2)}) async-start(bf16[32,48,512]{2,1,0:T(8,128)(2,1)} %copy-done.6), calls=%async_computation.3 | async-start | bytes 524288 | tf_op jit(solution)/shard_map/slice | solution.py:308
  107.1 4.4 %copy-start.7 = (bf16[16,3,512]{2,0,1:T(8,128)(2,1)S(1)}, bf16[16,3,512]{2,0,1:T(8,128)(2,1)}, u32[]{:S(2)}) copy-start(bf16[16,3,512]{2,0,1:T(8,128)(2,1)} %bitcast_multiply_fusion) | copy-start | bytes 147460
  107.1 14.5 %copy-start.10 = (f32[512]{0:T(512)S(1)}, f32[512]{0:T(512)}, u32[]{:S(2)}) copy-start(f32[512]{0:T(512)} %param.19) | copy-start | bytes 6148
  110.5 4.6 %collective-permute-start.17 = (f32[320]{0:T(512)S(1)}, f32[320]{0:T(512)S(1)}, u32[]{:S(2)}, u32[]{:S(2)}) collective-permute-start(f32[320]{0:T(512)S(1)} %fusion.53), channel_id=1, source_target_pairs={{0,2},{1,3},{2,4},{3,5},{4,6},{5,7},{6,0},{7,1},{8,10},{9,11},{10,... | collective-permute-start | bytes 3848 | tf_op jit(solution)/shard_map/ppermute | solution.py:212
  115.1 6.3 %collective-permute-start.18 = (f32[320]{0:T(512)S(1)}, f32[320]{0:T(512)S(1)}, u32[]{:S(2)}, u32[]{:S(2)}) collective-permute-start(f32[320]{0:T(512)S(1)} %add.212), channel_id=1, source_target_pairs={{0,4},{1,5},{2,6},{3,7},{4,0},{5,1},{6,2},{7,3},{8,12},{9,13},{10,... | collective-permute-start | bytes 3848 | tf_op jit(solution)/shard_map/ppermute | solution.py:212
  122.6 20.6 %all-to-all-start.2 = ((bf16[32,3,2,512]{3,2,1,0:T(2,128)(2,1)}), bf16[32,3,2,512]{3,2,1,0:T(2,128)(2,1)S(1)}, u32[]{:S(2)}, u32[]{:S(2)}) async-start(bf16[32,3,2,512]{3,2,1,0:T(2,128)(2,1)} %bitcast.43), calls=%async_computation.2 | async-start | bytes 393216 | tf_op jit(solution)/shard_map/all_to_all | solution.py:169

commit v3 on v2

--- a/solution.py
+++ b/solution.py
@@ -33,9 +33,10 @@
     ]
     alive0 = alive[0]
     q0 = [qkv[0, j].astype(F32) for j in range(3)]
-    l0 = [fir[j, 0].astype(F32) for j in range(3)]
+    l0 = [fir[:, j].astype(F32)[:, 0] for j in range(3)]
+    l1 = [fir[:, j].astype(F32)[:, 1] for j in range(3)]
     f = [
-        taps[j, 0:1] * q0[j] + taps[j, 1:2] * l0[j] + taps[j, 2:3] * fir[j, 1].astype(F32)
+        taps[j, 0:1] * q0[j] + taps[j, 1:2] * l0[j] + taps[j, 2:3] * l1[j]
         for j in range(3)
     ]
     product = f[1] * f[2]
@@ -89,10 +90,19 @@
 
 
 def band_kernel(
-    turns, got, taps, poles, residues, skip, sent, gated, lags, inputs, live, heads, products, y_rows
+    turns, place, got_hbm, weight_hbm, taps, poles, residues, skip, sent_hbm, far_hbm, part_hbm, *scratch
 ):
+    lags, inputs, live, heads, products, y_rows, got, weight, sent, far, part, sems = scratch
     groups, _, width = got.shape
     rows = 2 * groups
+    halves = [pl.ds(2 * MODES, 2 * KINDS), pl.ds(0, 2 * MODES)]
+    fetches = [
+        pltpu.make_async_copy(got_hbm.at[:, at], got.at[:, at], sems.at[i])
+        for i, at in enumerate(halves)
+    ] + [pltpu.make_async_copy(weight_hbm, weight, sems.at[2])]
+    for fetch in fetches:
+        fetch.start()
+    fetches[0].wait()
     kinds = got[:, 2 * MODES :].reshape(groups * 2 * KINDS, width)
 
     def taken(first, count, turn):
@@ -140,6 +150,8 @@
     last = lags[0:3].reshape(3 * rows, width).astype(BF16)
     sent[:, 2 * MODES :] = dot(order, last).reshape(groups, 16, width).astype(BF16)
 
+    fetches[1].wait()
+
     @pl.loop(0, groups)
     def _(g):
         final = []
@@ -158,7 +170,26 @@
         end = (g + turns[2]) & (groups - 1)
         sent[end, 0 : 2 * MODES] = jnp.concatenate(final, axis=0).astype(BF16)
 
-    gated[...] = y_rows[...].astype(BF16)
+    stores = [pltpu.make_async_copy(sent, sent_hbm, sems.at[3])]
+    stores[0].start()
+    fetches[2].wait()
+
+    gated = y_rows[...].reshape(3 * rows, width).astype(BF16)
+    n, _, own_cols = part.shape
+    for i in range(n):
+        away = (i + n // 2) % n
+        start = pl.multiple_of(((place[0] + away) % n) * own_cols, own_cols)
+        made = dot(gated, weight[:, pl.ds(start, own_cols)])
+        if away == n // 2:
+            far[...] = made.astype(BF16)
+            store = pltpu.make_async_copy(far, far_hbm, sems.at[4])
+        else:
+            part[away] = made
+            store = pltpu.make_async_copy(part.at[away], part_hbm.at[away], sems.at[5 + away])
+        store.start()
+        stores.append(store)
+    for store in stores:
+        store.wait()
 
 
 def whole(shape):
@@ -169,48 +200,35 @@
     return lax.all_to_all(blocks, "dp", split_axis=0, concat_axis=0, tiled=True)
 
 
-def ring_sums(gated, weight, block=None):
-    n = lax.axis_size("tensor")
-    me = lax.axis_index("tensor")
-    own_cols = weight.shape[1] // n
-    half = gated.shape[0] // 2
-
-    def piece(away, rows):
-        return dot(rows, lax.dynamic_slice_in_dim(weight, ((me + away) % n) * own_cols, own_cols, 1))
+def ring_sums(far, part, block):
+    n = part.shape[0]
+    half = far.shape[0] // 2
 
     def pass_on(right, left):
         right = lax.ppermute(right, "tensor", [(i, (i + 1) % n) for i in range(n)])
         left = lax.ppermute(left, "tensor", [(i, (i - 1) % n) for i in range(n)])
         return right, left
 
-    far = piece(n // 2, gated).astype(BF16)
     right, left = pass_on(far[:half], far[half:])
-    ahead, behind = piece(n // 2 - 1, gated), piece(1 - n // 2, gated)
+    right, left = lax.optimization_barrier((right, left))
     for away in range(n // 2 - 1, 0, -1):
-        right, left, gated, block = lax.optimization_barrier((right, left, gated, block))
+        ahead, behind = part[away], part[n - away]
         if right.shape[0] == half:
-            if block is not None:
-                block = swap(block)
-            ahead = jnp.concatenate([ahead[:half] + right.astype(F32), ahead[half:]], axis=0)
-            behind = jnp.concatenate([behind[:half], behind[half:] + left.astype(F32)], axis=0)
-            swapped, block = block, None
+            ahead = ahead.at[:half].add(right.astype(F32)).astype(BF16)
+            behind = behind.at[half:].add(left.astype(F32)).astype(BF16)
+            ahead, behind, block = lax.optimization_barrier((ahead, behind, block))
+            right, left = pass_on(ahead, behind)
+            block = swap(block)
         else:
             ahead, behind = ahead + right.astype(F32), behind + left.astype(F32)
-        right, left = pass_on(ahead.astype(BF16), behind.astype(BF16))
-        ahead = lax.optimization_barrier(piece(away - 1, gated))
-        behind = lax.optimization_barrier(piece(1 - away, gated)) if away > 1 else None
-    total = ahead + right.astype(F32) + left.astype(F32)
-    return total if swapped is None else lax.optimization_barrier((total, swapped))
+            right, left = pass_on(ahead.astype(BF16), behind.astype(BF16))
+        right, left = lax.optimization_barrier((right, left))
+    return lax.optimization_barrier((part[0] + right.astype(F32) + left.astype(F32), block))
 
 
 def row_scales(own):
     n = lax.axis_size("tensor")
-    squares = jnp.concatenate([jnp.sum(x * x, axis=1) for x in own])
-    away = 1
-    while away < n:
-        pairs = [(i, (i + away) % n) for i in range(n)]
-        squares = squares + lax.ppermute(squares, "tensor", pairs)
-        away *= 2
+    squares = lax.psum(jnp.concatenate([jnp.sum(x * x, axis=1) for x in own]), "tensor")
     return lax.rsqrt(squares / (n * own[0].shape[1]) + 1e-05)[:, None]
 
 
@@ -232,7 +250,6 @@
     slots, width = modal_state.shape[0], modal_state.shape[2]
     moving = groups * CAP
     qkv_kinds = jnp.transpose(qkv, (0, 2, 1, 3))
-    fir_kinds = jnp.transpose(fir_buffer, (1, 2, 0, 3))
     skip_row = skip[None]
     shifts = lax.dynamic_slice_in_dim(dest_group, own_group * CAP, 1, 1)[:, 0] - own_group + groups
     turns = jnp.cumsum(shifts).astype(jnp.int32) % groups
@@ -242,7 +259,7 @@
         grid=(slots // 16,),
         in_specs=[
             pl.BlockSpec((4, 3, 16, width), lambda i: (0, 0, i, 0)),
-            pl.BlockSpec((3, 2, 16, width), lambda i: (0, 0, i, 0)),
+            pl.BlockSpec((16, 3, 2, width), lambda i: (i, 0, 0, 0)),
             whole((3, 3, width)),
             pl.BlockSpec((16, MODES, width), lambda i: (i, 0, 0)),
             whole((MODES, width)),
@@ -263,20 +280,25 @@
         scratch_shapes=[pltpu.VMEM((16, width), F32)],
         compiler_params=pltpu.CompilerParams(vmem_limit_bytes=56 * 1024 * 1024),
         name="home_rows",
-    )(qkv_kinds, fir_kinds, fir_taps, modal_state, poles, residues, skip_row, finished)
+    )(qkv_kinds, fir_buffer, fir_taps, modal_state, poles, residues, skip_row, finished)
 
     got = swap(packed)
-    own_home = ring_sums(gated_home, out_weight)
-    got, own_home = lax.optimization_barrier((got, own_home))
-
-    sent, gated_band = pl.pallas_call(
+    own_home = lax.psum_scatter(
+        dot(gated_home, out_weight), "tensor", scatter_dimension=1, tiled=True
+    )
+
+    n, own_cols = lax.axis_size("tensor"), norm_gain.shape[0]
+    place = lax.axis_index("tensor").astype(jnp.int32)[None]
+    sent, far, part = pl.pallas_call(
         band_kernel,
-        in_specs=[pl.BlockSpec(memory_space=pltpu.SMEM)]
-        + [pl.BlockSpec(memory_space=pltpu.VMEM)] * 5,
-        out_specs=[pl.BlockSpec(memory_space=pltpu.VMEM)] * 2,
+        in_specs=[pl.BlockSpec(memory_space=pltpu.SMEM)] * 2
+        + [pl.BlockSpec(memory_space=pl.ANY)] * 2
+        + [pl.BlockSpec(memory_space=pltpu.VMEM)] * 4,
+        out_specs=[pl.BlockSpec(memory_space=pl.ANY)] * 3,
         out_shape=[
             jax.ShapeDtypeStruct((groups, 2 * MODES + 16, width), BF16),
-            jax.ShapeDtypeStruct((3, moving, width), BF16),
+            jax.ShapeDtypeStruct((3 * moving, own_cols), BF16),
+            jax.ShapeDtypeStruct((n, 3 * moving, own_cols), F32),
         ],
         scratch_shapes=[
             pltpu.VMEM((6, moving, width), F32),
@@ -285,15 +307,21 @@
             pltpu.VMEM((3, moving, width), F32),
             pltpu.VMEM((3, moving, width), F32),
             pltpu.VMEM((3, moving, width), F32),
-        ],
-        compiler_params=pltpu.CompilerParams(vmem_limit_bytes=32 * 1024 * 1024),
+            pltpu.VMEM(got.shape, BF16),
+            pltpu.VMEM(out_weight.shape, BF16),
+            pltpu.VMEM((groups, 2 * MODES + 16, width), BF16),
+            pltpu.VMEM((3 * moving, own_cols), BF16),
+            pltpu.VMEM((n, 3 * moving, own_cols), F32),
+            pltpu.SemaphoreType.DMA((5 + n,)),
+        ],
+        compiler_params=pltpu.CompilerParams(vmem_limit_bytes=40 * 1024 * 1024),
         name="band_rows",
-    )(turns, got, fir_taps, poles, residues, skip_row)
-
-    own_band, back = ring_sums(gated_band.reshape(3 * moving, width), out_weight, sent)
+    )(turns, place, got, out_weight, fir_taps, poles, residues, skip_row)
+
+    own_band, back = ring_sums(far, part, sent)
     scales = row_scales([own_band, own_home])
     mixed_band = (own_band * scales[: 3 * moving] * norm_gain[None]).astype(BF16)
-    own_cols = norm_gain.shape[0]
+    back, mixed_band = lax.optimization_barrier((back, mixed_band))
     mixed_band = jnp.transpose(mixed_band.reshape(3, groups, CAP, own_cols), (1, 0, 2, 3))
     mixed_back = swap(mixed_band)
     mixed_later = jnp.transpose(mixed_back, (1, 0, 2, 3)).reshape(3, moving, own_cols)

time: 146 us -> 148 us (1.014)
  matrix products: 21 us -> 4.37 us
  starting transfers between devices: 58.2 us -> 43.4 us
  blocking collectives: 0 us -> 13.7 us
  between operations: 1.38 us -> 14.4 us
  Pallas kernels: 11.6 us -> 16 us
  waiting for transfers between devices: 35.2 us -> 38.8 us
  other arithmetic: 9.48 us -> 7.18 us
  local copies, waits for them, and re-layouts: 7.38 us -> 9.12 us
    all_to_all x3, waiting for transfers between devices: 8.24 us -> 26.7 us  [swap(): return lax.all_to_all(blocks, 'dp', split_axis=0, concat_axis=0, tiled=True)]
    dot_general x16 -> x1, matrix products: 21 us -> 4.37 us  [dot(): return jnp.dot(a, b, preferred_element_type=F32)]
    psum x0 -> x1, blocking collectives: none -> 13.7 us  [row_scales(): lax.psum(jnp.concatenate([jnp.sum(x * x, axis=1) for x in own]), 'tensor')]
    ppermute x8 -> x4, starting transfers between devices: 16.8 us -> 8.93 us  [pass_on(): left = lax.ppermute(left, 'tensor', [(i, (i - 1) % n) for i in range(n)])]
    ppermute x3 -> x0, waiting for transfers between devices: 7.33 us -> none  [row_scales(): squares = squares + lax.ppermute(squares, 'tensor', pairs)]
    ppermute x8 -> x4, waiting for transfers between devices: 6.06 us -> 0.7 us  [pass_on(): left = lax.ppermute(left, 'tensor', [(i, (i - 1) % n) for i in range(n)])]
    all_to_all x3, starting transfers between devices: 34.1 us -> 28.9 us  [swap(): return lax.all_to_all(blocks, 'dp', split_axis=0, concat_axis=0, tiled=True)]
    pallas_call x1, Pallas kernels: 4.85 us -> 9.2 us  [per_device(): pl.pallas_call(band_kernel, in_specs=[pl.BlockSpec(memory_space=pltpu.SME...]
  transfers between devices with their start and end apart: 22 -> 12, of which waited for: 14 -> 9; matrix products, arithmetic and copies ran while one was open for 19% -> 9% of each run, Pallas kernels for 0% -> 6%
where the time goes in v3:
time: 148 us; the launch traced here: 147 us
  starting transfers between devices  43.4 us (29%)
  waiting for transfers between devices  38.8 us (26%)
  Pallas kernels  16 us (11%)
  between operations  14.4 us (10%)
  blocking collectives  13.7 us (9%)
  local copies, waits for them, and re-layouts  9.12 us (6%)
  other arithmetic  7.18 us (5%)
  matrix products  4.37 us (3%)
    all_to_all x3, starting transfers between devices, swap(): return lax.all_to_all(blocks, 'dp', split_axis=0, concat_axis=0, tiled=True)  28.9 us
    all_to_all x3, waiting for transfers between devices, swap(): return lax.all_to_all(blocks, 'dp', split_axis=0, concat_axis=0, tiled=True)  26.7 us
    psum x1, blocking collectives, row_scales(): lax.psum(jnp.concatenate([jnp.sum(x * x, axis=1) for x in own]), 'tensor')  13.7 us
    ppermute x4, waiting for transfers between devices, pass_on(): right = lax.ppermute(right, 'tensor', [(i, (i + 1) % n) for i in range(n)])  11.3 us
    pallas_call x1, Pallas kernels, per_device(): pl.pallas_call(band_kernel, in_specs=[pl.BlockSpec(memory_space=pltpu.SME...  9.2 us
    ppermute x4, starting transfers between devices, pass_on(): left = lax.ppermute(left, 'tensor', [(i, (i - 1) % n) for i in range(n)])  8.93 us
    pallas_call x1, Pallas kernels, per_device(): pl.pallas_call(home_kernel, grid=(slots // 16,), in_specs=[pl.BlockSpec((...  6.85 us
    ppermute x4, starting transfers between devices, pass_on(): right = lax.ppermute(right, 'tensor', [(i, (i + 1) % n) for i in range(n)])  5.53 us
  transfers between devices with their start and end apart: 12, of which 9 were waited for; matrix products, arithmetic and copies ran while one was open for 9% of the time, Pallas kernels for 6%

profile of v3, /device:TPU:1, one launch (start us, length us, event | category | flops | bytes accessed | tf_op | source)
XLA Modules:
  0.0 147.0 jit_solution(13326879895761628940)
XLA Ops:
  7.2 6.8 %home_rows.1 = (bf16[32,64,512]{2,1,0:T(8,128)(2,1)}, bf16[128,512]{1,0:T(8,128)(2,1)}, f32[16,16,512]{2,1,0:T(8,128)}) custom-call(bf16[4,3,80,512]{3,2,1,0:T(8,128)(2,1)} %bitcast.62, bf16[80,3,2,512]{3,2,1,0:T(2,128)(2,1)} %fir.1, f32[3,3,512]{2,1,0:T(4,128)} %taps.3, f32[80,16,512]{2,1,0:T(8,128)} %state.1, f32[16,512]{1,0:T(8,128)} %poles.3, ...), custom_call_target="tpu_custom_call" | custom-call | tf_op jit(solution)/shard_map/home_rows/pallas_call | solution.py:257
  14.0 8.7 %all-to-all-start = ((bf16[32,64,512]{2,1,0:T(8,128)(2,1)}), bf16[32,64,512]{2,1,0:T(8,128)(2,1)S(1)}, u32[]{:S(2)}, u32[]{:S(2)}) async-start(bf16[32,64,512]{2,1,0:T(8,128)(2,1)} %get-tuple-element.49), calls=%async_computation.1 | async-start | bytes 4194304 | tf_op jit(solution)/shard_map/all_to_all | solution.py:200
  22.9 4.4 %fusion.9 = f32[128,4096]{1,0:T(8,128)} fusion(bf16[128,512]{1,0:T(8,128)(2,1)S(1)} %copy-done.13, bf16[512,4096]{1,0:T(8,128)(2,1)} %weight_hbm.1), kind=kOutput, calls=%fused_computation.37 | convolution fusion | flops 536870912 | bytes 6422528 | tf_op jit(solution)/shard_map/dot_general | solution.py:15
  27.3 0.1 subtract_add_fusion
  27.4 0.1 reduce.4
  27.5 23.1 %all-to-all-done.got_hbm = bf16[32,64,512]{2,1,0:T(8,128)(2,1)S(1)} async-done(((bf16[32,64,512]{2,1,0:T(8,128)(2,1)}), bf16[32,64,512]{2,1,0:T(8,128)(2,1)S(1)}, u32[]{:S(2)}, u32[]{:S(2)}) %all-to-all-start) | async-done | bytes 2097184 | tf_op jit(solution)/shard_map/all_to_all | solution.py:200
  50.6 2.2 %copy-done = bf16[512,4096]{1,0:T(8,128)(2,1)S(1)} copy-done((bf16[512,4096]{1,0:T(8,128)(2,1)S(1)}, bf16[512,4096]{1,0:T(8,128)(2,1)}, u32[]{:S(2)}) %copy-start) | copy-done | bytes 4194328
  52.8 9.2 %band_rows.1 = (bf16[32,48,512]{2,1,0:T(8,128)(2,1)S(1)}, bf16[192,512]{1,0:T(8,128)(2,1)S(1)}, f32[8,192,512]{2,1,0:T(8,128)S(1)}) custom-call(s32[3]{0:T(128)S(1)} %and_select_fusion.turns, s32[1]{0:T(128)} %bitcast.2.place, bf16[32,64,512]{2,1,0:T(8,128)(2,1)S(1)} %all-to-all-done.got_hbm, bf16[512,4096]{1,0:T(8,128)(2,1)S(1)} %copy-done, ...), custom_call_target="tpu_custom_call" | custom-call | tf_op jit(solution)/shard_map/band_rows/pallas_call | solution.py:292
  62.1 1.7 %collective-permute-start = (bf16[96,512]{1,0:T(8,128)(2,1)S(1)}, bf16[96,512]{1,0:T(8,128)(2,1)S(1)}, u32[]{:S(2)}, u32[]{:S(2)}) collective-permute-start(bf16[96,512]{1,0:T(8,128)(2,1)S(1)} %get-tuple-element.90), channel_id=1, source_target_pairs={{0,1},{1,2},{2,3},{3,4},{4,5},{5,6},{6,7},{7,0},{8,9},{9,10},{10,1... | collective-permute-start | bytes 294920 | tf_op jit(solution)/shard_map/ppermute | solution.py:208
  63.8 4.0 %collective-permute-start.1 = (bf16[96,512]{1,0:T(8,128)(2,1)S(1)}, bf16[96,512]{1,0:T(8,128)(2,1)S(1)}, u32[]{:S(2)}, u32[]{:S(2)}) collective-permute-start(bf16[96,512]{1,0:T(8,128)(2,1)S(1)} %get-tuple-element.89), channel_id=1, source_target_pairs={{0,7},{1,0},{2,1},{3,2},{4,3},{5,4},{6,5},{7,6},{8,15},{9,8},{10,9... | collective-permute-start | bytes 294920 | tf_op jit(solution)/shard_map/ppermute | solution.py:209
  67.9 3.0 %collective-permute-done = bf16[96,512]{1,0:T(8,128)(2,1)S(1)} collective-permute-done((bf16[96,512]{1,0:T(8,128)(2,1)S(1)}, bf16[96,512]{1,0:T(8,128)(2,1)S(1)}, u32[]{:S(2)}, u32[]{:S(2)}) %collective-permute-start) | collective-permute-done | bytes 98336 | tf_op jit(solution)/shard_map/ppermute | solution.py:208
  70.9 6.7 %all-to-all-start.1 = ((bf16[32,48,512]{2,1,0:T(8,128)(2,1)}), bf16[32,48,512]{2,1,0:T(8,128)(2,1)}, u32[]{:S(2)}, u32[]{:S(2)}) async-start(bf16[32,48,512]{2,1,0:T(8,128)(2,1)} %copy-done.3), calls=%async_computation.2 | async-start | bytes 3145728 | tf_op jit(solution)/shard_map/all_to_all | solution.py:200
  77.6 0.5 collective-permute-start.2
  78.1 2.7 %collective-permute-start.3 = (bf16[192,512]{1,0:T(8,128)(2,1)S(1)}, bf16[192,512]{1,0:T(8,128)(2,1)S(1)}, u32[]{:S(2)}, u32[]{:S(2)}) collective-permute-start(bf16[192,512]{1,0:T(8,128)(2,1)S(1)} %get-tuple-element.56), channel_id=1, source_target_pairs={{0,7},{1,0},{2,1},{3,2},{4,3},{5,4},{6,5},{7,6},{8,15},{9,8},{10,9... | collective-permute-start | bytes 589832 | tf_op jit(solution)/shard_map/ppermute | solution.py:209
  80.8 1.7 %slice_bitcast_fusion.2 = bf16[80,3,1,512]{3,0,2,1:T(8,128)(2,1)} fusion(bf16[4,80,3,512]{3,1,2,0:T(8,128)(2,1)} %param.15), kind=kLoop, calls=%fused_computation.20 | loop fusion | bytes 491520 | tf_op jit(solution)/shard_map/stack;squeeze | solution.py:340
  82.5 3.3 %collective-permute-done.2 = bf16[192,512]{1,0:T(8,128)(2,1)S(1)} collective-permute-done((bf16[192,512]{1,0:T(8,128)(2,1)S(1)}, bf16[192,512]{1,0:T(8,128)(2,1)S(1)}, u32[]{:S(2)}, u32[]{:S(2)}) %collective-permute-start.2) | collective-permute-done | bytes 196640 | tf_op jit(solution)/shard_map/ppermute | solution.py:208
  85.8 0.1 fusion.1
  85.9 2.1 %collective-permute-start.4 = (bf16[192,512]{1,0:T(8,128)(2,1)S(1)}, bf16[192,512]{1,0:T(8,128)(2,1)S(1)}, u32[]{:S(2)}, u32[]{:S(2)}) collective-permute-start(bf16[192,512]{1,0:T(8,128)(2,1)S(1)} %get-tuple-element.84), channel_id=1, source_target_pairs={{0,1},{1,2},{2,3},{3,4},{4,5},{5,6},{6,7},{7,0},{8,9},{9,10},{10,1... | collective-permute-start | bytes 589832 | tf_op jit(solution)/shard_map/ppermute | solution.py:208
  88.0 0.6 collective-permute-start.5
  88.7 0.8 convert_bitcast_fusion
  89.4 3.5 %collective-permute-done.4 = bf16[192,512]{1,0:T(8,128)(2,1)S(1)} collective-permute-done((bf16[192,512]{1,0:T(8,128)(2,1)S(1)}, bf16[192,512]{1,0:T(8,128)(2,1)S(1)}, u32[]{:S(2)}, u32[]{:S(2)}) %collective-permute-start.4) | collective-permute-done | bytes 196640 | tf_op jit(solution)/shard_map/ppermute | solution.py:208
  92.9 0.2 collective-permute-done.5
  93.1 0.1 fusion
  93.2 1.2 collective-permute-start.6
  94.5 1.5 %collective-permute-start.7 = (bf16[192,512]{1,0:T(8,128)(2,1)S(1)}, bf16[192,512]{1,0:T(8,128)(2,1)S(1)}, u32[]{:S(2)}, u32[]{:S(2)}) collective-permute-start(bf16[192,512]{1,0:T(8,128)(2,1)S(1)} %get-tuple-element.81), channel_id=1, source_target_pairs={{0,7},{1,0},{2,1},{3,2},{4,3},{5,4},{6,5},{7,6},{8,15},{9,8},{10,9... | collective-permute-start | bytes 589832 | tf_op jit(solution)/shard_map/ppermute | solution.py:209
  96.0 1.5 %bitcast_multiply_fusion = bf16[16,3,512]{2,0,1:T(8,128)(2,1)} fusion(bf16[4,80,3,512]{3,1,2,0:T(8,128)(2,1)} %param.15, bf16[16]{0:T(256)(128)(2,1)S(1)} %convert_bitcast_fusion), kind=kLoop, calls=%fused_computation.27 | loop fusion | flops 24576 | bytes 98336 | tf_op jit(solution)/shard_map/mul | solution.py:339
  97.5 1.6 %collective-permute-done.6 = bf16[192,512]{1,0:T(8,128)(2,1)S(1)} collective-permute-done((bf16[192,512]{1,0:T(8,128)(2,1)S(1)}, bf16[192,512]{1,0:T(8,128)(2,1)S(1)}, u32[]{:S(2)}, u32[]{:S(2)}) %collective-permute-start.6) | collective-permute-done | bytes 196640 | tf_op jit(solution)/shard_map/ppermute | solution.py:208
  99.0 0.5 collective-permute-done.7
  99.6 0.3 all-to-all-done.1
  99.9 0.1 multiply_reduce_fusion
  100.1 1.1 multiply_reduce_fusion.1
  101.3 13.7 %psum.7 = f32[320]{0:T(512)S(1)} all-reduce(f32[320]{0:T(512)S(1)} %pad_maximum_fusion.2), channel_id=1, replica_groups=mesh['dp'=32,'tensor'=8] {'tensor'}, use_global_device_ids=true, to_apply=%region_4.5 | all-reduce | flops 320 | bytes 2560 | tf_op jit(solution)/shard_map/psum | solution.py:231
  115.1 0.1 multiply_convert_fusion
  115.2 1.0 slice.113
  116.2 0.2 copy.29
  116.4 0.1 reshape.120
  116.5 0.1 reshape.116
  116.6 0.8 copy.32
  117.4 13.5 %all-to-all-start.2 = ((bf16[32,3,2,512]{3,2,1,0:T(2,128)(2,1)}), bf16[32,3,2,512]{3,2,1,0:T(2,128)(2,1)S(1)}, u32[]{:S(2)}, u32[]{:S(2)}) async-start(bf16[32,3,2,512]{3,2,1,0:T(2,128)(2,1)} %bitcast.58), calls=%async_computation.3 | async-start | bytes 393216 | tf_op jit(solution)/shard_map/all_to_all | solution.py:200
  130.9 0.1 multiply_convert_fusion.1
  131.2 1.3 slice.111
  132.5 0.3 convert.1
  132.8 1.3 copy.30
  134.1 1.7 %pad_maximum_fusion = f32[80,16,512]{2,1,0:T(8,128)} fusion(f32[16,16,512]{2,1,0:T(8,128)S(1)} %copy-done.10, f32[64,16,512]{2,1,0:T(8,128)S(1)} %convert.1), kind=kLoop, calls=%fused_computation | loop fusion | flops 655360 | bytes 5242880 | tf_op jit(solution)/shard_map/concatenate | solution.py:335
  135.8 3.4 %all-to-all-done.2 = bf16[32,3,2,512]{3,2,1,0:T(2,128)(2,1)S(1)} async-done(((bf16[32,3,2,512]{3,2,1,0:T(2,128)(2,1)}), bf16[32,3,2,512]{3,2,1,0:T(2,128)(2,1)S(1)}, u32[]{:S(2)}, u32[]{:S(2)}) %all-to-all-start.2) | async-done | bytes 196640 | tf_op jit(solution)/shard_map/all_to_all | solution.py:200
  139.2 0.1 copy.27
  139.3 0.1 reshape.117
  139.4 0.8 maximum_maximum_fusion
  (52 shorter events, 0.7 us)
Async XLA Ops:
  14.0 8.8 %copy-start.13 = (bf16[128,512]{1,0:T(8,128)(2,1)S(1)}, bf16[128,512]{1,0:T(8,128)(2,1)}, u32[]{:S(2)}) copy-start(bf16[128,512]{1,0:T(8,128)(2,1)} %get-tuple-element.48) | copy-start | bytes 393220
  14.0 36.6 %all-to-all-start = ((bf16[32,64,512]{2,1,0:T(8,128)(2,1)}), bf16[32,64,512]{2,1,0:T(8,128)(2,1)S(1)}, u32[]{:S(2)}, u32[]{:S(2)}) async-start(bf16[32,64,512]{2,1,0:T(8,128)(2,1)} %get-tuple-element.49), calls=%async_computation.1 | async-start | bytes 4194304 | tf_op jit(solution)/shard_map/all_to_all | solution.py:200
  22.8 77.3 %reduce-scatter.2.cloned.1.call-start = ((), (), s32[]{:S(2)}) async-start(), calls=%async_computation.4 | async-start | bytes 2359296 | tf_op jit(solution)/shard_map/reduce_scatter | solution.py:286
  22.8 4.5 %copy-start.15 = (s32[3,80]{1,0:T(4,128)S(1)}, s32[3,80]{1,0:T(4,128)}, u32[]{:S(2)}) copy-start(s32[3,80]{1,0:T(4,128)} %param.25) | copy-start | bytes 2884
  22.8 27.8 %copy-start.4 = (f32[16,512]{1,0:T(8,128)S(1)}, f32[16,512]{1,0:T(8,128)}, u32[]{:S(2)}) copy-start(f32[16,512]{1,0:T(8,128)} %poles.3) | copy-start | bytes 98308
  22.8 27.8 %copy-start.5 = (f32[16,512]{1,0:T(8,128)S(1)}, f32[16,512]{1,0:T(8,128)}, u32[]{:S(2)}) copy-start(f32[16,512]{1,0:T(8,128)} %residues.3) | copy-start | bytes 98308
  22.9 27.8 %copy-start.6 = (f32[3,3,512]{2,1,0:T(4,128)S(1)}, f32[3,3,512]{2,1,0:T(4,128)}, u32[]{:S(2)}) copy-start(f32[3,3,512]{2,1,0:T(4,128)} %taps.3) | copy-start | bytes 55300
  22.9 27.8 %copy-start.7 = (f32[512]{0:T(512)S(1)}, f32[512]{0:T(512)}, u32[]{:S(2)}) copy-start(f32[512]{0:T(512)} %param.21) | copy-start | bytes 6148
  50.6 2.2 %copy-start = (bf16[512,4096]{1,0:T(8,128)(2,1)S(1)}, bf16[512,4096]{1,0:T(8,128)(2,1)}, u32[]{:S(2)}) copy-start(bf16[512,4096]{1,0:T(8,128)(2,1)} %weight_hbm.1) | copy-start | bytes 12582916
  62.1 8.8 %copy-start.1 = (f32[8,192,512]{2,1,0:T(8,128)}, f32[8,192,512]{2,1,0:T(8,128)S(1)}, u32[]{:S(2)}) copy-start(f32[8,192,512]{2,1,0:T(8,128)S(1)} %get-tuple-element.50) | copy-start | bytes 9437188
  62.1 8.9 %copy-start.3 = (bf16[32,48,512]{2,1,0:T(8,128)(2,1)}, bf16[32,48,512]{2,1,0:T(8,128)(2,1)S(1)}, u32[]{:S(2)}) copy-start(bf16[32,48,512]{2,1,0:T(8,128)(2,1)S(1)} %get-tuple-element.63) | copy-start | bytes 4718596
  62.1 8.8 %collective-permute-start = (bf16[96,512]{1,0:T(8,128)(2,1)S(1)}, bf16[96,512]{1,0:T(8,128)(2,1)S(1)}, u32[]{:S(2)}, u32[]{:S(2)}) collective-permute-start(bf16[96,512]{1,0:T(8,128)(2,1)S(1)} %get-tuple-element.90), channel_id=1, source_target_pairs={{0,1},{1,2},{2,3},{3,4},{4,5},{5,6},{6,7},{7,0},{8,9},{9,10},{10,1... | collective-permute-start | bytes 294920 | tf_op jit(solution)/shard_map/ppermute | solution.py:208
  63.8 7.1 %collective-permute-start.1 = (bf16[96,512]{1,0:T(8,128)(2,1)S(1)}, bf16[96,512]{1,0:T(8,128)(2,1)S(1)}, u32[]{:S(2)}, u32[]{:S(2)}) collective-permute-start(bf16[96,512]{1,0:T(8,128)(2,1)S(1)} %get-tuple-element.89), channel_id=1, source_target_pairs={{0,7},{1,0},{2,1},{3,2},{4,3},{5,4},{6,5},{7,6},{8,15},{9,8},{10,9... | collective-permute-start | bytes 294920 | tf_op jit(solution)/shard_map/ppermute | solution.py:209
  70.9 14.9 %copy-start.2 = (f32[8,192,512]{2,1,0:T(8,128)S(1)}, f32[8,192,512]{2,1,0:T(8,128)}, u32[]{:S(2)}) copy-start(f32[8,192,512]{2,1,0:T(8,128)} %copy-done.1) | copy-start | bytes 9437188
  70.9 29.0 %all-to-all-start.1 = ((bf16[32,48,512]{2,1,0:T(8,128)(2,1)}), bf16[32,48,512]{2,1,0:T(8,128)(2,1)}, u32[]{:S(2)}, u32[]{:S(2)}) async-start(bf16[32,48,512]{2,1,0:T(8,128)(2,1)} %copy-done.3), calls=%async_computation.2 | async-start | bytes 3145728 | tf_op jit(solution)/shard_map/all_to_all | solution.py:200
  77.6 8.1 %collective-permute-start.2 = (bf16[192,512]{1,0:T(8,128)(2,1)S(1)}, bf16[192,512]{1,0:T(8,128)(2,1)S(1)}, u32[]{:S(2)}, u32[]{:S(2)}) collective-permute-start(bf16[192,512]{1,0:T(8,128)(2,1)S(1)} %get-tuple-element.55), channel_id=1, source_target_pairs={{0,1},{1,2},{2,3},{3,4},{4,5},{5,6},{6,7},{7,0},{8,9},{9,10},{10,1... | collective-permute-start | bytes 589832 | tf_op jit(solution)/shard_map/ppermute | solution.py:208
  78.1 7.7 %collective-permute-start.3 = (bf16[192,512]{1,0:T(8,128)(2,1)S(1)}, bf16[192,512]{1,0:T(8,128)(2,1)S(1)}, u32[]{:S(2)}, u32[]{:S(2)}) collective-permute-start(bf16[192,512]{1,0:T(8,128)(2,1)S(1)} %get-tuple-element.56), channel_id=1, source_target_pairs={{0,7},{1,0},{2,1},{3,2},{4,3},{5,4},{6,5},{7,6},{8,15},{9,8},{10,9... | collective-permute-start | bytes 589832 | tf_op jit(solution)/shard_map/ppermute | solution.py:209
  82.5 32.6 %copy-start.14 = (f32[512]{0:T(512)S(1)}, f32[512]{0:T(512)}, u32[]{:S(2)}) copy-start(f32[512]{0:T(512)} %param.23) | copy-start | bytes 6148
  85.9 7.0 %collective-permute-start.4 = (bf16[192,512]{1,0:T(8,128)(2,1)S(1)}, bf16[192,512]{1,0:T(8,128)(2,1)S(1)}, u32[]{:S(2)}, u32[]{:S(2)}) collective-permute-start(bf16[192,512]{1,0:T(8,128)(2,1)S(1)} %get-tuple-element.84), channel_id=1, source_target_pairs={{0,1},{1,2},{2,3},{3,4},{4,5},{5,6},{6,7},{7,0},{8,9},{9,10},{10,1... | collective-permute-start | bytes 589832 | tf_op jit(solution)/shard_map/ppermute | solution.py:208
  88.0 5.1 %collective-permute-start.5 = (bf16[192,512]{1,0:T(8,128)(2,1)S(1)}, bf16[192,512]{1,0:T(8,128)(2,1)S(1)}, u32[]{:S(2)}, u32[]{:S(2)}) collective-permute-start(bf16[192,512]{1,0:T(8,128)(2,1)S(1)} %get-tuple-element.83), channel_id=1, source_target_pairs={{0,7},{1,0},{2,1},{3,2},{4,3},{5,4},{6,5},{7,6},{8,15},{9,8},{10,9... | collective-permute-start | bytes 589832 | tf_op jit(solution)/shard_map/ppermute | solution.py:209
  93.2 5.8 %collective-permute-start.6 = (bf16[192,512]{1,0:T(8,128)(2,1)S(1)}, bf16[192,512]{1,0:T(8,128)(2,1)S(1)}, u32[]{:S(2)}, u32[]{:S(2)}) collective-permute-start(bf16[192,512]{1,0:T(8,128)(2,1)S(1)} %get-tuple-element.82), channel_id=1, source_target_pairs={{0,1},{1,2},{2,3},{3,4},{4,5},{5,6},{6,7},{7,0},{8,9},{9,10},{10,1... | collective-permute-start | bytes 589832 | tf_op jit(solution)/shard_map/ppermute | solution.py:208
  94.5 5.1 %collective-permute-start.7 = (bf16[192,512]{1,0:T(8,128)(2,1)S(1)}, bf16[192,512]{1,0:T(8,128)(2,1)S(1)}, u32[]{:S(2)}, u32[]{:S(2)}) collective-permute-start(bf16[192,512]{1,0:T(8,128)(2,1)S(1)} %get-tuple-element.81), channel_id=1, source_target_pairs={{0,7},{1,0},{2,1},{3,2},{4,3},{5,4},{6,5},{7,6},{8,15},{9,8},{10,9... | collective-permute-start | bytes 589832 | tf_op jit(solution)/shard_map/ppermute | solution.py:209
  99.6 31.4 %copy-start.12 = (bf16[16,3,512]{2,0,1:T(8,128)(2,1)S(1)}, bf16[16,3,512]{2,0,1:T(8,128)(2,1)}, u32[]{:S(2)}) copy-start(bf16[16,3,512]{2,0,1:T(8,128)(2,1)} %bitcast_multiply_fusion) | copy-start | bytes 147460
  99.6 31.5 %copy-start.9 = (bf16[80,3,1,512]{3,0,2,1:T(8,128)(2,1)S(1)}, bf16[80,3,1,512]{3,0,2,1:T(8,128)(2,1)}, u32[]{:S(2)}) copy-start(bf16[80,3,1,512]{3,0,2,1:T(8,128)(2,1)} %slice_bitcast_fusion.2) | copy-start | bytes 737284
  100.1 30.9 %copy-start.8 = (f32[128,512]{1,0:T(8,128)S(1)}, f32[128,512]{1,0:T(8,128)}, u32[]{:S(2)}) copy-start(f32[128,512]{1,0:T(8,128)} %reduce-scatter.2.cloned.1.call-done) | copy-start | bytes 786436
  117.4 21.8 %all-to-all-start.2 = ((bf16[32,3,2,512]{3,2,1,0:T(2,128)(2,1)}), bf16[32,3,2,512]{3,2,1,0:T(2,128)(2,1)S(1)}, u32[]{:S(2)}, u32[]{:S(2)}) async-start(bf16[32,3,2,512]{3,2,1,0:T(2,128)(2,1)} %bitcast.58), calls=%async_computation.3 | async-start | bytes 393216 | tf_op jit(solution)/shard_map/all_to_all | solution.py:200
  131.0 1.7 %copy-start.11 = (bf16[128,512]{1,0:T(8,128)(2,1)}, bf16[128,512]{1,0:T(8,128)(2,1)S(1)}, u32[]{:S(2)}) copy-start(bf16[128,512]{1,0:T(8,128)(2,1)S(1)} %multiply_convert_fusion.1) | copy-start | bytes 393220
  132.5 1.6 %copy-start.10 = (f32[16,16,512]{2,1,0:T(8,128)S(1)}, f32[16,16,512]{2,1,0:T(8,128)}, u32[]{:S(2)}) copy-start(f32[16,16,512]{2,1,0:T(8,128)} %get-tuple-element.68) | copy-start | bytes 1572868
  134.1 5.4 %slice-start = ((bf16[128,512]{1,0:T(8,128)(2,1)}), bf16[48,512]{1,0:T(8,128)(2,1)S(1)}, s32[]{:S(2)}) async-start(bf16[128,512]{1,0:T(8,128)(2,1)} %copy-done.11), calls=%async_computation.5 | async-start | bytes 98304 | tf_op jit(solution)/shard_map/slice | solution.py:329
Sparse Core Ops, SparseCore 0:
  27.4 40.1 reduce-scatter.1

commit v4 on v3

--- a/solution.py
+++ b/solution.py
@@ -90,16 +90,16 @@
 
 
 def band_kernel(
-    turns, place, got_hbm, weight_hbm, taps, poles, residues, skip, sent_hbm, far_hbm, part_hbm, *scratch
+    turns, got_hbm, taps, poles, residues, skip, far_weight, sent, gated, far, *scratch
 ):
-    lags, inputs, live, heads, products, y_rows, got, weight, sent, far, part, sems = scratch
+    lags, inputs, live, heads, products, y_rows, got, sems = scratch
     groups, _, width = got.shape
     rows = 2 * groups
     halves = [pl.ds(2 * MODES, 2 * KINDS), pl.ds(0, 2 * MODES)]
     fetches = [
         pltpu.make_async_copy(got_hbm.at[:, at], got.at[:, at], sems.at[i])
         for i, at in enumerate(halves)
-    ] + [pltpu.make_async_copy(weight_hbm, weight, sems.at[2])]
+    ]
     for fetch in fetches:
         fetch.start()
     fetches[0].wait()
@@ -170,26 +170,73 @@
         end = (g + turns[2]) & (groups - 1)
         sent[end, 0 : 2 * MODES] = jnp.concatenate(final, axis=0).astype(BF16)
 
-    stores = [pltpu.make_async_copy(sent, sent_hbm, sems.at[3])]
-    stores[0].start()
-    fetches[2].wait()
-
-    gated = y_rows[...].reshape(3 * rows, width).astype(BF16)
-    n, _, own_cols = part.shape
-    for i in range(n):
-        away = (i + n // 2) % n
-        start = pl.multiple_of(((place[0] + away) % n) * own_cols, own_cols)
-        made = dot(gated, weight[:, pl.ds(start, own_cols)])
-        if away == n // 2:
-            far[...] = made.astype(BF16)
-            store = pltpu.make_async_copy(far, far_hbm, sems.at[4])
-        else:
-            part[away] = made
-            store = pltpu.make_async_copy(part.at[away], part_hbm.at[away], sems.at[5 + away])
-        store.start()
-        stores.append(store)
-    for store in stores:
-        store.wait()
+    gated[...] = y_rows[...].reshape(3 * rows, width).astype(BF16)
+    far[...] = dot(gated[...], far_weight[...]).astype(BF16)
+
+
+def products_kernel(place, gated, weight, part):
+    part[0] = dot(gated[...], weight[...])
+
+
+def products(place, gated, weight, n):
+    rows, width = gated.shape
+    own_cols = weight.shape[1] // n
+
+    def away(i):
+        return (n // 2 + 1 + i) % n
+
+    return pl.pallas_call(
+        products_kernel,
+        grid_spec=pltpu.PrefetchScalarGridSpec(
+            num_scalar_prefetch=1,
+            grid=(n - 1,),
+            in_specs=[
+                whole((rows, width)),
+                pl.BlockSpec((width, own_cols), lambda i, place: (0, (place[0] + away(i)) % n)),
+            ],
+            out_specs=pl.BlockSpec((1, rows, own_cols), lambda i, place: (away(i), 0, 0)),
+        ),
+        out_shape=jax.ShapeDtypeStruct((n, rows, own_cols), F32),
+        cost_estimate=pl.CostEstimate(
+            flops=16 * rows * width * weight.shape[1], bytes_accessed=2 * weight.size, transcendentals=0
+        ),
+        compiler_params=pltpu.CompilerParams(vmem_limit_bytes=56 * 1024 * 1024),
+        name="ring_products",
+    )(place, gated, weight)
+
+
+def finish_kernel(back, qkv, stay_state, finished, state, lagged):
+    block = pl.program_id(0)
+    rows, width = 16, qkv.shape[-1]
+
+    def put(j, last):
+        both = [qkv[1, j].astype(F32)[:, None], last[:, None]]
+        lagged[:, j] = jnp.concatenate(both, axis=1).astype(BF16)
+
+    @pl.when(block < 4)
+    def _():
+        n = back.shape[0]
+        for b in range(n):
+            for side in range(2):
+                state[2 * b + side] = back[b, side * MODES : (side + 1) * MODES].astype(F32)
+        shape = (3 * rows, n * 16)
+        r = lax.broadcasted_iota(jnp.int32, shape, 0)
+        c = lax.broadcasted_iota(jnp.int32, shape, 1)
+        source = ((r & 15) >> 1) * 16 + (r >> 4) * 2 + (r & 1)
+        order = jnp.where(c == source, 1.0, 0.0).astype(BF16)
+        last = dot(order, back[:, 2 * MODES :].reshape(n * 16, width))
+        for j in range(3):
+            put(j, last[j * rows : (j + 1) * rows])
+
+    @pl.when(block == 4)
+    def _():
+        state[...] = stay_state[...]
+        at = lax.broadcasted_iota(jnp.int32, (rows, finished.shape[1]), 0) + block * rows
+        own = at == lax.broadcasted_iota(jnp.int32, at.shape, 1)
+        ended = jnp.where(own, finished[2:3].astype(F32), 0.0)
+        alive = 1.0 - jnp.sum(ended, axis=1, keepdims=True)
+        for j in range(3):
+            put(j, qkv[0, j].astype(F32) * alive)
 
 
 def whole(shape):
@@ -200,30 +247,29 @@
     return lax.all_to_all(blocks, "dp", split_axis=0, concat_axis=0, tiled=True)
 
 
-def ring_sums(far, part, block):
+def ring_sums(far, part, block=None):
     n = part.shape[0]
     half = far.shape[0] // 2
 
     def pass_on(right, left):
         right = lax.ppermute(right, "tensor", [(i, (i + 1) % n) for i in range(n)])
         left = lax.ppermute(left, "tensor", [(i, (i - 1) % n) for i in range(n)])
-        return right, left
+        return lax.optimization_barrier((right, left))
 
     right, left = pass_on(far[:half], far[half:])
-    right, left = lax.optimization_barrier((right, left))
+    if block is not None:
+        part, block = lax.optimization_barrier((part, block))
+        block = swap(block)
     for away in range(n // 2 - 1, 0, -1):
         ahead, behind = part[away], part[n - away]
         if right.shape[0] == half:
-            ahead = ahead.at[:half].add(right.astype(F32)).astype(BF16)
-            behind = behind.at[half:].add(left.astype(F32)).astype(BF16)
-            ahead, behind, block = lax.optimization_barrier((ahead, behind, block))
-            right, left = pass_on(ahead, behind)
-            block = swap(block)
+            ahead = ahead.at[:half].add(right.astype(F32))
+            behind = behind.at[half:].add(left.astype(F32))
         else:
             ahead, behind = ahead + right.astype(F32), behind + left.astype(F32)
-            right, left = pass_on(ahead.astype(BF16), behind.astype(BF16))
-        right, left = lax.optimization_barrier((right, left))
-    return lax.optimization_barrier((part[0] + right.astype(F32) + left.astype(F32), block))
+        right, left = pass_on(ahead.astype(BF16), behind.astype(BF16))
+    total = part[0] + right.astype(F32) + left.astype(F32)
+    return total if block is None else lax.optimization_barrier((total, block))
 
 
 def row_scales(own):
@@ -282,23 +328,29 @@
         name="home_rows",
     )(qkv_kinds, fir_buffer, fir_taps, modal_state, poles, residues, skip_row, finished)
 
-    got = swap(packed)
-    own_home = lax.psum_scatter(
-        dot(gated_home, out_weight), "tensor", scatter_dimension=1, tiled=True
-    )
-
     n, own_cols = lax.axis_size("tensor"), norm_gain.shape[0]
     place = lax.axis_index("tensor").astype(jnp.int32)[None]
-    sent, far, part = pl.pallas_call(
+    far_weight = lax.dynamic_slice_in_dim(
+        out_weight, ((place[0] + n // 2) % n) * own_cols, own_cols, 1
+    )
+    got = swap(packed)
+    own_home = ring_sums(
+        dot(gated_home, far_weight).astype(BF16), products(place, gated_home, out_weight, n)
+    )
+    got, own_home = lax.optimization_barrier((got, own_home))
+
+    sent, gated_band, far = pl.pallas_call(
         band_kernel,
-        in_specs=[pl.BlockSpec(memory_space=pltpu.SMEM)] * 2
-        + [pl.BlockSpec(memory_space=pl.ANY)] * 2
-        + [pl.BlockSpec(memory_space=pltpu.VMEM)] * 4,
-        out_specs=[pl.BlockSpec(memory_space=pl.ANY)] * 3,
+        in_specs=[
+            pl.BlockSpec(memory_space=pltpu.SMEM),
+            pl.BlockSpec(memory_space=pl.ANY),
+        ]
+        + [pl.BlockSpec(memory_space=pltpu.VMEM)] * 5,
+        out_specs=[pl.BlockSpec(memory_space=pltpu.VMEM)] * 3,
         out_shape=[
             jax.ShapeDtypeStruct((groups, 2 * MODES + 16, width), BF16),
+            jax.ShapeDtypeStruct((3 * moving, width), BF16),
             jax.ShapeDtypeStruct((3 * moving, own_cols), BF16),
-            jax.ShapeDtypeStruct((n, 3 * moving, own_cols), F32),
         ],
         scratch_shapes=[
             pltpu.VMEM((6, moving, width), F32),
@@ -308,36 +360,45 @@
             pltpu.VMEM((3, moving, width), F32),
             pltpu.VMEM((3, moving, width), F32),
             pltpu.VMEM(got.shape, BF16),
-            pltpu.VMEM(out_weight.shape, BF16),
-            pltpu.VMEM((groups, 2 * MODES + 16, width), BF16),
-            pltpu.VMEM((3 * moving, own_cols), BF16),
-            pltpu.VMEM((n, 3 * moving, own_cols), F32),
-            pltpu.SemaphoreType.DMA((5 + n,)),
+            pltpu.SemaphoreType.DMA((2,)),
         ],
         compiler_params=pltpu.CompilerParams(vmem_limit_bytes=40 * 1024 * 1024),
         name="band_rows",
-    )(turns, place, got, out_weight, fir_taps, poles, residues, skip_row)
-
-    own_band, back = ring_sums(far, part, sent)
+    )(turns, got, fir_taps, poles, residues, skip_row, far_weight)
+
+    own_band, back = ring_sums(far, products(place, gated_band, out_weight, n), sent)
     scales = row_scales([own_band, own_home])
     mixed_band = (own_band * scales[: 3 * moving] * norm_gain[None]).astype(BF16)
+    mixed_band = jnp.transpose(mixed_band.reshape(3, groups, CAP, own_cols), (1, 0, 2, 3))
     back, mixed_band = lax.optimization_barrier((back, mixed_band))
-    mixed_band = jnp.transpose(mixed_band.reshape(3, groups, CAP, own_cols), (1, 0, 2, 3))
     mixed_back = swap(mixed_band)
+    final_state, final_lagged = pl.pallas_call(
+        finish_kernel,
+        grid=(slots // 16,),
+        in_specs=[
+            pl.BlockSpec((8, 2 * MODES + 16, width), lambda i: (jnp.minimum(i, 3), 0, 0)),
+            pl.BlockSpec((2, 3, 16, width), lambda i: (1, 0, i, 0)),
+            whole((16, MODES, width)),
+            whole((3, slots)),
+        ],
+        out_specs=[
+            pl.BlockSpec((16, MODES, width), lambda i: (i, 0, 0)),
+            pl.BlockSpec((16, 3, 2, width), lambda i: (i, 0, 0, 0)),
+        ],
+        out_shape=[
+            jax.ShapeDtypeStruct(modal_state.shape, F32),
+            jax.ShapeDtypeStruct(fir_buffer.shape, BF16),
+        ],
+        compiler_params=pltpu.CompilerParams(vmem_limit_bytes=56 * 1024 * 1024),
+        name="last_rows",
+    )(back, qkv_kinds, stay_state, finished)
+
     mixed_later = jnp.transpose(mixed_back, (1, 0, 2, 3)).reshape(3, moving, own_cols)
     mixed_home = (own_home * scales[3 * moving :] * norm_gain[None]).astype(BF16)
     mixed_stay = mixed_home[slots:].reshape(3, 16, own_cols)
     mixed = jnp.concatenate(
         [mixed_home[None, :slots], jnp.concatenate([mixed_later, mixed_stay], axis=1)], axis=0
     )
-
-    moved_state = back[:, : 2 * MODES].reshape(moving, MODES, width).astype(F32)
-    final_state = jnp.concatenate([moved_state, stay_state], axis=0)
-    moved_lag = back[:, 2 * MODES : 2 * MODES + 6].reshape(groups, 3, CAP, width)
-    moved_lag = jnp.transpose(moved_lag, (0, 2, 1, 3)).reshape(moving, 3, width)
-    stay_alive = (1 - finished[2, moving:]).astype(BF16)[:, None, None]
-    last_lag = jnp.concatenate([moved_lag, qkv[2, moving:] * stay_alive], axis=0)
-    final_lagged = jnp.stack([qkv[3], last_lag], axis=2)
     return (mixed, final_state, final_lagged)
 
 

time: 148 us -> 146 us (0.986)
  starting transfers between devices: 43.4 us -> 58.9 us
  Pallas kernels: 16 us -> 31.3 us
  waiting for transfers between devices: 38.8 us -> 23.8 us
  between operations: 14.4 us -> 0.96 us
  local copies, waits for them, and re-layouts: 9.12 us -> 5.26 us
  matrix products: 4.37 us -> 1.13 us
  other arithmetic: 7.18 us -> 10.3 us
    all_to_all x3, waiting for transfers between devices: 26.7 us -> 2.82 us  [swap(): return lax.all_to_all(blocks, 'dp', split_axis=0, concat_axis=0, tiled=True)]
    pallas_call x0 -> x3, Pallas kernels: none -> 18.2 us  [the longest x2 12.9 us: products(): pl.pallas_call(products_kernel, grid_spec=pltpu.PrefetchScalarGridSpec(nu...]
    ppermute x4 -> x8, starting transfers between devices: 8.93 us -> 18.3 us  [pass_on(): left = lax.ppermute(left, 'tensor', [(i, (i - 1) % n) for i in range(n)])]
    ppermute x4 -> x8, waiting for transfers between devices: 11.3 us -> 19.9 us  [pass_on(): right = lax.ppermute(right, 'tensor', [(i, (i + 1) % n) for i in range(n)])]
    convert_element_type x2 -> x4, other arithmetic: 0.24 us -> 4.68 us  [ring_sums(): right, left = pass_on(ahead.astype(BF16), behind.astype(BF16))]
    all_to_all x3, starting transfers between devices: 28.9 us -> 33 us  [swap(): return lax.all_to_all(blocks, 'dp', split_axis=0, concat_axis=0, tiled=True)]
    dot_general x1, matrix products: 4.37 us -> 1.13 us  [dot(): return jnp.dot(a, b, preferred_element_type=F32)]
    pallas_call x1, Pallas kernels: 9.2 us -> 6.19 us  [per_device(): pl.pallas_call(band_kernel, in_specs=[pl.BlockSpec(memory_space=pltpu.SME...]
  transfers between devices with their start and end apart: 12 -> 19, of which waited for: 9 -> 8; matrix products, arithmetic and copies ran while one was open for 9% -> 8% of each run, Pallas kernels for 6% -> 13%
where the time goes in v4:
time: 146 us; the launch traced here: 145 us
  starting transfers between devices  58.9 us (40%)
  Pallas kernels  31.3 us (21%)
  waiting for transfers between devices  23.8 us (16%)
  blocking collectives  13.1 us (9%)
  other arithmetic  10.3 us (7%)
  local copies, waits for them, and re-layouts  5.26 us (4%)
    all_to_all x3, starting transfers between devices, swap(): return lax.all_to_all(blocks, 'dp', split_axis=0, concat_axis=0, tiled=True)  33 us
    ppermute x8, waiting for transfers between devices, pass_on(): right = lax.ppermute(right, 'tensor', [(i, (i + 1) % n) for i in range(n)])  19.9 us
    ppermute x8, starting transfers between devices, pass_on(): left = lax.ppermute(left, 'tensor', [(i, (i - 1) % n) for i in range(n)])  18.3 us
    psum x1, blocking collectives, row_scales(): lax.psum(jnp.concatenate([jnp.sum(x * x, axis=1) for x in own]), 'tensor')  13.1 us
    pallas_call x2, Pallas kernels, products(): pl.pallas_call(products_kernel, grid_spec=pltpu.PrefetchScalarGridSpec(nu...  12.9 us
    ppermute x8, starting transfers between devices, pass_on(): right = lax.ppermute(right, 'tensor', [(i, (i + 1) % n) for i in range(n)])  7.54 us
    pallas_call x1, Pallas kernels, per_device(): pl.pallas_call(home_kernel, grid=(slots // 16,), in_specs=[pl.BlockSpec((...  6.87 us
    pallas_call x1, Pallas kernels, per_device(): pl.pallas_call(band_kernel, in_specs=[pl.BlockSpec(memory_space=pltpu.SME...  6.19 us
  transfers between devices with their start and end apart: 19, of which 8 were waited for; matrix products, arithmetic and copies ran while one was open for 8% of the time, Pallas kernels for 13%

profile of v4, /device:TPU:1, one launch (start us, length us, event | category | flops | bytes accessed | tf_op | source)
XLA Modules:
  0.0 144.8 jit_solution(12826507156454045941)
XLA Ops:
  0.6 1.1 constant_dynamic-slice_fusion.far_weight
  1.7 6.9 %home_rows.1 = (bf16[32,64,512]{2,1,0:T(8,128)(2,1)}, bf16[128,512]{1,0:T(8,128)(2,1)}, f32[16,16,512]{2,1,0:T(8,128)}) custom-call(bf16[4,3,80,512]{3,2,1,0:T(8,128)(2,1)} %bitcast.92, bf16[80,3,2,512]{3,2,1,0:T(2,128)(2,1)} %fir.1, f32[3,3,512]{2,1,0:T(4,128)} %taps.3, f32[80,16,512]{2,1,0:T(8,128)} %state.1, f32[16,512]{1,0:T(8,128)} %poles.3, ...), custom_call_target="tpu_custom_call" | custom-call | tf_op jit(solution)/shard_map/home_rows/pallas_call | solution.py:303
  8.6 1.1 convolution_convert_fusion
  9.8 2.5 %collective-permute-start = (bf16[64,512]{1,0:T(8,128)(2,1)S(1)}, bf16[64,512]{1,0:T(8,128)(2,1)S(1)}, u32[]{:S(2)}, u32[]{:S(2)}) collective-permute-start(bf16[64,512]{1,0:T(8,128)(2,1)S(1)} %get-tuple-element.134), channel_id=1, source_target_pairs={{0,1},{1,2},{2,3},{3,4},{4,5},{5,6},{6,7},{7,0},{8,9},{9,10},{10,1... | collective-permute-start | bytes 196616 | tf_op jit(solution)/shard_map/ppermute | solution.py:255
  12.3 4.0 %collective-permute-start.1 = (bf16[64,512]{1,0:T(8,128)(2,1)S(1)}, bf16[64,512]{1,0:T(8,128)(2,1)S(1)}, u32[]{:S(2)}, u32[]{:S(2)}) collective-permute-start(bf16[64,512]{1,0:T(8,128)(2,1)S(1)} %get-tuple-element.133), channel_id=1, source_target_pairs={{0,7},{1,0},{2,1},{3,2},{4,3},{5,4},{6,5},{7,6},{8,15},{9,8},{10,9... | collective-permute-start | bytes 196616 | tf_op jit(solution)/shard_map/ppermute | solution.py:256
  16.3 8.0 %all-to-all-start = ((bf16[32,64,512]{2,1,0:T(8,128)(2,1)}), bf16[32,64,512]{2,1,0:T(8,128)(2,1)S(1)}, u32[]{:S(2)}, u32[]{:S(2)}) async-start(bf16[32,64,512]{2,1,0:T(8,128)(2,1)} %get-tuple-element.83), calls=%async_computation | async-start | bytes 4194304 | tf_op jit(solution)/shard_map/all_to_all | solution.py:247
  24.4 6.3 %ring_products.2 = f32[8,128,512]{2,1,0:T(8,128)} custom-call(s32[1]{0:T(128)} %bitcast.2.place, bf16[128,512]{1,0:T(8,128)(2,1)} %get-tuple-element.84.gated, bf16[512,4096]{1,0:T(8,128)(2,1)} %weight.3), custom_call_target="tpu_custom_call" | custom-call | flops 4294967296 | bytes 4194304 | tf_op jit(solution)/shard_map/ring_products/pallas_call | solution.py:188
  30.7 1.1 slice_bitcast_fusion.4
  31.8 1.0 fusion.18
  32.9 2.7 %collective-permute-start.3 = (bf16[128,512]{1,0:T(8,128)(2,1)S(1)}, bf16[128,512]{1,0:T(8,128)(2,1)S(1)}, u32[]{:S(2)}, u32[]{:S(2)}) collective-permute-start(bf16[128,512]{1,0:T(8,128)(2,1)S(1)} %get-tuple-element.127), channel_id=1, source_target_pairs={{0,7},{1,0},{2,1},{3,2},{4,3},{5,4},{6,5},{7,6},{8,15},{9,8},{10,9... | collective-permute-start | bytes 393224 | tf_op jit(solution)/shard_map/ppermute | solution.py:256
  35.6 3.4 %collective-permute-done.2 = bf16[128,512]{1,0:T(8,128)(2,1)S(1)} collective-permute-done((bf16[128,512]{1,0:T(8,128)(2,1)S(1)}, bf16[128,512]{1,0:T(8,128)(2,1)S(1)}, u32[]{:S(2)}, u32[]{:S(2)}) %collective-permute-start.2) | collective-permute-done | bytes 131104 | tf_op jit(solution)/shard_map/ppermute | solution.py:255
  39.0 1.1 fusion.8
  40.2 2.7 %collective-permute-start.5 = (bf16[128,512]{1,0:T(8,128)(2,1)S(1)}, bf16[128,512]{1,0:T(8,128)(2,1)S(1)}, u32[]{:S(2)}, u32[]{:S(2)}) collective-permute-start(bf16[128,512]{1,0:T(8,128)(2,1)S(1)} %get-tuple-element.125), channel_id=1, source_target_pairs={{0,7},{1,0},{2,1},{3,2},{4,3},{5,4},{6,5},{7,6},{8,15},{9,8},{10,9... | collective-permute-start | bytes 393224 | tf_op jit(solution)/shard_map/ppermute | solution.py:256
  43.0 0.1 reduce.8
  43.1 2.4 %collective-permute-done.4 = bf16[128,512]{1,0:T(8,128)(2,1)S(1)} collective-permute-done((bf16[128,512]{1,0:T(8,128)(2,1)S(1)}, bf16[128,512]{1,0:T(8,128)(2,1)S(1)}, u32[]{:S(2)}, u32[]{:S(2)}) %collective-permute-start.4) | collective-permute-done | bytes 131104 | tf_op jit(solution)/shard_map/ppermute | solution.py:255
  45.5 1.1 fusion.6
  46.6 1.9 %collective-permute-start.6 = (bf16[128,512]{1,0:T(8,128)(2,1)S(1)}, bf16[128,512]{1,0:T(8,128)(2,1)S(1)}, u32[]{:S(2)}, u32[]{:S(2)}) collective-permute-start(bf16[128,512]{1,0:T(8,128)(2,1)S(1)} %get-tuple-element.124), channel_id=1, source_target_pairs={{0,1},{1,2},{2,3},{3,4},{4,5},{5,6},{6,7},{7,0},{8,9},{9,10},{10,1... | collective-permute-start | bytes 393224 | tf_op jit(solution)/shard_map/ppermute | solution.py:255
  48.6 0.9 collective-permute-start.7
  49.5 2.3 %collective-permute-done.6 = bf16[128,512]{1,0:T(8,128)(2,1)S(1)} collective-permute-done((bf16[128,512]{1,0:T(8,128)(2,1)S(1)}, bf16[128,512]{1,0:T(8,128)(2,1)S(1)}, u32[]{:S(2)}, u32[]{:S(2)}) %collective-permute-start.6) | collective-permute-done | bytes 131104 | tf_op jit(solution)/shard_map/ppermute | solution.py:255
  51.7 1.1 collective-permute-done.7
  52.8 1.0 fusion.14
  53.9 6.2 %band_rows.1 = (bf16[32,48,512]{2,1,0:T(8,128)(2,1)}, bf16[192,512]{1,0:T(8,128)(2,1)S(1)}, bf16[192,512]{1,0:T(8,128)(2,1)S(1)}) custom-call(s32[3]{0:T(128)S(1)} %and_select_fusion.turns, bf16[32,64,512]{2,1,0:T(8,128)(2,1)S(1)} %all-to-all-done.got_hbm, f32[3,3,512]{2,1,0:T(4,128)S(1)} %copy-done.2, f32[16,512]{1,0:T(8,128)S(1)} %copy-done, ...), custom_call_target="tpu_custom_call" | custom-call | tf_op jit(solution)/shard_map/band_rows/pallas_call | solution.py:342
  60.1 0.6 copy-done.4
  60.8 1.5 %collective-permute-start.8 = (bf16[96,512]{1,0:T(8,128)(2,1)S(1)}, bf16[96,512]{1,0:T(8,128)(2,1)S(1)}, u32[]{:S(2)}, u32[]{:S(2)}) collective-permute-start(bf16[96,512]{1,0:T(8,128)(2,1)S(1)} %get-tuple-element.132), channel_id=1, source_target_pairs={{0,1},{1,2},{2,3},{3,4},{4,5},{5,6},{6,7},{7,0},{8,9},{9,10},{10,1... | collective-permute-start | bytes 294920 | tf_op jit(solution)/shard_map/ppermute | solution.py:255
  62.3 1.1 collective-permute-start.9
  63.5 6.6 %ring_products.3 = f32[8,192,512]{2,1,0:T(8,128)} custom-call(s32[1]{0:T(128)} %bitcast.2.place, bf16[192,512]{1,0:T(8,128)(2,1)} %copy-done.4, bf16[512,4096]{1,0:T(8,128)(2,1)} %weight.3), custom_call_target="tpu_custom_call" | custom-call | flops 6442450944 | bytes 4194304 | tf_op jit(solution)/shard_map/ring_products/pallas_call | solution.py:188
  70.1 1.2 slice_bitcast_fusion
  71.2 11.0 %all-to-all-start.1 = ((bf16[32,48,512]{2,1,0:T(8,128)(2,1)}), bf16[32,48,512]{2,1,0:T(8,128)(2,1)S(1)}, u32[]{:S(2)}, u32[]{:S(2)}) async-start(bf16[32,48,512]{2,1,0:T(8,128)(2,1)} %get-tuple-element.107), calls=%async_computation.1 | async-start | bytes 3145728 | tf_op jit(solution)/shard_map/all_to_all | solution.py:247
  82.2 1.1 fusion.15
  83.3 0.6 collective-permute-start.10
  83.9 2.1 %collective-permute-start.11 = (bf16[192,512]{1,0:T(8,128)(2,1)S(1)}, bf16[192,512]{1,0:T(8,128)(2,1)S(1)}, u32[]{:S(2)}, u32[]{:S(2)}) collective-permute-start(bf16[192,512]{1,0:T(8,128)(2,1)S(1)} %get-tuple-element.119), channel_id=1, source_target_pairs={{0,7},{1,0},{2,1},{3,2},{4,3},{5,4},{6,5},{7,6},{8,15},{9,8},{10,9... | collective-permute-start | bytes 589832 | tf_op jit(solution)/shard_map/ppermute | solution.py:256
  86.1 4.8 %collective-permute-done.10 = bf16[192,512]{1,0:T(8,128)(2,1)S(1)} collective-permute-done((bf16[192,512]{1,0:T(8,128)(2,1)S(1)}, bf16[192,512]{1,0:T(8,128)(2,1)S(1)}, u32[]{:S(2)}, u32[]{:S(2)}) %collective-permute-start.10) | collective-permute-done | bytes 196640 | tf_op jit(solution)/shard_map/ppermute | solution.py:255
  90.9 1.2 fusion.1
  92.1 0.3 collective-permute-start.12
  92.4 2.5 %collective-permute-start.13 = (bf16[192,512]{1,0:T(8,128)(2,1)S(1)}, bf16[192,512]{1,0:T(8,128)(2,1)S(1)}, u32[]{:S(2)}, u32[]{:S(2)}) collective-permute-start(bf16[192,512]{1,0:T(8,128)(2,1)S(1)} %get-tuple-element.117), channel_id=1, source_target_pairs={{0,7},{1,0},{2,1},{3,2},{4,3},{5,4},{6,5},{7,6},{8,15},{9,8},{10,9... | collective-permute-start | bytes 589832 | tf_op jit(solution)/shard_map/ppermute | solution.py:256
  94.9 3.9 %collective-permute-done.12 = bf16[192,512]{1,0:T(8,128)(2,1)S(1)} collective-permute-done((bf16[192,512]{1,0:T(8,128)(2,1)S(1)}, bf16[192,512]{1,0:T(8,128)(2,1)S(1)}, u32[]{:S(2)}, u32[]{:S(2)}) %collective-permute-start.12) | collective-permute-done | bytes 196640 | tf_op jit(solution)/shard_map/ppermute | solution.py:255
  98.7 1.2 fusion
  100.0 0.5 collective-permute-start.14
  100.4 2.3 %collective-permute-start.15 = (bf16[192,512]{1,0:T(8,128)(2,1)S(1)}, bf16[192,512]{1,0:T(8,128)(2,1)S(1)}, u32[]{:S(2)}, u32[]{:S(2)}) collective-permute-start(bf16[192,512]{1,0:T(8,128)(2,1)S(1)} %get-tuple-element.115), channel_id=1, source_target_pairs={{0,7},{1,0},{2,1},{3,2},{4,3},{5,4},{6,5},{7,6},{8,15},{9,8},{10,9... | collective-permute-start | bytes 589832 | tf_op jit(solution)/shard_map/ppermute | solution.py:256
  102.8 3.1 %collective-permute-done.14 = bf16[192,512]{1,0:T(8,128)(2,1)S(1)} collective-permute-done((bf16[192,512]{1,0:T(8,128)(2,1)S(1)}, bf16[192,512]{1,0:T(8,128)(2,1)S(1)}, u32[]{:S(2)}, u32[]{:S(2)}) %collective-permute-start.14) | collective-permute-done | bytes 196640 | tf_op jit(solution)/shard_map/ppermute | solution.py:255
  106.0 1.1 fusion.4
  107.3 13.1 %psum.7 = f32[320]{0:T(512)S(1)} all-reduce(f32[320]{0:T(512)S(1)} %pad_maximum_fusion), channel_id=1, replica_groups=mesh['dp'=32,'tensor'=8] {'tensor'}, use_global_device_ids=true, to_apply=%region_3.4 | all-reduce | flops 320 | bytes 2560 | tf_op jit(solution)/shard_map/psum | solution.py:277
  120.7 0.8 copy.18
  121.5 14.0 %all-to-all-start.2 = ((bf16[32,3,2,512]{3,2,1,0:T(2,128)(2,1)}), bf16[32,3,2,512]{3,2,1,0:T(2,128)(2,1)S(1)}, u32[]{:S(2)}, u32[]{:S(2)}) async-start(bf16[32,3,2,512]{3,2,1,0:T(2,128)(2,1)} %bitcast.89), calls=%async_computation.2 | async-start | bytes 393216 | tf_op jit(solution)/shard_map/all_to_all | solution.py:247
  135.7 5.3 %last_rows.1 = (f32[80,16,512]{2,1,0:T(8,128)}, bf16[80,3,2,512]{3,2,1,0:T(2,128)(2,1)}) custom-call(bf16[32,48,512]{2,1,0:T(8,128)(2,1)} %copy-done.5, bf16[4,3,80,512]{3,2,1,0:T(8,128)(2,1)} %bitcast.93, f32[16,16,512]{2,1,0:T(8,128)} %get-tuple-element.112.stay_state, s32[3,80]{1,0:T(4,128)} %finished.3), custom_call_target="tpu_custom_call" | custom-call | tf_op jit(solution)/shard_map/last_rows/pallas_call | solution.py:375
  141.0 2.8 %all-to-all-done.2 = bf16[32,3,2,512]{3,2,1,0:T(2,128)(2,1)S(1)} async-done(((bf16[32,3,2,512]{3,2,1,0:T(2,128)(2,1)}), bf16[32,3,2,512]{3,2,1,0:T(2,128)(2,1)S(1)}, u32[]{:S(2)}, u32[]{:S(2)}) %all-to-all-start.2) | async-done | bytes 196640 | tf_op jit(solution)/shard_map/all_to_all | solution.py:247
  143.8 0.1 copy.16
  144.0 0.8 maximum_maximum_fusion
  (45 shorter events, 1.1 us)
Async XLA Ops:
  9.8 22.1 %collective-permute-start = (bf16[64,512]{1,0:T(8,128)(2,1)S(1)}, bf16[64,512]{1,0:T(8,128)(2,1)S(1)}, u32[]{:S(2)}, u32[]{:S(2)}) collective-permute-start(bf16[64,512]{1,0:T(8,128)(2,1)S(1)} %get-tuple-element.134), channel_id=1, source_target_pairs={{0,1},{1,2},{2,3},{3,4},{4,5},{5,6},{6,7},{7,0},{8,9},{9,10},{10,1... | collective-permute-start | bytes 196616 | tf_op jit(solution)/shard_map/ppermute | solution.py:255
  12.3 19.5 %collective-permute-start.1 = (bf16[64,512]{1,0:T(8,128)(2,1)S(1)}, bf16[64,512]{1,0:T(8,128)(2,1)S(1)}, u32[]{:S(2)}, u32[]{:S(2)}) collective-permute-start(bf16[64,512]{1,0:T(8,128)(2,1)S(1)} %get-tuple-element.133), channel_id=1, source_target_pairs={{0,7},{1,0},{2,1},{3,2},{4,3},{5,4},{6,5},{7,6},{8,15},{9,8},{10,9... | collective-permute-start | bytes 196616 | tf_op jit(solution)/shard_map/ppermute | solution.py:256
  16.3 37.5 %all-to-all-start = ((bf16[32,64,512]{2,1,0:T(8,128)(2,1)}), bf16[32,64,512]{2,1,0:T(8,128)(2,1)S(1)}, u32[]{:S(2)}, u32[]{:S(2)}) async-start(bf16[32,64,512]{2,1,0:T(8,128)(2,1)} %get-tuple-element.83), calls=%async_computation | async-start | bytes 4194304 | tf_op jit(solution)/shard_map/all_to_all | solution.py:247
  24.4 18.5 %copy-start.7 = (s32[3,80]{1,0:T(4,128)S(1)}, s32[3,80]{1,0:T(4,128)}, u32[]{:S(2)}) copy-start(s32[3,80]{1,0:T(4,128)} %param.29) | copy-start | bytes 2884
  30.7 23.2 %copy-start = (f32[16,512]{1,0:T(8,128)S(1)}, f32[16,512]{1,0:T(8,128)}, u32[]{:S(2)}) copy-start(f32[16,512]{1,0:T(8,128)} %poles.3) | copy-start | bytes 98308
  30.7 23.2 %copy-start.1 = (f32[16,512]{1,0:T(8,128)S(1)}, f32[16,512]{1,0:T(8,128)}, u32[]{:S(2)}) copy-start(f32[16,512]{1,0:T(8,128)} %residues.3) | copy-start | bytes 98308
  30.7 23.2 %copy-start.2 = (f32[3,3,512]{2,1,0:T(4,128)S(1)}, f32[3,3,512]{2,1,0:T(4,128)}, u32[]{:S(2)}) copy-start(f32[3,3,512]{2,1,0:T(4,128)} %taps.3) | copy-start | bytes 55300
  30.7 23.2 %copy-start.3 = (f32[512]{0:T(512)S(1)}, f32[512]{0:T(512)}, u32[]{:S(2)}) copy-start(f32[512]{0:T(512)} %param.25) | copy-start | bytes 6148
  32.8 6.2 %collective-permute-start.2 = (bf16[128,512]{1,0:T(8,128)(2,1)S(1)}, bf16[128,512]{1,0:T(8,128)(2,1)S(1)}, u32[]{:S(2)}, u32[]{:S(2)}) collective-permute-start(bf16[128,512]{1,0:T(8,128)(2,1)S(1)} %get-tuple-element.128), channel_id=1, source_target_pairs={{0,1},{1,2},{2,3},{3,4},{4,5},{5,6},{6,7},{7,0},{8,9},{9,10},{10,1... | collective-permute-start | bytes 393224 | tf_op jit(solution)/shard_map/ppermute | solution.py:255
  32.9 6.1 %collective-permute-start.3 = (bf16[128,512]{1,0:T(8,128)(2,1)S(1)}, bf16[128,512]{1,0:T(8,128)(2,1)S(1)}, u32[]{:S(2)}, u32[]{:S(2)}) collective-permute-start(bf16[128,512]{1,0:T(8,128)(2,1)S(1)} %get-tuple-element.127), channel_id=1, source_target_pairs={{0,7},{1,0},{2,1},{3,2},{4,3},{5,4},{6,5},{7,6},{8,15},{9,8},{10,9... | collective-permute-start | bytes 393224 | tf_op jit(solution)/shard_map/ppermute | solution.py:256
  40.1 5.4 %collective-permute-start.4 = (bf16[128,512]{1,0:T(8,128)(2,1)S(1)}, bf16[128,512]{1,0:T(8,128)(2,1)S(1)}, u32[]{:S(2)}, u32[]{:S(2)}) collective-permute-start(bf16[128,512]{1,0:T(8,128)(2,1)S(1)} %get-tuple-element.126), channel_id=1, source_target_pairs={{0,1},{1,2},{2,3},{3,4},{4,5},{5,6},{6,7},{7,0},{8,9},{9,10},{10,1... | collective-permute-start | bytes 393224 | tf_op jit(solution)/shard_map/ppermute | solution.py:255
  40.2 5.3 %collective-permute-start.5 = (bf16[128,512]{1,0:T(8,128)(2,1)S(1)}, bf16[128,512]{1,0:T(8,128)(2,1)S(1)}, u32[]{:S(2)}, u32[]{:S(2)}) collective-permute-start(bf16[128,512]{1,0:T(8,128)(2,1)S(1)} %get-tuple-element.125), channel_id=1, source_target_pairs={{0,7},{1,0},{2,1},{3,2},{4,3},{5,4},{6,5},{7,6},{8,15},{9,8},{10,9... | collective-permute-start | bytes 393224 | tf_op jit(solution)/shard_map/ppermute | solution.py:256
  46.6 5.1 %collective-permute-start.6 = (bf16[128,512]{1,0:T(8,128)(2,1)S(1)}, bf16[128,512]{1,0:T(8,128)(2,1)S(1)}, u32[]{:S(2)}, u32[]{:S(2)}) collective-permute-start(bf16[128,512]{1,0:T(8,128)(2,1)S(1)} %get-tuple-element.124), channel_id=1, source_target_pairs={{0,1},{1,2},{2,3},{3,4},{4,5},{5,6},{6,7},{7,0},{8,9},{9,10},{10,1... | collective-permute-start | bytes 393224 | tf_op jit(solution)/shard_map/ppermute | solution.py:255
  48.6 4.3 %collective-permute-start.7 = (bf16[128,512]{1,0:T(8,128)(2,1)S(1)}, bf16[128,512]{1,0:T(8,128)(2,1)S(1)}, u32[]{:S(2)}, u32[]{:S(2)}) collective-permute-start(bf16[128,512]{1,0:T(8,128)(2,1)S(1)} %get-tuple-element.123), channel_id=1, source_target_pairs={{0,7},{1,0},{2,1},{3,2},{4,3},{5,4},{6,5},{7,6},{8,15},{9,8},{10,9... | collective-permute-start | bytes 393224 | tf_op jit(solution)/shard_map/ppermute | solution.py:256
  60.1 0.7 copy-start.4
  60.8 21.4 %collective-permute-start.8 = (bf16[96,512]{1,0:T(8,128)(2,1)S(1)}, bf16[96,512]{1,0:T(8,128)(2,1)S(1)}, u32[]{:S(2)}, u32[]{:S(2)}) collective-permute-start(bf16[96,512]{1,0:T(8,128)(2,1)S(1)} %get-tuple-element.132), channel_id=1, source_target_pairs={{0,1},{1,2},{2,3},{3,4},{4,5},{5,6},{6,7},{7,0},{8,9},{9,10},{10,1... | collective-permute-start | bytes 294920 | tf_op jit(solution)/shard_map/ppermute | solution.py:255
  62.3 19.9 %collective-permute-start.9 = (bf16[96,512]{1,0:T(8,128)(2,1)S(1)}, bf16[96,512]{1,0:T(8,128)(2,1)S(1)}, u32[]{:S(2)}, u32[]{:S(2)}) collective-permute-start(bf16[96,512]{1,0:T(8,128)(2,1)S(1)} %get-tuple-element.131), channel_id=1, source_target_pairs={{0,7},{1,0},{2,1},{3,2},{4,3},{5,4},{6,5},{7,6},{8,15},{9,8},{10,9... | collective-permute-start | bytes 294920 | tf_op jit(solution)/shard_map/ppermute | solution.py:256
  71.2 35.8 %all-to-all-start.1 = ((bf16[32,48,512]{2,1,0:T(8,128)(2,1)}), bf16[32,48,512]{2,1,0:T(8,128)(2,1)S(1)}, u32[]{:S(2)}, u32[]{:S(2)}) async-start(bf16[32,48,512]{2,1,0:T(8,128)(2,1)} %get-tuple-element.107), calls=%async_computation.1 | async-start | bytes 3145728 | tf_op jit(solution)/shard_map/all_to_all | solution.py:247
  83.3 37.2 %copy-start.6 = (f32[512]{0:T(512)S(1)}, f32[512]{0:T(512)}, u32[]{:S(2)}) copy-start(f32[512]{0:T(512)} %param.27) | copy-start | bytes 6148
  83.3 7.6 %collective-permute-start.10 = (bf16[192,512]{1,0:T(8,128)(2,1)S(1)}, bf16[192,512]{1,0:T(8,128)(2,1)S(1)}, u32[]{:S(2)}, u32[]{:S(2)}) collective-permute-start(bf16[192,512]{1,0:T(8,128)(2,1)S(1)} %get-tuple-element.120), channel_id=1, source_target_pairs={{0,1},{1,2},{2,3},{3,4},{4,5},{5,6},{6,7},{7,0},{8,9},{9,10},{10,1... | collective-permute-start | bytes 589832 | tf_op jit(solution)/shard_map/ppermute | solution.py:255
  83.9 6.9 %collective-permute-start.11 = (bf16[192,512]{1,0:T(8,128)(2,1)S(1)}, bf16[192,512]{1,0:T(8,128)(2,1)S(1)}, u32[]{:S(2)}, u32[]{:S(2)}) collective-permute-start(bf16[192,512]{1,0:T(8,128)(2,1)S(1)} %get-tuple-element.119), channel_id=1, source_target_pairs={{0,7},{1,0},{2,1},{3,2},{4,3},{5,4},{6,5},{7,6},{8,15},{9,8},{10,9... | collective-permute-start | bytes 589832 | tf_op jit(solution)/shard_map/ppermute | solution.py:256
  92.1 6.6 %collective-permute-start.12 = (bf16[192,512]{1,0:T(8,128)(2,1)S(1)}, bf16[192,512]{1,0:T(8,128)(2,1)S(1)}, u32[]{:S(2)}, u32[]{:S(2)}) collective-permute-start(bf16[192,512]{1,0:T(8,128)(2,1)S(1)} %get-tuple-element.118), channel_id=1, source_target_pairs={{0,1},{1,2},{2,3},{3,4},{4,5},{5,6},{6,7},{7,0},{8,9},{9,10},{10,1... | collective-permute-start | bytes 589832 | tf_op jit(solution)/shard_map/ppermute | solution.py:255
  92.4 6.4 %collective-permute-start.13 = (bf16[192,512]{1,0:T(8,128)(2,1)S(1)}, bf16[192,512]{1,0:T(8,128)(2,1)S(1)}, u32[]{:S(2)}, u32[]{:S(2)}) collective-permute-start(bf16[192,512]{1,0:T(8,128)(2,1)S(1)} %get-tuple-element.117), channel_id=1, source_target_pairs={{0,7},{1,0},{2,1},{3,2},{4,3},{5,4},{6,5},{7,6},{8,15},{9,8},{10,9... | collective-permute-start | bytes 589832 | tf_op jit(solution)/shard_map/ppermute | solution.py:256
  100.0 6.0 %collective-permute-start.14 = (bf16[192,512]{1,0:T(8,128)(2,1)S(1)}, bf16[192,512]{1,0:T(8,128)(2,1)S(1)}, u32[]{:S(2)}, u32[]{:S(2)}) collective-permute-start(bf16[192,512]{1,0:T(8,128)(2,1)S(1)} %get-tuple-element.116), channel_id=1, source_target_pairs={{0,1},{1,2},{2,3},{3,4},{4,5},{5,6},{6,7},{7,0},{8,9},{9,10},{10,1... | collective-permute-start | bytes 589832 | tf_op jit(solution)/shard_map/ppermute | solution.py:255
  100.4 5.5 %collective-permute-start.15 = (bf16[192,512]{1,0:T(8,128)(2,1)S(1)}, bf16[192,512]{1,0:T(8,128)(2,1)S(1)}, u32[]{:S(2)}, u32[]{:S(2)}) collective-permute-start(bf16[192,512]{1,0:T(8,128)(2,1)S(1)} %get-tuple-element.115), channel_id=1, source_target_pairs={{0,7},{1,0},{2,1},{3,2},{4,3},{5,4},{6,5},{7,6},{8,15},{9,8},{10,9... | collective-permute-start | bytes 589832 | tf_op jit(solution)/shard_map/ppermute | solution.py:256
  107.1 28.6 %copy-start.5 = (bf16[32,48,512]{2,1,0:T(8,128)(2,1)}, bf16[32,48,512]{2,1,0:T(8,128)(2,1)S(1)}, u32[]{:S(2)}) copy-start(bf16[32,48,512]{2,1,0:T(8,128)(2,1)S(1)} %all-to-all-done.1.back) | copy-start | bytes 4718596
  121.5 22.3 %all-to-all-start.2 = ((bf16[32,3,2,512]{3,2,1,0:T(2,128)(2,1)}), bf16[32,3,2,512]{3,2,1,0:T(2,128)(2,1)S(1)}, u32[]{:S(2)}, u32[]{:S(2)}) async-start(bf16[32,3,2,512]{3,2,1,0:T(2,128)(2,1)} %bitcast.89), calls=%async_computation.2 | async-start | bytes 393216 | tf_op jit(solution)/shard_map/all_to_all | solution.py:247

commit v5 on v4

--- a/solution.py
+++ b/solution.py
@@ -178,31 +178,30 @@
     part[0] = dot(gated[...], weight[...])
 
 
-def products(place, gated, weight, n):
+def products(gated, weight, aways):
+    n = lax.axis_size("tensor")
     rows, width = gated.shape
     own_cols = weight.shape[1] // n
-
-    def away(i):
-        return (n // 2 + 1 + i) % n
-
-    return pl.pallas_call(
+    places = (lax.axis_index("tensor") + jnp.array(aways, jnp.int32)) % n
+    part = pl.pallas_call(
         products_kernel,
         grid_spec=pltpu.PrefetchScalarGridSpec(
             num_scalar_prefetch=1,
-            grid=(n - 1,),
+            grid=(len(aways),),
             in_specs=[
                 whole((rows, width)),
-                pl.BlockSpec((width, own_cols), lambda i, place: (0, (place[0] + away(i)) % n)),
+                pl.BlockSpec((width, own_cols), lambda i, places: (0, places[i])),
             ],
-            out_specs=pl.BlockSpec((1, rows, own_cols), lambda i, place: (away(i), 0, 0)),
+            out_specs=pl.BlockSpec((1, rows, own_cols), lambda i, places: (i, 0, 0)),
         ),
-        out_shape=jax.ShapeDtypeStruct((n, rows, own_cols), F32),
+        out_shape=jax.ShapeDtypeStruct((len(aways), rows, own_cols), F32),
         cost_estimate=pl.CostEstimate(
             flops=16 * rows * width * weight.shape[1], bytes_accessed=2 * weight.size, transcendentals=0
         ),
         compiler_params=pltpu.CompilerParams(vmem_limit_bytes=56 * 1024 * 1024),
         name="ring_products",
-    )(place, gated, weight)
+    )(places, gated, weight)
+    return dict(zip(aways, part))
 
 
 def finish_kernel(back, qkv, stay_state, finished, state, lagged):
@@ -247,29 +246,33 @@
     return lax.all_to_all(blocks, "dp", split_axis=0, concat_axis=0, tiled=True)
 
 
-def ring_sums(far, part, block=None):
-    n = part.shape[0]
+def ring_sums(far, gated, weight, block=None):
+    n = lax.axis_size("tensor")
     half = far.shape[0] // 2
 
     def pass_on(right, left):
         right = lax.ppermute(right, "tensor", [(i, (i + 1) % n) for i in range(n)])
         left = lax.ppermute(left, "tensor", [(i, (i - 1) % n) for i in range(n)])
-        return lax.optimization_barrier((right, left))
+        return right, left
 
     right, left = pass_on(far[:half], far[half:])
-    if block is not None:
-        part, block = lax.optimization_barrier((part, block))
-        block = swap(block)
+    made = products(gated, weight, (3, -3, 2, -2))
     for away in range(n // 2 - 1, 0, -1):
-        ahead, behind = part[away], part[n - away]
+        right, left, gated, block = lax.optimization_barrier((right, left, gated, block))
+        ahead, behind = made[away], made[-away]
         if right.shape[0] == half:
             ahead = ahead.at[:half].add(right.astype(F32))
             behind = behind.at[half:].add(left.astype(F32))
         else:
             ahead, behind = ahead + right.astype(F32), behind + left.astype(F32)
         right, left = pass_on(ahead.astype(BF16), behind.astype(BF16))
-    total = part[0] + right.astype(F32) + left.astype(F32)
-    return total if block is None else lax.optimization_barrier((total, block))
+        if away == 3:
+            swapped = None if block is None else swap(block)
+            block = None
+        if away == 2:
+            made |= products(gated, weight, (1, -1, 0))
+    total = made[0] + right.astype(F32) + left.astype(F32)
+    return lax.optimization_barrier((total, swapped))
 
 
 def row_scales(own):
@@ -329,14 +332,11 @@
     )(qkv_kinds, fir_buffer, fir_taps, modal_state, poles, residues, skip_row, finished)
 
     n, own_cols = lax.axis_size("tensor"), norm_gain.shape[0]
-    place = lax.axis_index("tensor").astype(jnp.int32)[None]
-    far_weight = lax.dynamic_slice_in_dim(
-        out_weight, ((place[0] + n // 2) % n) * own_cols, own_cols, 1
-    )
+    gated_home, later_weight = lax.optimization_barrier((gated_home, out_weight))
+    far_place = (lax.axis_index("tensor") + n // 2) % n
+    far_weight = lax.dynamic_slice_in_dim(later_weight, far_place * own_cols, own_cols, 1)
     got = swap(packed)
-    own_home = ring_sums(
-        dot(gated_home, far_weight).astype(BF16), products(place, gated_home, out_weight, n)
-    )
+    own_home, _ = ring_sums(dot(gated_home, far_weight).astype(BF16), gated_home, out_weight)
     got, own_home = lax.optimization_barrier((got, own_home))
 
     sent, gated_band, far = pl.pallas_call(
@@ -366,7 +366,7 @@
         name="band_rows",
     )(turns, got, fir_taps, poles, residues, skip_row, far_weight)
 
-    own_band, back = ring_sums(far, products(place, gated_band, out_weight, n), sent)
+    own_band, back = ring_sums(far, gated_band, out_weight, sent)
     scales = row_scales([own_band, own_home])
     mixed_band = (own_band * scales[: 3 * moving] * norm_gain[None]).astype(BF16)
     mixed_band = jnp.transpose(mixed_band.reshape(3, groups, CAP, own_cols), (1, 0, 2, 3))

time: 146 us -> 143 us (0.979)
  Pallas kernels: 31.3 us -> 36.6 us
  waiting for transfers between devices: 23.8 us -> 18.5 us
  starting transfers between devices: 58.9 us -> 55.5 us
    ppermute x8, waiting for transfers between devices: 19.9 us -> 12 us  [pass_on(): right = lax.ppermute(right, 'tensor', [(i, (i + 1) % n) for i in range(n)])]
    ppermute x8, starting transfers between devices: 7.54 us -> 1.53 us  [pass_on(): right = lax.ppermute(right, 'tensor', [(i, (i + 1) % n) for i in range(n)])]
    pallas_call x2 -> x4, Pallas kernels: 12.9 us -> 18.1 us  [products(): pl.pallas_call(products_kernel, grid_spec=pltpu.PrefetchScalarGridSpec(nu...]
    ppermute x8, starting transfers between devices: 18.3 us -> 22.6 us  [pass_on(): left = lax.ppermute(left, 'tensor', [(i, (i - 1) % n) for i in range(n)])]
    squeeze x2 -> x0, local copies, waits for them, and re-layouts: 2.27 us -> none  [ring_sums(): ahead, behind = (part[away], part[n - away])]
    another operation x0 -> x2, local copies, waits for them, and re-layouts: none -> 2.22 us  [products(): return dict(zip(aways, part))]
    all_to_all x3, waiting for transfers between devices: 2.82 us -> 5.01 us  [swap(): return lax.all_to_all(blocks, 'dp', split_axis=0, concat_axis=0, tiled=True)]
    all_to_all x3, starting transfers between devices: 33 us -> 31.4 us  [swap(): return lax.all_to_all(blocks, 'dp', split_axis=0, concat_axis=0, tiled=True)]
  transfers between devices with their start and end apart: 19 -> 19, of which waited for: 8 -> 7; matrix products, arithmetic and copies ran while one was open for 8% -> 9% of each run, Pallas kernels for 13% -> 17%
where the time goes in v5:
time: 143 us; the launch traced here: 142 us
  starting transfers between devices  55.5 us (39%)
  Pallas kernels  36.6 us (26%)
  waiting for transfers between devices  18.5 us (13%)
  blocking collectives  13.6 us (10%)
  other arithmetic  11.4 us (8%)
  local copies, waits for them, and re-layouts  5.22 us (4%)
    all_to_all x3, starting transfers between devices, swap(): return lax.all_to_all(blocks, 'dp', split_axis=0, concat_axis=0, tiled=True)  31.4 us
    ppermute x8, starting transfers between devices, pass_on(): left = lax.ppermute(left, 'tensor', [(i, (i - 1) % n) for i in range(n)])  22.6 us
    pallas_call x4, Pallas kernels, products(): pl.pallas_call(products_kernel, grid_spec=pltpu.PrefetchScalarGridSpec(nu...  18.1 us
    psum x1, blocking collectives, row_scales(): lax.psum(jnp.concatenate([jnp.sum(x * x, axis=1) for x in own]), 'tensor')  13.6 us
    ppermute x8, waiting for transfers between devices, pass_on(): right = lax.ppermute(right, 'tensor', [(i, (i + 1) % n) for i in range(n)])  12 us
    pallas_call x1, Pallas kernels, per_device(): pl.pallas_call(home_kernel, grid=(slots // 16,), in_specs=[pl.BlockSpec((...  6.86 us
    pallas_call x1, Pallas kernels, per_device(): pl.pallas_call(band_kernel, in_specs=[pl.BlockSpec(memory_space=pltpu.SME...  6.26 us
    pallas_call x1, Pallas kernels, per_device(): pl.pallas_call(finish_kernel, grid=(slots // 16,), in_specs=[pl.BlockSpec...  5.32 us
  transfers between devices with their start and end apart: 19, of which 7 were waited for; matrix products, arithmetic and copies ran while one was open for 9% of the time, Pallas kernels for 17%

profile of v5, /device:TPU:1, one launch (start us, length us, event | category | flops | bytes accessed | tf_op | source)
XLA Modules:
  0.0 142.0 jit_solution(5311107822367589631)
XLA Ops:
  0.6 6.9 %home_rows.1 = (bf16[32,64,512]{2,1,0:T(8,128)(2,1)}, bf16[128,512]{1,0:T(8,128)(2,1)}, f32[16,16,512]{2,1,0:T(8,128)}) custom-call(bf16[4,3,80,512]{3,2,1,0:T(8,128)(2,1)} %bitcast.105, bf16[80,3,2,512]{3,2,1,0:T(2,128)(2,1)} %fir.1, f32[3,3,512]{2,1,0:T(4,128)} %taps.3, f32[80,16,512]{2,1,0:T(8,128)} %state.1, f32[16,512]{1,0:T(8,128)} %poles.3, ...), custom_call_target="tpu_custom_call" | custom-call | tf_op jit(solution)/shard_map/home_rows/pallas_call | solution.py:306
  7.5 8.7 %all-to-all-start = ((bf16[32,64,512]{2,1,0:T(8,128)(2,1)}), bf16[32,64,512]{2,1,0:T(8,128)(2,1)S(1)}, u32[]{:S(2)}, u32[]{:S(2)}) async-start(bf16[32,64,512]{2,1,0:T(8,128)(2,1)} %get-tuple-element.84), calls=%async_computation | async-start | bytes 4194304 | tf_op jit(solution)/shard_map/all_to_all | solution.py:246
  16.3 1.1 constant_dynamic-slice_fusion.far_weight
  17.4 0.2 convolution_convert_fusion
  17.6 5.7 %collective-permute-start.1 = (bf16[64,512]{1,0:T(8,128)(2,1)S(1)}, bf16[64,512]{1,0:T(8,128)(2,1)S(1)}, u32[]{:S(2)}, u32[]{:S(2)}) collective-permute-start(bf16[64,512]{1,0:T(8,128)(2,1)S(1)} %get-tuple-element.135), channel_id=1, source_target_pairs={{0,7},{1,0},{2,1},{3,2},{4,3},{5,4},{6,5},{7,6},{8,15},{9,8},{10,9... | collective-permute-start | bytes 196616 | tf_op jit(solution)/shard_map/ppermute | solution.py:255
  23.3 0.6 and_select_fusion.1.place
  23.9 4.8 %ring_products.4 = f32[4,128,512]{2,1,0:T(8,128)} custom-call(s32[4]{0:T(128)} %and_select_fusion.1.place, bf16[128,512]{1,0:T(8,128)(2,1)} %get-tuple-element.91.gated, bf16[512,4096]{1,0:T(8,128)(2,1)} %weight.7), custom_call_target="tpu_custom_call" | custom-call | flops 4294967296 | bytes 4194304 | tf_op jit(solution)/shard_map/ring_products/pallas_call | solution.py:186
  28.7 1.1 slice_bitcast_fusion.12
  29.9 0.1 reduce.8
  30.0 1.0 fusion.25
  31.0 2.8 %collective-permute-start.3 = (bf16[128,512]{1,0:T(8,128)(2,1)S(1)}, bf16[128,512]{1,0:T(8,128)(2,1)S(1)}, u32[]{:S(2)}, u32[]{:S(2)}) collective-permute-start(bf16[128,512]{1,0:T(8,128)(2,1)S(1)} %get-tuple-element.127), channel_id=1, source_target_pairs={{0,7},{1,0},{2,1},{3,2},{4,3},{5,4},{6,5},{7,6},{8,15},{9,8},{10,9... | collective-permute-start | bytes 393224 | tf_op jit(solution)/shard_map/ppermute | solution.py:255
  33.8 0.5 and_select_fusion
  34.3 1.4 %collective-permute-done.3 = bf16[128,512]{1,0:T(8,128)(2,1)S(1)} collective-permute-done((bf16[128,512]{1,0:T(8,128)(2,1)S(1)}, bf16[128,512]{1,0:T(8,128)(2,1)S(1)}, u32[]{:S(2)}, u32[]{:S(2)}) %collective-permute-start.3) | collective-permute-done | bytes 131104 | tf_op jit(solution)/shard_map/ppermute | solution.py:255
  35.7 3.4 %collective-permute-done.2 = bf16[128,512]{1,0:T(8,128)(2,1)S(1)} collective-permute-done((bf16[128,512]{1,0:T(8,128)(2,1)S(1)}, bf16[128,512]{1,0:T(8,128)(2,1)S(1)}, u32[]{:S(2)}, u32[]{:S(2)}) %collective-permute-start.2) | collective-permute-done | bytes 131104 | tf_op jit(solution)/shard_map/ppermute | solution.py:254
  39.1 1.1 fusion.13
  40.2 0.2 collective-permute-start.5
  40.4 1.3 collective-permute-start.4
  41.8 4.1 %ring_products.5 = f32[3,128,512]{2,1,0:T(8,128)} custom-call(s32[3]{0:T(128)} %get-tuple-element.138.place, bf16[128,512]{1,0:T(8,128)(2,1)} %get-tuple-element.91.gated, bf16[512,4096]{1,0:T(8,128)(2,1)} %weight.7), custom_call_target="tpu_custom_call" | custom-call | flops 4294967296 | bytes 4194304 | tf_op jit(solution)/shard_map/ring_products/pallas_call | solution.py:186
  45.9 1.1 fusion.17
  47.1 2.7 %collective-permute-start.7 = (bf16[128,512]{1,0:T(8,128)(2,1)S(1)}, bf16[128,512]{1,0:T(8,128)(2,1)S(1)}, u32[]{:S(2)}, u32[]{:S(2)}) collective-permute-start(bf16[128,512]{1,0:T(8,128)(2,1)S(1)} %get-tuple-element.132), channel_id=1, source_target_pairs={{0,7},{1,0},{2,1},{3,2},{4,3},{5,4},{6,5},{7,6},{8,15},{9,8},{10,9... | collective-permute-start | bytes 393224 | tf_op jit(solution)/shard_map/ppermute | solution.py:255
  49.7 2.4 %collective-permute-done.6 = bf16[128,512]{1,0:T(8,128)(2,1)S(1)} collective-permute-done((bf16[128,512]{1,0:T(8,128)(2,1)S(1)}, bf16[128,512]{1,0:T(8,128)(2,1)S(1)}, u32[]{:S(2)}, u32[]{:S(2)}) %collective-permute-start.6) | collective-permute-done | bytes 131104 | tf_op jit(solution)/shard_map/ppermute | solution.py:254
  52.1 1.0 fusion.19
  53.2 6.3 %band_rows.1 = (bf16[32,48,512]{2,1,0:T(8,128)(2,1)}, bf16[192,512]{1,0:T(8,128)(2,1)S(1)}, bf16[192,512]{1,0:T(8,128)(2,1)S(1)}) custom-call(s32[3]{0:T(128)S(1)} %get-tuple-element.137.turns, bf16[32,64,512]{2,1,0:T(8,128)(2,1)S(1)} %all-to-all-done.got_hbm, f32[3,3,512]{2,1,0:T(4,128)S(1)} %copy-done.2, f32[16,512]{1,0:T(8,128)S(1)} %copy-done, ...), custom_call_target="tpu_custom_call" | custom-call | tf_op jit(solution)/shard_map/band_rows/pallas_call | solution.py:342
  59.5 0.6 copy-done.4
  60.1 2.7 %collective-permute-start.9 = (bf16[96,512]{1,0:T(8,128)(2,1)S(1)}, bf16[96,512]{1,0:T(8,128)(2,1)S(1)}, u32[]{:S(2)}, u32[]{:S(2)}) collective-permute-start(bf16[96,512]{1,0:T(8,128)(2,1)S(1)} %get-tuple-element.133), channel_id=1, source_target_pairs={{0,7},{1,0},{2,1},{3,2},{4,3},{5,4},{6,5},{7,6},{8,15},{9,8},{10,9... | collective-permute-start | bytes 294920 | tf_op jit(solution)/shard_map/ppermute | solution.py:255
  62.8 4.9 %ring_products.6 = f32[4,192,512]{2,1,0:T(8,128)} custom-call(s32[4]{0:T(128)} %and_select_fusion.1.place, bf16[192,512]{1,0:T(8,128)(2,1)} %copy-done.4, bf16[512,4096]{1,0:T(8,128)(2,1)} %weight.7), custom_call_target="tpu_custom_call" | custom-call | flops 6442450944 | bytes 4194304 | tf_op jit(solution)/shard_map/ring_products/pallas_call | solution.py:186
  67.7 1.2 slice_bitcast_fusion.5
  68.9 1.1 fusion.21
  69.9 2.9 %collective-permute-start.11 = (bf16[192,512]{1,0:T(8,128)(2,1)S(1)}, bf16[192,512]{1,0:T(8,128)(2,1)S(1)}, u32[]{:S(2)}, u32[]{:S(2)}) collective-permute-start(bf16[192,512]{1,0:T(8,128)(2,1)S(1)} %get-tuple-element.119), channel_id=1, source_target_pairs={{0,7},{1,0},{2,1},{3,2},{4,3},{5,4},{6,5},{7,6},{8,15},{9,8},{10,9... | collective-permute-start | bytes 589832 | tf_op jit(solution)/shard_map/ppermute | solution.py:255
  72.9 12.0 %all-to-all-start.1 = ((bf16[32,48,512]{2,1,0:T(8,128)(2,1)}), bf16[32,48,512]{2,1,0:T(8,128)(2,1)S(1)}, u32[]{:S(2)}, u32[]{:S(2)}) async-start(bf16[32,48,512]{2,1,0:T(8,128)(2,1)} %get-tuple-element.109), calls=%async_computation.1 | async-start | bytes 3145728 | tf_op jit(solution)/shard_map/all_to_all | solution.py:246
  84.9 1.2 fusion.3
  86.1 3.0 %collective-permute-start.13 = (bf16[192,512]{1,0:T(8,128)(2,1)S(1)}, bf16[192,512]{1,0:T(8,128)(2,1)S(1)}, u32[]{:S(2)}, u32[]{:S(2)}) collective-permute-start(bf16[192,512]{1,0:T(8,128)(2,1)S(1)} %get-tuple-element.117), channel_id=1, source_target_pairs={{0,7},{1,0},{2,1},{3,2},{4,3},{5,4},{6,5},{7,6},{8,15},{9,8},{10,9... | collective-permute-start | bytes 589832 | tf_op jit(solution)/shard_map/ppermute | solution.py:255
  89.2 4.3 %ring_products.7 = f32[3,192,512]{2,1,0:T(8,128)} custom-call(s32[3]{0:T(128)} %get-tuple-element.138.place, bf16[192,512]{1,0:T(8,128)(2,1)} %copy-done.4, bf16[512,4096]{1,0:T(8,128)(2,1)} %weight.7), custom_call_target="tpu_custom_call" | custom-call | flops 6442450944 | bytes 4194304 | tf_op jit(solution)/shard_map/ring_products/pallas_call | solution.py:186
  93.5 2.8 %collective-permute-done.12 = bf16[192,512]{1,0:T(8,128)(2,1)S(1)} collective-permute-done((bf16[192,512]{1,0:T(8,128)(2,1)S(1)}, bf16[192,512]{1,0:T(8,128)(2,1)S(1)}, u32[]{:S(2)}, u32[]{:S(2)}) %collective-permute-start.12) | collective-permute-done | bytes 196640 | tf_op jit(solution)/shard_map/ppermute | solution.py:254
  96.3 1.2 fusion.7
  97.7 2.7 %collective-permute-start.15 = (bf16[192,512]{1,0:T(8,128)(2,1)S(1)}, bf16[192,512]{1,0:T(8,128)(2,1)S(1)}, u32[]{:S(2)}, u32[]{:S(2)}) collective-permute-start(bf16[192,512]{1,0:T(8,128)(2,1)S(1)} %get-tuple-element.124), channel_id=1, source_target_pairs={{0,7},{1,0},{2,1},{3,2},{4,3},{5,4},{6,5},{7,6},{8,15},{9,8},{10,9... | collective-permute-start | bytes 589832 | tf_op jit(solution)/shard_map/ppermute | solution.py:255
  100.3 0.1 multiply_reduce_fusion.1
  100.4 3.5 %collective-permute-done.14 = bf16[192,512]{1,0:T(8,128)(2,1)S(1)} collective-permute-done((bf16[192,512]{1,0:T(8,128)(2,1)S(1)}, bf16[192,512]{1,0:T(8,128)(2,1)S(1)}, u32[]{:S(2)}, u32[]{:S(2)}) %collective-permute-start.14) | collective-permute-done | bytes 196640 | tf_op jit(solution)/shard_map/ppermute | solution.py:254
  103.9 1.1 fusion.9
  105.0 2.1 %all-to-all-done.1.back = bf16[32,48,512]{2,1,0:T(8,128)(2,1)S(1)} async-done(((bf16[32,48,512]{2,1,0:T(8,128)(2,1)}), bf16[32,48,512]{2,1,0:T(8,128)(2,1)S(1)}, u32[]{:S(2)}, u32[]{:S(2)}) %all-to-all-start.1) | async-done | bytes 1572896 | tf_op jit(solution)/shard_map/all_to_all | solution.py:246
  107.1 0.1 multiply_reduce_fusion
  107.3 13.6 %psum.7 = f32[320]{0:T(512)S(1)} all-reduce(f32[320]{0:T(512)S(1)} %pad_maximum_fusion), channel_id=1, replica_groups=mesh['dp'=32,'tensor'=8] {'tensor'}, use_global_device_ids=true, to_apply=%region_3.4 | all-reduce | flops 320 | bytes 2560 | tf_op jit(solution)/shard_map/psum | solution.py:280
  121.3 0.8 copy.22
  122.1 10.7 %all-to-all-start.2 = ((bf16[32,3,2,512]{3,2,1,0:T(2,128)(2,1)}), bf16[32,3,2,512]{3,2,1,0:T(2,128)(2,1)S(1)}, u32[]{:S(2)}, u32[]{:S(2)}) async-start(bf16[32,3,2,512]{3,2,1,0:T(2,128)(2,1)} %bitcast.102), calls=%async_computation.2 | async-start | bytes 393216 | tf_op jit(solution)/shard_map/all_to_all | solution.py:246
  132.8 5.3 %last_rows.1 = (f32[80,16,512]{2,1,0:T(8,128)}, bf16[80,3,2,512]{3,2,1,0:T(2,128)(2,1)}) custom-call(bf16[32,48,512]{2,1,0:T(8,128)(2,1)} %copy-done.5, bf16[4,3,80,512]{3,2,1,0:T(8,128)(2,1)} %bitcast.106, f32[16,16,512]{2,1,0:T(8,128)} %get-tuple-element.114.stay_state, s32[3,80]{1,0:T(4,128)} %finished.3), custom_call_target="tpu_custom_call" | custom-call | tf_op jit(solution)/shard_map/last_rows/pallas_call | solution.py:375
  138.1 2.9 %all-to-all-done.2 = bf16[32,3,2,512]{3,2,1,0:T(2,128)(2,1)S(1)} async-done(((bf16[32,3,2,512]{3,2,1,0:T(2,128)(2,1)}), bf16[32,3,2,512]{3,2,1,0:T(2,128)(2,1)S(1)}, u32[]{:S(2)}, u32[]{:S(2)}) %all-to-all-start.2) | async-done | bytes 196640 | tf_op jit(solution)/shard_map/all_to_all | solution.py:246
  141.0 0.1 copy.20
  141.3 0.8 maximum_maximum_fusion
  (54 shorter events, 0.9 us)
Async XLA Ops:
  7.5 9.9 %copy-start.6 = (bf16[128,512]{1,0:T(8,128)(2,1)S(1)}, bf16[128,512]{1,0:T(8,128)(2,1)}, u32[]{:S(2)}) copy-start(bf16[128,512]{1,0:T(8,128)(2,1)} %get-tuple-element.91.gated) | copy-start | bytes 393220
  7.5 45.6 %all-to-all-start = ((bf16[32,64,512]{2,1,0:T(8,128)(2,1)}), bf16[32,64,512]{2,1,0:T(8,128)(2,1)S(1)}, u32[]{:S(2)}, u32[]{:S(2)}) async-start(bf16[32,64,512]{2,1,0:T(8,128)(2,1)} %get-tuple-element.84), calls=%async_computation | async-start | bytes 4194304 | tf_op jit(solution)/shard_map/all_to_all | solution.py:246
  16.2 7.0 %copy-start.10 = (s32[4]{0:T(128)S(1)}, s32[4]{0:T(128)}, u32[]{:S(2)}) copy-start(s32[4]{0:T(128)} %constant.195.clone) | copy-start | bytes 52
  17.6 12.4 %collective-permute-start.1 = (bf16[64,512]{1,0:T(8,128)(2,1)S(1)}, bf16[64,512]{1,0:T(8,128)(2,1)S(1)}, u32[]{:S(2)}, u32[]{:S(2)}) collective-permute-start(bf16[64,512]{1,0:T(8,128)(2,1)S(1)} %get-tuple-element.135), channel_id=1, source_target_pairs={{0,7},{1,0},{2,1},{3,2},{4,3},{5,4},{6,5},{7,6},{8,15},{9,8},{10,9... | collective-permute-start | bytes 196616 | tf_op jit(solution)/shard_map/ppermute | solution.py:255
  23.3 6.8 %collective-permute-start = (bf16[64,512]{1,0:T(8,128)(2,1)S(1)}, bf16[64,512]{1,0:T(8,128)(2,1)S(1)}, u32[]{:S(2)}, u32[]{:S(2)}) collective-permute-start(bf16[64,512]{1,0:T(8,128)(2,1)S(1)} %get-tuple-element.136), channel_id=1, source_target_pairs={{0,1},{1,2},{2,3},{3,4},{4,5},{5,6},{6,7},{7,0},{8,9},{9,10},{10,1... | collective-permute-start | bytes 196616 | tf_op jit(solution)/shard_map/ppermute | solution.py:254
  23.9 5.9 %copy-start.8 = (s32[3,80]{1,0:T(4,128)S(1)}, s32[3,80]{1,0:T(4,128)}, u32[]{:S(2)}) copy-start(s32[3,80]{1,0:T(4,128)} %param.33) | copy-start | bytes 2884
  23.9 9.9 %copy-start.9 = (s32[3]{0:T(128)S(1)}, s32[3]{0:T(128)}, u32[]{:S(2)}) copy-start(s32[3]{0:T(128)} %constant.196.clone) | copy-start | bytes 40
  31.0 4.7 %collective-permute-start.3 = (bf16[128,512]{1,0:T(8,128)(2,1)S(1)}, bf16[128,512]{1,0:T(8,128)(2,1)S(1)}, u32[]{:S(2)}, u32[]{:S(2)}) collective-permute-start(bf16[128,512]{1,0:T(8,128)(2,1)S(1)} %get-tuple-element.127), channel_id=1, source_target_pairs={{0,7},{1,0},{2,1},{3,2},{4,3},{5,4},{6,5},{7,6},{8,15},{9,8},{10,9... | collective-permute-start | bytes 393224 | tf_op jit(solution)/shard_map/ppermute | solution.py:255
  33.8 5.3 %collective-permute-start.2 = (bf16[128,512]{1,0:T(8,128)(2,1)S(1)}, bf16[128,512]{1,0:T(8,128)(2,1)S(1)}, u32[]{:S(2)}, u32[]{:S(2)}) collective-permute-start(bf16[128,512]{1,0:T(8,128)(2,1)S(1)} %get-tuple-element.128), channel_id=1, source_target_pairs={{0,1},{1,2},{2,3},{3,4},{4,5},{5,6},{6,7},{7,0},{8,9},{9,10},{10,1... | collective-permute-start | bytes 393224 | tf_op jit(solution)/shard_map/ppermute | solution.py:254
  40.2 5.6 %collective-permute-start.5 = (bf16[128,512]{1,0:T(8,128)(2,1)S(1)}, bf16[128,512]{1,0:T(8,128)(2,1)S(1)}, u32[]{:S(2)}, u32[]{:S(2)}) collective-permute-start(bf16[128,512]{1,0:T(8,128)(2,1)S(1)} %get-tuple-element.125), channel_id=1, source_target_pairs={{0,7},{1,0},{2,1},{3,2},{4,3},{5,4},{6,5},{7,6},{8,15},{9,8},{10,9... | collective-permute-start | bytes 393224 | tf_op jit(solution)/shard_map/ppermute | solution.py:255
  40.4 5.5 %collective-permute-start.4 = (bf16[128,512]{1,0:T(8,128)(2,1)S(1)}, bf16[128,512]{1,0:T(8,128)(2,1)S(1)}, u32[]{:S(2)}, u32[]{:S(2)}) collective-permute-start(bf16[128,512]{1,0:T(8,128)(2,1)S(1)} %get-tuple-element.126), channel_id=1, source_target_pairs={{0,1},{1,2},{2,3},{3,4},{4,5},{5,6},{6,7},{7,0},{8,9},{9,10},{10,1... | collective-permute-start | bytes 393224 | tf_op jit(solution)/shard_map/ppermute | solution.py:254
  45.8 7.3 %copy-start = (f32[16,512]{1,0:T(8,128)S(1)}, f32[16,512]{1,0:T(8,128)}, u32[]{:S(2)}) copy-start(f32[16,512]{1,0:T(8,128)} %poles.3) | copy-start | bytes 98308
  45.8 7.3 %copy-start.1 = (f32[16,512]{1,0:T(8,128)S(1)}, f32[16,512]{1,0:T(8,128)}, u32[]{:S(2)}) copy-start(f32[16,512]{1,0:T(8,128)} %residues.3) | copy-start | bytes 98308
  45.8 7.3 %copy-start.2 = (f32[3,3,512]{2,1,0:T(4,128)S(1)}, f32[3,3,512]{2,1,0:T(4,128)}, u32[]{:S(2)}) copy-start(f32[3,3,512]{2,1,0:T(4,128)} %taps.3) | copy-start | bytes 55300
  45.8 7.3 %copy-start.3 = (f32[512]{0:T(512)S(1)}, f32[512]{0:T(512)}, u32[]{:S(2)}) copy-start(f32[512]{0:T(512)} %param.29) | copy-start | bytes 6148
  47.0 5.1 %collective-permute-start.6 = (bf16[128,512]{1,0:T(8,128)(2,1)S(1)}, bf16[128,512]{1,0:T(8,128)(2,1)S(1)}, u32[]{:S(2)}, u32[]{:S(2)}) collective-permute-start(bf16[128,512]{1,0:T(8,128)(2,1)S(1)} %get-tuple-element.131), channel_id=1, source_target_pairs={{0,1},{1,2},{2,3},{3,4},{4,5},{5,6},{6,7},{7,0},{8,9},{9,10},{10,1... | collective-permute-start | bytes 393224 | tf_op jit(solution)/shard_map/ppermute | solution.py:254
  47.1 5.0 %collective-permute-start.7 = (bf16[128,512]{1,0:T(8,128)(2,1)S(1)}, bf16[128,512]{1,0:T(8,128)(2,1)S(1)}, u32[]{:S(2)}, u32[]{:S(2)}) collective-permute-start(bf16[128,512]{1,0:T(8,128)(2,1)S(1)} %get-tuple-element.132), channel_id=1, source_target_pairs={{0,7},{1,0},{2,1},{3,2},{4,3},{5,4},{6,5},{7,6},{8,15},{9,8},{10,9... | collective-permute-start | bytes 393224 | tf_op jit(solution)/shard_map/ppermute | solution.py:255
  59.4 0.7 copy-start.4
  60.1 8.7 %collective-permute-start.9 = (bf16[96,512]{1,0:T(8,128)(2,1)S(1)}, bf16[96,512]{1,0:T(8,128)(2,1)S(1)}, u32[]{:S(2)}, u32[]{:S(2)}) collective-permute-start(bf16[96,512]{1,0:T(8,128)(2,1)S(1)} %get-tuple-element.133), channel_id=1, source_target_pairs={{0,7},{1,0},{2,1},{3,2},{4,3},{5,4},{6,5},{7,6},{8,15},{9,8},{10,9... | collective-permute-start | bytes 294920 | tf_op jit(solution)/shard_map/ppermute | solution.py:255
  62.8 6.1 %collective-permute-start.8 = (bf16[96,512]{1,0:T(8,128)(2,1)S(1)}, bf16[96,512]{1,0:T(8,128)(2,1)S(1)}, u32[]{:S(2)}, u32[]{:S(2)}) collective-permute-start(bf16[96,512]{1,0:T(8,128)(2,1)S(1)} %get-tuple-element.134), channel_id=1, source_target_pairs={{0,1},{1,2},{2,3},{3,4},{4,5},{5,6},{6,7},{7,0},{8,9},{9,10},{10,1... | collective-permute-start | bytes 294920 | tf_op jit(solution)/shard_map/ppermute | solution.py:254
  69.9 14.9 %collective-permute-start.11 = (bf16[192,512]{1,0:T(8,128)(2,1)S(1)}, bf16[192,512]{1,0:T(8,128)(2,1)S(1)}, u32[]{:S(2)}, u32[]{:S(2)}) collective-permute-start(bf16[192,512]{1,0:T(8,128)(2,1)S(1)} %get-tuple-element.119), channel_id=1, source_target_pairs={{0,7},{1,0},{2,1},{3,2},{4,3},{5,4},{6,5},{7,6},{8,15},{9,8},{10,9... | collective-permute-start | bytes 589832 | tf_op jit(solution)/shard_map/ppermute | solution.py:255
  72.9 12.0 %collective-permute-start.10 = (bf16[192,512]{1,0:T(8,128)(2,1)S(1)}, bf16[192,512]{1,0:T(8,128)(2,1)S(1)}, u32[]{:S(2)}, u32[]{:S(2)}) collective-permute-start(bf16[192,512]{1,0:T(8,128)(2,1)S(1)} %get-tuple-element.120), channel_id=1, source_target_pairs={{0,1},{1,2},{2,3},{3,4},{4,5},{5,6},{6,7},{7,0},{8,9},{9,10},{10,1... | collective-permute-start | bytes 589832 | tf_op jit(solution)/shard_map/ppermute | solution.py:254
  72.9 34.2 %all-to-all-start.1 = ((bf16[32,48,512]{2,1,0:T(8,128)(2,1)}), bf16[32,48,512]{2,1,0:T(8,128)(2,1)S(1)}, u32[]{:S(2)}, u32[]{:S(2)}) async-start(bf16[32,48,512]{2,1,0:T(8,128)(2,1)} %get-tuple-element.109), calls=%async_computation.1 | async-start | bytes 3145728 | tf_op jit(solution)/shard_map/all_to_all | solution.py:246
  86.1 7.4 %collective-permute-start.13 = (bf16[192,512]{1,0:T(8,128)(2,1)S(1)}, bf16[192,512]{1,0:T(8,128)(2,1)S(1)}, u32[]{:S(2)}, u32[]{:S(2)}) collective-permute-start(bf16[192,512]{1,0:T(8,128)(2,1)S(1)} %get-tuple-element.117), channel_id=1, source_target_pairs={{0,7},{1,0},{2,1},{3,2},{4,3},{5,4},{6,5},{7,6},{8,15},{9,8},{10,9... | collective-permute-start | bytes 589832 | tf_op jit(solution)/shard_map/ppermute | solution.py:255
  89.2 7.2 %collective-permute-start.12 = (bf16[192,512]{1,0:T(8,128)(2,1)S(1)}, bf16[192,512]{1,0:T(8,128)(2,1)S(1)}, u32[]{:S(2)}, u32[]{:S(2)}) collective-permute-start(bf16[192,512]{1,0:T(8,128)(2,1)S(1)} %get-tuple-element.118), channel_id=1, source_target_pairs={{0,1},{1,2},{2,3},{3,4},{4,5},{5,6},{6,7},{7,0},{8,9},{9,10},{10,1... | collective-permute-start | bytes 589832 | tf_op jit(solution)/shard_map/ppermute | solution.py:254
  93.5 27.5 %copy-start.7 = (f32[512]{0:T(512)S(1)}, f32[512]{0:T(512)}, u32[]{:S(2)}) copy-start(f32[512]{0:T(512)} %param.31) | copy-start | bytes 6148
  97.6 6.3 %collective-permute-start.14 = (bf16[192,512]{1,0:T(8,128)(2,1)S(1)}, bf16[192,512]{1,0:T(8,128)(2,1)S(1)}, u32[]{:S(2)}, u32[]{:S(2)}) collective-permute-start(bf16[192,512]{1,0:T(8,128)(2,1)S(1)} %get-tuple-element.123), channel_id=1, source_target_pairs={{0,1},{1,2},{2,3},{3,4},{4,5},{5,6},{6,7},{7,0},{8,9},{9,10},{10,1... | collective-permute-start | bytes 589832 | tf_op jit(solution)/shard_map/ppermute | solution.py:254
  97.7 6.2 %collective-permute-start.15 = (bf16[192,512]{1,0:T(8,128)(2,1)S(1)}, bf16[192,512]{1,0:T(8,128)(2,1)S(1)}, u32[]{:S(2)}, u32[]{:S(2)}) collective-permute-start(bf16[192,512]{1,0:T(8,128)(2,1)S(1)} %get-tuple-element.124), channel_id=1, source_target_pairs={{0,7},{1,0},{2,1},{3,2},{4,3},{5,4},{6,5},{7,6},{8,15},{9,8},{10,9... | collective-permute-start | bytes 589832 | tf_op jit(solution)/shard_map/ppermute | solution.py:255
  107.1 25.7 %copy-start.5 = (bf16[32,48,512]{2,1,0:T(8,128)(2,1)}, bf16[32,48,512]{2,1,0:T(8,128)(2,1)S(1)}, u32[]{:S(2)}) copy-start(bf16[32,48,512]{2,1,0:T(8,128)(2,1)S(1)} %all-to-all-done.1.back) | copy-start | bytes 4718596
  122.1 19.0 %all-to-all-start.2 = ((bf16[32,3,2,512]{3,2,1,0:T(2,128)(2,1)}), bf16[32,3,2,512]{3,2,1,0:T(2,128)(2,1)S(1)}, u32[]{:S(2)}, u32[]{:S(2)}) async-start(bf16[32,3,2,512]{3,2,1,0:T(2,128)(2,1)} %bitcast.102), calls=%async_computation.2 | async-start | bytes 393216 | tf_op jit(solution)/shard_map/all_to_all | solution.py:246

commit v6 on v5

--- a/solution.py
+++ b/solution.py
@@ -19,36 +19,65 @@
     return jnp.concatenate([x] * (width // x.shape[-1]), axis=-1)
 
 
-def home_kernel(qkv, fir, taps, state, poles, residues, skip, finished, packed, gated, stay_state, y_rows):
-    block = pl.program_id(0)
-    rows, width = 16, qkv.shape[-1]
-    at = lax.broadcasted_iota(jnp.int32, (rows, finished.shape[1]), 0) + block * rows
-    own = at == lax.broadcasted_iota(jnp.int32, at.shape, 1)
-    alive = [
-        jnp.broadcast_to(
-            1.0 - jnp.sum(jnp.where(own, finished[t : t + 1].astype(F32), 0.0), axis=1, keepdims=True),
-            (rows, width),
-        )
-        for t in range(3)
-    ]
-    alive0 = alive[0]
-    q0 = [qkv[0, j].astype(F32) for j in range(3)]
-    l0 = [fir[:, j].astype(F32)[:, 0] for j in range(3)]
-    l1 = [fir[:, j].astype(F32)[:, 1] for j in range(3)]
-    f = [
-        taps[j, 0:1] * q0[j] + taps[j, 1:2] * l0[j] + taps[j, 2:3] * l1[j]
-        for j in range(3)
-    ]
-    product = f[1] * f[2]
-    modes = []
-    for r in range(rows):
-        s = poles[...] * state[r] + product[r : r + 1]
-        y_rows[r : r + 1] = jnp.sum(residues[...] * s, axis=0, keepdims=True)
-        modes.append(s * alive0[r : r + 1])
-    gated[pl.ds(block * rows, rows)] = (f[0] * (y_rows[...] + skip[...] * product)).astype(BF16)
-
-    @pl.when(block < 4)
-    def _():
+def home_kernel(qkv_hbm, fir_hbm, state_hbm, taps, poles, residues, skip, finished, packed_hbm, *rest):
+    gated, stay_state, qkv_all, fir_all, state_all, packed_all, y_rows, sems = rest
+    rows, width = 16, qkv_hbm.shape[-1]
+    blocks = qkv_hbm.shape[2] // rows
+
+    def fetches(block):
+        at = pl.ds(block * rows, rows)
+        return [
+            pltpu.make_async_copy(state_hbm.at[at], state_all.at[at], sems.at[0, block]),
+            pltpu.make_async_copy(qkv_hbm.at[:, :, at], qkv_all.at[:, :, at], sems.at[1, block]),
+            pltpu.make_async_copy(fir_hbm.at[at], fir_all.at[at], sems.at[2, block]),
+        ]
+
+    def store(block):
+        at = pl.ds(block * (rows // 2), rows // 2)
+        return pltpu.make_async_copy(packed_all.at[at], packed_hbm.at[at], sems.at[3, block])
+
+    for block in range(blocks):
+        for fetch in fetches(block):
+            fetch.start()
+
+    def first_step(block):
+        for fetch in fetches(block):
+            fetch.wait()
+        start = pl.multiple_of(block * rows, rows)
+        qkv = qkv_all.at[:, :, pl.ds(start, rows)]
+        fir = fir_all.at[pl.ds(start, rows)]
+        state = state_all.at[pl.ds(start, rows)]
+        at = lax.broadcasted_iota(jnp.int32, (rows, finished.shape[1]), 0) + block * rows
+        own = at == lax.broadcasted_iota(jnp.int32, at.shape, 1)
+        alive = [
+            jnp.broadcast_to(
+                1.0 - jnp.sum(jnp.where(own, finished[t : t + 1].astype(F32), 0.0), axis=1, keepdims=True),
+                (rows, width),
+            )
+            for t in range(3)
+        ]
+        alive0 = alive[0]
+        q0 = [qkv[0, j].astype(F32) for j in range(3)]
+        l0 = [fir[:, j].astype(F32)[:, 0] for j in range(3)]
+        l1 = [fir[:, j].astype(F32)[:, 1] for j in range(3)]
+        f = [
+            taps[j, 0:1] * q0[j] + taps[j, 1:2] * l0[j] + taps[j, 2:3] * l1[j]
+            for j in range(3)
+        ]
+        product = f[1] * f[2]
+        modes = []
+        for r in range(rows):
+            s = poles[...] * state[r] + product[r : r + 1]
+            y_rows[r : r + 1] = jnp.sum(residues[...] * s, axis=0, keepdims=True)
+            modes.append(s * alive0[r : r + 1])
+        gated[pl.ds(block * rows, rows)] = (f[0] * (y_rows[...] + skip[...] * product)).astype(BF16)
+        return qkv, q0, l0, alive, modes
+
+    @pl.loop(0, blocks - 1)
+    def _(block):
+        qkv, q0, l0, alive, modes = first_step(block)
+        alive0 = alive[0]
+        packed = packed_all.at[pl.ds(pl.multiple_of(block * (rows // 2), rows // 2), rows // 2)]
         for pair in range(rows // 2):
             both = jnp.concatenate([modes[2 * pair], modes[2 * pair + 1]], axis=0)
             packed[pair, 0 : 2 * MODES] = both.astype(BF16)
@@ -64,33 +93,36 @@
         order = jnp.where(c == source, 1.0, 0.0).astype(BF16)
         moved = dot(order, stacked).reshape(rows // 2, 2 * KINDS, width)
         packed[:, 2 * MODES :] = moved.astype(BF16)
-
-    @pl.when(block == 4)
-    def _():
+        store(block).start()
+
+    qkv, q0, l0, alive, modes = first_step(blocks - 1)
+    alive0 = alive[0]
+    for r in range(rows):
+        stay_state[r] = modes[r]
+    lag0, lag1 = [x * alive0 for x in q0], [x * alive0 for x in l0]
+    for t in range(1, 4):
+        q = [qkv[t, j].astype(F32) for j in range(3)]
+        g = [
+            taps[j, 0:1] * q[j] + taps[j, 1:2] * lag0[j] + taps[j, 2:3] * lag1[j]
+            for j in range(3)
+        ]
+        prod = g[1] * g[2]
+        live = alive[t] if t < 3 else None
         for r in range(rows):
-            stay_state[r] = modes[r]
-        lag0, lag1 = [x * alive0 for x in q0], [x * alive0 for x in l0]
-        for t in range(1, 4):
-            q = [qkv[t, j].astype(F32) for j in range(3)]
-            g = [
-                taps[j, 0:1] * q[j] + taps[j, 1:2] * lag0[j] + taps[j, 2:3] * lag1[j]
-                for j in range(3)
-            ]
-            prod = g[1] * g[2]
-            live = alive[t] if t < 3 else None
-            for r in range(rows):
-                s = poles[...] * stay_state[r] + prod[r : r + 1]
-                y_rows[r : r + 1] = jnp.sum(residues[...] * s, axis=0, keepdims=True)
-                stay_state[r] = s * live[r : r + 1] if t < 3 else s
-            gated[64 + t * rows : 80 + t * rows] = (
-                g[0] * (y_rows[...] + skip[...] * prod)
-            ).astype(BF16)
-            if t < 3:
-                lag0, lag1 = [x * live for x in q], [x * live for x in lag0]
+            s = poles[...] * stay_state[r] + prod[r : r + 1]
+            y_rows[r : r + 1] = jnp.sum(residues[...] * s, axis=0, keepdims=True)
+            stay_state[r] = s * live[r : r + 1] if t < 3 else s
+        gated[64 + t * rows : 80 + t * rows] = (
+            g[0] * (y_rows[...] + skip[...] * prod)
+        ).astype(BF16)
+        if t < 3:
+            lag0, lag1 = [x * live for x in q], [x * live for x in lag0]
+    for block in range(blocks - 1):
+        store(block).wait()
 
 
 def band_kernel(
-    turns, got_hbm, taps, poles, residues, skip, far_weight, sent, gated, far, *scratch
+    turns, got_hbm, taps, poles, residues, skip, far_weight, ride, sent, gated, first, *scratch
 ):
     lags, inputs, live, heads, products, y_rows, got, sems = scratch
     groups, _, width = got.shape
@@ -171,7 +203,11 @@
         sent[end, 0 : 2 * MODES] = jnp.concatenate(final, axis=0).astype(BF16)
 
     gated[...] = y_rows[...].reshape(3 * rows, width).astype(BF16)
-    far[...] = dot(gated[...], far_weight[...]).astype(BF16)
+    half = 3 * rows // 2
+    for way in range(2):
+        load = dot(gated[way * half : (way + 1) * half], far_weight[...])
+        first[way, :half] = load.astype(BF16)
+        first[way, half:] = ride[way]
 
 
 def products_kernel(place, gated, weight, part):
@@ -246,33 +282,22 @@
     return lax.all_to_all(blocks, "dp", split_axis=0, concat_axis=0, tiled=True)
 
 
-def ring_sums(far, gated, weight, block=None):
+def pass_on(right, left):
     n = lax.axis_size("tensor")
-    half = far.shape[0] // 2
-
-    def pass_on(right, left):
-        right = lax.ppermute(right, "tensor", [(i, (i + 1) % n) for i in range(n)])
-        left = lax.ppermute(left, "tensor", [(i, (i - 1) % n) for i in range(n)])
-        return right, left
-
-    right, left = pass_on(far[:half], far[half:])
-    made = products(gated, weight, (3, -3, 2, -2))
-    for away in range(n // 2 - 1, 0, -1):
-        right, left, gated, block = lax.optimization_barrier((right, left, gated, block))
-        ahead, behind = made[away], made[-away]
-        if right.shape[0] == half:
-            ahead = ahead.at[:half].add(right.astype(F32))
-            behind = behind.at[half:].add(left.astype(F32))
-        else:
-            ahead, behind = ahead + right.astype(F32), behind + left.astype(F32)
-        right, left = pass_on(ahead.astype(BF16), behind.astype(BF16))
-        if away == 3:
-            swapped = None if block is None else swap(block)
-            block = None
-        if away == 2:
-            made |= products(gated, weight, (1, -1, 0))
-    total = made[0] + right.astype(F32) + left.astype(F32)
-    return lax.optimization_barrier((total, swapped))
+    right = lax.ppermute(right, "tensor", [(i, (i + 1) % n) for i in range(n)])
+    left = lax.ppermute(left, "tensor", [(i, (i - 1) % n) for i in range(n)])
+    return right, left
+
+
+def joined(made, away, right, left):
+    ahead, behind = made[away], made[-away]
+    half = right.shape[0]
+    if half < ahead.shape[0]:
+        ahead = ahead.at[:half].add(right.astype(F32))
+        behind = behind.at[half:].add(left.astype(F32))
+    else:
+        ahead, behind = ahead + right.astype(F32), behind + left.astype(F32)
+    return ahead.astype(BF16), behind.astype(BF16)
 
 
 def row_scales(own):
@@ -305,52 +330,56 @@
 
     packed, gated_home, stay_state = pl.pallas_call(
         home_kernel,
-        grid=(slots // 16,),
-        in_specs=[
-            pl.BlockSpec((4, 3, 16, width), lambda i: (0, 0, i, 0)),
-            pl.BlockSpec((16, 3, 2, width), lambda i: (i, 0, 0, 0)),
-            whole((3, 3, width)),
-            pl.BlockSpec((16, MODES, width), lambda i: (i, 0, 0)),
-            whole((MODES, width)),
-            whole((MODES, width)),
-            whole((1, width)),
-            whole((3, slots)),
-        ],
-        out_specs=[
-            pl.BlockSpec((8, 2 * MODES + 2 * KINDS, width), lambda i: (jnp.minimum(i, 3), 0, 0)),
-            whole((slots + 48, width)),
-            whole((16, MODES, width)),
-        ],
+        in_specs=[pl.BlockSpec(memory_space=pl.ANY)] * 3
+        + [pl.BlockSpec(memory_space=pltpu.VMEM)] * 5,
+        out_specs=[pl.BlockSpec(memory_space=pl.ANY)]
+        + [pl.BlockSpec(memory_space=pltpu.VMEM)] * 2,
         out_shape=[
             jax.ShapeDtypeStruct((groups, 2 * MODES + 2 * KINDS, width), BF16),
             jax.ShapeDtypeStruct((slots + 48, width), BF16),
             jax.ShapeDtypeStruct((16, MODES, width), F32),
         ],
-        scratch_shapes=[pltpu.VMEM((16, width), F32)],
+        scratch_shapes=[
+            pltpu.VMEM(qkv_kinds.shape, BF16),
+            pltpu.VMEM(fir_buffer.shape, BF16),
+            pltpu.VMEM(modal_state.shape, F32),
+            pltpu.VMEM((groups, 2 * MODES + 2 * KINDS, width), BF16),
+            pltpu.VMEM((16, width), F32),
+            pltpu.SemaphoreType.DMA((4, slots // 16)),
+        ],
         compiler_params=pltpu.CompilerParams(vmem_limit_bytes=56 * 1024 * 1024),
         name="home_rows",
-    )(qkv_kinds, fir_buffer, fir_taps, modal_state, poles, residues, skip_row, finished)
+    )(qkv_kinds, fir_buffer, modal_state, fir_taps, poles, residues, skip_row, finished)
 
     n, own_cols = lax.axis_size("tensor"), norm_gain.shape[0]
     gated_home, later_weight = lax.optimization_barrier((gated_home, out_weight))
     far_place = (lax.axis_index("tensor") + n // 2) % n
     far_weight = lax.dynamic_slice_in_dim(later_weight, far_place * own_cols, own_cols, 1)
     got = swap(packed)
-    own_home, _ = ring_sums(dot(gated_home, far_weight).astype(BF16), gated_home, out_weight)
-    got, own_home = lax.optimization_barrier((got, own_home))
-
-    sent, gated_band, far = pl.pallas_call(
+    far = dot(gated_home, far_weight).astype(BF16)
+    half = far.shape[0] // 2
+    right, left = pass_on(far[:half], far[half:])
+    made = products(gated_home, out_weight, (3, -3, 2, -2))
+    right, left = lax.optimization_barrier((right, left))
+    right, left, gated_home = lax.optimization_barrier((*pass_on(*joined(made, 3, right, left)), gated_home))
+    right, left = pass_on(*joined(made, 2, right, left))
+    made = products(gated_home, out_weight, (1, -1, 0))
+    right, left = lax.optimization_barrier((right, left))
+    ride = jnp.stack(joined(made, 1, right, left))
+    got, ride, own_home = lax.optimization_barrier((got, ride, made[0]))
+
+    sent, gated_band, first = pl.pallas_call(
         band_kernel,
         in_specs=[
             pl.BlockSpec(memory_space=pltpu.SMEM),
             pl.BlockSpec(memory_space=pl.ANY),
         ]
-        + [pl.BlockSpec(memory_space=pltpu.VMEM)] * 5,
+        + [pl.BlockSpec(memory_space=pltpu.VMEM)] * 6,
         out_specs=[pl.BlockSpec(memory_space=pltpu.VMEM)] * 3,
         out_shape=[
             jax.ShapeDtypeStruct((groups, 2 * MODES + 16, width), BF16),
             jax.ShapeDtypeStruct((3 * moving, width), BF16),
-            jax.ShapeDtypeStruct((3 * moving, own_cols), BF16),
+            jax.ShapeDtypeStruct((2, 3 * moving // 2 + slots + 48, own_cols), BF16),
         ],
         scratch_shapes=[
             pltpu.VMEM((6, moving, width), F32),
@@ -364,9 +393,23 @@
         ],
         compiler_params=pltpu.CompilerParams(vmem_limit_bytes=40 * 1024 * 1024),
         name="band_rows",
-    )(turns, got, fir_taps, poles, residues, skip_row, far_weight)
-
-    own_band, back = ring_sums(far, gated_band, out_weight, sent)
+    )(turns, got, fir_taps, poles, residues, skip_row, far_weight, ride)
+
+    half = 3 * moving // 2
+    right, left = pass_on(first[0], first[1])
+    made = products(gated_band, out_weight, (3, -3, 2, -2))
+    right, left, gated_band, sent = lax.optimization_barrier((right, left, gated_band, sent))
+    own_home = own_home + right[half:].astype(F32) + left[half:].astype(F32)
+    right, left = pass_on(*joined(made, 3, right[:half], left[:half]))
+    back = swap(sent)
+    right, left, gated_band = lax.optimization_barrier((right, left, gated_band))
+    right, left = pass_on(*joined(made, 2, right, left))
+    made = products(gated_band, out_weight, (1, -1, 0))
+    right, left = lax.optimization_barrier((right, left))
+    right, left = pass_on(*joined(made, 1, right, left))
+    right, left = lax.optimization_barrier((right, left))
+    own_band = made[0] + right.astype(F32) + left.astype(F32)
+    own_band, back = lax.optimization_barrier((own_band, back))
     scales = row_scales([own_band, own_home])
     mixed_band = (own_band * scales[: 3 * moving] * norm_gain[None]).astype(BF16)
     mixed_band = jnp.transpose(mixed_band.reshape(3, groups, CAP, own_cols), (1, 0, 2, 3))

time: 143 us -> 133 us (0.930)
  starting transfers between devices: 55.5 us -> 46.8 us
    ppermute x8 -> x7, starting transfers between devices: 22.6 us -> 15.9 us  [pass_on(): left = lax.ppermute(left, 'tensor', [(i, (i - 1) % n) for i in range(n)])]
    ppermute x8 -> x7, waiting for transfers between devices: 12 us -> 7.79 us  [pass_on(): right = lax.ppermute(right, 'tensor', [(i, (i + 1) % n) for i in range(n)])]
    ppermute x8 -> x7, waiting for transfers between devices: 1.44 us -> 5.38 us  [pass_on(): left = lax.ppermute(left, 'tensor', [(i, (i - 1) % n) for i in range(n)])]
    all_to_all x3, starting transfers between devices: 31.4 us -> 28.2 us  [swap(): return lax.all_to_all(blocks, 'dp', split_axis=0, concat_axis=0, tiled=True)]
    convert_element_type x4 -> x3, other arithmetic: 4.69 us -> 3.57 us  [joined(): return (ahead.astype(BF16), behind.astype(BF16))]
    another operation x2 -> x3, local copies, waits for them, and re-layouts: 2.22 us -> 3.23 us  [products(): return dict(zip(aways, part))]
  transfers between devices with their start and end apart: 19 -> 17, of which waited for: 7 -> 7; matrix products, arithmetic and copies ran while one was open for 9% -> 10% of each run, Pallas kernels for 17% -> 18%
where the time goes in v6:
time: 133 us; the launch traced here: 132 us
  starting transfers between devices  46.8 us (35%)
  Pallas kernels  35.6 us (27%)
  waiting for transfers between devices  17.9 us (13%)
  blocking collectives  13.6 us (10%)
  other arithmetic  10.4 us (8%)
  local copies, waits for them, and re-layouts  6.23 us (5%)
    all_to_all x3, starting transfers between devices, swap(): return lax.all_to_all(blocks, 'dp', split_axis=0, concat_axis=0, tiled=True)  28.2 us
    pallas_call x4, Pallas kernels, products(): pl.pallas_call(products_kernel, grid_spec=pltpu.PrefetchScalarGridSpec(nu...  18.1 us
    ppermute x7, starting transfers between devices, pass_on(): left = lax.ppermute(left, 'tensor', [(i, (i - 1) % n) for i in range(n)])  15.9 us
    psum x1, blocking collectives, row_scales(): lax.psum(jnp.concatenate([jnp.sum(x * x, axis=1) for x in own]), 'tensor')  13.6 us
    ppermute x7, waiting for transfers between devices, pass_on(): right = lax.ppermute(right, 'tensor', [(i, (i + 1) % n) for i in range(n)])  7.79 us
    pallas_call x1, Pallas kernels, per_device(): pl.pallas_call(band_kernel, in_specs=[pl.BlockSpec(memory_space=pltpu.SME...  6.4 us
    pallas_call x1, Pallas kernels, per_device(): pl.pallas_call(home_kernel, in_specs=[pl.BlockSpec(memory_space=pl.ANY)]...  5.8 us
    ppermute x7, waiting for transfers between devices, pass_on(): left = lax.ppermute(left, 'tensor', [(i, (i - 1) % n) for i in range(n)])  5.38 us
  transfers between devices with their start and end apart: 17, of which 7 were waited for; matrix products, arithmetic and copies ran while one was open for 10% of the time, Pallas kernels for 18%

profile of v6, /device:TPU:1, one launch (start us, length us, event | category | flops | bytes accessed | tf_op | source)
XLA Modules:
  0.0 131.8 jit_solution(10590843868408985900)
XLA Ops:
  0.6 5.8 %home_rows.1 = (bf16[32,64,512]{2,1,0:T(8,128)(2,1)}, bf16[128,512]{1,0:T(8,128)(2,1)}, f32[16,16,512]{2,1,0:T(8,128)}) custom-call(bf16[4,3,80,512]{3,2,1,0:T(8,128)(2,1)} %bitcast.113, bf16[80,3,2,512]{3,2,1,0:T(2,128)(2,1)} %fir_hbm.1, f32[80,16,512]{2,1,0:T(8,128)} %state_hbm.1, f32[3,3,512]{2,1,0:T(4,128)} %taps.3, f32[16,512]{1,0:T(8,128)} %poles.3, ...), custom_call_target="tpu_custom_call" | custom-call | tf_op jit(solution)/shard_map/home_rows/pallas_call | solution.py:331
  6.4 8.7 %all-to-all-start = ((bf16[32,64,512]{2,1,0:T(8,128)(2,1)}), bf16[32,64,512]{2,1,0:T(8,128)(2,1)S(1)}, u32[]{:S(2)}, u32[]{:S(2)}) async-start(bf16[32,64,512]{2,1,0:T(8,128)(2,1)} %get-tuple-element.86), calls=%async_computation | async-start | bytes 4194304 | tf_op jit(solution)/shard_map/all_to_all | solution.py:282
  15.2 1.1 constant_dynamic-slice_fusion.far_weight
  16.3 0.2 convolution_convert_fusion
  16.6 5.7 %collective-permute-start.1 = (bf16[64,512]{1,0:T(8,128)(2,1)S(1)}, bf16[64,512]{1,0:T(8,128)(2,1)S(1)}, u32[]{:S(2)}, u32[]{:S(2)}) collective-permute-start(bf16[64,512]{1,0:T(8,128)(2,1)S(1)} %get-tuple-element.139), channel_id=1, source_target_pairs={{0,7},{1,0},{2,1},{3,2},{4,3},{5,4},{6,5},{7,6},{8,15},{9,8},{10,9... | collective-permute-start | bytes 196616 | tf_op jit(solution)/shard_map/ppermute | solution.py:288
  22.2 0.5 and_select_fusion.1.place
  22.8 4.8 %ring_products.4 = f32[4,128,512]{2,1,0:T(8,128)} custom-call(s32[4]{0:T(128)} %and_select_fusion.1.place, bf16[128,512]{1,0:T(8,128)(2,1)} %get-tuple-element.92.gated, bf16[512,4096]{1,0:T(8,128)(2,1)} %weight.7), custom_call_target="tpu_custom_call" | custom-call | flops 4294967296 | bytes 4194304 | tf_op jit(solution)/shard_map/ring_products/pallas_call | solution.py:222
  27.6 1.1 slice_bitcast_fusion.12
  28.7 0.5 and_select_fusion.2.place
  29.3 0.1 reduce.8
  29.4 1.0 fusion.25
  30.4 2.7 %collective-permute-start.3 = (bf16[128,512]{1,0:T(8,128)(2,1)S(1)}, bf16[128,512]{1,0:T(8,128)(2,1)S(1)}, u32[]{:S(2)}, u32[]{:S(2)}) collective-permute-start(bf16[128,512]{1,0:T(8,128)(2,1)S(1)} %get-tuple-element.131), channel_id=1, source_target_pairs={{0,7},{1,0},{2,1},{3,2},{4,3},{5,4},{6,5},{7,6},{8,15},{9,8},{10,9... | collective-permute-start | bytes 393224 | tf_op jit(solution)/shard_map/ppermute | solution.py:288
  33.2 1.9 %collective-permute-done.3 = bf16[128,512]{1,0:T(8,128)(2,1)S(1)} collective-permute-done((bf16[128,512]{1,0:T(8,128)(2,1)S(1)}, bf16[128,512]{1,0:T(8,128)(2,1)S(1)}, u32[]{:S(2)}, u32[]{:S(2)}) %collective-permute-start.3) | collective-permute-done | bytes 131104 | tf_op jit(solution)/shard_map/ppermute | solution.py:288
  35.1 3.4 %collective-permute-done.2 = bf16[128,512]{1,0:T(8,128)(2,1)S(1)} collective-permute-done((bf16[128,512]{1,0:T(8,128)(2,1)S(1)}, bf16[128,512]{1,0:T(8,128)(2,1)S(1)}, u32[]{:S(2)}, u32[]{:S(2)}) %collective-permute-start.2) | collective-permute-done | bytes 131104 | tf_op jit(solution)/shard_map/ppermute | solution.py:287
  38.5 1.1 fusion.13
  39.6 0.2 collective-permute-start.5
  39.8 1.4 %collective-permute-start.4 = (bf16[128,512]{1,0:T(8,128)(2,1)S(1)}, bf16[128,512]{1,0:T(8,128)(2,1)S(1)}, u32[]{:S(2)}, u32[]{:S(2)}) collective-permute-start(bf16[128,512]{1,0:T(8,128)(2,1)S(1)} %get-tuple-element.130), channel_id=1, source_target_pairs={{0,1},{1,2},{2,3},{3,4},{4,5},{5,6},{6,7},{7,0},{8,9},{9,10},{10,1... | collective-permute-start | bytes 393224 | tf_op jit(solution)/shard_map/ppermute | solution.py:287
  41.2 4.1 %ring_products.5 = f32[3,128,512]{2,1,0:T(8,128)} custom-call(s32[3]{0:T(128)} %and_select_fusion.2.place, bf16[128,512]{1,0:T(8,128)(2,1)} %get-tuple-element.92.gated, bf16[512,4096]{1,0:T(8,128)(2,1)} %weight.7), custom_call_target="tpu_custom_call" | custom-call | flops 4294967296 | bytes 4194304 | tf_op jit(solution)/shard_map/ring_products/pallas_call | solution.py:222
  45.3 1.0 slice_bitcast_fusion.7
  46.3 1.1 fusion.22
  47.5 6.4 %band_rows.1 = (bf16[32,48,512]{2,1,0:T(8,128)(2,1)}, bf16[192,512]{1,0:T(8,128)(2,1)S(1)}, bf16[2,224,512]{2,1,0:T(8,128)(2,1)S(1)}) custom-call(s32[3]{0:T(128)S(1)} %and_select_fusion.turns, bf16[32,64,512]{2,1,0:T(8,128)(2,1)S(1)} %all-to-all-done.got_hbm, f32[3,3,512]{2,1,0:T(4,128)S(1)} %copy-done.2, f32[16,512]{1,0:T(8,128)S(1)} %copy-done, ...), custom_call_target="tpu_custom_call" | custom-call | tf_op jit(solution)/shard_map/band_rows/pallas_call | solution.py:371
  53.9 0.6 copy-done.4
  54.6 1.3 %collective-permute-start.7 = (bf16[224,512]{1,0:T(8,128)(2,1)S(1)}, bf16[224,512]{1,0:T(8,128)(2,1)S(1)}, u32[]{:S(2)}, u32[]{:S(2)}) collective-permute-start(bf16[224,512]{1,0:T(8,128)(2,1)S(1)} %get-tuple-element.137), channel_id=1, source_target_pairs={{0,7},{1,0},{2,1},{3,2},{4,3},{5,4},{6,5},{7,6},{8,15},{9,8},{10,9... | collective-permute-start | bytes 688136 | tf_op jit(solution)/shard_map/ppermute | solution.py:288
  55.9 0.1 collective-permute-start.6
  56.0 4.9 %ring_products.6 = f32[4,192,512]{2,1,0:T(8,128)} custom-call(s32[4]{0:T(128)} %and_select_fusion.1.place, bf16[192,512]{1,0:T(8,128)(2,1)} %copy-done.4, bf16[512,4096]{1,0:T(8,128)(2,1)} %weight.7), custom_call_target="tpu_custom_call" | custom-call | flops 6442450944 | bytes 4194304 | tf_op jit(solution)/shard_map/ring_products/pallas_call | solution.py:222
  60.9 1.2 slice_bitcast_fusion.5
  62.1 1.1 fusion.19
  63.2 2.6 %collective-permute-start.9 = (bf16[192,512]{1,0:T(8,128)(2,1)S(1)}, bf16[192,512]{1,0:T(8,128)(2,1)S(1)}, u32[]{:S(2)}, u32[]{:S(2)}) collective-permute-start(bf16[192,512]{1,0:T(8,128)(2,1)S(1)} %get-tuple-element.123), channel_id=1, source_target_pairs={{0,7},{1,0},{2,1},{3,2},{4,3},{5,4},{6,5},{7,6},{8,15},{9,8},{10,9... | collective-permute-start | bytes 589832 | tf_op jit(solution)/shard_map/ppermute | solution.py:288
  65.8 10.2 %all-to-all-start.1 = ((bf16[32,48,512]{2,1,0:T(8,128)(2,1)}), bf16[32,48,512]{2,1,0:T(8,128)(2,1)S(1)}, u32[]{:S(2)}, u32[]{:S(2)}) async-start(bf16[32,48,512]{2,1,0:T(8,128)(2,1)} %get-tuple-element.113), calls=%async_computation.1 | async-start | bytes 3145728 | tf_op jit(solution)/shard_map/all_to_all | solution.py:282
  76.0 1.2 fusion.3
  77.2 3.0 %collective-permute-start.11 = (bf16[192,512]{1,0:T(8,128)(2,1)S(1)}, bf16[192,512]{1,0:T(8,128)(2,1)S(1)}, u32[]{:S(2)}, u32[]{:S(2)}) collective-permute-start(bf16[192,512]{1,0:T(8,128)(2,1)S(1)} %get-tuple-element.121), channel_id=1, source_target_pairs={{0,7},{1,0},{2,1},{3,2},{4,3},{5,4},{6,5},{7,6},{8,15},{9,8},{10,9... | collective-permute-start | bytes 589832 | tf_op jit(solution)/shard_map/ppermute | solution.py:288
  80.3 4.3 %ring_products.7 = f32[3,192,512]{2,1,0:T(8,128)} custom-call(s32[3]{0:T(128)} %and_select_fusion.2.place, bf16[192,512]{1,0:T(8,128)(2,1)} %copy-done.4, bf16[512,4096]{1,0:T(8,128)(2,1)} %weight.7), custom_call_target="tpu_custom_call" | custom-call | flops 6442450944 | bytes 4194304 | tf_op jit(solution)/shard_map/ring_products/pallas_call | solution.py:222
  84.6 2.8 %collective-permute-done.10 = bf16[192,512]{1,0:T(8,128)(2,1)S(1)} collective-permute-done((bf16[192,512]{1,0:T(8,128)(2,1)S(1)}, bf16[192,512]{1,0:T(8,128)(2,1)S(1)}, u32[]{:S(2)}, u32[]{:S(2)}) %collective-permute-start.10) | collective-permute-done | bytes 196640 | tf_op jit(solution)/shard_map/ppermute | solution.py:287
  87.4 1.2 fusion.1
  88.7 0.4 collective-permute-start.13
  89.1 1.1 collective-permute-start.12
  90.2 0.1 multiply_reduce_fusion.1
  90.3 3.4 %collective-permute-done.13 = bf16[192,512]{1,0:T(8,128)(2,1)S(1)} collective-permute-done((bf16[192,512]{1,0:T(8,128)(2,1)S(1)}, bf16[192,512]{1,0:T(8,128)(2,1)S(1)}, u32[]{:S(2)}, u32[]{:S(2)}) %collective-permute-start.13) | collective-permute-done | bytes 196640 | tf_op jit(solution)/shard_map/ppermute | solution.py:288
  93.8 1.6 %collective-permute-done.12 = bf16[192,512]{1,0:T(8,128)(2,1)S(1)} collective-permute-done((bf16[192,512]{1,0:T(8,128)(2,1)S(1)}, bf16[192,512]{1,0:T(8,128)(2,1)S(1)}, u32[]{:S(2)}, u32[]{:S(2)}) %collective-permute-start.12) | collective-permute-done | bytes 196640 | tf_op jit(solution)/shard_map/ppermute | solution.py:287
  95.3 1.1 fusion.9
  96.4 1.8 %all-to-all-done.1.back = bf16[32,48,512]{2,1,0:T(8,128)(2,1)S(1)} async-done(((bf16[32,48,512]{2,1,0:T(8,128)(2,1)}), bf16[32,48,512]{2,1,0:T(8,128)(2,1)S(1)}, u32[]{:S(2)}, u32[]{:S(2)}) %all-to-all-start.1) | async-done | bytes 1572896 | tf_op jit(solution)/shard_map/all_to_all | solution.py:282
  98.4 13.6 %psum.7 = f32[320]{0:T(512)S(1)} all-reduce(f32[320]{0:T(512)S(1)} %pad_maximum_fusion.1), channel_id=1, replica_groups=mesh['dp'=32,'tensor'=8] {'tensor'}, use_global_device_ids=true, to_apply=%region_3.4 | all-reduce | flops 320 | bytes 2560 | tf_op jit(solution)/shard_map/psum | solution.py:305
  112.3 0.8 copy.22
  113.2 9.3 %all-to-all-start.2 = ((bf16[32,3,2,512]{3,2,1,0:T(2,128)(2,1)}), bf16[32,3,2,512]{3,2,1,0:T(2,128)(2,1)S(1)}, u32[]{:S(2)}, u32[]{:S(2)}) async-start(bf16[32,3,2,512]{3,2,1,0:T(2,128)(2,1)} %bitcast.110), calls=%async_computation.2 | async-start | bytes 393216 | tf_op jit(solution)/shard_map/all_to_all | solution.py:282
  122.4 5.3 %last_rows.1 = (f32[80,16,512]{2,1,0:T(8,128)}, bf16[80,3,2,512]{3,2,1,0:T(2,128)(2,1)}) custom-call(bf16[32,48,512]{2,1,0:T(8,128)(2,1)} %copy-done.5, bf16[4,3,80,512]{3,2,1,0:T(8,128)(2,1)} %bitcast.114, f32[16,16,512]{2,1,0:T(8,128)} %get-tuple-element.118.stay_state, s32[3,80]{1,0:T(4,128)} %finished.3), custom_call_target="tpu_custom_call" | custom-call | tf_op jit(solution)/shard_map/last_rows/pallas_call | solution.py:418
  127.8 3.0 %all-to-all-done.2 = bf16[32,3,2,512]{3,2,1,0:T(2,128)(2,1)S(1)} async-done(((bf16[32,3,2,512]{3,2,1,0:T(2,128)(2,1)}), bf16[32,3,2,512]{3,2,1,0:T(2,128)(2,1)S(1)}, u32[]{:S(2)}, u32[]{:S(2)}) %all-to-all-start.2) | async-done | bytes 196640 | tf_op jit(solution)/shard_map/all_to_all | solution.py:282
  130.8 0.1 copy.20
  131.0 0.8 maximum_maximum_fusion
  (52 shorter events, 0.9 us)
Async XLA Ops:
  6.4 9.9 %copy-start.6 = (bf16[128,512]{1,0:T(8,128)(2,1)S(1)}, bf16[128,512]{1,0:T(8,128)(2,1)}, u32[]{:S(2)}) copy-start(bf16[128,512]{1,0:T(8,128)(2,1)} %get-tuple-element.92.gated) | copy-start | bytes 393220
  6.4 41.0 %all-to-all-start = ((bf16[32,64,512]{2,1,0:T(8,128)(2,1)}), bf16[32,64,512]{2,1,0:T(8,128)(2,1)S(1)}, u32[]{:S(2)}, u32[]{:S(2)}) async-start(bf16[32,64,512]{2,1,0:T(8,128)(2,1)} %get-tuple-element.86), calls=%async_computation | async-start | bytes 4194304 | tf_op jit(solution)/shard_map/all_to_all | solution.py:282
  15.2 7.0 %copy-start.10 = (s32[4]{0:T(128)S(1)}, s32[4]{0:T(128)}, u32[]{:S(2)}) copy-start(s32[4]{0:T(128)} %constant.195.clone) | copy-start | bytes 52
  16.6 12.9 %collective-permute-start.1 = (bf16[64,512]{1,0:T(8,128)(2,1)S(1)}, bf16[64,512]{1,0:T(8,128)(2,1)S(1)}, u32[]{:S(2)}, u32[]{:S(2)}) collective-permute-start(bf16[64,512]{1,0:T(8,128)(2,1)S(1)} %get-tuple-element.139), channel_id=1, source_target_pairs={{0,7},{1,0},{2,1},{3,2},{4,3},{5,4},{6,5},{7,6},{8,15},{9,8},{10,9... | collective-permute-start | bytes 196616 | tf_op jit(solution)/shard_map/ppermute | solution.py:288
  22.2 7.2 %collective-permute-start = (bf16[64,512]{1,0:T(8,128)(2,1)S(1)}, bf16[64,512]{1,0:T(8,128)(2,1)S(1)}, u32[]{:S(2)}, u32[]{:S(2)}) collective-permute-start(bf16[64,512]{1,0:T(8,128)(2,1)S(1)} %get-tuple-element.140), channel_id=1, source_target_pairs={{0,1},{1,2},{2,3},{3,4},{4,5},{5,6},{6,7},{7,0},{8,9},{9,10},{10,1... | collective-permute-start | bytes 196616 | tf_op jit(solution)/shard_map/ppermute | solution.py:287
  22.7 5.9 %copy-start.9 = (s32[3]{0:T(128)S(1)}, s32[3]{0:T(128)}, u32[]{:S(2)}) copy-start(s32[3]{0:T(128)} %constant.196.clone) | copy-start | bytes 40
  22.7 6.4 %copy-start.8 = (s32[3,80]{1,0:T(4,128)S(1)}, s32[3,80]{1,0:T(4,128)}, u32[]{:S(2)}) copy-start(s32[3,80]{1,0:T(4,128)} %param.33) | copy-start | bytes 2884
  30.4 4.7 %collective-permute-start.3 = (bf16[128,512]{1,0:T(8,128)(2,1)S(1)}, bf16[128,512]{1,0:T(8,128)(2,1)S(1)}, u32[]{:S(2)}, u32[]{:S(2)}) collective-permute-start(bf16[128,512]{1,0:T(8,128)(2,1)S(1)} %get-tuple-element.131), channel_id=1, source_target_pairs={{0,7},{1,0},{2,1},{3,2},{4,3},{5,4},{6,5},{7,6},{8,15},{9,8},{10,9... | collective-permute-start | bytes 393224 | tf_op jit(solution)/shard_map/ppermute | solution.py:288
  33.2 5.3 %collective-permute-start.2 = (bf16[128,512]{1,0:T(8,128)(2,1)S(1)}, bf16[128,512]{1,0:T(8,128)(2,1)S(1)}, u32[]{:S(2)}, u32[]{:S(2)}) collective-permute-start(bf16[128,512]{1,0:T(8,128)(2,1)S(1)} %get-tuple-element.132), channel_id=1, source_target_pairs={{0,1},{1,2},{2,3},{3,4},{4,5},{5,6},{6,7},{7,0},{8,9},{9,10},{10,1... | collective-permute-start | bytes 393224 | tf_op jit(solution)/shard_map/ppermute | solution.py:287
  39.6 6.7 %collective-permute-start.5 = (bf16[128,512]{1,0:T(8,128)(2,1)S(1)}, bf16[128,512]{1,0:T(8,128)(2,1)S(1)}, u32[]{:S(2)}, u32[]{:S(2)}) collective-permute-start(bf16[128,512]{1,0:T(8,128)(2,1)S(1)} %get-tuple-element.129), channel_id=1, source_target_pairs={{0,7},{1,0},{2,1},{3,2},{4,3},{5,4},{6,5},{7,6},{8,15},{9,8},{10,9... | collective-permute-start | bytes 393224 | tf_op jit(solution)/shard_map/ppermute | solution.py:288
  39.8 6.5 %collective-permute-start.4 = (bf16[128,512]{1,0:T(8,128)(2,1)S(1)}, bf16[128,512]{1,0:T(8,128)(2,1)S(1)}, u32[]{:S(2)}, u32[]{:S(2)}) collective-permute-start(bf16[128,512]{1,0:T(8,128)(2,1)S(1)} %get-tuple-element.130), channel_id=1, source_target_pairs={{0,1},{1,2},{2,3},{3,4},{4,5},{5,6},{6,7},{7,0},{8,9},{9,10},{10,1... | collective-permute-start | bytes 393224 | tf_op jit(solution)/shard_map/ppermute | solution.py:287
  45.2 2.2 %copy-start = (f32[16,512]{1,0:T(8,128)S(1)}, f32[16,512]{1,0:T(8,128)}, u32[]{:S(2)}) copy-start(f32[16,512]{1,0:T(8,128)} %poles.3) | copy-start | bytes 98308
  45.2 2.2 %copy-start.1 = (f32[16,512]{1,0:T(8,128)S(1)}, f32[16,512]{1,0:T(8,128)}, u32[]{:S(2)}) copy-start(f32[16,512]{1,0:T(8,128)} %residues.3) | copy-start | bytes 98308
  45.2 2.2 %copy-start.2 = (f32[3,3,512]{2,1,0:T(4,128)S(1)}, f32[3,3,512]{2,1,0:T(4,128)}, u32[]{:S(2)}) copy-start(f32[3,3,512]{2,1,0:T(4,128)} %taps.3) | copy-start | bytes 55300
  45.2 2.2 %copy-start.3 = (f32[512]{0:T(512)S(1)}, f32[512]{0:T(512)}, u32[]{:S(2)}) copy-start(f32[512]{0:T(512)} %param.29) | copy-start | bytes 6148
  53.9 0.7 copy-start.4
  54.6 7.5 %collective-permute-start.7 = (bf16[224,512]{1,0:T(8,128)(2,1)S(1)}, bf16[224,512]{1,0:T(8,128)(2,1)S(1)}, u32[]{:S(2)}, u32[]{:S(2)}) collective-permute-start(bf16[224,512]{1,0:T(8,128)(2,1)S(1)} %get-tuple-element.137), channel_id=1, source_target_pairs={{0,7},{1,0},{2,1},{3,2},{4,3},{5,4},{6,5},{7,6},{8,15},{9,8},{10,9... | collective-permute-start | bytes 688136 | tf_op jit(solution)/shard_map/ppermute | solution.py:288
  55.9 6.2 %collective-permute-start.6 = (bf16[224,512]{1,0:T(8,128)(2,1)S(1)}, bf16[224,512]{1,0:T(8,128)(2,1)S(1)}, u32[]{:S(2)}, u32[]{:S(2)}) collective-permute-start(bf16[224,512]{1,0:T(8,128)(2,1)S(1)} %get-tuple-element.138), channel_id=1, source_target_pairs={{0,1},{1,2},{2,3},{3,4},{4,5},{5,6},{6,7},{7,0},{8,9},{9,10},{10,1... | collective-permute-start | bytes 688136 | tf_op jit(solution)/shard_map/ppermute | solution.py:287
  63.2 12.8 %collective-permute-start.9 = (bf16[192,512]{1,0:T(8,128)(2,1)S(1)}, bf16[192,512]{1,0:T(8,128)(2,1)S(1)}, u32[]{:S(2)}, u32[]{:S(2)}) collective-permute-start(bf16[192,512]{1,0:T(8,128)(2,1)S(1)} %get-tuple-element.123), channel_id=1, source_target_pairs={{0,7},{1,0},{2,1},{3,2},{4,3},{5,4},{6,5},{7,6},{8,15},{9,8},{10,9... | collective-permute-start | bytes 589832 | tf_op jit(solution)/shard_map/ppermute | solution.py:288
  65.8 10.2 %collective-permute-start.8 = (bf16[192,512]{1,0:T(8,128)(2,1)S(1)}, bf16[192,512]{1,0:T(8,128)(2,1)S(1)}, u32[]{:S(2)}, u32[]{:S(2)}) collective-permute-start(bf16[192,512]{1,0:T(8,128)(2,1)S(1)} %get-tuple-element.124), channel_id=1, source_target_pairs={{0,1},{1,2},{2,3},{3,4},{4,5},{5,6},{6,7},{7,0},{8,9},{9,10},{10,1... | collective-permute-start | bytes 589832 | tf_op jit(solution)/shard_map/ppermute | solution.py:287
  65.8 32.4 %all-to-all-start.1 = ((bf16[32,48,512]{2,1,0:T(8,128)(2,1)}), bf16[32,48,512]{2,1,0:T(8,128)(2,1)S(1)}, u32[]{:S(2)}, u32[]{:S(2)}) async-start(bf16[32,48,512]{2,1,0:T(8,128)(2,1)} %get-tuple-element.113), calls=%async_computation.1 | async-start | bytes 3145728 | tf_op jit(solution)/shard_map/all_to_all | solution.py:282
  77.2 7.4 %collective-permute-start.11 = (bf16[192,512]{1,0:T(8,128)(2,1)S(1)}, bf16[192,512]{1,0:T(8,128)(2,1)S(1)}, u32[]{:S(2)}, u32[]{:S(2)}) collective-permute-start(bf16[192,512]{1,0:T(8,128)(2,1)S(1)} %get-tuple-element.121), channel_id=1, source_target_pairs={{0,7},{1,0},{2,1},{3,2},{4,3},{5,4},{6,5},{7,6},{8,15},{9,8},{10,9... | collective-permute-start | bytes 589832 | tf_op jit(solution)/shard_map/ppermute | solution.py:288
  80.3 7.2 %collective-permute-start.10 = (bf16[192,512]{1,0:T(8,128)(2,1)S(1)}, bf16[192,512]{1,0:T(8,128)(2,1)S(1)}, u32[]{:S(2)}, u32[]{:S(2)}) collective-permute-start(bf16[192,512]{1,0:T(8,128)(2,1)S(1)} %get-tuple-element.122), channel_id=1, source_target_pairs={{0,1},{1,2},{2,3},{3,4},{4,5},{5,6},{6,7},{7,0},{8,9},{9,10},{10,1... | collective-permute-start | bytes 589832 | tf_op jit(solution)/shard_map/ppermute | solution.py:287
  84.6 27.5 %copy-start.7 = (f32[512]{0:T(512)S(1)}, f32[512]{0:T(512)}, u32[]{:S(2)}) copy-start(f32[512]{0:T(512)} %param.31) | copy-start | bytes 6148
  88.7 5.1 %collective-permute-start.13 = (bf16[192,512]{1,0:T(8,128)(2,1)S(1)}, bf16[192,512]{1,0:T(8,128)(2,1)S(1)}, u32[]{:S(2)}, u32[]{:S(2)}) collective-permute-start(bf16[192,512]{1,0:T(8,128)(2,1)S(1)} %get-tuple-element.127), channel_id=1, source_target_pairs={{0,7},{1,0},{2,1},{3,2},{4,3},{5,4},{6,5},{7,6},{8,15},{9,8},{10,9... | collective-permute-start | bytes 589832 | tf_op jit(solution)/shard_map/ppermute | solution.py:288
  89.1 6.3 %collective-permute-start.12 = (bf16[192,512]{1,0:T(8,128)(2,1)S(1)}, bf16[192,512]{1,0:T(8,128)(2,1)S(1)}, u32[]{:S(2)}, u32[]{:S(2)}) collective-permute-start(bf16[192,512]{1,0:T(8,128)(2,1)S(1)} %get-tuple-element.128), channel_id=1, source_target_pairs={{0,1},{1,2},{2,3},{3,4},{4,5},{5,6},{6,7},{7,0},{8,9},{9,10},{10,1... | collective-permute-start | bytes 589832 | tf_op jit(solution)/shard_map/ppermute | solution.py:287
  98.2 24.3 %copy-start.5 = (bf16[32,48,512]{2,1,0:T(8,128)(2,1)}, bf16[32,48,512]{2,1,0:T(8,128)(2,1)S(1)}, u32[]{:S(2)}) copy-start(bf16[32,48,512]{2,1,0:T(8,128)(2,1)S(1)} %all-to-all-done.1.back) | copy-start | bytes 4718596
  113.2 17.6 %all-to-all-start.2 = ((bf16[32,3,2,512]{3,2,1,0:T(2,128)(2,1)}), bf16[32,3,2,512]{3,2,1,0:T(2,128)(2,1)S(1)}, u32[]{:S(2)}, u32[]{:S(2)}) async-start(bf16[32,3,2,512]{3,2,1,0:T(2,128)(2,1)} %bitcast.110), calls=%async_computation.2 | async-start | bytes 393216 | tf_op jit(solution)/shard_map/all_to_all | solution.py:282

commit v7 on v6

--- a/solution.py
+++ b/solution.py
@@ -122,7 +122,7 @@
 
 
 def band_kernel(
-    turns, got_hbm, taps, poles, residues, skip, far_weight, ride, sent, gated, first, *scratch
+    turns, got_hbm, taps, poles, residues, skip, far_weight, ride, sent, gated, first_right, first_left, *scratch
 ):
     lags, inputs, live, heads, products, y_rows, got, sems = scratch
     groups, _, width = got.shape
@@ -204,21 +204,25 @@
 
     gated[...] = y_rows[...].reshape(3 * rows, width).astype(BF16)
     half = 3 * rows // 2
-    for way in range(2):
+    for way, first in enumerate((first_right, first_left)):
         load = dot(gated[way * half : (way + 1) * half], far_weight[...])
-        first[way, :half] = load.astype(BF16)
-        first[way, half:] = ride[way]
+        first[:half] = load.astype(BF16)
+        first[half:] = ride[way]
 
 
 def products_kernel(place, gated, weight, part):
     part[0] = dot(gated[...], weight[...])
 
 
-def products(gated, weight, aways):
+def products(place, gated, weight, aways):
     n = lax.axis_size("tensor")
     rows, width = gated.shape
     own_cols = weight.shape[1] // n
-    places = (lax.axis_index("tensor") + jnp.array(aways, jnp.int32)) % n
+    assert aways == tuple((aways[0] - i // 2) * (1 - 2 * (i % 2)) for i in range(len(aways)))
+
+    def column(i, place):
+        return 0, (place[0] + n + (aways[0] - i // 2) * (1 - 2 * (i % 2))) % n
+
     part = pl.pallas_call(
         products_kernel,
         grid_spec=pltpu.PrefetchScalarGridSpec(
@@ -226,9 +230,9 @@
             grid=(len(aways),),
             in_specs=[
                 whole((rows, width)),
-                pl.BlockSpec((width, own_cols), lambda i, places: (0, places[i])),
+                pl.BlockSpec((width, own_cols), column),
             ],
-            out_specs=pl.BlockSpec((1, rows, own_cols), lambda i, places: (i, 0, 0)),
+            out_specs=pl.BlockSpec((1, rows, own_cols), lambda i, place: (i, 0, 0)),
         ),
         out_shape=jax.ShapeDtypeStruct((len(aways), rows, own_cols), F32),
         cost_estimate=pl.CostEstimate(
@@ -236,7 +240,7 @@
         ),
         compiler_params=pltpu.CompilerParams(vmem_limit_bytes=56 * 1024 * 1024),
         name="ring_products",
-    )(places, gated, weight)
+    )(place, gated, weight)
     return dict(zip(aways, part))
 
 
@@ -302,7 +306,14 @@
 
 def row_scales(own):
     n = lax.axis_size("tensor")
-    squares = lax.psum(jnp.concatenate([jnp.sum(x * x, axis=1) for x in own]), "tensor")
+    squares = jnp.concatenate([jnp.sum(x * x, axis=1) for x in own])
+
+    def sent_on(x, away):
+        return lax.ppermute(x, "tensor", [(i, (i + away) % n) for i in range(n)])
+
+    near = [sent_on(squares, away) for away in (1, -1, 2)]
+    squares = squares + near[0] + near[1] + near[2]
+    squares = squares + sent_on(squares, 4)
     return lax.rsqrt(squares / (n * own[0].shape[1]) + 1e-05)[:, None]
 
 
@@ -353,33 +364,35 @@
 
     n, own_cols = lax.axis_size("tensor"), norm_gain.shape[0]
     gated_home, later_weight = lax.optimization_barrier((gated_home, out_weight))
-    far_place = (lax.axis_index("tensor") + n // 2) % n
+    place = lax.axis_index("tensor").astype(jnp.int32)[None]
+    far_place = (place[0] + n // 2) % n
     far_weight = lax.dynamic_slice_in_dim(later_weight, far_place * own_cols, own_cols, 1)
     got = swap(packed)
     far = dot(gated_home, far_weight).astype(BF16)
     half = far.shape[0] // 2
     right, left = pass_on(far[:half], far[half:])
-    made = products(gated_home, out_weight, (3, -3, 2, -2))
+    made = products(place, gated_home, out_weight, (3, -3, 2, -2))
     right, left = lax.optimization_barrier((right, left))
     right, left, gated_home = lax.optimization_barrier((*pass_on(*joined(made, 3, right, left)), gated_home))
     right, left = pass_on(*joined(made, 2, right, left))
-    made = products(gated_home, out_weight, (1, -1, 0))
+    made = products(place, gated_home, out_weight, (1, -1, 0))
     right, left = lax.optimization_barrier((right, left))
     ride = jnp.stack(joined(made, 1, right, left))
     got, ride, own_home = lax.optimization_barrier((got, ride, made[0]))
 
-    sent, gated_band, first = pl.pallas_call(
+    sent, gated_band, right, left = pl.pallas_call(
         band_kernel,
         in_specs=[
             pl.BlockSpec(memory_space=pltpu.SMEM),
             pl.BlockSpec(memory_space=pl.ANY),
         ]
         + [pl.BlockSpec(memory_space=pltpu.VMEM)] * 6,
-        out_specs=[pl.BlockSpec(memory_space=pltpu.VMEM)] * 3,
+        out_specs=[pl.BlockSpec(memory_space=pltpu.VMEM)] * 4,
         out_shape=[
             jax.ShapeDtypeStruct((groups, 2 * MODES + 16, width), BF16),
             jax.ShapeDtypeStruct((3 * moving, width), BF16),
-            jax.ShapeDtypeStruct((2, 3 * moving // 2 + slots + 48, own_cols), BF16),
+            jax.ShapeDtypeStruct((3 * moving // 2 + slots + 48, own_cols), BF16),
+            jax.ShapeDtypeStruct((3 * moving // 2 + slots + 48, own_cols), BF16),
         ],
         scratch_shapes=[
             pltpu.VMEM((6, moving, width), F32),
@@ -396,15 +409,15 @@
     )(turns, got, fir_taps, poles, residues, skip_row, far_weight, ride)
 
     half = 3 * moving // 2
-    right, left = pass_on(first[0], first[1])
-    made = products(gated_band, out_weight, (3, -3, 2, -2))
+    right, left = pass_on(right, left)
+    made = products(place, gated_band, out_weight, (3, -3, 2, -2))
     right, left, gated_band, sent = lax.optimization_barrier((right, left, gated_band, sent))
     own_home = own_home + right[half:].astype(F32) + left[half:].astype(F32)
     right, left = pass_on(*joined(made, 3, right[:half], left[:half]))
     back = swap(sent)
     right, left, gated_band = lax.optimization_barrier((right, left, gated_band))
     right, left = pass_on(*joined(made, 2, right, left))
-    made = products(gated_band, out_weight, (1, -1, 0))
+    made = products(place, gated_band, out_weight, (1, -1, 0))
     right, left = lax.optimization_barrier((right, left))
     right, left = pass_on(*joined(made, 1, right, left))
     right, left = lax.optimization_barrier((right, left))

time: 133 us -> 129 us (0.970)
  blocking collectives: 13.6 us -> 0 us
  waiting for transfers between devices: 17.9 us -> 27.4 us
  starting transfers between devices: 46.8 us -> 51.2 us
  Pallas kernels: 35.6 us -> 32.7 us
    psum x1 -> x0, blocking collectives: 13.6 us -> none  [row_scales(): lax.psum(jnp.concatenate([jnp.sum(x * x, axis=1) for x in own]), 'tensor')]
    ppermute x0 -> x4, waiting for transfers between devices: none -> 8.6 us  [sent_on(): return lax.ppermute(x, 'tensor', [(i, (i + away) % n) for i in range(n)])]
    ppermute x0 -> x4, starting transfers between devices: none -> 5.11 us  [sent_on(): return lax.ppermute(x, 'tensor', [(i, (i + away) % n) for i in range(n)])]
    pallas_call x4, Pallas kernels: 18.1 us -> 15.2 us  [products(): pl.pallas_call(products_kernel, grid_spec=pltpu.PrefetchScalarGridSpec(nu...]
    all_to_all x3, starting transfers between devices: 28.2 us -> 26.6 us  [swap(): return lax.all_to_all(blocks, 'dp', split_axis=0, concat_axis=0, tiled=True)]
  transfers between devices with their start and end apart: 17 -> 21, of which waited for: 7 -> 11; matrix products, arithmetic and copies ran while one was open for 10% -> 9% of each run, Pallas kernels for 18% -> 16%
where the time goes in v7:
time: 129 us; the launch traced here: 128 us
  starting transfers between devices  51.2 us (40%)
  Pallas kernels  32.7 us (25%)
  waiting for transfers between devices  27.4 us (21%)
  other arithmetic  9.43 us (7%)
  local copies, waits for them, and re-layouts  6.23 us (5%)
    all_to_all x3, starting transfers between devices, swap(): return lax.all_to_all(blocks, 'dp', split_axis=0, concat_axis=0, tiled=True)  26.6 us
    ppermute x7, starting transfers between devices, pass_on(): left = lax.ppermute(left, 'tensor', [(i, (i - 1) % n) for i in range(n)])  17 us
    pallas_call x4, Pallas kernels, products(): pl.pallas_call(products_kernel, grid_spec=pltpu.PrefetchScalarGridSpec(nu...  15.2 us
    ppermute x4, waiting for transfers between devices, sent_on(): return lax.ppermute(x, 'tensor', [(i, (i + away) % n) for i in range(n)])  8.6 us
    ppermute x7, waiting for transfers between devices, pass_on(): right = lax.ppermute(right, 'tensor', [(i, (i + 1) % n) for i in range(n)])  8.05 us
    pallas_call x1, Pallas kernels, per_device(): pl.pallas_call(band_kernel, in_specs=[pl.BlockSpec(memory_space=pltpu.SME...  6.39 us
    ppermute x7, waiting for transfers between devices, pass_on(): left = lax.ppermute(left, 'tensor', [(i, (i - 1) % n) for i in range(n)])  5.85 us
    pallas_call x1, Pallas kernels, per_device(): pl.pallas_call(home_kernel, in_specs=[pl.BlockSpec(memory_space=pl.ANY)]...  5.79 us
  transfers between devices with their start and end apart: 21, of which 11 were waited for; matrix products, arithmetic and copies ran while one was open for 9% of the time, Pallas kernels for 16%

profile of v7, /device:TPU:1, one launch (start us, length us, event | category | flops | bytes accessed | tf_op | source)
XLA Modules:
  0.0 128.3 jit_solution(535365496048804077)
XLA Ops:
  0.6 5.8 %home_rows.1 = (bf16[32,64,512]{2,1,0:T(8,128)(2,1)}, bf16[128,512]{1,0:T(8,128)(2,1)}, f32[16,16,512]{2,1,0:T(8,128)}) custom-call(bf16[4,3,80,512]{3,2,1,0:T(8,128)(2,1)} %bitcast.110, bf16[80,3,2,512]{3,2,1,0:T(2,128)(2,1)} %fir_hbm.1, f32[80,16,512]{2,1,0:T(8,128)} %state_hbm.1, f32[3,3,512]{2,1,0:T(4,128)} %taps.3, f32[16,512]{1,0:T(8,128)} %poles.3, ...), custom_call_target="tpu_custom_call" | custom-call | tf_op jit(solution)/shard_map/home_rows/pallas_call | solution.py:342
  6.4 8.7 %all-to-all-start = ((bf16[32,64,512]{2,1,0:T(8,128)(2,1)}), bf16[32,64,512]{2,1,0:T(8,128)(2,1)S(1)}, u32[]{:S(2)}, u32[]{:S(2)}) async-start(bf16[32,64,512]{2,1,0:T(8,128)(2,1)} %get-tuple-element.87), calls=%async_computation | async-start | bytes 4194304 | tf_op jit(solution)/shard_map/all_to_all | solution.py:286
  15.2 1.1 constant_dynamic-slice_fusion.far_weight
  16.3 0.2 convolution_convert_fusion
  16.5 5.7 %collective-permute-start.1 = (bf16[64,512]{1,0:T(8,128)(2,1)S(1)}, bf16[64,512]{1,0:T(8,128)(2,1)S(1)}, u32[]{:S(2)}, u32[]{:S(2)}) collective-permute-start(bf16[64,512]{1,0:T(8,128)(2,1)S(1)} %get-tuple-element.139), channel_id=1, source_target_pairs={{0,7},{1,0},{2,1},{3,2},{4,3},{5,4},{6,5},{7,6},{8,15},{9,8},{10,9... | collective-permute-start | bytes 196616 | tf_op jit(solution)/shard_map/ppermute | solution.py:292
  22.2 4.0 %ring_products.4 = f32[4,128,512]{2,1,0:T(8,128)} custom-call(s32[1]{0:T(128)} %bitcast.2.place, bf16[128,512]{1,0:T(8,128)(2,1)} %get-tuple-element.93.gated, bf16[512,4096]{1,0:T(8,128)(2,1)} %weight.7), custom_call_target="tpu_custom_call" | custom-call | flops 4294967296 | bytes 4194304 | tf_op jit(solution)/shard_map/ring_products/pallas_call | solution.py:226
  26.3 1.1 slice_bitcast_fusion.12
  27.6 1.0 fusion.25
  28.6 2.7 %collective-permute-start.3 = (bf16[128,512]{1,0:T(8,128)(2,1)S(1)}, bf16[128,512]{1,0:T(8,128)(2,1)S(1)}, u32[]{:S(2)}, u32[]{:S(2)}) collective-permute-start(bf16[128,512]{1,0:T(8,128)(2,1)S(1)} %get-tuple-element.133), channel_id=1, source_target_pairs={{0,7},{1,0},{2,1},{3,2},{4,3},{5,4},{6,5},{7,6},{8,15},{9,8},{10,9... | collective-permute-start | bytes 393224 | tf_op jit(solution)/shard_map/ppermute | solution.py:292
  31.3 1.9 %collective-permute-done.3 = bf16[128,512]{1,0:T(8,128)(2,1)S(1)} collective-permute-done((bf16[128,512]{1,0:T(8,128)(2,1)S(1)}, bf16[128,512]{1,0:T(8,128)(2,1)S(1)}, u32[]{:S(2)}, u32[]{:S(2)}) %collective-permute-start.3) | collective-permute-done | bytes 131104 | tf_op jit(solution)/shard_map/ppermute | solution.py:292
  33.3 3.4 %collective-permute-done.2 = bf16[128,512]{1,0:T(8,128)(2,1)S(1)} collective-permute-done((bf16[128,512]{1,0:T(8,128)(2,1)S(1)}, bf16[128,512]{1,0:T(8,128)(2,1)S(1)}, u32[]{:S(2)}, u32[]{:S(2)}) %collective-permute-start.2) | collective-permute-done | bytes 131104 | tf_op jit(solution)/shard_map/ppermute | solution.py:291
  36.6 1.1 fusion.13
  37.7 0.2 collective-permute-start.5
  37.9 1.4 %collective-permute-start.4 = (bf16[128,512]{1,0:T(8,128)(2,1)S(1)}, bf16[128,512]{1,0:T(8,128)(2,1)S(1)}, u32[]{:S(2)}, u32[]{:S(2)}) collective-permute-start(bf16[128,512]{1,0:T(8,128)(2,1)S(1)} %get-tuple-element.132), channel_id=1, source_target_pairs={{0,1},{1,2},{2,3},{3,4},{4,5},{5,6},{6,7},{7,0},{8,9},{9,10},{10,1... | collective-permute-start | bytes 393224 | tf_op jit(solution)/shard_map/ppermute | solution.py:291
  39.3 3.4 %ring_products.5 = f32[3,128,512]{2,1,0:T(8,128)} custom-call(s32[1]{0:T(128)} %bitcast.2.place, bf16[128,512]{1,0:T(8,128)(2,1)} %get-tuple-element.93.gated, bf16[512,4096]{1,0:T(8,128)(2,1)} %weight.7), custom_call_target="tpu_custom_call" | custom-call | flops 4294967296 | bytes 4194304 | tf_op jit(solution)/shard_map/ring_products/pallas_call | solution.py:226
  42.7 1.0 slice_bitcast_fusion.7
  43.8 1.1 fusion.22
  44.9 6.4 %band_rows.1 = (bf16[32,48,512]{2,1,0:T(8,128)(2,1)}, bf16[192,512]{1,0:T(8,128)(2,1)S(1)}, bf16[224,512]{1,0:T(8,128)(2,1)S(1)}, bf16[224,512]{1,0:T(8,128)(2,1)S(1)}) custom-call(s32[3]{0:T(128)S(1)} %and_select_fusion.turns, bf16[32,64,512]{2,1,0:T(8,128)(2,1)S(1)} %all-to-all-done.got_hbm, f32[3,3,512]{2,1,0:T(4,128)S(1)} %copy-done.2, ...), custom_call_target="tpu_custom_call" | custom-call | tf_op jit(solution)/shard_map/band_rows/pallas_call | solution.py:383
  51.4 0.7 copy-done.4
  52.0 3.7 %collective-permute-start.7 = (bf16[224,512]{1,0:T(8,128)(2,1)S(1)}, bf16[224,512]{1,0:T(8,128)(2,1)S(1)}, u32[]{:S(2)}, u32[]{:S(2)}) collective-permute-start(bf16[224,512]{1,0:T(8,128)(2,1)S(1)} %get-tuple-element.102), channel_id=1, source_target_pairs={{0,7},{1,0},{2,1},{3,2},{4,3},{5,4},{6,5},{7,6},{8,15},{9,8},{10,9... | collective-permute-start | bytes 688136 | tf_op jit(solution)/shard_map/ppermute | solution.py:292
  55.7 4.2 %ring_products.6 = f32[4,192,512]{2,1,0:T(8,128)} custom-call(s32[1]{0:T(128)} %bitcast.2.place, bf16[192,512]{1,0:T(8,128)(2,1)} %copy-done.4, bf16[512,4096]{1,0:T(8,128)(2,1)} %weight.7), custom_call_target="tpu_custom_call" | custom-call | flops 6442450944 | bytes 4194304 | tf_op jit(solution)/shard_map/ring_products/pallas_call | solution.py:226
  59.9 1.2 slice_bitcast_fusion.5
  61.1 1.1 fusion.19
  62.2 1.5 %collective-permute-start.9 = (bf16[192,512]{1,0:T(8,128)(2,1)S(1)}, bf16[192,512]{1,0:T(8,128)(2,1)S(1)}, u32[]{:S(2)}, u32[]{:S(2)}) collective-permute-start(bf16[192,512]{1,0:T(8,128)(2,1)S(1)} %get-tuple-element.125), channel_id=1, source_target_pairs={{0,7},{1,0},{2,1},{3,2},{4,3},{5,4},{6,5},{7,6},{8,15},{9,8},{10,9... | collective-permute-start | bytes 589832 | tf_op jit(solution)/shard_map/ppermute | solution.py:292
  63.7 9.8 %all-to-all-start.1 = ((bf16[32,48,512]{2,1,0:T(8,128)(2,1)}), bf16[32,48,512]{2,1,0:T(8,128)(2,1)S(1)}, u32[]{:S(2)}, u32[]{:S(2)}) async-start(bf16[32,48,512]{2,1,0:T(8,128)(2,1)} %get-tuple-element.115), calls=%async_computation.1 | async-start | bytes 3145728 | tf_op jit(solution)/shard_map/all_to_all | solution.py:286
  73.5 1.2 fusion.3
  74.7 2.9 %collective-permute-start.11 = (bf16[192,512]{1,0:T(8,128)(2,1)S(1)}, bf16[192,512]{1,0:T(8,128)(2,1)S(1)}, u32[]{:S(2)}, u32[]{:S(2)}) collective-permute-start(bf16[192,512]{1,0:T(8,128)(2,1)S(1)} %get-tuple-element.123), channel_id=1, source_target_pairs={{0,7},{1,0},{2,1},{3,2},{4,3},{5,4},{6,5},{7,6},{8,15},{9,8},{10,9... | collective-permute-start | bytes 589832 | tf_op jit(solution)/shard_map/ppermute | solution.py:292
  77.6 3.6 %ring_products.7 = f32[3,192,512]{2,1,0:T(8,128)} custom-call(s32[1]{0:T(128)} %bitcast.2.place, bf16[192,512]{1,0:T(8,128)(2,1)} %copy-done.4, bf16[512,4096]{1,0:T(8,128)(2,1)} %weight.7), custom_call_target="tpu_custom_call" | custom-call | flops 6442450944 | bytes 4194304 | tf_op jit(solution)/shard_map/ring_products/pallas_call | solution.py:226
  81.2 0.5 collective-permute-done.11
  81.6 3.1 %collective-permute-done.10 = bf16[192,512]{1,0:T(8,128)(2,1)S(1)} collective-permute-done((bf16[192,512]{1,0:T(8,128)(2,1)S(1)}, bf16[192,512]{1,0:T(8,128)(2,1)S(1)}, u32[]{:S(2)}, u32[]{:S(2)}) %collective-permute-start.10) | collective-permute-done | bytes 196640 | tf_op jit(solution)/shard_map/ppermute | solution.py:291
  84.7 1.2 fusion.1
  86.0 0.4 collective-permute-start.13
  86.4 1.1 collective-permute-start.12
  87.7 3.4 %collective-permute-done.13 = bf16[192,512]{1,0:T(8,128)(2,1)S(1)} collective-permute-done((bf16[192,512]{1,0:T(8,128)(2,1)S(1)}, bf16[192,512]{1,0:T(8,128)(2,1)S(1)}, u32[]{:S(2)}, u32[]{:S(2)}) %collective-permute-start.13) | collective-permute-done | bytes 196640 | tf_op jit(solution)/shard_map/ppermute | solution.py:292
  91.1 1.6 %collective-permute-done.12 = bf16[192,512]{1,0:T(8,128)(2,1)S(1)} collective-permute-done((bf16[192,512]{1,0:T(8,128)(2,1)S(1)}, bf16[192,512]{1,0:T(8,128)(2,1)S(1)}, u32[]{:S(2)}, u32[]{:S(2)}) %collective-permute-start.12) | collective-permute-done | bytes 196640 | tf_op jit(solution)/shard_map/ppermute | solution.py:291
  92.7 1.1 fusion.9
  93.7 1.9 %all-to-all-done.1.back = bf16[32,48,512]{2,1,0:T(8,128)(2,1)S(1)} async-done(((bf16[32,48,512]{2,1,0:T(8,128)(2,1)}), bf16[32,48,512]{2,1,0:T(8,128)(2,1)S(1)}, u32[]{:S(2)}, u32[]{:S(2)}) %all-to-all-start.1) | async-done | bytes 1572896 | tf_op jit(solution)/shard_map/all_to_all | solution.py:286
  95.8 2.8 %collective-permute-start.15 = (f32[320]{0:T(512)S(1)}, f32[320]{0:T(512)S(1)}, u32[]{:S(2)}, u32[]{:S(2)}) collective-permute-start(f32[320]{0:T(512)S(1)} %pad_maximum_fusion.1), channel_id=1, source_target_pairs={{0,7},{1,0},{2,1},{3,2},{4,3},{5,4},{6,5},{7,6},{8,15},{9,8},{10,9... | collective-permute-start | bytes 3848 | tf_op jit(solution)/shard_map/ppermute | solution.py:312
  98.8 0.6 collective-permute-done.15
  99.4 3.8 %collective-permute-done.16 = f32[320]{0:T(512)S(1)} collective-permute-done((f32[320]{0:T(512)S(1)}, f32[320]{0:T(512)S(1)}, u32[]{:S(2)}, u32[]{:S(2)}) %collective-permute-start.16) | collective-permute-done | bytes 1312 | tf_op jit(solution)/shard_map/ppermute | solution.py:312
  103.3 2.2 %collective-permute-start.17 = (f32[320]{0:T(512)S(1)}, f32[320]{0:T(512)S(1)}, u32[]{:S(2)}, u32[]{:S(2)}) collective-permute-start(f32[320]{0:T(512)S(1)} %add_add_fusion), channel_id=1, source_target_pairs={{0,4},{1,5},{2,6},{3,7},{4,0},{5,1},{6,2},{7,3},{8,12},{9,13},{10,... | collective-permute-start | bytes 3848 | tf_op jit(solution)/shard_map/ppermute | solution.py:312
  105.4 4.2 %collective-permute-done.17 = f32[320]{0:T(512)S(1)} collective-permute-done((f32[320]{0:T(512)S(1)}, f32[320]{0:T(512)S(1)}, u32[]{:S(2)}, u32[]{:S(2)}) %collective-permute-start.17) | collective-permute-done | bytes 1312 | tf_op jit(solution)/shard_map/ppermute | solution.py:312
  110.0 0.8 copy.18
  110.8 8.1 %all-to-all-start.2 = ((bf16[32,3,2,512]{3,2,1,0:T(2,128)(2,1)}), bf16[32,3,2,512]{3,2,1,0:T(2,128)(2,1)S(1)}, u32[]{:S(2)}, u32[]{:S(2)}) async-start(bf16[32,3,2,512]{3,2,1,0:T(2,128)(2,1)} %bitcast.107), calls=%async_computation.2 | async-start | bytes 393216 | tf_op jit(solution)/shard_map/all_to_all | solution.py:286
  118.9 5.3 %last_rows.1 = (f32[80,16,512]{2,1,0:T(8,128)}, bf16[80,3,2,512]{3,2,1,0:T(2,128)(2,1)}) custom-call(bf16[32,48,512]{2,1,0:T(8,128)(2,1)} %copy-done.5, bf16[4,3,80,512]{3,2,1,0:T(8,128)(2,1)} %bitcast.111, f32[16,16,512]{2,1,0:T(8,128)} %get-tuple-element.120.stay_state, s32[3,80]{1,0:T(4,128)} %finished.3), custom_call_target="tpu_custom_call" | custom-call | tf_op jit(solution)/shard_map/last_rows/pallas_call | solution.py:431
  124.3 3.0 %all-to-all-done.2 = bf16[32,3,2,512]{3,2,1,0:T(2,128)(2,1)S(1)} async-done(((bf16[32,3,2,512]{3,2,1,0:T(2,128)(2,1)}), bf16[32,3,2,512]{3,2,1,0:T(2,128)(2,1)S(1)}, u32[]{:S(2)}, u32[]{:S(2)}) %all-to-all-start.2) | async-done | bytes 196640 | tf_op jit(solution)/shard_map/all_to_all | solution.py:286
  127.3 0.1 copy.16
  127.5 0.8 maximum_maximum_fusion
  (53 shorter events, 1.4 us)
Async XLA Ops:
  6.4 9.9 %copy-start.6 = (bf16[128,512]{1,0:T(8,128)(2,1)S(1)}, bf16[128,512]{1,0:T(8,128)(2,1)}, u32[]{:S(2)}) copy-start(bf16[128,512]{1,0:T(8,128)(2,1)} %get-tuple-element.93.gated) | copy-start | bytes 393220
  6.4 38.5 %all-to-all-start = ((bf16[32,64,512]{2,1,0:T(8,128)(2,1)}), bf16[32,64,512]{2,1,0:T(8,128)(2,1)S(1)}, u32[]{:S(2)}, u32[]{:S(2)}) async-start(bf16[32,64,512]{2,1,0:T(8,128)(2,1)} %get-tuple-element.87), calls=%async_computation | async-start | bytes 4194304 | tf_op jit(solution)/shard_map/all_to_all | solution.py:286
  16.5 11.0 %collective-permute-start.1 = (bf16[64,512]{1,0:T(8,128)(2,1)S(1)}, bf16[64,512]{1,0:T(8,128)(2,1)S(1)}, u32[]{:S(2)}, u32[]{:S(2)}) collective-permute-start(bf16[64,512]{1,0:T(8,128)(2,1)S(1)} %get-tuple-element.139), channel_id=1, source_target_pairs={{0,7},{1,0},{2,1},{3,2},{4,3},{5,4},{6,5},{7,6},{8,15},{9,8},{10,9... | collective-permute-start | bytes 196616 | tf_op jit(solution)/shard_map/ppermute | solution.py:292
  22.2 5.4 %collective-permute-start = (bf16[64,512]{1,0:T(8,128)(2,1)S(1)}, bf16[64,512]{1,0:T(8,128)(2,1)S(1)}, u32[]{:S(2)}, u32[]{:S(2)}) collective-permute-start(bf16[64,512]{1,0:T(8,128)(2,1)S(1)} %get-tuple-element.140), channel_id=1, source_target_pairs={{0,1},{1,2},{2,3},{3,4},{4,5},{5,6},{6,7},{7,0},{8,9},{9,10},{10,1... | collective-permute-start | bytes 196616 | tf_op jit(solution)/shard_map/ppermute | solution.py:291
  22.2 5.1 %copy-start.8 = (s32[3,80]{1,0:T(4,128)S(1)}, s32[3,80]{1,0:T(4,128)}, u32[]{:S(2)}) copy-start(s32[3,80]{1,0:T(4,128)} %param.29) | copy-start | bytes 2884
  28.6 4.7 %collective-permute-start.3 = (bf16[128,512]{1,0:T(8,128)(2,1)S(1)}, bf16[128,512]{1,0:T(8,128)(2,1)S(1)}, u32[]{:S(2)}, u32[]{:S(2)}) collective-permute-start(bf16[128,512]{1,0:T(8,128)(2,1)S(1)} %get-tuple-element.133), channel_id=1, source_target_pairs={{0,7},{1,0},{2,1},{3,2},{4,3},{5,4},{6,5},{7,6},{8,15},{9,8},{10,9... | collective-permute-start | bytes 393224 | tf_op jit(solution)/shard_map/ppermute | solution.py:292
  31.3 5.3 %collective-permute-start.2 = (bf16[128,512]{1,0:T(8,128)(2,1)S(1)}, bf16[128,512]{1,0:T(8,128)(2,1)S(1)}, u32[]{:S(2)}, u32[]{:S(2)}) collective-permute-start(bf16[128,512]{1,0:T(8,128)(2,1)S(1)} %get-tuple-element.134), channel_id=1, source_target_pairs={{0,1},{1,2},{2,3},{3,4},{4,5},{5,6},{6,7},{7,0},{8,9},{9,10},{10,1... | collective-permute-start | bytes 393224 | tf_op jit(solution)/shard_map/ppermute | solution.py:291
  37.7 6.0 %collective-permute-start.5 = (bf16[128,512]{1,0:T(8,128)(2,1)S(1)}, bf16[128,512]{1,0:T(8,128)(2,1)S(1)}, u32[]{:S(2)}, u32[]{:S(2)}) collective-permute-start(bf16[128,512]{1,0:T(8,128)(2,1)S(1)} %get-tuple-element.131), channel_id=1, source_target_pairs={{0,7},{1,0},{2,1},{3,2},{4,3},{5,4},{6,5},{7,6},{8,15},{9,8},{10,9... | collective-permute-start | bytes 393224 | tf_op jit(solution)/shard_map/ppermute | solution.py:292
  37.9 5.8 %collective-permute-start.4 = (bf16[128,512]{1,0:T(8,128)(2,1)S(1)}, bf16[128,512]{1,0:T(8,128)(2,1)S(1)}, u32[]{:S(2)}, u32[]{:S(2)}) collective-permute-start(bf16[128,512]{1,0:T(8,128)(2,1)S(1)} %get-tuple-element.132), channel_id=1, source_target_pairs={{0,1},{1,2},{2,3},{3,4},{4,5},{5,6},{6,7},{7,0},{8,9},{9,10},{10,1... | collective-permute-start | bytes 393224 | tf_op jit(solution)/shard_map/ppermute | solution.py:291
  42.7 2.2 %copy-start = (f32[16,512]{1,0:T(8,128)S(1)}, f32[16,512]{1,0:T(8,128)}, u32[]{:S(2)}) copy-start(f32[16,512]{1,0:T(8,128)} %poles.3) | copy-start | bytes 98308
  42.7 2.2 %copy-start.1 = (f32[16,512]{1,0:T(8,128)S(1)}, f32[16,512]{1,0:T(8,128)}, u32[]{:S(2)}) copy-start(f32[16,512]{1,0:T(8,128)} %residues.3) | copy-start | bytes 98308
  42.7 2.2 %copy-start.2 = (f32[3,3,512]{2,1,0:T(4,128)S(1)}, f32[3,3,512]{2,1,0:T(4,128)}, u32[]{:S(2)}) copy-start(f32[3,3,512]{2,1,0:T(4,128)} %taps.3) | copy-start | bytes 55300
  42.7 2.2 %copy-start.3 = (f32[512]{0:T(512)S(1)}, f32[512]{0:T(512)}, u32[]{:S(2)}) copy-start(f32[512]{0:T(512)} %param.25) | copy-start | bytes 6148
  51.3 0.7 copy-start.4
  52.0 9.0 %collective-permute-start.6 = (bf16[224,512]{1,0:T(8,128)(2,1)S(1)}, bf16[224,512]{1,0:T(8,128)(2,1)S(1)}, u32[]{:S(2)}, u32[]{:S(2)}) collective-permute-start(bf16[224,512]{1,0:T(8,128)(2,1)S(1)} %get-tuple-element.101), channel_id=1, source_target_pairs={{0,1},{1,2},{2,3},{3,4},{4,5},{5,6},{6,7},{7,0},{8,9},{9,10},{10,1... | collective-permute-start | bytes 688136 | tf_op jit(solution)/shard_map/ppermute | solution.py:291
  52.0 9.0 %collective-permute-start.7 = (bf16[224,512]{1,0:T(8,128)(2,1)S(1)}, bf16[224,512]{1,0:T(8,128)(2,1)S(1)}, u32[]{:S(2)}, u32[]{:S(2)}) collective-permute-start(bf16[224,512]{1,0:T(8,128)(2,1)S(1)} %get-tuple-element.102), channel_id=1, source_target_pairs={{0,7},{1,0},{2,1},{3,2},{4,3},{5,4},{6,5},{7,6},{8,15},{9,8},{10,9... | collective-permute-start | bytes 688136 | tf_op jit(solution)/shard_map/ppermute | solution.py:292
  62.2 11.3 %collective-permute-start.9 = (bf16[192,512]{1,0:T(8,128)(2,1)S(1)}, bf16[192,512]{1,0:T(8,128)(2,1)S(1)}, u32[]{:S(2)}, u32[]{:S(2)}) collective-permute-start(bf16[192,512]{1,0:T(8,128)(2,1)S(1)} %get-tuple-element.125), channel_id=1, source_target_pairs={{0,7},{1,0},{2,1},{3,2},{4,3},{5,4},{6,5},{7,6},{8,15},{9,8},{10,9... | collective-permute-start | bytes 589832 | tf_op jit(solution)/shard_map/ppermute | solution.py:292
  63.7 9.8 %collective-permute-start.8 = (bf16[192,512]{1,0:T(8,128)(2,1)S(1)}, bf16[192,512]{1,0:T(8,128)(2,1)S(1)}, u32[]{:S(2)}, u32[]{:S(2)}) collective-permute-start(bf16[192,512]{1,0:T(8,128)(2,1)S(1)} %get-tuple-element.126), channel_id=1, source_target_pairs={{0,1},{1,2},{2,3},{3,4},{4,5},{5,6},{6,7},{7,0},{8,9},{9,10},{10,1... | collective-permute-start | bytes 589832 | tf_op jit(solution)/shard_map/ppermute | solution.py:291
  63.7 32.0 %all-to-all-start.1 = ((bf16[32,48,512]{2,1,0:T(8,128)(2,1)}), bf16[32,48,512]{2,1,0:T(8,128)(2,1)S(1)}, u32[]{:S(2)}, u32[]{:S(2)}) async-start(bf16[32,48,512]{2,1,0:T(8,128)(2,1)} %get-tuple-element.115), calls=%async_computation.1 | async-start | bytes 3145728 | tf_op jit(solution)/shard_map/all_to_all | solution.py:286
  74.7 6.9 %collective-permute-start.11 = (bf16[192,512]{1,0:T(8,128)(2,1)S(1)}, bf16[192,512]{1,0:T(8,128)(2,1)S(1)}, u32[]{:S(2)}, u32[]{:S(2)}) collective-permute-start(bf16[192,512]{1,0:T(8,128)(2,1)S(1)} %get-tuple-element.123), channel_id=1, source_target_pairs={{0,7},{1,0},{2,1},{3,2},{4,3},{5,4},{6,5},{7,6},{8,15},{9,8},{10,9... | collective-permute-start | bytes 589832 | tf_op jit(solution)/shard_map/ppermute | solution.py:292
  77.6 7.2 %collective-permute-start.10 = (bf16[192,512]{1,0:T(8,128)(2,1)S(1)}, bf16[192,512]{1,0:T(8,128)(2,1)S(1)}, u32[]{:S(2)}, u32[]{:S(2)}) collective-permute-start(bf16[192,512]{1,0:T(8,128)(2,1)S(1)} %get-tuple-element.124), channel_id=1, source_target_pairs={{0,1},{1,2},{2,3},{3,4},{4,5},{5,6},{6,7},{7,0},{8,9},{9,10},{10,1... | collective-permute-start | bytes 589832 | tf_op jit(solution)/shard_map/ppermute | solution.py:291
  81.2 28.5 %copy-start.7 = (f32[512]{0:T(512)S(1)}, f32[512]{0:T(512)}, u32[]{:S(2)}) copy-start(f32[512]{0:T(512)} %param.27) | copy-start | bytes 6148
  86.0 5.1 %collective-permute-start.13 = (bf16[192,512]{1,0:T(8,128)(2,1)S(1)}, bf16[192,512]{1,0:T(8,128)(2,1)S(1)}, u32[]{:S(2)}, u32[]{:S(2)}) collective-permute-start(bf16[192,512]{1,0:T(8,128)(2,1)S(1)} %get-tuple-element.129), channel_id=1, source_target_pairs={{0,7},{1,0},{2,1},{3,2},{4,3},{5,4},{6,5},{7,6},{8,15},{9,8},{10,9... | collective-permute-start | bytes 589832 | tf_op jit(solution)/shard_map/ppermute | solution.py:292
  86.4 6.3 %collective-permute-start.12 = (bf16[192,512]{1,0:T(8,128)(2,1)S(1)}, bf16[192,512]{1,0:T(8,128)(2,1)S(1)}, u32[]{:S(2)}, u32[]{:S(2)}) collective-permute-start(bf16[192,512]{1,0:T(8,128)(2,1)S(1)} %get-tuple-element.130), channel_id=1, source_target_pairs={{0,1},{1,2},{2,3},{3,4},{4,5},{5,6},{6,7},{7,0},{8,9},{9,10},{10,1... | collective-permute-start | bytes 589832 | tf_op jit(solution)/shard_map/ppermute | solution.py:291
  95.7 23.3 %copy-start.5 = (bf16[32,48,512]{2,1,0:T(8,128)(2,1)}, bf16[32,48,512]{2,1,0:T(8,128)(2,1)S(1)}, u32[]{:S(2)}) copy-start(bf16[32,48,512]{2,1,0:T(8,128)(2,1)S(1)} %all-to-all-done.1.back) | copy-start | bytes 4718596
  95.8 3.5 %collective-permute-start.15 = (f32[320]{0:T(512)S(1)}, f32[320]{0:T(512)S(1)}, u32[]{:S(2)}, u32[]{:S(2)}) collective-permute-start(f32[320]{0:T(512)S(1)} %pad_maximum_fusion.1), channel_id=1, source_target_pairs={{0,7},{1,0},{2,1},{3,2},{4,3},{5,4},{6,5},{7,6},{8,15},{9,8},{10,9... | collective-permute-start | bytes 3848 | tf_op jit(solution)/shard_map/ppermute | solution.py:312
  98.6 4.5 %collective-permute-start.16 = (f32[320]{0:T(512)S(1)}, f32[320]{0:T(512)S(1)}, u32[]{:S(2)}, u32[]{:S(2)}) collective-permute-start(f32[320]{0:T(512)S(1)} %pad_maximum_fusion.1), channel_id=1, source_target_pairs={{0,2},{1,3},{2,4},{3,5},{4,6},{5,7},{6,0},{7,1},{8,10},{9,11},{10,... | collective-permute-start | bytes 3848 | tf_op jit(solution)/shard_map/ppermute | solution.py:312
  98.6 4.5 %collective-permute-start.14 = (f32[320]{0:T(512)S(1)}, f32[320]{0:T(512)S(1)}, u32[]{:S(2)}, u32[]{:S(2)}) collective-permute-start(f32[320]{0:T(512)S(1)} %pad_maximum_fusion.1), channel_id=1, source_target_pairs={{0,1},{1,2},{2,3},{3,4},{4,5},{5,6},{6,7},{7,0},{8,9},{9,10},{10,1... | collective-permute-start | bytes 3848 | tf_op jit(solution)/shard_map/ppermute | solution.py:312
  103.3 6.4 %collective-permute-start.17 = (f32[320]{0:T(512)S(1)}, f32[320]{0:T(512)S(1)}, u32[]{:S(2)}, u32[]{:S(2)}) collective-permute-start(f32[320]{0:T(512)S(1)} %add_add_fusion), channel_id=1, source_target_pairs={{0,4},{1,5},{2,6},{3,7},{4,0},{5,1},{6,2},{7,3},{8,12},{9,13},{10,... | collective-permute-start | bytes 3848 | tf_op jit(solution)/shard_map/ppermute | solution.py:312
  110.8 16.5 %all-to-all-start.2 = ((bf16[32,3,2,512]{3,2,1,0:T(2,128)(2,1)}), bf16[32,3,2,512]{3,2,1,0:T(2,128)(2,1)S(1)}, u32[]{:S(2)}, u32[]{:S(2)}) async-start(bf16[32,3,2,512]{3,2,1,0:T(2,128)(2,1)} %bitcast.107), calls=%async_computation.2 | async-start | bytes 393216 | tf_op jit(solution)/shard_map/all_to_all | solution.py:286

commit v8 on v7

--- a/solution.py
+++ b/solution.py
@@ -238,7 +238,7 @@
         cost_estimate=pl.CostEstimate(
             flops=16 * rows * width * weight.shape[1], bytes_accessed=2 * weight.size, transcendentals=0
         ),
-        compiler_params=pltpu.CompilerParams(vmem_limit_bytes=56 * 1024 * 1024),
+        compiler_params=pltpu.CompilerParams(vmem_limit_bytes=52 * 1024 * 1024),
         name="ring_products",
     )(place, gated, weight)
     return dict(zip(aways, part))
@@ -311,9 +311,8 @@
     def sent_on(x, away):
         return lax.ppermute(x, "tensor", [(i, (i + away) % n) for i in range(n)])
 
-    near = [sent_on(squares, away) for away in (1, -1, 2)]
-    squares = squares + near[0] + near[1] + near[2]
-    squares = squares + sent_on(squares, 4)
+    four = squares + (sent_on(squares, 1) + sent_on(squares, -1)) + sent_on(squares, 2)
+    squares = sent_on(four, 2) + sent_on(four, -2)
     return lax.rsqrt(squares / (n * own[0].shape[1]) + 1e-05)[:, None]
 
 

time: 129 us -> 125 us (0.969)
  other arithmetic: 9.43 us -> 4.15 us
  starting transfers between devices: 51.2 us -> 56.2 us
  Pallas kernels: 32.7 us -> 28.7 us
  waiting for transfers between devices: 27.4 us -> 29.9 us
  local copies, waits for them, and re-layouts: 6.23 us -> 4.43 us
    pallas_call x4, Pallas kernels: 15.2 us -> 11.2 us  [products(): pl.pallas_call(products_kernel, grid_spec=pltpu.PrefetchScalarGridSpec(nu...]
    all_to_all x3, waiting for transfers between devices: 4.95 us -> 7.99 us  [swap(): return lax.all_to_all(blocks, 'dp', split_axis=0, concat_axis=0, tiled=True)]
    ppermute x4 -> x5, waiting for transfers between devices: 8.6 us -> 5.66 us  [sent_on(): return lax.ppermute(x, 'tensor', [(i, (i + away) % n) for i in range(n)])]
    convert_element_type x3, other arithmetic: 3.57 us -> 1.34 us  [joined(): return (ahead.astype(BF16), behind.astype(BF16))]
    another operation x3, local copies, waits for them, and re-layouts: 3.23 us -> 1.13 us  [products(): return dict(zip(aways, part))]
    ppermute x7, starting transfers between devices: 17 us -> 18.9 us  [pass_on(): left = lax.ppermute(left, 'tensor', [(i, (i - 1) % n) for i in range(n)])]
    ppermute x7, starting transfers between devices: 2.52 us -> 4.22 us  [pass_on(): right = lax.ppermute(right, 'tensor', [(i, (i + 1) % n) for i in range(n)])]
    ppermute x4 -> x5, starting transfers between devices: 5.11 us -> 6.67 us  [sent_on(): return lax.ppermute(x, 'tensor', [(i, (i + away) % n) for i in range(n)])]
  transfers between devices with their start and end apart: 21 -> 22, of which waited for: 11 -> 16; matrix products, arithmetic and copies ran while one was open for 9% -> 4% of each run, Pallas kernels for 16% -> 13%
where the time goes in v8:
time: 125 us; the launch traced here: 124 us
  starting transfers between devices  56.2 us (45%)
  waiting for transfers between devices  29.9 us (24%)
  Pallas kernels  28.7 us (23%)
  local copies, waits for them, and re-layouts  4.43 us (4%)
  other arithmetic  4.15 us (3%)
    all_to_all x3, starting transfers between devices, swap(): return lax.all_to_all(blocks, 'dp', split_axis=0, concat_axis=0, tiled=True)  26.4 us
    ppermute x7, starting transfers between devices, pass_on(): left = lax.ppermute(left, 'tensor', [(i, (i - 1) % n) for i in range(n)])  18.9 us
    pallas_call x4, Pallas kernels, products(): pl.pallas_call(products_kernel, grid_spec=pltpu.PrefetchScalarGridSpec(nu...  11.2 us
    ppermute x7, waiting for transfers between devices, pass_on(): right = lax.ppermute(right, 'tensor', [(i, (i + 1) % n) for i in range(n)])  9.4 us
    all_to_all x3, waiting for transfers between devices, swap(): return lax.all_to_all(blocks, 'dp', split_axis=0, concat_axis=0, tiled=True)  7.99 us
    ppermute x7, waiting for transfers between devices, pass_on(): left = lax.ppermute(left, 'tensor', [(i, (i - 1) % n) for i in range(n)])  6.82 us
    ppermute x5, starting transfers between devices, sent_on(): return lax.ppermute(x, 'tensor', [(i, (i + away) % n) for i in range(n)])  6.67 us
    pallas_call x1, Pallas kernels, per_device(): pl.pallas_call(band_kernel, in_specs=[pl.BlockSpec(memory_space=pltpu.SME...  6.4 us
  transfers between devices with their start and end apart: 22, of which 16 were waited for; matrix products, arithmetic and copies ran while one was open for 4% of the time, Pallas kernels for 13%

profile of v8, /device:TPU:1, one launch (start us, length us, event | category | flops | bytes accessed | tf_op | source)
XLA Modules:
  0.0 124.5 jit_solution(5925542103012900488)
XLA Ops:
  0.6 5.8 %home_rows.1 = (bf16[32,64,512]{2,1,0:T(8,128)(2,1)}, bf16[128,512]{1,0:T(8,128)(2,1)}, f32[16,16,512]{2,1,0:T(8,128)}) custom-call(bf16[4,3,80,512]{3,2,1,0:T(8,128)(2,1)} %bitcast.110, bf16[80,3,2,512]{3,2,1,0:T(2,128)(2,1)} %fir_hbm.1, f32[80,16,512]{2,1,0:T(8,128)} %state_hbm.1, f32[3,3,512]{2,1,0:T(4,128)} %taps.3, f32[16,512]{1,0:T(8,128)} %poles.3, ...), custom_call_target="tpu_custom_call" | custom-call | tf_op jit(solution)/shard_map/home_rows/pallas_call | solution.py:341
  6.4 8.7 %all-to-all-start = ((bf16[32,64,512]{2,1,0:T(8,128)(2,1)}), bf16[32,64,512]{2,1,0:T(8,128)(2,1)S(1)}, u32[]{:S(2)}, u32[]{:S(2)}) async-start(bf16[32,64,512]{2,1,0:T(8,128)(2,1)} %get-tuple-element.87), calls=%async_computation | async-start | bytes 4194304 | tf_op jit(solution)/shard_map/all_to_all | solution.py:286
  15.2 1.1 constant_dynamic-slice_fusion.far_weight
  16.3 0.2 convolution_convert_fusion
  16.5 5.7 %collective-permute-start.1 = (bf16[64,512]{1,0:T(8,128)(2,1)S(1)}, bf16[64,512]{1,0:T(8,128)(2,1)S(1)}, u32[]{:S(2)}, u32[]{:S(2)}) collective-permute-start(bf16[64,512]{1,0:T(8,128)(2,1)S(1)} %get-tuple-element.139), channel_id=1, source_target_pairs={{0,7},{1,0},{2,1},{3,2},{4,3},{5,4},{6,5},{7,6},{8,15},{9,8},{10,9... | collective-permute-start | bytes 196616 | tf_op jit(solution)/shard_map/ppermute | solution.py:292
  22.2 2.9 %ring_products.4 = f32[4,128,512]{2,1,0:T(8,128)S(1)} custom-call(s32[1]{0:T(128)} %bitcast.2.place, bf16[128,512]{1,0:T(8,128)(2,1)S(1)} %copy-done.3, bf16[512,4096]{1,0:T(8,128)(2,1)} %weight.7), custom_call_target="tpu_custom_call" | custom-call | flops 4294967296 | bytes 4194304 | tf_op jit(solution)/shard_map/ring_products/pallas_call | solution.py:226
  25.1 1.0 copy-done
  26.1 1.1 slice_bitcast_fusion.12
  27.4 1.0 fusion.25
  28.4 2.7 %collective-permute-start.3 = (bf16[128,512]{1,0:T(8,128)(2,1)S(1)}, bf16[128,512]{1,0:T(8,128)(2,1)S(1)}, u32[]{:S(2)}, u32[]{:S(2)}) collective-permute-start(bf16[128,512]{1,0:T(8,128)(2,1)S(1)} %get-tuple-element.133), channel_id=1, source_target_pairs={{0,7},{1,0},{2,1},{3,2},{4,3},{5,4},{6,5},{7,6},{8,15},{9,8},{10,9... | collective-permute-start | bytes 393224 | tf_op jit(solution)/shard_map/ppermute | solution.py:292
  31.2 1.9 %collective-permute-done.3 = bf16[128,512]{1,0:T(8,128)(2,1)S(1)} collective-permute-done((bf16[128,512]{1,0:T(8,128)(2,1)S(1)}, bf16[128,512]{1,0:T(8,128)(2,1)S(1)}, u32[]{:S(2)}, u32[]{:S(2)}) %collective-permute-start.3) | collective-permute-done | bytes 131104 | tf_op jit(solution)/shard_map/ppermute | solution.py:292
  33.1 3.4 %collective-permute-done.2 = bf16[128,512]{1,0:T(8,128)(2,1)S(1)} collective-permute-done((bf16[128,512]{1,0:T(8,128)(2,1)S(1)}, bf16[128,512]{1,0:T(8,128)(2,1)S(1)}, u32[]{:S(2)}, u32[]{:S(2)}) %collective-permute-start.2) | collective-permute-done | bytes 131104 | tf_op jit(solution)/shard_map/ppermute | solution.py:291
  36.5 1.1 fusion.13
  37.6 0.2 collective-permute-start.5
  37.8 1.4 %collective-permute-start.4 = (bf16[128,512]{1,0:T(8,128)(2,1)S(1)}, bf16[128,512]{1,0:T(8,128)(2,1)S(1)}, u32[]{:S(2)}, u32[]{:S(2)}) collective-permute-start(bf16[128,512]{1,0:T(8,128)(2,1)S(1)} %get-tuple-element.132), channel_id=1, source_target_pairs={{0,1},{1,2},{2,3},{3,4},{4,5},{5,6},{6,7},{7,0},{8,9},{9,10},{10,1... | collective-permute-start | bytes 393224 | tf_op jit(solution)/shard_map/ppermute | solution.py:291
  39.1 2.6 %ring_products.5 = f32[3,128,512]{2,1,0:T(8,128)S(1)} custom-call(s32[1]{0:T(128)} %bitcast.2.place, bf16[128,512]{1,0:T(8,128)(2,1)S(1)} %copy-done.3, bf16[512,4096]{1,0:T(8,128)(2,1)} %weight.7), custom_call_target="tpu_custom_call" | custom-call | flops 4294967296 | bytes 4194304 | tf_op jit(solution)/shard_map/ring_products/pallas_call | solution.py:226
  41.8 1.0 collective-permute-done.4
  43.0 6.4 %band_rows.1 = (bf16[32,48,512]{2,1,0:T(8,128)(2,1)}, bf16[192,512]{1,0:T(8,128)(2,1)S(1)}, bf16[224,512]{1,0:T(8,128)(2,1)S(1)}, bf16[224,512]{1,0:T(8,128)(2,1)S(1)}) custom-call(s32[3]{0:T(128)S(1)} %and_select_fusion.turns, bf16[32,64,512]{2,1,0:T(8,128)(2,1)S(1)} %all-to-all-done.got_hbm, f32[3,3,512]{2,1,0:T(4,128)S(1)} %copy-done.4, ...), custom_call_target="tpu_custom_call" | custom-call | tf_op jit(solution)/shard_map/band_rows/pallas_call | solution.py:382
  49.4 1.7 %collective-permute-start.6 = (bf16[224,512]{1,0:T(8,128)(2,1)S(1)}, bf16[224,512]{1,0:T(8,128)(2,1)S(1)}, u32[]{:S(2)}, u32[]{:S(2)}) collective-permute-start(bf16[224,512]{1,0:T(8,128)(2,1)S(1)} %get-tuple-element.101), channel_id=1, source_target_pairs={{0,1},{1,2},{2,3},{3,4},{4,5},{5,6},{6,7},{7,0},{8,9},{9,10},{10,1... | collective-permute-start | bytes 688136 | tf_op jit(solution)/shard_map/ppermute | solution.py:291
  51.2 4.0 %collective-permute-start.7 = (bf16[224,512]{1,0:T(8,128)(2,1)S(1)}, bf16[224,512]{1,0:T(8,128)(2,1)S(1)}, u32[]{:S(2)}, u32[]{:S(2)}) collective-permute-start(bf16[224,512]{1,0:T(8,128)(2,1)S(1)} %get-tuple-element.102), channel_id=1, source_target_pairs={{0,7},{1,0},{2,1},{3,2},{4,3},{5,4},{6,5},{7,6},{8,15},{9,8},{10,9... | collective-permute-start | bytes 688136 | tf_op jit(solution)/shard_map/ppermute | solution.py:292
  55.2 3.0 %ring_products.6 = f32[4,192,512]{2,1,0:T(8,128)S(1)} custom-call(s32[1]{0:T(128)} %bitcast.2.place, bf16[192,512]{1,0:T(8,128)(2,1)S(1)} %get-tuple-element.108.gated, bf16[512,4096]{1,0:T(8,128)(2,1)} %weight.7), custom_call_target="tpu_custom_call" | custom-call | flops 6442450944 | bytes 4194304 | tf_op jit(solution)/shard_map/ring_products/pallas_call | solution.py:226
  58.3 0.3 collective-permute-done.6
  58.6 2.8 %collective-permute-start.9 = (bf16[192,512]{1,0:T(8,128)(2,1)S(1)}, bf16[192,512]{1,0:T(8,128)(2,1)S(1)}, u32[]{:S(2)}, u32[]{:S(2)}) collective-permute-start(bf16[192,512]{1,0:T(8,128)(2,1)S(1)} %get-tuple-element.125), channel_id=1, source_target_pairs={{0,7},{1,0},{2,1},{3,2},{4,3},{5,4},{6,5},{7,6},{8,15},{9,8},{10,9... | collective-permute-start | bytes 589832 | tf_op jit(solution)/shard_map/ppermute | solution.py:292
  61.4 9.0 %all-to-all-start.1 = ((bf16[32,48,512]{2,1,0:T(8,128)(2,1)}), bf16[32,48,512]{2,1,0:T(8,128)(2,1)}, u32[]{:S(2)}, u32[]{:S(2)}) async-start(bf16[32,48,512]{2,1,0:T(8,128)(2,1)} %get-tuple-element.115), calls=%async_computation.1 | async-start | bytes 3145728 | tf_op jit(solution)/shard_map/all_to_all | solution.py:286
  70.6 3.0 %collective-permute-start.11 = (bf16[192,512]{1,0:T(8,128)(2,1)S(1)}, bf16[192,512]{1,0:T(8,128)(2,1)S(1)}, u32[]{:S(2)}, u32[]{:S(2)}) collective-permute-start(bf16[192,512]{1,0:T(8,128)(2,1)S(1)} %get-tuple-element.123), channel_id=1, source_target_pairs={{0,7},{1,0},{2,1},{3,2},{4,3},{5,4},{6,5},{7,6},{8,15},{9,8},{10,9... | collective-permute-start | bytes 589832 | tf_op jit(solution)/shard_map/ppermute | solution.py:292
  73.6 2.7 %ring_products.7 = f32[3,192,512]{2,1,0:T(8,128)S(1)} custom-call(s32[1]{0:T(128)} %bitcast.2.place, bf16[192,512]{1,0:T(8,128)(2,1)S(1)} %get-tuple-element.108.gated, bf16[512,4096]{1,0:T(8,128)(2,1)} %weight.7), custom_call_target="tpu_custom_call" | custom-call | flops 6442450944 | bytes 4194304 | tf_op jit(solution)/shard_map/ring_products/pallas_call | solution.py:226
  76.3 1.3 %collective-permute-done.11 = bf16[192,512]{1,0:T(8,128)(2,1)S(1)} collective-permute-done((bf16[192,512]{1,0:T(8,128)(2,1)S(1)}, bf16[192,512]{1,0:T(8,128)(2,1)S(1)}, u32[]{:S(2)}, u32[]{:S(2)}) %collective-permute-start.11) | collective-permute-done | bytes 196640 | tf_op jit(solution)/shard_map/ppermute | solution.py:292
  77.6 3.2 %collective-permute-done.10 = bf16[192,512]{1,0:T(8,128)(2,1)S(1)} collective-permute-done((bf16[192,512]{1,0:T(8,128)(2,1)S(1)}, bf16[192,512]{1,0:T(8,128)(2,1)S(1)}, u32[]{:S(2)}, u32[]{:S(2)}) %collective-permute-start.10) | collective-permute-done | bytes 196640 | tf_op jit(solution)/shard_map/ppermute | solution.py:291
  80.9 0.4 collective-permute-start.13
  81.3 1.1 collective-permute-start.12
  82.6 3.6 %collective-permute-done.13 = bf16[192,512]{1,0:T(8,128)(2,1)S(1)} collective-permute-done((bf16[192,512]{1,0:T(8,128)(2,1)S(1)}, bf16[192,512]{1,0:T(8,128)(2,1)S(1)}, u32[]{:S(2)}, u32[]{:S(2)}) %collective-permute-start.13) | collective-permute-done | bytes 196640 | tf_op jit(solution)/shard_map/ppermute | solution.py:292
  86.2 1.6 %collective-permute-done.12 = bf16[192,512]{1,0:T(8,128)(2,1)S(1)} collective-permute-done((bf16[192,512]{1,0:T(8,128)(2,1)S(1)}, bf16[192,512]{1,0:T(8,128)(2,1)S(1)}, u32[]{:S(2)}, u32[]{:S(2)}) %collective-permute-start.12) | collective-permute-done | bytes 196640 | tf_op jit(solution)/shard_map/ppermute | solution.py:291
  87.8 4.9 %all-to-all-done.1.back = bf16[32,48,512]{2,1,0:T(8,128)(2,1)} async-done(((bf16[32,48,512]{2,1,0:T(8,128)(2,1)}), bf16[32,48,512]{2,1,0:T(8,128)(2,1)}, u32[]{:S(2)}, u32[]{:S(2)}) %all-to-all-start.1) | async-done | bytes 1572896 | tf_op jit(solution)/shard_map/all_to_all | solution.py:286
  92.9 1.6 %collective-permute-start.16 = (f32[320]{0:T(512)S(1)}, f32[320]{0:T(512)S(1)}, u32[]{:S(2)}, u32[]{:S(2)}) collective-permute-start(f32[320]{0:T(512)S(1)} %pad_maximum_fusion.1), channel_id=1, source_target_pairs={{0,2},{1,3},{2,4},{3,5},{4,6},{5,7},{6,0},{7,1},{8,10},{9,11},{10,... | collective-permute-start | bytes 3848 | tf_op jit(solution)/shard_map/ppermute | solution.py:312
  94.5 1.5 %collective-permute-start.15 = (f32[320]{0:T(512)S(1)}, f32[320]{0:T(512)S(1)}, u32[]{:S(2)}, u32[]{:S(2)}) collective-permute-start(f32[320]{0:T(512)S(1)} %pad_maximum_fusion.1), channel_id=1, source_target_pairs={{0,7},{1,0},{2,1},{3,2},{4,3},{5,4},{6,5},{7,6},{8,15},{9,8},{10,9... | collective-permute-start | bytes 3848 | tf_op jit(solution)/shard_map/ppermute | solution.py:312
  95.9 1.2 collective-permute-start.14
  97.2 0.3 collective-permute-done.16
  97.4 0.7 collective-permute-done.15
  98.1 1.7 %collective-permute-done.14 = f32[320]{0:T(512)S(1)} collective-permute-done((f32[320]{0:T(512)S(1)}, f32[320]{0:T(512)S(1)}, u32[]{:S(2)}, u32[]{:S(2)}) %collective-permute-start.14) | collective-permute-done | bytes 1312 | tf_op jit(solution)/shard_map/ppermute | solution.py:312
  100.0 0.8 collective-permute-start.18
  100.7 1.6 %collective-permute-start.17 = (f32[320]{0:T(512)S(1)}, f32[320]{0:T(512)S(1)}, u32[]{:S(2)}, u32[]{:S(2)}) collective-permute-start(f32[320]{0:T(512)S(1)} %add_add_fusion), channel_id=1, source_target_pairs={{0,2},{1,3},{2,4},{3,5},{4,6},{5,7},{6,0},{7,1},{8,10},{9,11},{10,... | collective-permute-start | bytes 3848 | tf_op jit(solution)/shard_map/ppermute | solution.py:312
  102.3 1.0 collective-permute-done.18
  103.3 2.0 %collective-permute-done.17 = f32[320]{0:T(512)S(1)} collective-permute-done((f32[320]{0:T(512)S(1)}, f32[320]{0:T(512)S(1)}, u32[]{:S(2)}, u32[]{:S(2)}) %collective-permute-start.17) | collective-permute-done | bytes 1312 | tf_op jit(solution)/shard_map/ppermute | solution.py:312
  105.7 0.8 copy.18
  106.5 8.6 %all-to-all-start.2 = ((bf16[32,3,2,512]{3,2,1,0:T(2,128)(2,1)}), bf16[32,3,2,512]{3,2,1,0:T(2,128)(2,1)S(1)}, u32[]{:S(2)}, u32[]{:S(2)}) async-start(bf16[32,3,2,512]{3,2,1,0:T(2,128)(2,1)} %bitcast.107), calls=%async_computation.2 | async-start | bytes 393216 | tf_op jit(solution)/shard_map/all_to_all | solution.py:286
  115.1 5.3 %last_rows.1 = (f32[80,16,512]{2,1,0:T(8,128)}, bf16[80,3,2,512]{3,2,1,0:T(2,128)(2,1)}) custom-call(bf16[32,48,512]{2,1,0:T(8,128)(2,1)} %all-to-all-done.1.back, bf16[4,3,80,512]{3,2,1,0:T(8,128)(2,1)} %bitcast.111, f32[16,16,512]{2,1,0:T(8,128)} %get-tuple-element.120.stay_state, s32[3,80]{1,0:T(4,128)} %finished.3), custom_call_target="tpu_custom_call" | custom-call | tf_op jit(solution)/shard_map/last_rows/pallas_call | solution.py:430
  120.5 3.0 %all-to-all-done.2 = bf16[32,3,2,512]{3,2,1,0:T(2,128)(2,1)S(1)} async-done(((bf16[32,3,2,512]{3,2,1,0:T(2,128)(2,1)}), bf16[32,3,2,512]{3,2,1,0:T(2,128)(2,1)S(1)}, u32[]{:S(2)}, u32[]{:S(2)}) %all-to-all-start.2) | async-done | bytes 196640 | tf_op jit(solution)/shard_map/all_to_all | solution.py:286
  123.7 0.8 maximum_maximum_fusion
  (53 shorter events, 1.9 us)
Async XLA Ops:
  6.4 9.9 %copy-start.3 = (bf16[128,512]{1,0:T(8,128)(2,1)S(1)}, bf16[128,512]{1,0:T(8,128)(2,1)}, u32[]{:S(2)}) copy-start(bf16[128,512]{1,0:T(8,128)(2,1)} %get-tuple-element.93.gated) | copy-start | bytes 393220
  6.4 36.6 %all-to-all-start = ((bf16[32,64,512]{2,1,0:T(8,128)(2,1)}), bf16[32,64,512]{2,1,0:T(8,128)(2,1)S(1)}, u32[]{:S(2)}, u32[]{:S(2)}) async-start(bf16[32,64,512]{2,1,0:T(8,128)(2,1)} %get-tuple-element.87), calls=%async_computation | async-start | bytes 4194304 | tf_op jit(solution)/shard_map/all_to_all | solution.py:286
  16.5 10.9 %collective-permute-start.1 = (bf16[64,512]{1,0:T(8,128)(2,1)S(1)}, bf16[64,512]{1,0:T(8,128)(2,1)S(1)}, u32[]{:S(2)}, u32[]{:S(2)}) collective-permute-start(bf16[64,512]{1,0:T(8,128)(2,1)S(1)} %get-tuple-element.139), channel_id=1, source_target_pairs={{0,7},{1,0},{2,1},{3,2},{4,3},{5,4},{6,5},{7,6},{8,15},{9,8},{10,9... | collective-permute-start | bytes 196616 | tf_op jit(solution)/shard_map/ppermute | solution.py:292
  22.2 5.2 %collective-permute-start = (bf16[64,512]{1,0:T(8,128)(2,1)S(1)}, bf16[64,512]{1,0:T(8,128)(2,1)S(1)}, u32[]{:S(2)}, u32[]{:S(2)}) collective-permute-start(bf16[64,512]{1,0:T(8,128)(2,1)S(1)} %get-tuple-element.140), channel_id=1, source_target_pairs={{0,1},{1,2},{2,3},{3,4},{4,5},{5,6},{6,7},{7,0},{8,9},{9,10},{10,1... | collective-permute-start | bytes 196616 | tf_op jit(solution)/shard_map/ppermute | solution.py:291
  22.2 5.0 %copy-start.7 = (s32[3,80]{1,0:T(4,128)S(1)}, s32[3,80]{1,0:T(4,128)}, u32[]{:S(2)}) copy-start(s32[3,80]{1,0:T(4,128)} %param.29) | copy-start | bytes 2884
  25.1 1.0 copy-start
  28.4 4.7 %collective-permute-start.3 = (bf16[128,512]{1,0:T(8,128)(2,1)S(1)}, bf16[128,512]{1,0:T(8,128)(2,1)S(1)}, u32[]{:S(2)}, u32[]{:S(2)}) collective-permute-start(bf16[128,512]{1,0:T(8,128)(2,1)S(1)} %get-tuple-element.133), channel_id=1, source_target_pairs={{0,7},{1,0},{2,1},{3,2},{4,3},{5,4},{6,5},{7,6},{8,15},{9,8},{10,9... | collective-permute-start | bytes 393224 | tf_op jit(solution)/shard_map/ppermute | solution.py:292
  31.2 5.3 %collective-permute-start.2 = (bf16[128,512]{1,0:T(8,128)(2,1)S(1)}, bf16[128,512]{1,0:T(8,128)(2,1)S(1)}, u32[]{:S(2)}, u32[]{:S(2)}) collective-permute-start(bf16[128,512]{1,0:T(8,128)(2,1)S(1)} %get-tuple-element.134), channel_id=1, source_target_pairs={{0,1},{1,2},{2,3},{3,4},{4,5},{5,6},{6,7},{7,0},{8,9},{9,10},{10,1... | collective-permute-start | bytes 393224 | tf_op jit(solution)/shard_map/ppermute | solution.py:291
  37.6 4.2 %collective-permute-start.5 = (bf16[128,512]{1,0:T(8,128)(2,1)S(1)}, bf16[128,512]{1,0:T(8,128)(2,1)S(1)}, u32[]{:S(2)}, u32[]{:S(2)}) collective-permute-start(bf16[128,512]{1,0:T(8,128)(2,1)S(1)} %get-tuple-element.131), channel_id=1, source_target_pairs={{0,7},{1,0},{2,1},{3,2},{4,3},{5,4},{6,5},{7,6},{8,15},{9,8},{10,9... | collective-permute-start | bytes 393224 | tf_op jit(solution)/shard_map/ppermute | solution.py:292
  37.8 5.0 %collective-permute-start.4 = (bf16[128,512]{1,0:T(8,128)(2,1)S(1)}, bf16[128,512]{1,0:T(8,128)(2,1)S(1)}, u32[]{:S(2)}, u32[]{:S(2)}) collective-permute-start(bf16[128,512]{1,0:T(8,128)(2,1)S(1)} %get-tuple-element.132), channel_id=1, source_target_pairs={{0,1},{1,2},{2,3},{3,4},{4,5},{5,6},{6,7},{7,0},{8,9},{9,10},{10,1... | collective-permute-start | bytes 393224 | tf_op jit(solution)/shard_map/ppermute | solution.py:291
  41.7 1.3 %copy-start.1 = (f32[16,512]{1,0:T(8,128)S(1)}, f32[16,512]{1,0:T(8,128)}, u32[]{:S(2)}) copy-start(f32[16,512]{1,0:T(8,128)} %poles.3) | copy-start | bytes 98308
  41.7 1.3 %copy-start.2 = (f32[16,512]{1,0:T(8,128)S(1)}, f32[16,512]{1,0:T(8,128)}, u32[]{:S(2)}) copy-start(f32[16,512]{1,0:T(8,128)} %residues.3) | copy-start | bytes 98308
  41.8 1.3 %copy-start.4 = (f32[3,3,512]{2,1,0:T(4,128)S(1)}, f32[3,3,512]{2,1,0:T(4,128)}, u32[]{:S(2)}) copy-start(f32[3,3,512]{2,1,0:T(4,128)} %taps.3) | copy-start | bytes 55300
  41.8 1.3 %copy-start.5 = (f32[512]{0:T(512)S(1)}, f32[512]{0:T(512)}, u32[]{:S(2)}) copy-start(f32[512]{0:T(512)} %param.25) | copy-start | bytes 6148
  49.4 9.1 %collective-permute-start.6 = (bf16[224,512]{1,0:T(8,128)(2,1)S(1)}, bf16[224,512]{1,0:T(8,128)(2,1)S(1)}, u32[]{:S(2)}, u32[]{:S(2)}) collective-permute-start(bf16[224,512]{1,0:T(8,128)(2,1)S(1)} %get-tuple-element.101), channel_id=1, source_target_pairs={{0,1},{1,2},{2,3},{3,4},{4,5},{5,6},{6,7},{7,0},{8,9},{9,10},{10,1... | collective-permute-start | bytes 688136 | tf_op jit(solution)/shard_map/ppermute | solution.py:291
  51.2 7.3 %collective-permute-start.7 = (bf16[224,512]{1,0:T(8,128)(2,1)S(1)}, bf16[224,512]{1,0:T(8,128)(2,1)S(1)}, u32[]{:S(2)}, u32[]{:S(2)}) collective-permute-start(bf16[224,512]{1,0:T(8,128)(2,1)S(1)} %get-tuple-element.102), channel_id=1, source_target_pairs={{0,7},{1,0},{2,1},{3,2},{4,3},{5,4},{6,5},{7,6},{8,15},{9,8},{10,9... | collective-permute-start | bytes 688136 | tf_op jit(solution)/shard_map/ppermute | solution.py:292
  58.6 11.9 %collective-permute-start.9 = (bf16[192,512]{1,0:T(8,128)(2,1)S(1)}, bf16[192,512]{1,0:T(8,128)(2,1)S(1)}, u32[]{:S(2)}, u32[]{:S(2)}) collective-permute-start(bf16[192,512]{1,0:T(8,128)(2,1)S(1)} %get-tuple-element.125), channel_id=1, source_target_pairs={{0,7},{1,0},{2,1},{3,2},{4,3},{5,4},{6,5},{7,6},{8,15},{9,8},{10,9... | collective-permute-start | bytes 589832 | tf_op jit(solution)/shard_map/ppermute | solution.py:292
  61.4 9.1 %collective-permute-start.8 = (bf16[192,512]{1,0:T(8,128)(2,1)S(1)}, bf16[192,512]{1,0:T(8,128)(2,1)S(1)}, u32[]{:S(2)}, u32[]{:S(2)}) collective-permute-start(bf16[192,512]{1,0:T(8,128)(2,1)S(1)} %get-tuple-element.126), channel_id=1, source_target_pairs={{0,1},{1,2},{2,3},{3,4},{4,5},{5,6},{6,7},{7,0},{8,9},{9,10},{10,1... | collective-permute-start | bytes 589832 | tf_op jit(solution)/shard_map/ppermute | solution.py:291
  61.4 31.3 %all-to-all-start.1 = ((bf16[32,48,512]{2,1,0:T(8,128)(2,1)}), bf16[32,48,512]{2,1,0:T(8,128)(2,1)}, u32[]{:S(2)}, u32[]{:S(2)}) async-start(bf16[32,48,512]{2,1,0:T(8,128)(2,1)} %get-tuple-element.115), calls=%async_computation.1 | async-start | bytes 3145728 | tf_op jit(solution)/shard_map/all_to_all | solution.py:286
  70.6 7.0 %collective-permute-start.11 = (bf16[192,512]{1,0:T(8,128)(2,1)S(1)}, bf16[192,512]{1,0:T(8,128)(2,1)S(1)}, u32[]{:S(2)}, u32[]{:S(2)}) collective-permute-start(bf16[192,512]{1,0:T(8,128)(2,1)S(1)} %get-tuple-element.123), channel_id=1, source_target_pairs={{0,7},{1,0},{2,1},{3,2},{4,3},{5,4},{6,5},{7,6},{8,15},{9,8},{10,9... | collective-permute-start | bytes 589832 | tf_op jit(solution)/shard_map/ppermute | solution.py:292
  73.6 7.2 %collective-permute-start.10 = (bf16[192,512]{1,0:T(8,128)(2,1)S(1)}, bf16[192,512]{1,0:T(8,128)(2,1)S(1)}, u32[]{:S(2)}, u32[]{:S(2)}) collective-permute-start(bf16[192,512]{1,0:T(8,128)(2,1)S(1)} %get-tuple-element.124), channel_id=1, source_target_pairs={{0,1},{1,2},{2,3},{3,4},{4,5},{5,6},{6,7},{7,0},{8,9},{9,10},{10,1... | collective-permute-start | bytes 589832 | tf_op jit(solution)/shard_map/ppermute | solution.py:291
  76.3 29.1 %copy-start.6 = (f32[512]{0:T(512)S(1)}, f32[512]{0:T(512)}, u32[]{:S(2)}) copy-start(f32[512]{0:T(512)} %param.27) | copy-start | bytes 6148
  80.9 5.2 %collective-permute-start.13 = (bf16[192,512]{1,0:T(8,128)(2,1)S(1)}, bf16[192,512]{1,0:T(8,128)(2,1)S(1)}, u32[]{:S(2)}, u32[]{:S(2)}) collective-permute-start(bf16[192,512]{1,0:T(8,128)(2,1)S(1)} %get-tuple-element.129), channel_id=1, source_target_pairs={{0,7},{1,0},{2,1},{3,2},{4,3},{5,4},{6,5},{7,6},{8,15},{9,8},{10,9... | collective-permute-start | bytes 589832 | tf_op jit(solution)/shard_map/ppermute | solution.py:292
  81.3 6.4 %collective-permute-start.12 = (bf16[192,512]{1,0:T(8,128)(2,1)S(1)}, bf16[192,512]{1,0:T(8,128)(2,1)S(1)}, u32[]{:S(2)}, u32[]{:S(2)}) collective-permute-start(bf16[192,512]{1,0:T(8,128)(2,1)S(1)} %get-tuple-element.130), channel_id=1, source_target_pairs={{0,1},{1,2},{2,3},{3,4},{4,5},{5,6},{6,7},{7,0},{8,9},{9,10},{10,1... | collective-permute-start | bytes 589832 | tf_op jit(solution)/shard_map/ppermute | solution.py:291
  92.9 4.6 %collective-permute-start.16 = (f32[320]{0:T(512)S(1)}, f32[320]{0:T(512)S(1)}, u32[]{:S(2)}, u32[]{:S(2)}) collective-permute-start(f32[320]{0:T(512)S(1)} %pad_maximum_fusion.1), channel_id=1, source_target_pairs={{0,2},{1,3},{2,4},{3,5},{4,6},{5,7},{6,0},{7,1},{8,10},{9,11},{10,... | collective-permute-start | bytes 3848 | tf_op jit(solution)/shard_map/ppermute | solution.py:312
  94.5 3.7 %collective-permute-start.15 = (f32[320]{0:T(512)S(1)}, f32[320]{0:T(512)S(1)}, u32[]{:S(2)}, u32[]{:S(2)}) collective-permute-start(f32[320]{0:T(512)S(1)} %pad_maximum_fusion.1), channel_id=1, source_target_pairs={{0,7},{1,0},{2,1},{3,2},{4,3},{5,4},{6,5},{7,6},{8,15},{9,8},{10,9... | collective-permute-start | bytes 3848 | tf_op jit(solution)/shard_map/ppermute | solution.py:312
  95.9 3.9 %collective-permute-start.14 = (f32[320]{0:T(512)S(1)}, f32[320]{0:T(512)S(1)}, u32[]{:S(2)}, u32[]{:S(2)}) collective-permute-start(f32[320]{0:T(512)S(1)} %pad_maximum_fusion.1), channel_id=1, source_target_pairs={{0,1},{1,2},{2,3},{3,4},{4,5},{5,6},{6,7},{7,0},{8,9},{9,10},{10,1... | collective-permute-start | bytes 3848 | tf_op jit(solution)/shard_map/ppermute | solution.py:312
  100.0 3.3 %collective-permute-start.18 = (f32[320]{0:T(512)S(1)}, f32[320]{0:T(512)S(1)}, u32[]{:S(2)}, u32[]{:S(2)}) collective-permute-start(f32[320]{0:T(512)S(1)} %add_add_fusion), channel_id=1, source_target_pairs={{0,6},{1,7},{2,0},{3,1},{4,2},{5,3},{6,4},{7,5},{8,14},{9,15},{10,... | collective-permute-start | bytes 3848 | tf_op jit(solution)/shard_map/ppermute | solution.py:312
  100.7 4.5 %collective-permute-start.17 = (f32[320]{0:T(512)S(1)}, f32[320]{0:T(512)S(1)}, u32[]{:S(2)}, u32[]{:S(2)}) collective-permute-start(f32[320]{0:T(512)S(1)} %add_add_fusion), channel_id=1, source_target_pairs={{0,2},{1,3},{2,4},{3,5},{4,6},{5,7},{6,0},{7,1},{8,10},{9,11},{10,... | collective-permute-start | bytes 3848 | tf_op jit(solution)/shard_map/ppermute | solution.py:312
  106.5 17.0 %all-to-all-start.2 = ((bf16[32,3,2,512]{3,2,1,0:T(2,128)(2,1)}), bf16[32,3,2,512]{3,2,1,0:T(2,128)(2,1)S(1)}, u32[]{:S(2)}, u32[]{:S(2)}) async-start(bf16[32,3,2,512]{3,2,1,0:T(2,128)(2,1)} %bitcast.107), calls=%async_computation.2 | async-start | bytes 393216 | tf_op jit(solution)/shard_map/all_to_all | solution.py:286

commit v9 on v8

--- a/solution.py
+++ b/solution.py
@@ -122,36 +122,31 @@
 
 
 def band_kernel(
-    turns, got_hbm, taps, poles, residues, skip, far_weight, ride, sent, gated, first_right, first_left, *scratch
+    turns, got, taps, poles, residues, skip, far_weight, ride, sent, gated, first_right, first_left, *scratch
 ):
-    lags, inputs, live, heads, products, y_rows, got, sems = scratch
+    lags, inputs, live, heads, products, y_rows, kinds = scratch
     groups, _, width = got.shape
     rows = 2 * groups
-    halves = [pl.ds(2 * MODES, 2 * KINDS), pl.ds(0, 2 * MODES)]
-    fetches = [
-        pltpu.make_async_copy(got_hbm.at[:, at], got.at[:, at], sems.at[i])
-        for i, at in enumerate(halves)
-    ]
-    for fetch in fetches:
-        fetch.start()
-    fetches[0].wait()
-    kinds = got[:, 2 * MODES :].reshape(groups * 2 * KINDS, width)
-
-    def taken(first, count, turn):
-        shape = (count * rows, groups * 2 * KINDS)
-        r = lax.broadcasted_iota(jnp.int32, shape, 0)
-        c = lax.broadcasted_iota(jnp.int32, shape, 1)
-        group = (((r & (rows - 1)) >> 1) + turn) & (groups - 1)
-        source = group * (2 * KINDS) + (first + r // rows) * 2 + (r & 1)
-        order = jnp.where(c == source, 1.0, 0.0).astype(BF16)
-        return dot(order, kinds).reshape(count, rows, width)
-
-    lags[...] = taken(0, 6, 0)
+
+    n = 16 * KINDS
+    r = lax.broadcasted_iota(jnp.int32, (n, n), 0)
+    c = lax.broadcasted_iota(jnp.int32, (n, n), 1)
+    source = ((r >> 1) & 7) * (2 * KINDS) + (r >> 4) * 2 + (r & 1)
+    order = jnp.where(c == source, 1.0, 0.0).astype(BF16)
+    for g in range(0, groups, 8):
+        part = dot(order, got[g : g + 8, 2 * MODES :].reshape(n, width)).reshape(KINDS, 16, width)
+        lags[:, 2 * g : 2 * g + 16] = part[:6]
+        kinds[:, 2 * g : 2 * g + 16] = part[6:].astype(BF16)
+
+    r = lax.broadcasted_iota(jnp.int32, (rows, rows), 0)
+    c = lax.broadcasted_iota(jnp.int32, (rows, rows), 1)
+    half = width // 2
     for t in range(3):
-        inputs[t] = taken(6 + 3 * t, 3, turns[t])
-    half = width // 2
-    live[0] = wide(taken(15, 1, turns[0])[0, :, :half], width)
-    live[1] = wide(taken(15, 1, turns[1])[0, :, half:], width)
+        turn = jnp.where(c == ((r + 2 * turns[t]) & (rows - 1)), 1.0, 0.0).astype(BF16)
+        for j in range(3):
+            inputs[t, j] = dot(turn, kinds[3 * t + j])
+        if t < 2:
+            live[t] = wide(dot(turn, kinds[9, :, t * half : (t + 1) * half]), width)
 
     @pl.loop(0, rows // 8)
     def _(i):
@@ -182,8 +177,6 @@
     last = lags[0:3].reshape(3 * rows, width).astype(BF16)
     sent[:, 2 * MODES :] = dot(order, last).reshape(groups, 16, width).astype(BF16)
 
-    fetches[1].wait()
-
     @pl.loop(0, groups)
     def _(g):
         final = []
@@ -304,16 +297,18 @@
     return ahead.astype(BF16), behind.astype(BF16)
 
 
-def row_scales(own):
+def row_scales(own, back):
     n = lax.axis_size("tensor")
     squares = jnp.concatenate([jnp.sum(x * x, axis=1) for x in own])
 
     def sent_on(x, away):
         return lax.ppermute(x, "tensor", [(i, (i + away) % n) for i in range(n)])
 
-    four = squares + (sent_on(squares, 1) + sent_on(squares, -1)) + sent_on(squares, 2)
-    squares = sent_on(four, 2) + sent_on(four, -2)
-    return lax.rsqrt(squares / (n * own[0].shape[1]) + 1e-05)[:, None]
+    below = squares + sent_on(squares, 1)
+    three = below + sent_on(squares, -1)
+    three, below, back = lax.optimization_barrier((three, below, back))
+    squares = three + (sent_on(three, 3) + sent_on(below, -3))
+    return lax.rsqrt(squares / (n * own[0].shape[1]) + 1e-05)[:, None], back
 
 
 def per_device(
@@ -383,9 +378,8 @@
         band_kernel,
         in_specs=[
             pl.BlockSpec(memory_space=pltpu.SMEM),
-            pl.BlockSpec(memory_space=pl.ANY),
         ]
-        + [pl.BlockSpec(memory_space=pltpu.VMEM)] * 6,
+        + [pl.BlockSpec(memory_space=pltpu.VMEM)] * 7,
         out_specs=[pl.BlockSpec(memory_space=pltpu.VMEM)] * 4,
         out_shape=[
             jax.ShapeDtypeStruct((groups, 2 * MODES + 16, width), BF16),
@@ -400,8 +394,7 @@
             pltpu.VMEM((3, moving, width), F32),
             pltpu.VMEM((3, moving, width), F32),
             pltpu.VMEM((3, moving, width), F32),
-            pltpu.VMEM(got.shape, BF16),
-            pltpu.SemaphoreType.DMA((2,)),
+            pltpu.VMEM((KINDS - 6, moving, width), BF16),
         ],
         compiler_params=pltpu.CompilerParams(vmem_limit_bytes=40 * 1024 * 1024),
         name="band_rows",
@@ -421,8 +414,7 @@
     right, left = pass_on(*joined(made, 1, right, left))
     right, left = lax.optimization_barrier((right, left))
     own_band = made[0] + right.astype(F32) + left.astype(F32)
-    own_band, back = lax.optimization_barrier((own_band, back))
-    scales = row_scales([own_band, own_home])
+    scales, back = row_scales([own_band, own_home], back)
     mixed_band = (own_band * scales[: 3 * moving] * norm_gain[None]).astype(BF16)
     mixed_band = jnp.transpose(mixed_band.reshape(3, groups, CAP, own_cols), (1, 0, 2, 3))
     back, mixed_band = lax.optimization_barrier((back, mixed_band))

time: 125 us -> 122 us (0.976)
  waiting for transfers between devices: 29.9 us -> 25.7 us
  starting transfers between devices: 56.2 us -> 58 us
    all_to_all x3, waiting for transfers between devices: 7.99 us -> 3.7 us  [swap(): return lax.all_to_all(blocks, 'dp', split_axis=0, concat_axis=0, tiled=True)]
    all_to_all x3, starting transfers between devices: 26.4 us -> 29.6 us  [swap(): return lax.all_to_all(blocks, 'dp', split_axis=0, concat_axis=0, tiled=True)]
    ppermute x5 -> x4, starting transfers between devices: 6.67 us -> 5.52 us  [sent_on(): return lax.ppermute(x, 'tensor', [(i, (i + away) % n) for i in range(n)])]
    ppermute x5 -> x4, waiting for transfers between devices: 5.66 us -> 5.71 us  [sent_on(): return lax.ppermute(x, 'tensor', [(i, (i + away) % n) for i in range(n)])]
  transfers between devices with their start and end apart: 22 -> 21, of which waited for: 16 -> 15; matrix products, arithmetic and copies ran while one was open for 4% -> 5% of each run, Pallas kernels for 13% -> 14%
where the time goes in v9:
time: 122 us; the launch traced here: 121 us
  starting transfers between devices  58 us (48%)
  Pallas kernels  27.8 us (23%)
  waiting for transfers between devices  25.7 us (21%)
  local copies, waits for them, and re-layouts  4.43 us (4%)
  other arithmetic  4.12 us (3%)
    all_to_all x3, starting transfers between devices, swap(): return lax.all_to_all(blocks, 'dp', split_axis=0, concat_axis=0, tiled=True)  29.6 us
    ppermute x7, starting transfers between devices, pass_on(): left = lax.ppermute(left, 'tensor', [(i, (i - 1) % n) for i in range(n)])  18.7 us
    pallas_call x4, Pallas kernels, products(): pl.pallas_call(products_kernel, grid_spec=pltpu.PrefetchScalarGridSpec(nu...  11.2 us
    ppermute x7, waiting for transfers between devices, pass_on(): right = lax.ppermute(right, 'tensor', [(i, (i + 1) % n) for i in range(n)])  9.48 us
    ppermute x7, waiting for transfers between devices, pass_on(): left = lax.ppermute(left, 'tensor', [(i, (i - 1) % n) for i in range(n)])  6.82 us
    pallas_call x1, Pallas kernels, per_device(): pl.pallas_call(home_kernel, in_specs=[pl.BlockSpec(memory_space=pl.ANY)]...  5.79 us
    ppermute x4, waiting for transfers between devices, sent_on(): return lax.ppermute(x, 'tensor', [(i, (i + away) % n) for i in range(n)])  5.71 us
    pallas_call x1, Pallas kernels, per_device(): pl.pallas_call(band_kernel, in_specs=[pl.BlockSpec(memory_space=pltpu.SME...  5.56 us
  transfers between devices with their start and end apart: 21, of which 15 were waited for; matrix products, arithmetic and copies ran while one was open for 5% of the time, Pallas kernels for 14%

profile of v9, /device:TPU:1, one launch (start us, length us, event | category | flops | bytes accessed | tf_op | source)
XLA Modules:
  0.0 121.3 jit_solution(13251404878391993471)
XLA Ops:
  0.6 5.8 %home_rows.1 = (bf16[32,64,512]{2,1,0:T(8,128)(2,1)}, bf16[128,512]{1,0:T(8,128)(2,1)}, f32[16,16,512]{2,1,0:T(8,128)}) custom-call(bf16[4,3,80,512]{3,2,1,0:T(8,128)(2,1)} %bitcast.114, bf16[80,3,2,512]{3,2,1,0:T(2,128)(2,1)} %fir_hbm.1, f32[80,16,512]{2,1,0:T(8,128)} %state_hbm.1, f32[3,3,512]{2,1,0:T(4,128)} %taps.3, f32[16,512]{1,0:T(8,128)} %poles.3, ...), custom_call_target="tpu_custom_call" | custom-call | tf_op jit(solution)/shard_map/home_rows/pallas_call | solution.py:336
  6.4 8.7 %all-to-all-start = ((bf16[32,64,512]{2,1,0:T(8,128)(2,1)}), bf16[32,64,512]{2,1,0:T(8,128)(2,1)S(1)}, u32[]{:S(2)}, u32[]{:S(2)}) async-start(bf16[32,64,512]{2,1,0:T(8,128)(2,1)} %get-tuple-element.88), calls=%async_computation | async-start | bytes 4194304 | tf_op jit(solution)/shard_map/all_to_all | solution.py:279
  15.2 1.1 constant_dynamic-slice_fusion.far_weight
  16.3 0.2 convolution_convert_fusion
  16.5 5.7 %collective-permute-start.1 = (bf16[64,512]{1,0:T(8,128)(2,1)S(1)}, bf16[64,512]{1,0:T(8,128)(2,1)S(1)}, u32[]{:S(2)}, u32[]{:S(2)}) collective-permute-start(bf16[64,512]{1,0:T(8,128)(2,1)S(1)} %get-tuple-element.143), channel_id=1, source_target_pairs={{0,7},{1,0},{2,1},{3,2},{4,3},{5,4},{6,5},{7,6},{8,15},{9,8},{10,9... | collective-permute-start | bytes 196616 | tf_op jit(solution)/shard_map/ppermute | solution.py:285
  22.2 2.9 %ring_products.4 = f32[4,128,512]{2,1,0:T(8,128)S(1)} custom-call(s32[1]{0:T(128)} %bitcast.2.place, bf16[128,512]{1,0:T(8,128)(2,1)S(1)} %copy-done.3, bf16[512,4096]{1,0:T(8,128)(2,1)} %weight.7), custom_call_target="tpu_custom_call" | custom-call | flops 4294967296 | bytes 4194304 | tf_op jit(solution)/shard_map/ring_products/pallas_call | solution.py:219
  25.1 1.0 copy-done
  26.1 1.1 slice_bitcast_fusion.12
  27.4 1.0 fusion.25
  28.4 2.7 %collective-permute-start.3 = (bf16[128,512]{1,0:T(8,128)(2,1)S(1)}, bf16[128,512]{1,0:T(8,128)(2,1)S(1)}, u32[]{:S(2)}, u32[]{:S(2)}) collective-permute-start(bf16[128,512]{1,0:T(8,128)(2,1)S(1)} %get-tuple-element.137), channel_id=1, source_target_pairs={{0,7},{1,0},{2,1},{3,2},{4,3},{5,4},{6,5},{7,6},{8,15},{9,8},{10,9... | collective-permute-start | bytes 393224 | tf_op jit(solution)/shard_map/ppermute | solution.py:285
  31.2 1.9 %collective-permute-done.3 = bf16[128,512]{1,0:T(8,128)(2,1)S(1)} collective-permute-done((bf16[128,512]{1,0:T(8,128)(2,1)S(1)}, bf16[128,512]{1,0:T(8,128)(2,1)S(1)}, u32[]{:S(2)}, u32[]{:S(2)}) %collective-permute-start.3) | collective-permute-done | bytes 131104 | tf_op jit(solution)/shard_map/ppermute | solution.py:285
  33.1 3.4 %collective-permute-done.2 = bf16[128,512]{1,0:T(8,128)(2,1)S(1)} collective-permute-done((bf16[128,512]{1,0:T(8,128)(2,1)S(1)}, bf16[128,512]{1,0:T(8,128)(2,1)S(1)}, u32[]{:S(2)}, u32[]{:S(2)}) %collective-permute-start.2) | collective-permute-done | bytes 131104 | tf_op jit(solution)/shard_map/ppermute | solution.py:284
  36.5 1.1 fusion.13
  37.6 0.2 collective-permute-start.5
  37.8 1.4 %collective-permute-start.4 = (bf16[128,512]{1,0:T(8,128)(2,1)S(1)}, bf16[128,512]{1,0:T(8,128)(2,1)S(1)}, u32[]{:S(2)}, u32[]{:S(2)}) collective-permute-start(bf16[128,512]{1,0:T(8,128)(2,1)S(1)} %get-tuple-element.136), channel_id=1, source_target_pairs={{0,1},{1,2},{2,3},{3,4},{4,5},{5,6},{6,7},{7,0},{8,9},{9,10},{10,1... | collective-permute-start | bytes 393224 | tf_op jit(solution)/shard_map/ppermute | solution.py:284
  39.1 2.6 %ring_products.5 = f32[3,128,512]{2,1,0:T(8,128)S(1)} custom-call(s32[1]{0:T(128)} %bitcast.2.place, bf16[128,512]{1,0:T(8,128)(2,1)S(1)} %copy-done.3, bf16[512,4096]{1,0:T(8,128)(2,1)} %weight.7), custom_call_target="tpu_custom_call" | custom-call | flops 4294967296 | bytes 4194304 | tf_op jit(solution)/shard_map/ring_products/pallas_call | solution.py:219
  41.8 1.0 collective-permute-done.4
  43.0 5.6 %band_rows.1 = (bf16[32,48,512]{2,1,0:T(8,128)(2,1)}, bf16[192,512]{1,0:T(8,128)(2,1)S(1)}, bf16[224,512]{1,0:T(8,128)(2,1)S(1)}, bf16[224,512]{1,0:T(8,128)(2,1)S(1)}) custom-call(s32[3]{0:T(128)S(1)} %and_select_fusion.turns, bf16[32,64,512]{2,1,0:T(8,128)(2,1)S(1)} %all-to-all-done.got, f32[3,3,512]{2,1,0:T(4,128)S(1)} %copy-done.4, ...), custom_call_target="tpu_custom_call" | custom-call | tf_op jit(solution)/shard_map/band_rows/pallas_call | solution.py:377
  48.6 1.6 %collective-permute-start.6 = (bf16[224,512]{1,0:T(8,128)(2,1)S(1)}, bf16[224,512]{1,0:T(8,128)(2,1)S(1)}, u32[]{:S(2)}, u32[]{:S(2)}) collective-permute-start(bf16[224,512]{1,0:T(8,128)(2,1)S(1)} %get-tuple-element.102), channel_id=1, source_target_pairs={{0,1},{1,2},{2,3},{3,4},{4,5},{5,6},{6,7},{7,0},{8,9},{9,10},{10,1... | collective-permute-start | bytes 688136 | tf_op jit(solution)/shard_map/ppermute | solution.py:284
  50.2 3.9 %collective-permute-start.7 = (bf16[224,512]{1,0:T(8,128)(2,1)S(1)}, bf16[224,512]{1,0:T(8,128)(2,1)S(1)}, u32[]{:S(2)}, u32[]{:S(2)}) collective-permute-start(bf16[224,512]{1,0:T(8,128)(2,1)S(1)} %get-tuple-element.103), channel_id=1, source_target_pairs={{0,7},{1,0},{2,1},{3,2},{4,3},{5,4},{6,5},{7,6},{8,15},{9,8},{10,9... | collective-permute-start | bytes 688136 | tf_op jit(solution)/shard_map/ppermute | solution.py:285
  54.2 3.0 %ring_products.6 = f32[4,192,512]{2,1,0:T(8,128)S(1)} custom-call(s32[1]{0:T(128)} %bitcast.2.place, bf16[192,512]{1,0:T(8,128)(2,1)S(1)} %get-tuple-element.109.gated, bf16[512,4096]{1,0:T(8,128)(2,1)} %weight.7), custom_call_target="tpu_custom_call" | custom-call | flops 6442450944 | bytes 4194304 | tf_op jit(solution)/shard_map/ring_products/pallas_call | solution.py:219
  57.3 0.3 collective-permute-done.6
  57.6 2.7 %collective-permute-start.9 = (bf16[192,512]{1,0:T(8,128)(2,1)S(1)}, bf16[192,512]{1,0:T(8,128)(2,1)S(1)}, u32[]{:S(2)}, u32[]{:S(2)}) collective-permute-start(bf16[192,512]{1,0:T(8,128)(2,1)S(1)} %get-tuple-element.129), channel_id=1, source_target_pairs={{0,7},{1,0},{2,1},{3,2},{4,3},{5,4},{6,5},{7,6},{8,15},{9,8},{10,9... | collective-permute-start | bytes 589832 | tf_op jit(solution)/shard_map/ppermute | solution.py:285
  60.4 9.1 %all-to-all-start.1 = ((bf16[32,48,512]{2,1,0:T(8,128)(2,1)}), bf16[32,48,512]{2,1,0:T(8,128)(2,1)}, u32[]{:S(2)}, u32[]{:S(2)}) async-start(bf16[32,48,512]{2,1,0:T(8,128)(2,1)} %get-tuple-element.116), calls=%async_computation.1 | async-start | bytes 3145728 | tf_op jit(solution)/shard_map/all_to_all | solution.py:279
  69.7 3.0 %collective-permute-start.11 = (bf16[192,512]{1,0:T(8,128)(2,1)S(1)}, bf16[192,512]{1,0:T(8,128)(2,1)S(1)}, u32[]{:S(2)}, u32[]{:S(2)}) collective-permute-start(bf16[192,512]{1,0:T(8,128)(2,1)S(1)} %get-tuple-element.127), channel_id=1, source_target_pairs={{0,7},{1,0},{2,1},{3,2},{4,3},{5,4},{6,5},{7,6},{8,15},{9,8},{10,9... | collective-permute-start | bytes 589832 | tf_op jit(solution)/shard_map/ppermute | solution.py:285
  72.7 2.7 %ring_products.7 = f32[3,192,512]{2,1,0:T(8,128)S(1)} custom-call(s32[1]{0:T(128)} %bitcast.2.place, bf16[192,512]{1,0:T(8,128)(2,1)S(1)} %get-tuple-element.109.gated, bf16[512,4096]{1,0:T(8,128)(2,1)} %weight.7), custom_call_target="tpu_custom_call" | custom-call | flops 6442450944 | bytes 4194304 | tf_op jit(solution)/shard_map/ring_products/pallas_call | solution.py:219
  75.4 1.3 %collective-permute-done.11 = bf16[192,512]{1,0:T(8,128)(2,1)S(1)} collective-permute-done((bf16[192,512]{1,0:T(8,128)(2,1)S(1)}, bf16[192,512]{1,0:T(8,128)(2,1)S(1)}, u32[]{:S(2)}, u32[]{:S(2)}) %collective-permute-start.11) | collective-permute-done | bytes 196640 | tf_op jit(solution)/shard_map/ppermute | solution.py:285
  76.7 3.2 %collective-permute-done.10 = bf16[192,512]{1,0:T(8,128)(2,1)S(1)} collective-permute-done((bf16[192,512]{1,0:T(8,128)(2,1)S(1)}, bf16[192,512]{1,0:T(8,128)(2,1)S(1)}, u32[]{:S(2)}, u32[]{:S(2)}) %collective-permute-start.10) | collective-permute-done | bytes 196640 | tf_op jit(solution)/shard_map/ppermute | solution.py:284
  80.0 0.4 collective-permute-start.13
  80.4 1.1 collective-permute-start.12
  81.7 3.6 %collective-permute-done.13 = bf16[192,512]{1,0:T(8,128)(2,1)S(1)} collective-permute-done((bf16[192,512]{1,0:T(8,128)(2,1)S(1)}, bf16[192,512]{1,0:T(8,128)(2,1)S(1)}, u32[]{:S(2)}, u32[]{:S(2)}) %collective-permute-start.13) | collective-permute-done | bytes 196640 | tf_op jit(solution)/shard_map/ppermute | solution.py:285
  85.3 1.6 %collective-permute-done.12 = bf16[192,512]{1,0:T(8,128)(2,1)S(1)} collective-permute-done((bf16[192,512]{1,0:T(8,128)(2,1)S(1)}, bf16[192,512]{1,0:T(8,128)(2,1)S(1)}, u32[]{:S(2)}, u32[]{:S(2)}) %collective-permute-start.12) | collective-permute-done | bytes 196640 | tf_op jit(solution)/shard_map/ppermute | solution.py:284
  86.8 0.2 multiply_reduce_fusion
  87.1 0.3 collective-permute-start.15
  87.4 1.2 collective-permute-start.14
  88.5 1.0 collective-permute-done.15
  89.5 1.5 %collective-permute-done.14 = f32[320]{0:T(512)S(1)} collective-permute-done((f32[320]{0:T(512)S(1)}, f32[320]{0:T(512)S(1)}, u32[]{:S(2)}, u32[]{:S(2)}) %collective-permute-start.14) | collective-permute-done | bytes 1312 | tf_op jit(solution)/shard_map/ppermute | solution.py:305
  91.1 0.7 all-to-all-done.1.back
  91.8 1.9 %collective-permute-start.17 = (f32[320]{0:T(512)S(1)}, f32[320]{0:T(512)S(1)}, u32[]{:S(2)}, u32[]{:S(2)}) collective-permute-start(f32[320]{0:T(512)S(1)} %get-tuple-element.118), channel_id=1, source_target_pairs={{0,5},{1,6},{2,7},{3,0},{4,1},{5,2},{6,3},{7,4},{8,13},{9,14},{10,... | collective-permute-start | bytes 3848 | tf_op jit(solution)/shard_map/ppermute | solution.py:305
  93.6 2.2 %collective-permute-start.16 = (f32[320]{0:T(512)S(1)}, f32[320]{0:T(512)S(1)}, u32[]{:S(2)}, u32[]{:S(2)}) collective-permute-start(f32[320]{0:T(512)S(1)} %get-tuple-element.117), channel_id=1, source_target_pairs={{0,3},{1,4},{2,5},{3,6},{4,7},{5,0},{6,1},{7,2},{8,11},{9,12},{10,... | collective-permute-start | bytes 3848 | tf_op jit(solution)/shard_map/ppermute | solution.py:305
  95.8 1.0 collective-permute-done.17
  96.8 2.3 %collective-permute-done.16 = f32[320]{0:T(512)S(1)} collective-permute-done((f32[320]{0:T(512)S(1)}, f32[320]{0:T(512)S(1)}, u32[]{:S(2)}, u32[]{:S(2)}) %collective-permute-start.16) | collective-permute-done | bytes 1312 | tf_op jit(solution)/shard_map/ppermute | solution.py:305
  99.4 0.8 copy.18
  100.3 11.8 %all-to-all-start.2 = ((bf16[32,3,2,512]{3,2,1,0:T(2,128)(2,1)}), bf16[32,3,2,512]{3,2,1,0:T(2,128)(2,1)S(1)}, u32[]{:S(2)}, u32[]{:S(2)}) async-start(bf16[32,3,2,512]{3,2,1,0:T(2,128)(2,1)} %bitcast.111), calls=%async_computation.2 | async-start | bytes 393216 | tf_op jit(solution)/shard_map/all_to_all | solution.py:279
  112.0 5.3 %last_rows.1 = (f32[80,16,512]{2,1,0:T(8,128)}, bf16[80,3,2,512]{3,2,1,0:T(2,128)(2,1)}) custom-call(bf16[32,48,512]{2,1,0:T(8,128)(2,1)} %all-to-all-done.1.back, bf16[4,3,80,512]{3,2,1,0:T(8,128)(2,1)} %bitcast.115, f32[16,16,512]{2,1,0:T(8,128)} %get-tuple-element.122.stay_state, s32[3,80]{1,0:T(4,128)} %finished.3), custom_call_target="tpu_custom_call" | custom-call | tf_op jit(solution)/shard_map/last_rows/pallas_call | solution.py:422
  117.4 2.9 %all-to-all-done.2 = bf16[32,3,2,512]{3,2,1,0:T(2,128)(2,1)S(1)} async-done(((bf16[32,3,2,512]{3,2,1,0:T(2,128)(2,1)}), bf16[32,3,2,512]{3,2,1,0:T(2,128)(2,1)S(1)}, u32[]{:S(2)}, u32[]{:S(2)}) %all-to-all-start.2) | async-done | bytes 196640 | tf_op jit(solution)/shard_map/all_to_all | solution.py:279
  120.3 0.1 copy.16
  120.5 0.8 maximum_maximum_fusion
  (50 shorter events, 1.6 us)
Async XLA Ops:
  6.4 9.9 %copy-start.3 = (bf16[128,512]{1,0:T(8,128)(2,1)S(1)}, bf16[128,512]{1,0:T(8,128)(2,1)}, u32[]{:S(2)}) copy-start(bf16[128,512]{1,0:T(8,128)(2,1)} %get-tuple-element.94.gated) | copy-start | bytes 393220
  6.4 36.6 %all-to-all-start = ((bf16[32,64,512]{2,1,0:T(8,128)(2,1)}), bf16[32,64,512]{2,1,0:T(8,128)(2,1)S(1)}, u32[]{:S(2)}, u32[]{:S(2)}) async-start(bf16[32,64,512]{2,1,0:T(8,128)(2,1)} %get-tuple-element.88), calls=%async_computation | async-start | bytes 4194304 | tf_op jit(solution)/shard_map/all_to_all | solution.py:279
  16.5 10.9 %collective-permute-start.1 = (bf16[64,512]{1,0:T(8,128)(2,1)S(1)}, bf16[64,512]{1,0:T(8,128)(2,1)S(1)}, u32[]{:S(2)}, u32[]{:S(2)}) collective-permute-start(bf16[64,512]{1,0:T(8,128)(2,1)S(1)} %get-tuple-element.143), channel_id=1, source_target_pairs={{0,7},{1,0},{2,1},{3,2},{4,3},{5,4},{6,5},{7,6},{8,15},{9,8},{10,9... | collective-permute-start | bytes 196616 | tf_op jit(solution)/shard_map/ppermute | solution.py:285
  22.2 5.2 %collective-permute-start = (bf16[64,512]{1,0:T(8,128)(2,1)S(1)}, bf16[64,512]{1,0:T(8,128)(2,1)S(1)}, u32[]{:S(2)}, u32[]{:S(2)}) collective-permute-start(bf16[64,512]{1,0:T(8,128)(2,1)S(1)} %get-tuple-element.144), channel_id=1, source_target_pairs={{0,1},{1,2},{2,3},{3,4},{4,5},{5,6},{6,7},{7,0},{8,9},{9,10},{10,1... | collective-permute-start | bytes 196616 | tf_op jit(solution)/shard_map/ppermute | solution.py:284
  22.2 5.0 %copy-start.7 = (s32[3,80]{1,0:T(4,128)S(1)}, s32[3,80]{1,0:T(4,128)}, u32[]{:S(2)}) copy-start(s32[3,80]{1,0:T(4,128)} %param.29) | copy-start | bytes 2884
  25.1 1.0 copy-start
  28.4 4.7 %collective-permute-start.3 = (bf16[128,512]{1,0:T(8,128)(2,1)S(1)}, bf16[128,512]{1,0:T(8,128)(2,1)S(1)}, u32[]{:S(2)}, u32[]{:S(2)}) collective-permute-start(bf16[128,512]{1,0:T(8,128)(2,1)S(1)} %get-tuple-element.137), channel_id=1, source_target_pairs={{0,7},{1,0},{2,1},{3,2},{4,3},{5,4},{6,5},{7,6},{8,15},{9,8},{10,9... | collective-permute-start | bytes 393224 | tf_op jit(solution)/shard_map/ppermute | solution.py:285
  31.2 5.3 %collective-permute-start.2 = (bf16[128,512]{1,0:T(8,128)(2,1)S(1)}, bf16[128,512]{1,0:T(8,128)(2,1)S(1)}, u32[]{:S(2)}, u32[]{:S(2)}) collective-permute-start(bf16[128,512]{1,0:T(8,128)(2,1)S(1)} %get-tuple-element.138), channel_id=1, source_target_pairs={{0,1},{1,2},{2,3},{3,4},{4,5},{5,6},{6,7},{7,0},{8,9},{9,10},{10,1... | collective-permute-start | bytes 393224 | tf_op jit(solution)/shard_map/ppermute | solution.py:284
  37.6 4.2 %collective-permute-start.5 = (bf16[128,512]{1,0:T(8,128)(2,1)S(1)}, bf16[128,512]{1,0:T(8,128)(2,1)S(1)}, u32[]{:S(2)}, u32[]{:S(2)}) collective-permute-start(bf16[128,512]{1,0:T(8,128)(2,1)S(1)} %get-tuple-element.135), channel_id=1, source_target_pairs={{0,7},{1,0},{2,1},{3,2},{4,3},{5,4},{6,5},{7,6},{8,15},{9,8},{10,9... | collective-permute-start | bytes 393224 | tf_op jit(solution)/shard_map/ppermute | solution.py:285
  37.8 5.0 %collective-permute-start.4 = (bf16[128,512]{1,0:T(8,128)(2,1)S(1)}, bf16[128,512]{1,0:T(8,128)(2,1)S(1)}, u32[]{:S(2)}, u32[]{:S(2)}) collective-permute-start(bf16[128,512]{1,0:T(8,128)(2,1)S(1)} %get-tuple-element.136), channel_id=1, source_target_pairs={{0,1},{1,2},{2,3},{3,4},{4,5},{5,6},{6,7},{7,0},{8,9},{9,10},{10,1... | collective-permute-start | bytes 393224 | tf_op jit(solution)/shard_map/ppermute | solution.py:284
  41.7 1.3 %copy-start.1 = (f32[16,512]{1,0:T(8,128)S(1)}, f32[16,512]{1,0:T(8,128)}, u32[]{:S(2)}) copy-start(f32[16,512]{1,0:T(8,128)} %poles.3) | copy-start | bytes 98308
  41.7 1.3 %copy-start.2 = (f32[16,512]{1,0:T(8,128)S(1)}, f32[16,512]{1,0:T(8,128)}, u32[]{:S(2)}) copy-start(f32[16,512]{1,0:T(8,128)} %residues.3) | copy-start | bytes 98308
  41.8 1.3 %copy-start.4 = (f32[3,3,512]{2,1,0:T(4,128)S(1)}, f32[3,3,512]{2,1,0:T(4,128)}, u32[]{:S(2)}) copy-start(f32[3,3,512]{2,1,0:T(4,128)} %taps.3) | copy-start | bytes 55300
  41.8 1.3 %copy-start.5 = (f32[512]{0:T(512)S(1)}, f32[512]{0:T(512)}, u32[]{:S(2)}) copy-start(f32[512]{0:T(512)} %param.25) | copy-start | bytes 6148
  48.6 9.0 %collective-permute-start.6 = (bf16[224,512]{1,0:T(8,128)(2,1)S(1)}, bf16[224,512]{1,0:T(8,128)(2,1)S(1)}, u32[]{:S(2)}, u32[]{:S(2)}) collective-permute-start(bf16[224,512]{1,0:T(8,128)(2,1)S(1)} %get-tuple-element.102), channel_id=1, source_target_pairs={{0,1},{1,2},{2,3},{3,4},{4,5},{5,6},{6,7},{7,0},{8,9},{9,10},{10,1... | collective-permute-start | bytes 688136 | tf_op jit(solution)/shard_map/ppermute | solution.py:284
  50.2 7.3 %collective-permute-start.7 = (bf16[224,512]{1,0:T(8,128)(2,1)S(1)}, bf16[224,512]{1,0:T(8,128)(2,1)S(1)}, u32[]{:S(2)}, u32[]{:S(2)}) collective-permute-start(bf16[224,512]{1,0:T(8,128)(2,1)S(1)} %get-tuple-element.103), channel_id=1, source_target_pairs={{0,7},{1,0},{2,1},{3,2},{4,3},{5,4},{6,5},{7,6},{8,15},{9,8},{10,9... | collective-permute-start | bytes 688136 | tf_op jit(solution)/shard_map/ppermute | solution.py:285
  57.6 11.9 %collective-permute-start.9 = (bf16[192,512]{1,0:T(8,128)(2,1)S(1)}, bf16[192,512]{1,0:T(8,128)(2,1)S(1)}, u32[]{:S(2)}, u32[]{:S(2)}) collective-permute-start(bf16[192,512]{1,0:T(8,128)(2,1)S(1)} %get-tuple-element.129), channel_id=1, source_target_pairs={{0,7},{1,0},{2,1},{3,2},{4,3},{5,4},{6,5},{7,6},{8,15},{9,8},{10,9... | collective-permute-start | bytes 589832 | tf_op jit(solution)/shard_map/ppermute | solution.py:285
  60.4 9.1 %collective-permute-start.8 = (bf16[192,512]{1,0:T(8,128)(2,1)S(1)}, bf16[192,512]{1,0:T(8,128)(2,1)S(1)}, u32[]{:S(2)}, u32[]{:S(2)}) collective-permute-start(bf16[192,512]{1,0:T(8,128)(2,1)S(1)} %get-tuple-element.130), channel_id=1, source_target_pairs={{0,1},{1,2},{2,3},{3,4},{4,5},{5,6},{6,7},{7,0},{8,9},{9,10},{10,1... | collective-permute-start | bytes 589832 | tf_op jit(solution)/shard_map/ppermute | solution.py:284
  60.4 31.4 %all-to-all-start.1 = ((bf16[32,48,512]{2,1,0:T(8,128)(2,1)}), bf16[32,48,512]{2,1,0:T(8,128)(2,1)}, u32[]{:S(2)}, u32[]{:S(2)}) async-start(bf16[32,48,512]{2,1,0:T(8,128)(2,1)} %get-tuple-element.116), calls=%async_computation.1 | async-start | bytes 3145728 | tf_op jit(solution)/shard_map/all_to_all | solution.py:279
  69.7 7.0 %collective-permute-start.11 = (bf16[192,512]{1,0:T(8,128)(2,1)S(1)}, bf16[192,512]{1,0:T(8,128)(2,1)S(1)}, u32[]{:S(2)}, u32[]{:S(2)}) collective-permute-start(bf16[192,512]{1,0:T(8,128)(2,1)S(1)} %get-tuple-element.127), channel_id=1, source_target_pairs={{0,7},{1,0},{2,1},{3,2},{4,3},{5,4},{6,5},{7,6},{8,15},{9,8},{10,9... | collective-permute-start | bytes 589832 | tf_op jit(solution)/shard_map/ppermute | solution.py:285
  72.7 7.2 %collective-permute-start.10 = (bf16[192,512]{1,0:T(8,128)(2,1)S(1)}, bf16[192,512]{1,0:T(8,128)(2,1)S(1)}, u32[]{:S(2)}, u32[]{:S(2)}) collective-permute-start(bf16[192,512]{1,0:T(8,128)(2,1)S(1)} %get-tuple-element.128), channel_id=1, source_target_pairs={{0,1},{1,2},{2,3},{3,4},{4,5},{5,6},{6,7},{7,0},{8,9},{9,10},{10,1... | collective-permute-start | bytes 589832 | tf_op jit(solution)/shard_map/ppermute | solution.py:284
  75.4 23.8 %copy-start.6 = (f32[512]{0:T(512)S(1)}, f32[512]{0:T(512)}, u32[]{:S(2)}) copy-start(f32[512]{0:T(512)} %param.27) | copy-start | bytes 6148
  80.0 5.2 %collective-permute-start.13 = (bf16[192,512]{1,0:T(8,128)(2,1)S(1)}, bf16[192,512]{1,0:T(8,128)(2,1)S(1)}, u32[]{:S(2)}, u32[]{:S(2)}) collective-permute-start(bf16[192,512]{1,0:T(8,128)(2,1)S(1)} %get-tuple-element.133), channel_id=1, source_target_pairs={{0,7},{1,0},{2,1},{3,2},{4,3},{5,4},{6,5},{7,6},{8,15},{9,8},{10,9... | collective-permute-start | bytes 589832 | tf_op jit(solution)/shard_map/ppermute | solution.py:285
  80.4 6.4 %collective-permute-start.12 = (bf16[192,512]{1,0:T(8,128)(2,1)S(1)}, bf16[192,512]{1,0:T(8,128)(2,1)S(1)}, u32[]{:S(2)}, u32[]{:S(2)}) collective-permute-start(bf16[192,512]{1,0:T(8,128)(2,1)S(1)} %get-tuple-element.134), channel_id=1, source_target_pairs={{0,1},{1,2},{2,3},{3,4},{4,5},{5,6},{6,7},{7,0},{8,9},{9,10},{10,1... | collective-permute-start | bytes 589832 | tf_op jit(solution)/shard_map/ppermute | solution.py:284
  87.1 2.4 %collective-permute-start.15 = (f32[320]{0:T(512)S(1)}, f32[320]{0:T(512)S(1)}, u32[]{:S(2)}, u32[]{:S(2)}) collective-permute-start(f32[320]{0:T(512)S(1)} %pad_maximum_fusion.1), channel_id=1, source_target_pairs={{0,7},{1,0},{2,1},{3,2},{4,3},{5,4},{6,5},{7,6},{8,15},{9,8},{10,9... | collective-permute-start | bytes 3848 | tf_op jit(solution)/shard_map/ppermute | solution.py:305
  87.4 3.6 %collective-permute-start.14 = (f32[320]{0:T(512)S(1)}, f32[320]{0:T(512)S(1)}, u32[]{:S(2)}, u32[]{:S(2)}) collective-permute-start(f32[320]{0:T(512)S(1)} %pad_maximum_fusion.1), channel_id=1, source_target_pairs={{0,1},{1,2},{2,3},{3,4},{4,5},{5,6},{6,7},{7,0},{8,9},{9,10},{10,1... | collective-permute-start | bytes 3848 | tf_op jit(solution)/shard_map/ppermute | solution.py:305
  91.8 5.0 %collective-permute-start.17 = (f32[320]{0:T(512)S(1)}, f32[320]{0:T(512)S(1)}, u32[]{:S(2)}, u32[]{:S(2)}) collective-permute-start(f32[320]{0:T(512)S(1)} %get-tuple-element.118), channel_id=1, source_target_pairs={{0,5},{1,6},{2,7},{3,0},{4,1},{5,2},{6,3},{7,4},{8,13},{9,14},{10,... | collective-permute-start | bytes 3848 | tf_op jit(solution)/shard_map/ppermute | solution.py:305
  93.6 5.4 %collective-permute-start.16 = (f32[320]{0:T(512)S(1)}, f32[320]{0:T(512)S(1)}, u32[]{:S(2)}, u32[]{:S(2)}) collective-permute-start(f32[320]{0:T(512)S(1)} %get-tuple-element.117), channel_id=1, source_target_pairs={{0,3},{1,4},{2,5},{3,6},{4,7},{5,0},{6,1},{7,2},{8,11},{9,12},{10,... | collective-permute-start | bytes 3848 | tf_op jit(solution)/shard_map/ppermute | solution.py:305
  100.3 20.0 %all-to-all-start.2 = ((bf16[32,3,2,512]{3,2,1,0:T(2,128)(2,1)}), bf16[32,3,2,512]{3,2,1,0:T(2,128)(2,1)S(1)}, u32[]{:S(2)}, u32[]{:S(2)}) async-start(bf16[32,3,2,512]{3,2,1,0:T(2,128)(2,1)} %bitcast.111), calls=%async_computation.2 | async-start | bytes 393216 | tf_op jit(solution)/shard_map/all_to_all | solution.py:279

commit v10 on v9

--- a/solution.py
+++ b/solution.py
@@ -17,6 +17,16 @@
 
 def wide(x, width):
     return jnp.concatenate([x] * (width // x.shape[-1]), axis=-1)
+
+
+def going_on(finished, block, rows, width):
+    at = lax.broadcasted_iota(jnp.int32, (rows, finished.shape[1]), 0) + block * rows
+    own = at == lax.broadcasted_iota(jnp.int32, at.shape, 1)
+    ended = [
+        jnp.sum(jnp.where(own, finished[t : t + 1].astype(F32), 0.0), axis=1, keepdims=True)
+        for t in range(3)
+    ]
+    return [jnp.broadcast_to(1.0 - x, (rows, width)) for x in ended]
 
 
 def home_kernel(qkv_hbm, fir_hbm, state_hbm, taps, poles, residues, skip, finished, packed_hbm, *rest):
@@ -47,15 +57,7 @@
         qkv = qkv_all.at[:, :, pl.ds(start, rows)]
         fir = fir_all.at[pl.ds(start, rows)]
         state = state_all.at[pl.ds(start, rows)]
-        at = lax.broadcasted_iota(jnp.int32, (rows, finished.shape[1]), 0) + block * rows
-        own = at == lax.broadcasted_iota(jnp.int32, at.shape, 1)
-        alive = [
-            jnp.broadcast_to(
-                1.0 - jnp.sum(jnp.where(own, finished[t : t + 1].astype(F32), 0.0), axis=1, keepdims=True),
-                (rows, width),
-            )
-            for t in range(3)
-        ]
+        alive = going_on(finished, block, rows, width)
         alive0 = alive[0]
         q0 = [qkv[0, j].astype(F32) for j in range(3)]
         l0 = [fir[:, j].astype(F32)[:, 0] for j in range(3)]
@@ -95,30 +97,35 @@
         packed[:, 2 * MODES :] = moved.astype(BF16)
         store(block).start()
 
-    qkv, q0, l0, alive, modes = first_step(blocks - 1)
-    alive0 = alive[0]
+    modes = first_step(blocks - 1)[-1]
     for r in range(rows):
         stay_state[r] = modes[r]
-    lag0, lag1 = [x * alive0 for x in q0], [x * alive0 for x in l0]
+    for block in range(blocks - 1):
+        store(block).wait()
+
+
+def stay_kernel(gated, qkv, fir, state, taps, poles, residues, skip, finished, all_gated, stay_state, y_rows):
+    rows, width = 16, qkv.shape[-1]
+    first = gated.shape[0]
+    all_gated[:first] = gated[...]
+    alive = going_on(finished, first // rows - 1, rows, width)
+    lag0 = [qkv[0, j].astype(F32) * alive[0] for j in range(3)]
+    lag1 = [fir[:, j].astype(F32)[:, 0] * alive[0] for j in range(3)]
     for t in range(1, 4):
         q = [qkv[t, j].astype(F32) for j in range(3)]
-        g = [
+        f = [
             taps[j, 0:1] * q[j] + taps[j, 1:2] * lag0[j] + taps[j, 2:3] * lag1[j]
             for j in range(3)
         ]
-        prod = g[1] * g[2]
-        live = alive[t] if t < 3 else None
+        product = f[1] * f[2]
         for r in range(rows):
-            s = poles[...] * stay_state[r] + prod[r : r + 1]
+            s = poles[...] * (state if t == 1 else stay_state)[r] + product[r : r + 1]
             y_rows[r : r + 1] = jnp.sum(residues[...] * s, axis=0, keepdims=True)
-            stay_state[r] = s * live[r : r + 1] if t < 3 else s
-        gated[64 + t * rows : 80 + t * rows] = (
-            g[0] * (y_rows[...] + skip[...] * prod)
-        ).astype(BF16)
+            stay_state[r] = s * alive[t][r : r + 1] if t < 3 else s
+        at = first + (t - 1) * rows
+        all_gated[at : at + rows] = (f[0] * (y_rows[...] + skip[...] * product)).astype(BF16)
         if t < 3:
-            lag0, lag1 = [x * live for x in q], [x * live for x in lag0]
-    for block in range(blocks - 1):
-        store(block).wait()
+            lag0, lag1 = [x * alive[t] for x in q], [x * alive[t] for x in lag0]
 
 
 def band_kernel(
@@ -304,10 +311,9 @@
     def sent_on(x, away):
         return lax.ppermute(x, "tensor", [(i, (i + away) % n) for i in range(n)])
 
-    below = squares + sent_on(squares, 1)
-    three = below + sent_on(squares, -1)
-    three, below, back = lax.optimization_barrier((three, below, back))
-    squares = three + (sent_on(three, 3) + sent_on(below, -3))
+    four = squares + (sent_on(squares, 1) + sent_on(squares, -1)) + sent_on(squares, 2)
+    four, back = lax.optimization_barrier((four, back))
+    squares = sent_on(four, 2) + sent_on(four, -2)
     return lax.rsqrt(squares / (n * own[0].shape[1]) + 1e-05)[:, None], back
 
 
@@ -333,7 +339,7 @@
     shifts = lax.dynamic_slice_in_dim(dest_group, own_group * CAP, 1, 1)[:, 0] - own_group + groups
     turns = jnp.cumsum(shifts).astype(jnp.int32) % groups
 
-    packed, gated_home, stay_state = pl.pallas_call(
+    packed, gated_first, stay_first = pl.pallas_call(
         home_kernel,
         in_specs=[pl.BlockSpec(memory_space=pl.ANY)] * 3
         + [pl.BlockSpec(memory_space=pltpu.VMEM)] * 5,
@@ -341,7 +347,7 @@
         + [pl.BlockSpec(memory_space=pltpu.VMEM)] * 2,
         out_shape=[
             jax.ShapeDtypeStruct((groups, 2 * MODES + 2 * KINDS, width), BF16),
-            jax.ShapeDtypeStruct((slots + 48, width), BF16),
+            jax.ShapeDtypeStruct((slots, width), BF16),
             jax.ShapeDtypeStruct((16, MODES, width), F32),
         ],
         scratch_shapes=[
@@ -357,6 +363,31 @@
     )(qkv_kinds, fir_buffer, modal_state, fir_taps, poles, residues, skip_row, finished)
 
     n, own_cols = lax.axis_size("tensor"), norm_gain.shape[0]
+    last = slots // 16 - 1
+    gated_home, stay_state = pl.pallas_call(
+        stay_kernel,
+        grid=(1,),
+        in_specs=[
+            whole((slots, width)),
+            pl.BlockSpec((4, 3, 16, width), lambda i: (0, 0, last, 0)),
+            pl.BlockSpec((16, 3, 2, width), lambda i: (last, 0, 0, 0)),
+            whole((16, MODES, width)),
+            whole((3, 3, width)),
+            whole((MODES, width)),
+            whole((MODES, width)),
+            whole((1, width)),
+            whole((3, slots)),
+        ],
+        out_specs=[whole((slots + 48, width)), whole((16, MODES, width))],
+        out_shape=[
+            jax.ShapeDtypeStruct((slots + 48, width), BF16),
+            jax.ShapeDtypeStruct((16, MODES, width), F32),
+        ],
+        scratch_shapes=[pltpu.VMEM((16, width), F32)],
+        compiler_params=pltpu.CompilerParams(vmem_limit_bytes=56 * 1024 * 1024),
+        name="stay_rows",
+    )(gated_first, qkv_kinds, fir_buffer, stay_first, fir_taps, poles, residues, skip_row, finished)
+
     gated_home, later_weight = lax.optimization_barrier((gated_home, out_weight))
     place = lax.axis_index("tensor").astype(jnp.int32)[None]
     far_place = (place[0] + n // 2) % n

time: 122 us -> 125 us (1.025)
  Pallas kernels: 27.8 us -> 30.4 us
    all_to_all x3, starting transfers between devices: 29.6 us -> 32.4 us  [swap(): return lax.all_to_all(blocks, 'dp', split_axis=0, concat_axis=0, tiled=True)]
    pallas_call x0 -> x1, Pallas kernels: none -> 2.66 us  [per_device(): pl.pallas_call(stay_kernel, grid=(1,), in_specs=[whole((slots, width)), p...]
    ppermute x7, starting transfers between devices: 18.7 us -> 17.2 us  [pass_on(): left = lax.ppermute(left, 'tensor', [(i, (i - 1) % n) for i in range(n)])]
    ppermute x7, starting transfers between devices: 4.15 us -> 2.74 us  [pass_on(): right = lax.ppermute(right, 'tensor', [(i, (i + 1) % n) for i in range(n)])]
    ppermute x4 -> x5, starting transfers between devices: 5.52 us -> 4.43 us  [sent_on(): return lax.ppermute(x, 'tensor', [(i, (i + away) % n) for i in range(n)])]
    ppermute x4 -> x5, waiting for transfers between devices: 5.71 us -> 6.55 us  [sent_on(): return lax.ppermute(x, 'tensor', [(i, (i + away) % n) for i in range(n)])]
  transfers between devices with their start and end apart: 21 -> 22, of which waited for: 15 -> 13; matrix products, arithmetic and copies ran while one was open for 5% -> 5% of each run, Pallas kernels for 14% -> 15%
where the time goes in v10:
time: 125 us; the launch traced here: 124 us
  starting transfers between devices  56.8 us (45%)
  Pallas kernels  30.4 us (24%)
  waiting for transfers between devices  25.8 us (21%)
  local copies, waits for them, and re-layouts  4.47 us (4%)
  other arithmetic  4.12 us (3%)
    all_to_all x3, starting transfers between devices, swap(): return lax.all_to_all(blocks, 'dp', split_axis=0, concat_axis=0, tiled=True)  32.4 us
    ppermute x7, starting transfers between devices, pass_on(): left = lax.ppermute(left, 'tensor', [(i, (i - 1) % n) for i in range(n)])  17.2 us
    pallas_call x4, Pallas kernels, products(): pl.pallas_call(products_kernel, grid_spec=pltpu.PrefetchScalarGridSpec(nu...  11.2 us
    ppermute x7, waiting for transfers between devices, pass_on(): right = lax.ppermute(right, 'tensor', [(i, (i + 1) % n) for i in range(n)])  9.48 us
    ppermute x7, waiting for transfers between devices, pass_on(): left = lax.ppermute(left, 'tensor', [(i, (i - 1) % n) for i in range(n)])  6.82 us
    ppermute x5, waiting for transfers between devices, sent_on(): return lax.ppermute(x, 'tensor', [(i, (i + away) % n) for i in range(n)])  6.55 us
    pallas_call x1, Pallas kernels, per_device(): pl.pallas_call(home_kernel, in_specs=[pl.BlockSpec(memory_space=pl.ANY)]...  5.74 us
    pallas_call x1, Pallas kernels, per_device(): pl.pallas_call(band_kernel, in_specs=[pl.BlockSpec(memory_space=pltpu.SME...  5.56 us
  transfers between devices with their start and end apart: 22, of which 13 were waited for; matrix products, arithmetic and copies ran while one was open for 5% of the time, Pallas kernels for 15%

profile of v10, /device:TPU:1, one launch (start us, length us, event | category | flops | bytes accessed | tf_op | source)
XLA Modules:
  0.0 123.7 jit_solution(2119592417110292958)
XLA Ops:
  0.6 5.7 %home_rows.1 = (bf16[32,64,512]{2,1,0:T(8,128)(2,1)}, bf16[80,512]{1,0:T(8,128)(2,1)}, f32[16,16,512]{2,1,0:T(8,128)}) custom-call(bf16[4,3,80,512]{3,2,1,0:T(8,128)(2,1)} %bitcast.115, bf16[80,3,2,512]{3,2,1,0:T(2,128)(2,1)} %fir.1, f32[80,16,512]{2,1,0:T(8,128)} %state_hbm.1, f32[3,3,512]{2,1,0:T(4,128)} %taps.5, f32[16,512]{1,0:T(8,128)} %poles.5, ...), custom_call_target="tpu_custom_call" | custom-call | tf_op jit(solution)/shard_map/home_rows/pallas_call | solution.py:342
  6.4 8.6 %all-to-all-start = ((bf16[32,64,512]{2,1,0:T(8,128)(2,1)}), bf16[32,64,512]{2,1,0:T(8,128)(2,1)S(1)}, u32[]{:S(2)}, u32[]{:S(2)}) async-start(bf16[32,64,512]{2,1,0:T(8,128)(2,1)} %get-tuple-element.89), calls=%async_computation | async-start | bytes 4194304 | tf_op jit(solution)/shard_map/all_to_all | solution.py:286
  15.0 2.7 %stay_rows.1 = (bf16[128,512]{1,0:T(8,128)(2,1)}, f32[16,16,512]{2,1,0:T(8,128)}) custom-call(bf16[80,512]{1,0:T(8,128)(2,1)} %get-tuple-element.90.gated, bf16[4,3,80,512]{3,2,1,0:T(8,128)(2,1)} %bitcast.116, bf16[80,3,2,512]{3,2,1,0:T(2,128)(2,1)} %fir.1, f32[16,16,512]{2,1,0:T(8,128)} %get-tuple-element.91.state, f32[3,3,512]{2,1,0:T(4,128)} %taps.5, ...), custom_call_target="tpu_custom_call" | custom-call | tf_op jit(solution)/shard_map/stay_rows/pallas_call | solution.py:367
  17.7 1.1 constant_dynamic-slice_fusion.far_weight
  18.8 1.1 convolution_convert_fusion
  19.9 5.7 %collective-permute-start.1 = (bf16[64,512]{1,0:T(8,128)(2,1)S(1)}, bf16[64,512]{1,0:T(8,128)(2,1)S(1)}, u32[]{:S(2)}, u32[]{:S(2)}) collective-permute-start(bf16[64,512]{1,0:T(8,128)(2,1)S(1)} %get-tuple-element.143), channel_id=1, source_target_pairs={{0,7},{1,0},{2,1},{3,2},{4,3},{5,4},{6,5},{7,6},{8,15},{9,8},{10,9... | collective-permute-start | bytes 196616 | tf_op jit(solution)/shard_map/ppermute | solution.py:292
  25.6 2.9 %ring_products.4 = f32[4,128,512]{2,1,0:T(8,128)S(1)} custom-call(s32[1]{0:T(128)} %bitcast.2.place, bf16[128,512]{1,0:T(8,128)(2,1)S(1)} %copy-done.4, bf16[512,4096]{1,0:T(8,128)(2,1)} %weight.7), custom_call_target="tpu_custom_call" | custom-call | flops 4294967296 | bytes 4194304 | tf_op jit(solution)/shard_map/ring_products/pallas_call | solution.py:226
  28.5 1.0 copy-done
  29.5 1.1 slice_bitcast_fusion.12
  30.8 1.0 fusion.25
  31.8 2.7 %collective-permute-start.3 = (bf16[128,512]{1,0:T(8,128)(2,1)S(1)}, bf16[128,512]{1,0:T(8,128)(2,1)S(1)}, u32[]{:S(2)}, u32[]{:S(2)}) collective-permute-start(bf16[128,512]{1,0:T(8,128)(2,1)S(1)} %get-tuple-element.137), channel_id=1, source_target_pairs={{0,7},{1,0},{2,1},{3,2},{4,3},{5,4},{6,5},{7,6},{8,15},{9,8},{10,9... | collective-permute-start | bytes 393224 | tf_op jit(solution)/shard_map/ppermute | solution.py:292
  34.6 1.9 %collective-permute-done.3 = bf16[128,512]{1,0:T(8,128)(2,1)S(1)} collective-permute-done((bf16[128,512]{1,0:T(8,128)(2,1)S(1)}, bf16[128,512]{1,0:T(8,128)(2,1)S(1)}, u32[]{:S(2)}, u32[]{:S(2)}) %collective-permute-start.3) | collective-permute-done | bytes 131104 | tf_op jit(solution)/shard_map/ppermute | solution.py:292
  36.5 3.4 %collective-permute-done.2 = bf16[128,512]{1,0:T(8,128)(2,1)S(1)} collective-permute-done((bf16[128,512]{1,0:T(8,128)(2,1)S(1)}, bf16[128,512]{1,0:T(8,128)(2,1)S(1)}, u32[]{:S(2)}, u32[]{:S(2)}) %collective-permute-start.2) | collective-permute-done | bytes 131104 | tf_op jit(solution)/shard_map/ppermute | solution.py:291
  39.9 1.1 fusion.13
  41.0 0.2 collective-permute-start.5
  41.2 1.4 %collective-permute-start.4 = (bf16[128,512]{1,0:T(8,128)(2,1)S(1)}, bf16[128,512]{1,0:T(8,128)(2,1)S(1)}, u32[]{:S(2)}, u32[]{:S(2)}) collective-permute-start(bf16[128,512]{1,0:T(8,128)(2,1)S(1)} %get-tuple-element.136), channel_id=1, source_target_pairs={{0,1},{1,2},{2,3},{3,4},{4,5},{5,6},{6,7},{7,0},{8,9},{9,10},{10,1... | collective-permute-start | bytes 393224 | tf_op jit(solution)/shard_map/ppermute | solution.py:291
  42.5 2.6 %ring_products.5 = f32[3,128,512]{2,1,0:T(8,128)S(1)} custom-call(s32[1]{0:T(128)} %bitcast.2.place, bf16[128,512]{1,0:T(8,128)(2,1)S(1)} %copy-done.4, bf16[512,4096]{1,0:T(8,128)(2,1)} %weight.7), custom_call_target="tpu_custom_call" | custom-call | flops 4294967296 | bytes 4194304 | tf_op jit(solution)/shard_map/ring_products/pallas_call | solution.py:226
  45.2 1.0 collective-permute-done.4
  46.4 5.6 %band_rows.1 = (bf16[32,48,512]{2,1,0:T(8,128)(2,1)}, bf16[192,512]{1,0:T(8,128)(2,1)S(1)}, bf16[224,512]{1,0:T(8,128)(2,1)S(1)}, bf16[224,512]{1,0:T(8,128)(2,1)S(1)}) custom-call(s32[3]{0:T(128)S(1)} %and_select_fusion.turns, bf16[32,64,512]{2,1,0:T(8,128)(2,1)S(1)} %all-to-all-done.got, f32[3,3,512]{2,1,0:T(4,128)S(1)} %copy-done.3, ...), custom_call_target="tpu_custom_call" | custom-call | tf_op jit(solution)/shard_map/band_rows/pallas_call | solution.py:408
  51.9 0.2 collective-permute-start.6
  52.2 2.4 %collective-permute-start.7 = (bf16[224,512]{1,0:T(8,128)(2,1)S(1)}, bf16[224,512]{1,0:T(8,128)(2,1)S(1)}, u32[]{:S(2)}, u32[]{:S(2)}) collective-permute-start(bf16[224,512]{1,0:T(8,128)(2,1)S(1)} %get-tuple-element.106), channel_id=1, source_target_pairs={{0,7},{1,0},{2,1},{3,2},{4,3},{5,4},{6,5},{7,6},{8,15},{9,8},{10,9... | collective-permute-start | bytes 688136 | tf_op jit(solution)/shard_map/ppermute | solution.py:292
  54.6 3.0 %ring_products.6 = f32[4,192,512]{2,1,0:T(8,128)S(1)} custom-call(s32[1]{0:T(128)} %bitcast.2.place, bf16[192,512]{1,0:T(8,128)(2,1)S(1)} %get-tuple-element.112.gated, bf16[512,4096]{1,0:T(8,128)(2,1)} %weight.7), custom_call_target="tpu_custom_call" | custom-call | flops 6442450944 | bytes 4194304 | tf_op jit(solution)/shard_map/ring_products/pallas_call | solution.py:226
  57.7 0.3 collective-permute-done.6
  58.1 2.7 %collective-permute-start.9 = (bf16[192,512]{1,0:T(8,128)(2,1)S(1)}, bf16[192,512]{1,0:T(8,128)(2,1)S(1)}, u32[]{:S(2)}, u32[]{:S(2)}) collective-permute-start(bf16[192,512]{1,0:T(8,128)(2,1)S(1)} %get-tuple-element.129), channel_id=1, source_target_pairs={{0,7},{1,0},{2,1},{3,2},{4,3},{5,4},{6,5},{7,6},{8,15},{9,8},{10,9... | collective-permute-start | bytes 589832 | tf_op jit(solution)/shard_map/ppermute | solution.py:292
  60.8 12.2 %all-to-all-start.1 = ((bf16[32,48,512]{2,1,0:T(8,128)(2,1)}), bf16[32,48,512]{2,1,0:T(8,128)(2,1)}, u32[]{:S(2)}, u32[]{:S(2)}) async-start(bf16[32,48,512]{2,1,0:T(8,128)(2,1)} %get-tuple-element.119), calls=%async_computation.1 | async-start | bytes 3145728 | tf_op jit(solution)/shard_map/all_to_all | solution.py:286
  73.2 3.0 %collective-permute-start.11 = (bf16[192,512]{1,0:T(8,128)(2,1)S(1)}, bf16[192,512]{1,0:T(8,128)(2,1)S(1)}, u32[]{:S(2)}, u32[]{:S(2)}) collective-permute-start(bf16[192,512]{1,0:T(8,128)(2,1)S(1)} %get-tuple-element.127), channel_id=1, source_target_pairs={{0,7},{1,0},{2,1},{3,2},{4,3},{5,4},{6,5},{7,6},{8,15},{9,8},{10,9... | collective-permute-start | bytes 589832 | tf_op jit(solution)/shard_map/ppermute | solution.py:292
  76.2 2.7 %ring_products.7 = f32[3,192,512]{2,1,0:T(8,128)S(1)} custom-call(s32[1]{0:T(128)} %bitcast.2.place, bf16[192,512]{1,0:T(8,128)(2,1)S(1)} %get-tuple-element.112.gated, bf16[512,4096]{1,0:T(8,128)(2,1)} %weight.7), custom_call_target="tpu_custom_call" | custom-call | flops 6442450944 | bytes 4194304 | tf_op jit(solution)/shard_map/ring_products/pallas_call | solution.py:226
  78.9 1.3 %collective-permute-done.11 = bf16[192,512]{1,0:T(8,128)(2,1)S(1)} collective-permute-done((bf16[192,512]{1,0:T(8,128)(2,1)S(1)}, bf16[192,512]{1,0:T(8,128)(2,1)S(1)}, u32[]{:S(2)}, u32[]{:S(2)}) %collective-permute-start.11) | collective-permute-done | bytes 196640 | tf_op jit(solution)/shard_map/ppermute | solution.py:292
  80.2 3.2 %collective-permute-done.10 = bf16[192,512]{1,0:T(8,128)(2,1)S(1)} collective-permute-done((bf16[192,512]{1,0:T(8,128)(2,1)S(1)}, bf16[192,512]{1,0:T(8,128)(2,1)S(1)}, u32[]{:S(2)}, u32[]{:S(2)}) %collective-permute-start.10) | collective-permute-done | bytes 196640 | tf_op jit(solution)/shard_map/ppermute | solution.py:291
  83.5 0.4 collective-permute-start.13
  83.9 1.1 collective-permute-start.12
  85.0 0.1 multiply_reduce_fusion.1
  85.2 3.6 %collective-permute-done.13 = bf16[192,512]{1,0:T(8,128)(2,1)S(1)} collective-permute-done((bf16[192,512]{1,0:T(8,128)(2,1)S(1)}, bf16[192,512]{1,0:T(8,128)(2,1)S(1)}, u32[]{:S(2)}, u32[]{:S(2)}) %collective-permute-start.13) | collective-permute-done | bytes 196640 | tf_op jit(solution)/shard_map/ppermute | solution.py:292
  88.7 1.6 %collective-permute-done.12 = bf16[192,512]{1,0:T(8,128)(2,1)S(1)} collective-permute-done((bf16[192,512]{1,0:T(8,128)(2,1)S(1)}, bf16[192,512]{1,0:T(8,128)(2,1)S(1)}, u32[]{:S(2)}, u32[]{:S(2)}) %collective-permute-start.12) | collective-permute-done | bytes 196640 | tf_op jit(solution)/shard_map/ppermute | solution.py:291
  90.3 0.2 multiply_reduce_fusion
  90.6 2.0 %collective-permute-start.15 = (f32[320]{0:T(512)S(1)}, f32[320]{0:T(512)S(1)}, u32[]{:S(2)}, u32[]{:S(2)}) collective-permute-start(f32[320]{0:T(512)S(1)} %pad_maximum_fusion.1), channel_id=1, source_target_pairs={{0,7},{1,0},{2,1},{3,2},{4,3},{5,4},{6,5},{7,6},{8,15},{9,8},{10,9... | collective-permute-start | bytes 3848 | tf_op jit(solution)/shard_map/ppermute | solution.py:312
  92.6 2.5 %collective-permute-done.16 = f32[320]{0:T(512)S(1)} collective-permute-done((f32[320]{0:T(512)S(1)}, f32[320]{0:T(512)S(1)}, u32[]{:S(2)}, u32[]{:S(2)}) %collective-permute-start.16) | collective-permute-done | bytes 1312 | tf_op jit(solution)/shard_map/ppermute | solution.py:312
  95.1 1.5 %collective-permute-done.14 = f32[320]{0:T(512)S(1)} collective-permute-done((f32[320]{0:T(512)S(1)}, f32[320]{0:T(512)S(1)}, u32[]{:S(2)}, u32[]{:S(2)}) %collective-permute-start.14) | collective-permute-done | bytes 1312 | tf_op jit(solution)/shard_map/ppermute | solution.py:312
  96.7 0.4 collective-permute-start.18
  97.1 2.0 %collective-permute-start.17 = (f32[320]{0:T(512)S(1)}, f32[320]{0:T(512)S(1)}, u32[]{:S(2)}, u32[]{:S(2)}) collective-permute-start(f32[320]{0:T(512)S(1)} %add_add_fusion), channel_id=1, source_target_pairs={{0,2},{1,3},{2,4},{3,5},{4,6},{5,7},{6,0},{7,1},{8,10},{9,11},{10,... | collective-permute-start | bytes 3848 | tf_op jit(solution)/shard_map/ppermute | solution.py:312
  99.1 1.0 collective-permute-done.18
  100.1 1.5 %collective-permute-done.17 = f32[320]{0:T(512)S(1)} collective-permute-done((f32[320]{0:T(512)S(1)}, f32[320]{0:T(512)S(1)}, u32[]{:S(2)}, u32[]{:S(2)}) %collective-permute-start.17) | collective-permute-done | bytes 1312 | tf_op jit(solution)/shard_map/ppermute | solution.py:312
  102.0 0.8 copy.18
  102.8 11.6 %all-to-all-start.2 = ((bf16[32,3,2,512]{3,2,1,0:T(2,128)(2,1)}), bf16[32,3,2,512]{3,2,1,0:T(2,128)(2,1)S(1)}, u32[]{:S(2)}, u32[]{:S(2)}) async-start(bf16[32,3,2,512]{3,2,1,0:T(2,128)(2,1)} %bitcast.111), calls=%async_computation.2 | async-start | bytes 393216 | tf_op jit(solution)/shard_map/all_to_all | solution.py:286
  114.4 5.3 %last_rows.1 = (f32[80,16,512]{2,1,0:T(8,128)}, bf16[80,3,2,512]{3,2,1,0:T(2,128)(2,1)}) custom-call(bf16[32,48,512]{2,1,0:T(8,128)(2,1)} %all-to-all-done.1.back, bf16[4,3,80,512]{3,2,1,0:T(8,128)(2,1)} %bitcast.117, f32[16,16,512]{2,1,0:T(8,128)} %get-tuple-element.124.stay_state, s32[3,80]{1,0:T(4,128)} %finished.5), custom_call_target="tpu_custom_call" | custom-call | tf_op jit(solution)/shard_map/last_rows/pallas_call | solution.py:453
  119.8 2.9 %all-to-all-done.2 = bf16[32,3,2,512]{3,2,1,0:T(2,128)(2,1)S(1)} async-done(((bf16[32,3,2,512]{3,2,1,0:T(2,128)(2,1)}), bf16[32,3,2,512]{3,2,1,0:T(2,128)(2,1)S(1)}, u32[]{:S(2)}, u32[]{:S(2)}) %all-to-all-start.2) | async-done | bytes 196640 | tf_op jit(solution)/shard_map/all_to_all | solution.py:286
  122.7 0.1 copy.16
  122.9 0.8 maximum_maximum_fusion
  (53 shorter events, 1.4 us)
Async XLA Ops:
  6.4 39.9 %all-to-all-start = ((bf16[32,64,512]{2,1,0:T(8,128)(2,1)}), bf16[32,64,512]{2,1,0:T(8,128)(2,1)S(1)}, u32[]{:S(2)}, u32[]{:S(2)}) async-start(bf16[32,64,512]{2,1,0:T(8,128)(2,1)} %get-tuple-element.89), calls=%async_computation | async-start | bytes 4194304 | tf_op jit(solution)/shard_map/all_to_all | solution.py:286
  17.7 7.9 %copy-start.4 = (bf16[128,512]{1,0:T(8,128)(2,1)S(1)}, bf16[128,512]{1,0:T(8,128)(2,1)}, u32[]{:S(2)}) copy-start(bf16[128,512]{1,0:T(8,128)(2,1)} %get-tuple-element.97.gated) | copy-start | bytes 393220
  19.9 10.9 %collective-permute-start.1 = (bf16[64,512]{1,0:T(8,128)(2,1)S(1)}, bf16[64,512]{1,0:T(8,128)(2,1)S(1)}, u32[]{:S(2)}, u32[]{:S(2)}) collective-permute-start(bf16[64,512]{1,0:T(8,128)(2,1)S(1)} %get-tuple-element.143), channel_id=1, source_target_pairs={{0,7},{1,0},{2,1},{3,2},{4,3},{5,4},{6,5},{7,6},{8,15},{9,8},{10,9... | collective-permute-start | bytes 196616 | tf_op jit(solution)/shard_map/ppermute | solution.py:292
  25.6 5.2 %collective-permute-start = (bf16[64,512]{1,0:T(8,128)(2,1)S(1)}, bf16[64,512]{1,0:T(8,128)(2,1)S(1)}, u32[]{:S(2)}, u32[]{:S(2)}) collective-permute-start(bf16[64,512]{1,0:T(8,128)(2,1)S(1)} %get-tuple-element.144), channel_id=1, source_target_pairs={{0,1},{1,2},{2,3},{3,4},{4,5},{5,6},{6,7},{7,0},{8,9},{9,10},{10,1... | collective-permute-start | bytes 196616 | tf_op jit(solution)/shard_map/ppermute | solution.py:291
  25.6 5.0 %copy-start.7 = (s32[3,80]{1,0:T(4,128)S(1)}, s32[3,80]{1,0:T(4,128)}, u32[]{:S(2)}) copy-start(s32[3,80]{1,0:T(4,128)} %param.29) | copy-start | bytes 2884
  28.5 1.0 copy-start
  31.8 4.7 %collective-permute-start.3 = (bf16[128,512]{1,0:T(8,128)(2,1)S(1)}, bf16[128,512]{1,0:T(8,128)(2,1)S(1)}, u32[]{:S(2)}, u32[]{:S(2)}) collective-permute-start(bf16[128,512]{1,0:T(8,128)(2,1)S(1)} %get-tuple-element.137), channel_id=1, source_target_pairs={{0,7},{1,0},{2,1},{3,2},{4,3},{5,4},{6,5},{7,6},{8,15},{9,8},{10,9... | collective-permute-start | bytes 393224 | tf_op jit(solution)/shard_map/ppermute | solution.py:292
  34.6 5.3 %collective-permute-start.2 = (bf16[128,512]{1,0:T(8,128)(2,1)S(1)}, bf16[128,512]{1,0:T(8,128)(2,1)S(1)}, u32[]{:S(2)}, u32[]{:S(2)}) collective-permute-start(bf16[128,512]{1,0:T(8,128)(2,1)S(1)} %get-tuple-element.138), channel_id=1, source_target_pairs={{0,1},{1,2},{2,3},{3,4},{4,5},{5,6},{6,7},{7,0},{8,9},{9,10},{10,1... | collective-permute-start | bytes 393224 | tf_op jit(solution)/shard_map/ppermute | solution.py:291
  41.0 4.2 %collective-permute-start.5 = (bf16[128,512]{1,0:T(8,128)(2,1)S(1)}, bf16[128,512]{1,0:T(8,128)(2,1)S(1)}, u32[]{:S(2)}, u32[]{:S(2)}) collective-permute-start(bf16[128,512]{1,0:T(8,128)(2,1)S(1)} %get-tuple-element.135), channel_id=1, source_target_pairs={{0,7},{1,0},{2,1},{3,2},{4,3},{5,4},{6,5},{7,6},{8,15},{9,8},{10,9... | collective-permute-start | bytes 393224 | tf_op jit(solution)/shard_map/ppermute | solution.py:292
  41.2 5.0 %collective-permute-start.4 = (bf16[128,512]{1,0:T(8,128)(2,1)S(1)}, bf16[128,512]{1,0:T(8,128)(2,1)S(1)}, u32[]{:S(2)}, u32[]{:S(2)}) collective-permute-start(bf16[128,512]{1,0:T(8,128)(2,1)S(1)} %get-tuple-element.136), channel_id=1, source_target_pairs={{0,1},{1,2},{2,3},{3,4},{4,5},{5,6},{6,7},{7,0},{8,9},{9,10},{10,1... | collective-permute-start | bytes 393224 | tf_op jit(solution)/shard_map/ppermute | solution.py:291
  45.1 1.2 copy-start.1
  45.1 1.2 copy-start.2
  45.2 1.2 copy-start.3
  45.2 1.2 copy-start.5
  51.9 6.1 %collective-permute-start.6 = (bf16[224,512]{1,0:T(8,128)(2,1)S(1)}, bf16[224,512]{1,0:T(8,128)(2,1)S(1)}, u32[]{:S(2)}, u32[]{:S(2)}) collective-permute-start(bf16[224,512]{1,0:T(8,128)(2,1)S(1)} %get-tuple-element.105), channel_id=1, source_target_pairs={{0,1},{1,2},{2,3},{3,4},{4,5},{5,6},{6,7},{7,0},{8,9},{9,10},{10,1... | collective-permute-start | bytes 688136 | tf_op jit(solution)/shard_map/ppermute | solution.py:291
  52.2 5.8 %collective-permute-start.7 = (bf16[224,512]{1,0:T(8,128)(2,1)S(1)}, bf16[224,512]{1,0:T(8,128)(2,1)S(1)}, u32[]{:S(2)}, u32[]{:S(2)}) collective-permute-start(bf16[224,512]{1,0:T(8,128)(2,1)S(1)} %get-tuple-element.106), channel_id=1, source_target_pairs={{0,7},{1,0},{2,1},{3,2},{4,3},{5,4},{6,5},{7,6},{8,15},{9,8},{10,9... | collective-permute-start | bytes 688136 | tf_op jit(solution)/shard_map/ppermute | solution.py:292
  58.1 14.9 %collective-permute-start.9 = (bf16[192,512]{1,0:T(8,128)(2,1)S(1)}, bf16[192,512]{1,0:T(8,128)(2,1)S(1)}, u32[]{:S(2)}, u32[]{:S(2)}) collective-permute-start(bf16[192,512]{1,0:T(8,128)(2,1)S(1)} %get-tuple-element.129), channel_id=1, source_target_pairs={{0,7},{1,0},{2,1},{3,2},{4,3},{5,4},{6,5},{7,6},{8,15},{9,8},{10,9... | collective-permute-start | bytes 589832 | tf_op jit(solution)/shard_map/ppermute | solution.py:292
  60.8 12.2 %collective-permute-start.8 = (bf16[192,512]{1,0:T(8,128)(2,1)S(1)}, bf16[192,512]{1,0:T(8,128)(2,1)S(1)}, u32[]{:S(2)}, u32[]{:S(2)}) collective-permute-start(bf16[192,512]{1,0:T(8,128)(2,1)S(1)} %get-tuple-element.130), channel_id=1, source_target_pairs={{0,1},{1,2},{2,3},{3,4},{4,5},{5,6},{6,7},{7,0},{8,9},{9,10},{10,1... | collective-permute-start | bytes 589832 | tf_op jit(solution)/shard_map/ppermute | solution.py:291
  60.8 35.9 %all-to-all-start.1 = ((bf16[32,48,512]{2,1,0:T(8,128)(2,1)}), bf16[32,48,512]{2,1,0:T(8,128)(2,1)}, u32[]{:S(2)}, u32[]{:S(2)}) async-start(bf16[32,48,512]{2,1,0:T(8,128)(2,1)} %get-tuple-element.119), calls=%async_computation.1 | async-start | bytes 3145728 | tf_op jit(solution)/shard_map/all_to_all | solution.py:286
  73.2 7.0 %collective-permute-start.11 = (bf16[192,512]{1,0:T(8,128)(2,1)S(1)}, bf16[192,512]{1,0:T(8,128)(2,1)S(1)}, u32[]{:S(2)}, u32[]{:S(2)}) collective-permute-start(bf16[192,512]{1,0:T(8,128)(2,1)S(1)} %get-tuple-element.127), channel_id=1, source_target_pairs={{0,7},{1,0},{2,1},{3,2},{4,3},{5,4},{6,5},{7,6},{8,15},{9,8},{10,9... | collective-permute-start | bytes 589832 | tf_op jit(solution)/shard_map/ppermute | solution.py:292
  76.2 7.2 %collective-permute-start.10 = (bf16[192,512]{1,0:T(8,128)(2,1)S(1)}, bf16[192,512]{1,0:T(8,128)(2,1)S(1)}, u32[]{:S(2)}, u32[]{:S(2)}) collective-permute-start(bf16[192,512]{1,0:T(8,128)(2,1)S(1)} %get-tuple-element.128), channel_id=1, source_target_pairs={{0,1},{1,2},{2,3},{3,4},{4,5},{5,6},{6,7},{7,0},{8,9},{9,10},{10,1... | collective-permute-start | bytes 589832 | tf_op jit(solution)/shard_map/ppermute | solution.py:291
  78.9 22.9 %copy-start.6 = (f32[512]{0:T(512)S(1)}, f32[512]{0:T(512)}, u32[]{:S(2)}) copy-start(f32[512]{0:T(512)} %param.27) | copy-start | bytes 6148
  83.5 5.2 %collective-permute-start.13 = (bf16[192,512]{1,0:T(8,128)(2,1)S(1)}, bf16[192,512]{1,0:T(8,128)(2,1)S(1)}, u32[]{:S(2)}, u32[]{:S(2)}) collective-permute-start(bf16[192,512]{1,0:T(8,128)(2,1)S(1)} %get-tuple-element.133), channel_id=1, source_target_pairs={{0,7},{1,0},{2,1},{3,2},{4,3},{5,4},{6,5},{7,6},{8,15},{9,8},{10,9... | collective-permute-start | bytes 589832 | tf_op jit(solution)/shard_map/ppermute | solution.py:292
  83.9 6.4 %collective-permute-start.12 = (bf16[192,512]{1,0:T(8,128)(2,1)S(1)}, bf16[192,512]{1,0:T(8,128)(2,1)S(1)}, u32[]{:S(2)}, u32[]{:S(2)}) collective-permute-start(bf16[192,512]{1,0:T(8,128)(2,1)S(1)} %get-tuple-element.134), channel_id=1, source_target_pairs={{0,1},{1,2},{2,3},{3,4},{4,5},{5,6},{6,7},{7,0},{8,9},{9,10},{10,1... | collective-permute-start | bytes 589832 | tf_op jit(solution)/shard_map/ppermute | solution.py:291
  90.6 4.6 %collective-permute-start.16 = (f32[320]{0:T(512)S(1)}, f32[320]{0:T(512)S(1)}, u32[]{:S(2)}, u32[]{:S(2)}) collective-permute-start(f32[320]{0:T(512)S(1)} %pad_maximum_fusion.1), channel_id=1, source_target_pairs={{0,2},{1,3},{2,4},{3,5},{4,6},{5,7},{6,0},{7,1},{8,10},{9,11},{10,... | collective-permute-start | bytes 3848 | tf_op jit(solution)/shard_map/ppermute | solution.py:312
  90.6 4.5 %collective-permute-start.15 = (f32[320]{0:T(512)S(1)}, f32[320]{0:T(512)S(1)}, u32[]{:S(2)}, u32[]{:S(2)}) collective-permute-start(f32[320]{0:T(512)S(1)} %pad_maximum_fusion.1), channel_id=1, source_target_pairs={{0,7},{1,0},{2,1},{3,2},{4,3},{5,4},{6,5},{7,6},{8,15},{9,8},{10,9... | collective-permute-start | bytes 3848 | tf_op jit(solution)/shard_map/ppermute | solution.py:312
  92.6 4.0 %collective-permute-start.14 = (f32[320]{0:T(512)S(1)}, f32[320]{0:T(512)S(1)}, u32[]{:S(2)}, u32[]{:S(2)}) collective-permute-start(f32[320]{0:T(512)S(1)} %pad_maximum_fusion.1), channel_id=1, source_target_pairs={{0,1},{1,2},{2,3},{3,4},{4,5},{5,6},{6,7},{7,0},{8,9},{9,10},{10,1... | collective-permute-start | bytes 3848 | tf_op jit(solution)/shard_map/ppermute | solution.py:312
  96.7 3.4 %collective-permute-start.18 = (f32[320]{0:T(512)S(1)}, f32[320]{0:T(512)S(1)}, u32[]{:S(2)}, u32[]{:S(2)}) collective-permute-start(f32[320]{0:T(512)S(1)} %add_add_fusion), channel_id=1, source_target_pairs={{0,6},{1,7},{2,0},{3,1},{4,2},{5,3},{6,4},{7,5},{8,14},{9,15},{10,... | collective-permute-start | bytes 3848 | tf_op jit(solution)/shard_map/ppermute | solution.py:312
  97.1 4.5 %collective-permute-start.17 = (f32[320]{0:T(512)S(1)}, f32[320]{0:T(512)S(1)}, u32[]{:S(2)}, u32[]{:S(2)}) collective-permute-start(f32[320]{0:T(512)S(1)} %add_add_fusion), channel_id=1, source_target_pairs={{0,2},{1,3},{2,4},{3,5},{4,6},{5,7},{6,0},{7,1},{8,10},{9,11},{10,... | collective-permute-start | bytes 3848 | tf_op jit(solution)/shard_map/ppermute | solution.py:312
  102.8 19.9 %all-to-all-start.2 = ((bf16[32,3,2,512]{3,2,1,0:T(2,128)(2,1)}), bf16[32,3,2,512]{3,2,1,0:T(2,128)(2,1)S(1)}, u32[]{:S(2)}, u32[]{:S(2)}) async-start(bf16[32,3,2,512]{3,2,1,0:T(2,128)(2,1)} %bitcast.111), calls=%async_computation.2 | async-start | bytes 393216 | tf_op jit(solution)/shard_map/all_to_all | solution.py:286

commit v11 on v9

--- a/solution.py
+++ b/solution.py
@@ -36,11 +36,16 @@
         at = pl.ds(block * (rows // 2), rows // 2)
         return pltpu.make_async_copy(packed_all.at[at], packed_hbm.at[at], sems.at[3, block])
 
-    for block in range(blocks):
+    for block in range(2):
         for fetch in fetches(block):
             fetch.start()
 
     def first_step(block):
+        @pl.when(block + 2 < blocks)
+        def _():
+            for fetch in fetches(block + 2):
+                fetch.start()
+
         for fetch in fetches(block):
             fetch.wait()
         start = pl.multiple_of(block * rows, rows)
@@ -237,38 +242,73 @@
     return dict(zip(aways, part))
 
 
-def finish_kernel(back, qkv, stay_state, finished, state, lagged):
-    block = pl.program_id(0)
-    rows, width = 16, qkv.shape[-1]
-
-    def put(j, last):
-        both = [qkv[1, j].astype(F32)[:, None], last[:, None]]
-        lagged[:, j] = jnp.concatenate(both, axis=1).astype(BF16)
-
-    @pl.when(block < 4)
-    def _():
-        n = back.shape[0]
+def finish_kernel(back_hbm, qkv_hbm, stay_hbm, finished, state_hbm, lagged_hbm, *rest):
+    back_all, qkv_all, state_all, lagged_all, sems = rest
+    rows, width = 16, qkv_hbm.shape[-1]
+    blocks = qkv_hbm.shape[2] // rows
+    n = rows // 2
+
+    def qkv_fetch(block):
+        at = pl.ds(block * rows, rows)
+        return pltpu.make_async_copy(qkv_hbm.at[2:4, :, at], qkv_all.at[:, :, at], sems.at[0, block])
+
+    def back_fetch(block):
+        at = pl.ds(block * n, n)
+        return pltpu.make_async_copy(back_hbm.at[at], back_all.at[at], sems.at[1, block])
+
+    def stores(block):
+        at = pl.ds(block * rows, rows)
+        return [
+            pltpu.make_async_copy(state_all.at[at], state_hbm.at[at], sems.at[2, block]),
+            pltpu.make_async_copy(lagged_all.at[at], lagged_hbm.at[at], sems.at[3, block]),
+        ]
+
+    for block in range(blocks):
+        qkv_fetch(block).start()
+        if block < blocks - 1:
+            back_fetch(block).start()
+    last_at = pl.ds((blocks - 1) * rows, rows)
+    stay = pltpu.make_async_copy(stay_hbm, state_all.at[last_at], sems.at[1, blocks - 1])
+    stay.start()
+
+    def put(block, j, last):
+        at = pl.ds(pl.multiple_of(block * rows, rows), rows)
+        both = [qkv_all[1, j, at].astype(F32)[:, None], last[:, None]]
+        lagged_all[at, j] = jnp.concatenate(both, axis=1).astype(BF16)
+
+    r = lax.broadcasted_iota(jnp.int32, (3 * rows, n * 16), 0)
+    c = lax.broadcasted_iota(jnp.int32, (3 * rows, n * 16), 1)
+    source = ((r & 15) >> 1) * 16 + (r >> 4) * 2 + (r & 1)
+    order = jnp.where(c == source, 1.0, 0.0).astype(BF16)
+
+    @pl.loop(0, blocks - 1)
+    def _(block):
+        qkv_fetch(block).wait()
+        back_fetch(block).wait()
+        back = back_all.at[pl.ds(pl.multiple_of(block * n, n), n)]
         for b in range(n):
             for side in range(2):
-                state[2 * b + side] = back[b, side * MODES : (side + 1) * MODES].astype(F32)
-        shape = (3 * rows, n * 16)
-        r = lax.broadcasted_iota(jnp.int32, shape, 0)
-        c = lax.broadcasted_iota(jnp.int32, shape, 1)
-        source = ((r & 15) >> 1) * 16 + (r >> 4) * 2 + (r & 1)
-        order = jnp.where(c == source, 1.0, 0.0).astype(BF16)
+                part = back[b, side * MODES : (side + 1) * MODES].astype(F32)
+                state_all[block * rows + 2 * b + side] = part
         last = dot(order, back[:, 2 * MODES :].reshape(n * 16, width))
         for j in range(3):
-            put(j, last[j * rows : (j + 1) * rows])
-
-    @pl.when(block == 4)
-    def _():
-        state[...] = stay_state[...]
-        at = lax.broadcasted_iota(jnp.int32, (rows, finished.shape[1]), 0) + block * rows
-        own = at == lax.broadcasted_iota(jnp.int32, at.shape, 1)
-        ended = jnp.where(own, finished[2:3].astype(F32), 0.0)
-        alive = 1.0 - jnp.sum(ended, axis=1, keepdims=True)
-        for j in range(3):
-            put(j, qkv[0, j].astype(F32) * alive)
+            put(block, j, last[j * rows : (j + 1) * rows])
+        for store in stores(block):
+            store.start()
+
+    qkv_fetch(blocks - 1).wait()
+    stay.wait()
+    at = lax.broadcasted_iota(jnp.int32, (rows, finished.shape[1]), 0) + (blocks - 1) * rows
+    own = at == lax.broadcasted_iota(jnp.int32, at.shape, 1)
+    ended = jnp.where(own, finished[2:3].astype(F32), 0.0)
+    alive = 1.0 - jnp.sum(ended, axis=1, keepdims=True)
+    for j in range(3):
+        put(blocks - 1, j, qkv_all[0, j, last_at].astype(F32) * alive)
+    for store in stores(blocks - 1):
+        store.start()
+    for block in range(blocks):
+        for store in stores(block):
+            store.wait()
 
 
 def whole(shape):
@@ -421,20 +461,18 @@
     mixed_back = swap(mixed_band)
     final_state, final_lagged = pl.pallas_call(
         finish_kernel,
-        grid=(slots // 16,),
-        in_specs=[
-            pl.BlockSpec((8, 2 * MODES + 16, width), lambda i: (jnp.minimum(i, 3), 0, 0)),
-            pl.BlockSpec((2, 3, 16, width), lambda i: (1, 0, i, 0)),
-            whole((16, MODES, width)),
-            whole((3, slots)),
-        ],
-        out_specs=[
-            pl.BlockSpec((16, MODES, width), lambda i: (i, 0, 0)),
-            pl.BlockSpec((16, 3, 2, width), lambda i: (i, 0, 0, 0)),
-        ],
+        in_specs=[pl.BlockSpec(memory_space=pl.ANY)] * 3 + [pl.BlockSpec(memory_space=pltpu.VMEM)],
+        out_specs=[pl.BlockSpec(memory_space=pl.ANY)] * 2,
         out_shape=[
             jax.ShapeDtypeStruct(modal_state.shape, F32),
             jax.ShapeDtypeStruct(fir_buffer.shape, BF16),
+        ],
+        scratch_shapes=[
+            pltpu.VMEM(back.shape, BF16),
+            pltpu.VMEM((2, 3, slots, width), BF16),
+            pltpu.VMEM(modal_state.shape, F32),
+            pltpu.VMEM(fir_buffer.shape, BF16),
+            pltpu.SemaphoreType.DMA((4, slots // 16)),
         ],
         compiler_params=pltpu.CompilerParams(vmem_limit_bytes=56 * 1024 * 1024),
         name="last_rows",

time: 122 us -> 123 us (level)
  transfers between devices with their start and end apart: 21 -> 21, of which waited for: 15 -> 15; matrix products, arithmetic and copies ran while one was open for 5% -> 5% of each run, Pallas kernels for 14% -> 13%
where the time goes in v11:
time: 123 us; the launch traced here: 122 us
  starting transfers between devices  58 us (47%)
  Pallas kernels  27 us (22%)
  waiting for transfers between devices  26.9 us (22%)
  local copies, waits for them, and re-layouts  4.43 us (4%)
  other arithmetic  4.12 us (3%)
    all_to_all x3, starting transfers between devices, swap(): return lax.all_to_all(blocks, 'dp', split_axis=0, concat_axis=0, tiled=True)  29.6 us
    ppermute x7, starting transfers between devices, pass_on(): left = lax.ppermute(left, 'tensor', [(i, (i - 1) % n) for i in range(n)])  18.7 us
    pallas_call x4, Pallas kernels, products(): pl.pallas_call(products_kernel, grid_spec=pltpu.PrefetchScalarGridSpec(nu...  11.2 us
    ppermute x7, waiting for transfers between devices, pass_on(): right = lax.ppermute(right, 'tensor', [(i, (i + 1) % n) for i in range(n)])  9.49 us
    ppermute x7, waiting for transfers between devices, pass_on(): left = lax.ppermute(left, 'tensor', [(i, (i - 1) % n) for i in range(n)])  6.82 us
    pallas_call x1, Pallas kernels, per_device(): pl.pallas_call(home_kernel, in_specs=[pl.BlockSpec(memory_space=pl.ANY)]...  6.13 us
    ppermute x4, waiting for transfers between devices, sent_on(): return lax.ppermute(x, 'tensor', [(i, (i + away) % n) for i in range(n)])  5.71 us
    pallas_call x1, Pallas kernels, per_device(): pl.pallas_call(band_kernel, in_specs=[pl.BlockSpec(memory_space=pltpu.SME...  5.56 us
  transfers between devices with their start and end apart: 21, of which 15 were waited for; matrix products, arithmetic and copies ran while one was open for 5% of the time, Pallas kernels for 13%

profile of v11, /device:TPU:1, one launch (start us, length us, event | category | flops | bytes accessed | tf_op | source)
XLA Modules:
  0.0 121.6 jit_solution(12310571147549668873)
XLA Ops:
  0.6 6.1 %home_rows.1 = (bf16[32,64,512]{2,1,0:T(8,128)(2,1)}, bf16[128,512]{1,0:T(8,128)(2,1)}, f32[16,16,512]{2,1,0:T(8,128)}) custom-call(bf16[4,3,80,512]{3,2,1,0:T(8,128)(2,1)} %bitcast.114, bf16[80,3,2,512]{3,2,1,0:T(2,128)(2,1)} %fir_hbm.1, f32[80,16,512]{2,1,0:T(8,128)} %state_hbm.1, f32[3,3,512]{2,1,0:T(4,128)} %taps.3, f32[16,512]{1,0:T(8,128)} %poles.3, ...), custom_call_target="tpu_custom_call" | custom-call | tf_op jit(solution)/shard_map/home_rows/pallas_call | solution.py:376
  6.8 8.7 %all-to-all-start = ((bf16[32,64,512]{2,1,0:T(8,128)(2,1)}), bf16[32,64,512]{2,1,0:T(8,128)(2,1)S(1)}, u32[]{:S(2)}, u32[]{:S(2)}) async-start(bf16[32,64,512]{2,1,0:T(8,128)(2,1)} %get-tuple-element.88), calls=%async_computation | async-start | bytes 4194304 | tf_op jit(solution)/shard_map/all_to_all | solution.py:319
  15.5 1.1 constant_dynamic-slice_fusion.far_weight
  16.6 0.2 convolution_convert_fusion
  16.9 5.7 %collective-permute-start.1 = (bf16[64,512]{1,0:T(8,128)(2,1)S(1)}, bf16[64,512]{1,0:T(8,128)(2,1)S(1)}, u32[]{:S(2)}, u32[]{:S(2)}) collective-permute-start(bf16[64,512]{1,0:T(8,128)(2,1)S(1)} %get-tuple-element.143), channel_id=1, source_target_pairs={{0,7},{1,0},{2,1},{3,2},{4,3},{5,4},{6,5},{7,6},{8,15},{9,8},{10,9... | collective-permute-start | bytes 196616 | tf_op jit(solution)/shard_map/ppermute | solution.py:325
  22.5 2.9 %ring_products.4 = f32[4,128,512]{2,1,0:T(8,128)S(1)} custom-call(s32[1]{0:T(128)} %bitcast.2.place, bf16[128,512]{1,0:T(8,128)(2,1)S(1)} %copy-done.3, bf16[512,4096]{1,0:T(8,128)(2,1)} %weight.7), custom_call_target="tpu_custom_call" | custom-call | flops 4294967296 | bytes 4194304 | tf_op jit(solution)/shard_map/ring_products/pallas_call | solution.py:224
  25.5 1.0 copy-done
  26.4 1.1 slice_bitcast_fusion.12
  27.8 1.0 fusion.25
  28.8 2.8 %collective-permute-start.3 = (bf16[128,512]{1,0:T(8,128)(2,1)S(1)}, bf16[128,512]{1,0:T(8,128)(2,1)S(1)}, u32[]{:S(2)}, u32[]{:S(2)}) collective-permute-start(bf16[128,512]{1,0:T(8,128)(2,1)S(1)} %get-tuple-element.137), channel_id=1, source_target_pairs={{0,7},{1,0},{2,1},{3,2},{4,3},{5,4},{6,5},{7,6},{8,15},{9,8},{10,9... | collective-permute-start | bytes 393224 | tf_op jit(solution)/shard_map/ppermute | solution.py:325
  31.5 1.9 %collective-permute-done.3 = bf16[128,512]{1,0:T(8,128)(2,1)S(1)} collective-permute-done((bf16[128,512]{1,0:T(8,128)(2,1)S(1)}, bf16[128,512]{1,0:T(8,128)(2,1)S(1)}, u32[]{:S(2)}, u32[]{:S(2)}) %collective-permute-start.3) | collective-permute-done | bytes 131104 | tf_op jit(solution)/shard_map/ppermute | solution.py:325
  33.5 3.4 %collective-permute-done.2 = bf16[128,512]{1,0:T(8,128)(2,1)S(1)} collective-permute-done((bf16[128,512]{1,0:T(8,128)(2,1)S(1)}, bf16[128,512]{1,0:T(8,128)(2,1)S(1)}, u32[]{:S(2)}, u32[]{:S(2)}) %collective-permute-start.2) | collective-permute-done | bytes 131104 | tf_op jit(solution)/shard_map/ppermute | solution.py:324
  36.8 1.1 fusion.13
  37.9 0.2 collective-permute-start.5
  38.1 1.3 %collective-permute-start.4 = (bf16[128,512]{1,0:T(8,128)(2,1)S(1)}, bf16[128,512]{1,0:T(8,128)(2,1)S(1)}, u32[]{:S(2)}, u32[]{:S(2)}) collective-permute-start(bf16[128,512]{1,0:T(8,128)(2,1)S(1)} %get-tuple-element.136), channel_id=1, source_target_pairs={{0,1},{1,2},{2,3},{3,4},{4,5},{5,6},{6,7},{7,0},{8,9},{9,10},{10,1... | collective-permute-start | bytes 393224 | tf_op jit(solution)/shard_map/ppermute | solution.py:324
  39.5 2.6 %ring_products.5 = f32[3,128,512]{2,1,0:T(8,128)S(1)} custom-call(s32[1]{0:T(128)} %bitcast.2.place, bf16[128,512]{1,0:T(8,128)(2,1)S(1)} %copy-done.3, bf16[512,4096]{1,0:T(8,128)(2,1)} %weight.7), custom_call_target="tpu_custom_call" | custom-call | flops 4294967296 | bytes 4194304 | tf_op jit(solution)/shard_map/ring_products/pallas_call | solution.py:224
  42.2 1.0 collective-permute-done.4
  43.4 5.6 %band_rows.1 = (bf16[32,48,512]{2,1,0:T(8,128)(2,1)}, bf16[192,512]{1,0:T(8,128)(2,1)S(1)}, bf16[224,512]{1,0:T(8,128)(2,1)S(1)}, bf16[224,512]{1,0:T(8,128)(2,1)S(1)}) custom-call(s32[3]{0:T(128)S(1)} %and_select_fusion.turns, bf16[32,64,512]{2,1,0:T(8,128)(2,1)S(1)} %all-to-all-done.got, f32[3,3,512]{2,1,0:T(4,128)S(1)} %copy-done.4, ...), custom_call_target="tpu_custom_call" | custom-call | tf_op jit(solution)/shard_map/band_rows/pallas_call | solution.py:417
  48.9 1.6 %collective-permute-start.6 = (bf16[224,512]{1,0:T(8,128)(2,1)S(1)}, bf16[224,512]{1,0:T(8,128)(2,1)S(1)}, u32[]{:S(2)}, u32[]{:S(2)}) collective-permute-start(bf16[224,512]{1,0:T(8,128)(2,1)S(1)} %get-tuple-element.102), channel_id=1, source_target_pairs={{0,1},{1,2},{2,3},{3,4},{4,5},{5,6},{6,7},{7,0},{8,9},{9,10},{10,1... | collective-permute-start | bytes 688136 | tf_op jit(solution)/shard_map/ppermute | solution.py:324
  50.6 3.9 %collective-permute-start.7 = (bf16[224,512]{1,0:T(8,128)(2,1)S(1)}, bf16[224,512]{1,0:T(8,128)(2,1)S(1)}, u32[]{:S(2)}, u32[]{:S(2)}) collective-permute-start(bf16[224,512]{1,0:T(8,128)(2,1)S(1)} %get-tuple-element.103), channel_id=1, source_target_pairs={{0,7},{1,0},{2,1},{3,2},{4,3},{5,4},{6,5},{7,6},{8,15},{9,8},{10,9... | collective-permute-start | bytes 688136 | tf_op jit(solution)/shard_map/ppermute | solution.py:325
  54.5 3.0 %ring_products.6 = f32[4,192,512]{2,1,0:T(8,128)S(1)} custom-call(s32[1]{0:T(128)} %bitcast.2.place, bf16[192,512]{1,0:T(8,128)(2,1)S(1)} %get-tuple-element.109.gated, bf16[512,4096]{1,0:T(8,128)(2,1)} %weight.7), custom_call_target="tpu_custom_call" | custom-call | flops 6442450944 | bytes 4194304 | tf_op jit(solution)/shard_map/ring_products/pallas_call | solution.py:224
  57.6 0.3 collective-permute-done.6
  58.0 2.7 %collective-permute-start.9 = (bf16[192,512]{1,0:T(8,128)(2,1)S(1)}, bf16[192,512]{1,0:T(8,128)(2,1)S(1)}, u32[]{:S(2)}, u32[]{:S(2)}) collective-permute-start(bf16[192,512]{1,0:T(8,128)(2,1)S(1)} %get-tuple-element.129), channel_id=1, source_target_pairs={{0,7},{1,0},{2,1},{3,2},{4,3},{5,4},{6,5},{7,6},{8,15},{9,8},{10,9... | collective-permute-start | bytes 589832 | tf_op jit(solution)/shard_map/ppermute | solution.py:325
  60.7 9.1 %all-to-all-start.1 = ((bf16[32,48,512]{2,1,0:T(8,128)(2,1)}), bf16[32,48,512]{2,1,0:T(8,128)(2,1)}, u32[]{:S(2)}, u32[]{:S(2)}) async-start(bf16[32,48,512]{2,1,0:T(8,128)(2,1)} %get-tuple-element.116), calls=%async_computation.1 | async-start | bytes 3145728 | tf_op jit(solution)/shard_map/all_to_all | solution.py:319
  70.0 3.0 %collective-permute-start.11 = (bf16[192,512]{1,0:T(8,128)(2,1)S(1)}, bf16[192,512]{1,0:T(8,128)(2,1)S(1)}, u32[]{:S(2)}, u32[]{:S(2)}) collective-permute-start(bf16[192,512]{1,0:T(8,128)(2,1)S(1)} %get-tuple-element.127), channel_id=1, source_target_pairs={{0,7},{1,0},{2,1},{3,2},{4,3},{5,4},{6,5},{7,6},{8,15},{9,8},{10,9... | collective-permute-start | bytes 589832 | tf_op jit(solution)/shard_map/ppermute | solution.py:325
  73.0 2.7 %ring_products.7 = f32[3,192,512]{2,1,0:T(8,128)S(1)} custom-call(s32[1]{0:T(128)} %bitcast.2.place, bf16[192,512]{1,0:T(8,128)(2,1)S(1)} %get-tuple-element.109.gated, bf16[512,4096]{1,0:T(8,128)(2,1)} %weight.7), custom_call_target="tpu_custom_call" | custom-call | flops 6442450944 | bytes 4194304 | tf_op jit(solution)/shard_map/ring_products/pallas_call | solution.py:224
  75.7 1.3 %collective-permute-done.11 = bf16[192,512]{1,0:T(8,128)(2,1)S(1)} collective-permute-done((bf16[192,512]{1,0:T(8,128)(2,1)S(1)}, bf16[192,512]{1,0:T(8,128)(2,1)S(1)}, u32[]{:S(2)}, u32[]{:S(2)}) %collective-permute-start.11) | collective-permute-done | bytes 196640 | tf_op jit(solution)/shard_map/ppermute | solution.py:325
  77.0 3.2 %collective-permute-done.10 = bf16[192,512]{1,0:T(8,128)(2,1)S(1)} collective-permute-done((bf16[192,512]{1,0:T(8,128)(2,1)S(1)}, bf16[192,512]{1,0:T(8,128)(2,1)S(1)}, u32[]{:S(2)}, u32[]{:S(2)}) %collective-permute-start.10) | collective-permute-done | bytes 196640 | tf_op jit(solution)/shard_map/ppermute | solution.py:324
  80.4 0.4 collective-permute-start.13
  80.8 1.1 collective-permute-start.12
  82.0 3.6 %collective-permute-done.13 = bf16[192,512]{1,0:T(8,128)(2,1)S(1)} collective-permute-done((bf16[192,512]{1,0:T(8,128)(2,1)S(1)}, bf16[192,512]{1,0:T(8,128)(2,1)S(1)}, u32[]{:S(2)}, u32[]{:S(2)}) %collective-permute-start.13) | collective-permute-done | bytes 196640 | tf_op jit(solution)/shard_map/ppermute | solution.py:325
  85.6 1.6 %collective-permute-done.12 = bf16[192,512]{1,0:T(8,128)(2,1)S(1)} collective-permute-done((bf16[192,512]{1,0:T(8,128)(2,1)S(1)}, bf16[192,512]{1,0:T(8,128)(2,1)S(1)}, u32[]{:S(2)}, u32[]{:S(2)}) %collective-permute-start.12) | collective-permute-done | bytes 196640 | tf_op jit(solution)/shard_map/ppermute | solution.py:324
  87.2 0.2 multiply_reduce_fusion
  87.4 0.3 collective-permute-start.15
  87.7 1.2 collective-permute-start.14
  88.9 1.0 collective-permute-done.15
  89.9 1.5 %collective-permute-done.14 = f32[320]{0:T(512)S(1)} collective-permute-done((f32[320]{0:T(512)S(1)}, f32[320]{0:T(512)S(1)}, u32[]{:S(2)}, u32[]{:S(2)}) %collective-permute-start.14) | collective-permute-done | bytes 1312 | tf_op jit(solution)/shard_map/ppermute | solution.py:345
  91.4 0.7 all-to-all-done.1.back_hbm
  92.1 1.9 %collective-permute-start.17 = (f32[320]{0:T(512)S(1)}, f32[320]{0:T(512)S(1)}, u32[]{:S(2)}, u32[]{:S(2)}) collective-permute-start(f32[320]{0:T(512)S(1)} %get-tuple-element.118), channel_id=1, source_target_pairs={{0,5},{1,6},{2,7},{3,0},{4,1},{5,2},{6,3},{7,4},{8,13},{9,14},{10,... | collective-permute-start | bytes 3848 | tf_op jit(solution)/shard_map/ppermute | solution.py:345
  94.0 2.2 %collective-permute-start.16 = (f32[320]{0:T(512)S(1)}, f32[320]{0:T(512)S(1)}, u32[]{:S(2)}, u32[]{:S(2)}) collective-permute-start(f32[320]{0:T(512)S(1)} %get-tuple-element.117), channel_id=1, source_target_pairs={{0,3},{1,4},{2,5},{3,6},{4,7},{5,0},{6,1},{7,2},{8,11},{9,12},{10,... | collective-permute-start | bytes 3848 | tf_op jit(solution)/shard_map/ppermute | solution.py:345
  96.2 1.0 collective-permute-done.17
  97.1 2.3 %collective-permute-done.16 = f32[320]{0:T(512)S(1)} collective-permute-done((f32[320]{0:T(512)S(1)}, f32[320]{0:T(512)S(1)}, u32[]{:S(2)}, u32[]{:S(2)}) %collective-permute-start.16) | collective-permute-done | bytes 1312 | tf_op jit(solution)/shard_map/ppermute | solution.py:345
  99.8 0.8 copy.18
  100.6 11.8 %all-to-all-start.2 = ((bf16[32,3,2,512]{3,2,1,0:T(2,128)(2,1)}), bf16[32,3,2,512]{3,2,1,0:T(2,128)(2,1)S(1)}, u32[]{:S(2)}, u32[]{:S(2)}) async-start(bf16[32,3,2,512]{3,2,1,0:T(2,128)(2,1)} %bitcast.111), calls=%async_computation.2 | async-start | bytes 393216 | tf_op jit(solution)/shard_map/all_to_all | solution.py:319
  112.4 4.1 %last_rows.1 = (f32[80,16,512]{2,1,0:T(8,128)}, bf16[80,3,2,512]{3,2,1,0:T(2,128)(2,1)}) custom-call(bf16[32,48,512]{2,1,0:T(8,128)(2,1)} %all-to-all-done.1.back_hbm, bf16[4,3,80,512]{3,2,1,0:T(8,128)(2,1)} %bitcast.115, f32[16,16,512]{2,1,0:T(8,128)} %get-tuple-element.122.stay_hbm, s32[3,80]{1,0:T(4,128)} %finished.3), custom_call_target="tpu_custom_call" | custom-call | tf_op jit(solution)/shard_map/last_rows/pallas_call | solution.py:462
  116.5 4.1 %all-to-all-done.2 = bf16[32,3,2,512]{3,2,1,0:T(2,128)(2,1)S(1)} async-done(((bf16[32,3,2,512]{3,2,1,0:T(2,128)(2,1)}), bf16[32,3,2,512]{3,2,1,0:T(2,128)(2,1)S(1)}, u32[]{:S(2)}, u32[]{:S(2)}) %all-to-all-start.2) | async-done | bytes 196640 | tf_op jit(solution)/shard_map/all_to_all | solution.py:319
  120.6 0.1 copy.16
  120.9 0.8 maximum_maximum_fusion
  (50 shorter events, 1.6 us)
Async XLA Ops:
  6.8 9.9 %copy-start.3 = (bf16[128,512]{1,0:T(8,128)(2,1)S(1)}, bf16[128,512]{1,0:T(8,128)(2,1)}, u32[]{:S(2)}) copy-start(bf16[128,512]{1,0:T(8,128)(2,1)} %get-tuple-element.94.gated) | copy-start | bytes 393220
  6.8 36.6 %all-to-all-start = ((bf16[32,64,512]{2,1,0:T(8,128)(2,1)}), bf16[32,64,512]{2,1,0:T(8,128)(2,1)S(1)}, u32[]{:S(2)}, u32[]{:S(2)}) async-start(bf16[32,64,512]{2,1,0:T(8,128)(2,1)} %get-tuple-element.88), calls=%async_computation | async-start | bytes 4194304 | tf_op jit(solution)/shard_map/all_to_all | solution.py:319
  16.9 10.9 %collective-permute-start.1 = (bf16[64,512]{1,0:T(8,128)(2,1)S(1)}, bf16[64,512]{1,0:T(8,128)(2,1)S(1)}, u32[]{:S(2)}, u32[]{:S(2)}) collective-permute-start(bf16[64,512]{1,0:T(8,128)(2,1)S(1)} %get-tuple-element.143), channel_id=1, source_target_pairs={{0,7},{1,0},{2,1},{3,2},{4,3},{5,4},{6,5},{7,6},{8,15},{9,8},{10,9... | collective-permute-start | bytes 196616 | tf_op jit(solution)/shard_map/ppermute | solution.py:325
  22.5 5.2 %collective-permute-start = (bf16[64,512]{1,0:T(8,128)(2,1)S(1)}, bf16[64,512]{1,0:T(8,128)(2,1)S(1)}, u32[]{:S(2)}, u32[]{:S(2)}) collective-permute-start(bf16[64,512]{1,0:T(8,128)(2,1)S(1)} %get-tuple-element.144), channel_id=1, source_target_pairs={{0,1},{1,2},{2,3},{3,4},{4,5},{5,6},{6,7},{7,0},{8,9},{9,10},{10,1... | collective-permute-start | bytes 196616 | tf_op jit(solution)/shard_map/ppermute | solution.py:324
  22.5 5.0 %copy-start.7 = (s32[3,80]{1,0:T(4,128)S(1)}, s32[3,80]{1,0:T(4,128)}, u32[]{:S(2)}) copy-start(s32[3,80]{1,0:T(4,128)} %param.29) | copy-start | bytes 2884
  25.5 1.0 copy-start
  28.8 4.7 %collective-permute-start.3 = (bf16[128,512]{1,0:T(8,128)(2,1)S(1)}, bf16[128,512]{1,0:T(8,128)(2,1)S(1)}, u32[]{:S(2)}, u32[]{:S(2)}) collective-permute-start(bf16[128,512]{1,0:T(8,128)(2,1)S(1)} %get-tuple-element.137), channel_id=1, source_target_pairs={{0,7},{1,0},{2,1},{3,2},{4,3},{5,4},{6,5},{7,6},{8,15},{9,8},{10,9... | collective-permute-start | bytes 393224 | tf_op jit(solution)/shard_map/ppermute | solution.py:325
  31.5 5.3 %collective-permute-start.2 = (bf16[128,512]{1,0:T(8,128)(2,1)S(1)}, bf16[128,512]{1,0:T(8,128)(2,1)S(1)}, u32[]{:S(2)}, u32[]{:S(2)}) collective-permute-start(bf16[128,512]{1,0:T(8,128)(2,1)S(1)} %get-tuple-element.138), channel_id=1, source_target_pairs={{0,1},{1,2},{2,3},{3,4},{4,5},{5,6},{6,7},{7,0},{8,9},{9,10},{10,1... | collective-permute-start | bytes 393224 | tf_op jit(solution)/shard_map/ppermute | solution.py:324
  37.9 4.2 %collective-permute-start.5 = (bf16[128,512]{1,0:T(8,128)(2,1)S(1)}, bf16[128,512]{1,0:T(8,128)(2,1)S(1)}, u32[]{:S(2)}, u32[]{:S(2)}) collective-permute-start(bf16[128,512]{1,0:T(8,128)(2,1)S(1)} %get-tuple-element.135), channel_id=1, source_target_pairs={{0,7},{1,0},{2,1},{3,2},{4,3},{5,4},{6,5},{7,6},{8,15},{9,8},{10,9... | collective-permute-start | bytes 393224 | tf_op jit(solution)/shard_map/ppermute | solution.py:325
  38.1 5.0 %collective-permute-start.4 = (bf16[128,512]{1,0:T(8,128)(2,1)S(1)}, bf16[128,512]{1,0:T(8,128)(2,1)S(1)}, u32[]{:S(2)}, u32[]{:S(2)}) collective-permute-start(bf16[128,512]{1,0:T(8,128)(2,1)S(1)} %get-tuple-element.136), channel_id=1, source_target_pairs={{0,1},{1,2},{2,3},{3,4},{4,5},{5,6},{6,7},{7,0},{8,9},{9,10},{10,1... | collective-permute-start | bytes 393224 | tf_op jit(solution)/shard_map/ppermute | solution.py:324
  42.1 1.3 %copy-start.1 = (f32[16,512]{1,0:T(8,128)S(1)}, f32[16,512]{1,0:T(8,128)}, u32[]{:S(2)}) copy-start(f32[16,512]{1,0:T(8,128)} %poles.3) | copy-start | bytes 98308
  42.1 1.3 %copy-start.2 = (f32[16,512]{1,0:T(8,128)S(1)}, f32[16,512]{1,0:T(8,128)}, u32[]{:S(2)}) copy-start(f32[16,512]{1,0:T(8,128)} %residues.3) | copy-start | bytes 98308
  42.1 1.3 %copy-start.4 = (f32[3,3,512]{2,1,0:T(4,128)S(1)}, f32[3,3,512]{2,1,0:T(4,128)}, u32[]{:S(2)}) copy-start(f32[3,3,512]{2,1,0:T(4,128)} %taps.3) | copy-start | bytes 55300
  42.1 1.3 %copy-start.5 = (f32[512]{0:T(512)S(1)}, f32[512]{0:T(512)}, u32[]{:S(2)}) copy-start(f32[512]{0:T(512)} %param.25) | copy-start | bytes 6148
  48.9 9.0 %collective-permute-start.6 = (bf16[224,512]{1,0:T(8,128)(2,1)S(1)}, bf16[224,512]{1,0:T(8,128)(2,1)S(1)}, u32[]{:S(2)}, u32[]{:S(2)}) collective-permute-start(bf16[224,512]{1,0:T(8,128)(2,1)S(1)} %get-tuple-element.102), channel_id=1, source_target_pairs={{0,1},{1,2},{2,3},{3,4},{4,5},{5,6},{6,7},{7,0},{8,9},{9,10},{10,1... | collective-permute-start | bytes 688136 | tf_op jit(solution)/shard_map/ppermute | solution.py:324
  50.6 7.4 %collective-permute-start.7 = (bf16[224,512]{1,0:T(8,128)(2,1)S(1)}, bf16[224,512]{1,0:T(8,128)(2,1)S(1)}, u32[]{:S(2)}, u32[]{:S(2)}) collective-permute-start(bf16[224,512]{1,0:T(8,128)(2,1)S(1)} %get-tuple-element.103), channel_id=1, source_target_pairs={{0,7},{1,0},{2,1},{3,2},{4,3},{5,4},{6,5},{7,6},{8,15},{9,8},{10,9... | collective-permute-start | bytes 688136 | tf_op jit(solution)/shard_map/ppermute | solution.py:325
  58.0 11.9 %collective-permute-start.9 = (bf16[192,512]{1,0:T(8,128)(2,1)S(1)}, bf16[192,512]{1,0:T(8,128)(2,1)S(1)}, u32[]{:S(2)}, u32[]{:S(2)}) collective-permute-start(bf16[192,512]{1,0:T(8,128)(2,1)S(1)} %get-tuple-element.129), channel_id=1, source_target_pairs={{0,7},{1,0},{2,1},{3,2},{4,3},{5,4},{6,5},{7,6},{8,15},{9,8},{10,9... | collective-permute-start | bytes 589832 | tf_op jit(solution)/shard_map/ppermute | solution.py:325
  60.7 9.1 %collective-permute-start.8 = (bf16[192,512]{1,0:T(8,128)(2,1)S(1)}, bf16[192,512]{1,0:T(8,128)(2,1)S(1)}, u32[]{:S(2)}, u32[]{:S(2)}) collective-permute-start(bf16[192,512]{1,0:T(8,128)(2,1)S(1)} %get-tuple-element.130), channel_id=1, source_target_pairs={{0,1},{1,2},{2,3},{3,4},{4,5},{5,6},{6,7},{7,0},{8,9},{9,10},{10,1... | collective-permute-start | bytes 589832 | tf_op jit(solution)/shard_map/ppermute | solution.py:324
  60.7 31.4 %all-to-all-start.1 = ((bf16[32,48,512]{2,1,0:T(8,128)(2,1)}), bf16[32,48,512]{2,1,0:T(8,128)(2,1)}, u32[]{:S(2)}, u32[]{:S(2)}) async-start(bf16[32,48,512]{2,1,0:T(8,128)(2,1)} %get-tuple-element.116), calls=%async_computation.1 | async-start | bytes 3145728 | tf_op jit(solution)/shard_map/all_to_all | solution.py:319
  70.0 7.0 %collective-permute-start.11 = (bf16[192,512]{1,0:T(8,128)(2,1)S(1)}, bf16[192,512]{1,0:T(8,128)(2,1)S(1)}, u32[]{:S(2)}, u32[]{:S(2)}) collective-permute-start(bf16[192,512]{1,0:T(8,128)(2,1)S(1)} %get-tuple-element.127), channel_id=1, source_target_pairs={{0,7},{1,0},{2,1},{3,2},{4,3},{5,4},{6,5},{7,6},{8,15},{9,8},{10,9... | collective-permute-start | bytes 589832 | tf_op jit(solution)/shard_map/ppermute | solution.py:325
  73.0 7.2 %collective-permute-start.10 = (bf16[192,512]{1,0:T(8,128)(2,1)S(1)}, bf16[192,512]{1,0:T(8,128)(2,1)S(1)}, u32[]{:S(2)}, u32[]{:S(2)}) collective-permute-start(bf16[192,512]{1,0:T(8,128)(2,1)S(1)} %get-tuple-element.128), channel_id=1, source_target_pairs={{0,1},{1,2},{2,3},{3,4},{4,5},{5,6},{6,7},{7,0},{8,9},{9,10},{10,1... | collective-permute-start | bytes 589832 | tf_op jit(solution)/shard_map/ppermute | solution.py:324
  75.7 23.8 %copy-start.6 = (f32[512]{0:T(512)S(1)}, f32[512]{0:T(512)}, u32[]{:S(2)}) copy-start(f32[512]{0:T(512)} %param.27) | copy-start | bytes 6148
  80.4 5.2 %collective-permute-start.13 = (bf16[192,512]{1,0:T(8,128)(2,1)S(1)}, bf16[192,512]{1,0:T(8,128)(2,1)S(1)}, u32[]{:S(2)}, u32[]{:S(2)}) collective-permute-start(bf16[192,512]{1,0:T(8,128)(2,1)S(1)} %get-tuple-element.133), channel_id=1, source_target_pairs={{0,7},{1,0},{2,1},{3,2},{4,3},{5,4},{6,5},{7,6},{8,15},{9,8},{10,9... | collective-permute-start | bytes 589832 | tf_op jit(solution)/shard_map/ppermute | solution.py:325
  80.8 6.4 %collective-permute-start.12 = (bf16[192,512]{1,0:T(8,128)(2,1)S(1)}, bf16[192,512]{1,0:T(8,128)(2,1)S(1)}, u32[]{:S(2)}, u32[]{:S(2)}) collective-permute-start(bf16[192,512]{1,0:T(8,128)(2,1)S(1)} %get-tuple-element.134), channel_id=1, source_target_pairs={{0,1},{1,2},{2,3},{3,4},{4,5},{5,6},{6,7},{7,0},{8,9},{9,10},{10,1... | collective-permute-start | bytes 589832 | tf_op jit(solution)/shard_map/ppermute | solution.py:324
  87.4 2.4 %collective-permute-start.15 = (f32[320]{0:T(512)S(1)}, f32[320]{0:T(512)S(1)}, u32[]{:S(2)}, u32[]{:S(2)}) collective-permute-start(f32[320]{0:T(512)S(1)} %pad_maximum_fusion.1), channel_id=1, source_target_pairs={{0,7},{1,0},{2,1},{3,2},{4,3},{5,4},{6,5},{7,6},{8,15},{9,8},{10,9... | collective-permute-start | bytes 3848 | tf_op jit(solution)/shard_map/ppermute | solution.py:345
  87.7 3.6 %collective-permute-start.14 = (f32[320]{0:T(512)S(1)}, f32[320]{0:T(512)S(1)}, u32[]{:S(2)}, u32[]{:S(2)}) collective-permute-start(f32[320]{0:T(512)S(1)} %pad_maximum_fusion.1), channel_id=1, source_target_pairs={{0,1},{1,2},{2,3},{3,4},{4,5},{5,6},{6,7},{7,0},{8,9},{9,10},{10,1... | collective-permute-start | bytes 3848 | tf_op jit(solution)/shard_map/ppermute | solution.py:345
  92.1 5.0 %collective-permute-start.17 = (f32[320]{0:T(512)S(1)}, f32[320]{0:T(512)S(1)}, u32[]{:S(2)}, u32[]{:S(2)}) collective-permute-start(f32[320]{0:T(512)S(1)} %get-tuple-element.118), channel_id=1, source_target_pairs={{0,5},{1,6},{2,7},{3,0},{4,1},{5,2},{6,3},{7,4},{8,13},{9,14},{10,... | collective-permute-start | bytes 3848 | tf_op jit(solution)/shard_map/ppermute | solution.py:345
  94.0 5.4 %collective-permute-start.16 = (f32[320]{0:T(512)S(1)}, f32[320]{0:T(512)S(1)}, u32[]{:S(2)}, u32[]{:S(2)}) collective-permute-start(f32[320]{0:T(512)S(1)} %get-tuple-element.117), channel_id=1, source_target_pairs={{0,3},{1,4},{2,5},{3,6},{4,7},{5,0},{6,1},{7,2},{8,11},{9,12},{10,... | collective-permute-start | bytes 3848 | tf_op jit(solution)/shard_map/ppermute | solution.py:345
  100.6 20.0 %all-to-all-start.2 = ((bf16[32,3,2,512]{3,2,1,0:T(2,128)(2,1)}), bf16[32,3,2,512]{3,2,1,0:T(2,128)(2,1)S(1)}, u32[]{:S(2)}, u32[]{:S(2)}) async-start(bf16[32,3,2,512]{3,2,1,0:T(2,128)(2,1)} %bitcast.111), calls=%async_computation.2 | async-start | bytes 393216 | tf_op jit(solution)/shard_map/all_to_all | solution.py:319

commit v12 on v11

--- a/solution.py
+++ b/solution.py
@@ -19,8 +19,9 @@
     return jnp.concatenate([x] * (width // x.shape[-1]), axis=-1)
 
 
-def home_kernel(qkv_hbm, fir_hbm, state_hbm, taps, poles, residues, skip, finished, packed_hbm, *rest):
-    gated, stay_state, qkv_all, fir_all, state_all, packed_all, y_rows, sems = rest
+def home_kernel(qkv_hbm, fir_hbm, state_hbm, *rest):
+    small_hbm, (packed_hbm, gated_hbm, stay_hbm), rest = rest[:5], rest[5:8], rest[8:]
+    small_all, (gated, stay_state, qkv_all, fir_all, state_all, packed_all, y_rows, sems) = rest[:5], rest[5:]
     rows, width = 16, qkv_hbm.shape[-1]
     blocks = qkv_hbm.shape[2] // rows
 
@@ -36,16 +37,20 @@
         at = pl.ds(block * (rows // 2), rows // 2)
         return pltpu.make_async_copy(packed_all.at[at], packed_hbm.at[at], sems.at[3, block])
 
-    for block in range(2):
+    small = [
+        pltpu.make_async_copy(source, target, sems.at[4, i])
+        for i, (source, target) in enumerate(zip(small_hbm, small_all))
+    ]
+    for fetch in small:
+        fetch.start()
+    for block in (blocks - 1, *range(blocks - 1)):
         for fetch in fetches(block):
             fetch.start()
+    for fetch in small:
+        fetch.wait()
+    taps, poles, residues, skip, finished = small_all
 
     def first_step(block):
-        @pl.when(block + 2 < blocks)
-        def _():
-            for fetch in fetches(block + 2):
-                fetch.start()
-
         for fetch in fetches(block):
             fetch.wait()
         start = pl.multiple_of(block * rows, rows)
@@ -78,28 +83,6 @@
         gated[pl.ds(block * rows, rows)] = (f[0] * (y_rows[...] + skip[...] * product)).astype(BF16)
         return qkv, q0, l0, alive, modes
 
-    @pl.loop(0, blocks - 1)
-    def _(block):
-        qkv, q0, l0, alive, modes = first_step(block)
-        alive0 = alive[0]
-        packed = packed_all.at[pl.ds(pl.multiple_of(block * (rows // 2), rows // 2), rows // 2)]
-        for pair in range(rows // 2):
-            both = jnp.concatenate([modes[2 * pair], modes[2 * pair + 1]], axis=0)
-            packed[pair, 0 : 2 * MODES] = both.astype(BF16)
-        sent = [(x * alive0).astype(BF16) for x in q0 + l0]
-        sent += [qkv[t, j] for t in range(1, 4) for j in range(3)]
-        half = width // 2
-        sent.append(jnp.concatenate([alive[1][:, :half], alive[2][:, :half]], axis=-1).astype(BF16))
-        stacked = jnp.concatenate(sent, axis=0)
-        n = KINDS * rows
-        r = lax.broadcasted_iota(jnp.int32, (n, n), 0)
-        c = lax.broadcasted_iota(jnp.int32, (n, n), 1)
-        source = ((r >> 1) & 15) * rows + (r >> 5) * 2 + (r & 1)
-        order = jnp.where(c == source, 1.0, 0.0).astype(BF16)
-        moved = dot(order, stacked).reshape(rows // 2, 2 * KINDS, width)
-        packed[:, 2 * MODES :] = moved.astype(BF16)
-        store(block).start()
-
     qkv, q0, l0, alive, modes = first_step(blocks - 1)
     alive0 = alive[0]
     for r in range(rows):
@@ -122,14 +105,43 @@
         ).astype(BF16)
         if t < 3:
             lag0, lag1 = [x * live for x in q], [x * live for x in lag0]
+    stay_store = pltpu.make_async_copy(stay_state, stay_hbm, sems.at[3, blocks - 1])
+    stay_store.start()
+
+    @pl.loop(0, blocks - 1)
+    def _(block):
+        qkv, q0, l0, alive, modes = first_step(block)
+        alive0 = alive[0]
+        packed = packed_all.at[pl.ds(pl.multiple_of(block * (rows // 2), rows // 2), rows // 2)]
+        for pair in range(rows // 2):
+            both = jnp.concatenate([modes[2 * pair], modes[2 * pair + 1]], axis=0)
+            packed[pair, 0 : 2 * MODES] = both.astype(BF16)
+        sent = [(x * alive0).astype(BF16) for x in q0 + l0]
+        sent += [qkv[t, j] for t in range(1, 4) for j in range(3)]
+        half = width // 2
+        sent.append(jnp.concatenate([alive[1][:, :half], alive[2][:, :half]], axis=-1).astype(BF16))
+        stacked = jnp.concatenate(sent, axis=0)
+        n = KINDS * rows
+        r = lax.broadcasted_iota(jnp.int32, (n, n), 0)
+        c = lax.broadcasted_iota(jnp.int32, (n, n), 1)
+        source = ((r >> 1) & 15) * rows + (r >> 5) * 2 + (r & 1)
+        order = jnp.where(c == source, 1.0, 0.0).astype(BF16)
+        moved = dot(order, stacked).reshape(rows // 2, 2 * KINDS, width)
+        packed[:, 2 * MODES :] = moved.astype(BF16)
+        store(block).start()
+
+    gated_store = pltpu.make_async_copy(gated, gated_hbm, sems.at[5, 0])
+    gated_store.start()
+    stay_store.wait()
     for block in range(blocks - 1):
         store(block).wait()
+    gated_store.wait()
 
 
 def band_kernel(
-    turns, got, taps, poles, residues, skip, far_weight, ride, sent, gated, first_right, first_left, *scratch
+    turns, got, taps, poles, residues, skip, far_weight, ride, sent_hbm, gated, first_right, first_left, *scratch
 ):
-    lags, inputs, live, heads, products, y_rows, kinds = scratch
+    lags, inputs, live, heads, products, y_rows, kinds, sent, sem = scratch
     groups, _, width = got.shape
     rows = 2 * groups
 
@@ -200,12 +212,15 @@
         end = (g + turns[2]) & (groups - 1)
         sent[end, 0 : 2 * MODES] = jnp.concatenate(final, axis=0).astype(BF16)
 
+    store = pltpu.make_async_copy(sent, sent_hbm, sem)
+    store.start()
     gated[...] = y_rows[...].reshape(3 * rows, width).astype(BF16)
     half = 3 * rows // 2
     for way, first in enumerate((first_right, first_left)):
         load = dot(gated[way * half : (way + 1) * half], far_weight[...])
         first[:half] = load.astype(BF16)
         first[half:] = ride[way]
+    store.wait()
 
 
 def products_kernel(place, gated, weight, part):
@@ -375,22 +390,27 @@
 
     packed, gated_home, stay_state = pl.pallas_call(
         home_kernel,
-        in_specs=[pl.BlockSpec(memory_space=pl.ANY)] * 3
-        + [pl.BlockSpec(memory_space=pltpu.VMEM)] * 5,
-        out_specs=[pl.BlockSpec(memory_space=pl.ANY)]
-        + [pl.BlockSpec(memory_space=pltpu.VMEM)] * 2,
+        in_specs=[pl.BlockSpec(memory_space=pl.ANY)] * 8,
+        out_specs=[pl.BlockSpec(memory_space=pl.ANY)] * 3,
         out_shape=[
             jax.ShapeDtypeStruct((groups, 2 * MODES + 2 * KINDS, width), BF16),
             jax.ShapeDtypeStruct((slots + 48, width), BF16),
             jax.ShapeDtypeStruct((16, MODES, width), F32),
         ],
         scratch_shapes=[
+            pltpu.VMEM(fir_taps.shape, F32),
+            pltpu.VMEM(poles.shape, F32),
+            pltpu.VMEM(residues.shape, F32),
+            pltpu.VMEM(skip_row.shape, F32),
+            pltpu.VMEM(finished.shape, jnp.int32),
+            pltpu.VMEM((slots + 48, width), BF16),
+            pltpu.VMEM((16, MODES, width), F32),
             pltpu.VMEM(qkv_kinds.shape, BF16),
             pltpu.VMEM(fir_buffer.shape, BF16),
             pltpu.VMEM(modal_state.shape, F32),
             pltpu.VMEM((groups, 2 * MODES + 2 * KINDS, width), BF16),
             pltpu.VMEM((16, width), F32),
-            pltpu.SemaphoreType.DMA((4, slots // 16)),
+            pltpu.SemaphoreType.DMA((6, slots // 16)),
         ],
         compiler_params=pltpu.CompilerParams(vmem_limit_bytes=56 * 1024 * 1024),
         name="home_rows",
@@ -420,7 +440,8 @@
             pl.BlockSpec(memory_space=pltpu.SMEM),
         ]
         + [pl.BlockSpec(memory_space=pltpu.VMEM)] * 7,
-        out_specs=[pl.BlockSpec(memory_space=pltpu.VMEM)] * 4,
+        out_specs=[pl.BlockSpec(memory_space=pl.ANY)]
+        + [pl.BlockSpec(memory_space=pltpu.VMEM)] * 3,
         out_shape=[
             jax.ShapeDtypeStruct((groups, 2 * MODES + 16, width), BF16),
             jax.ShapeDtypeStruct((3 * moving, width), BF16),
@@ -435,6 +456,8 @@
             pltpu.VMEM((3, moving, width), F32),
             pltpu.VMEM((3, moving, width), F32),
             pltpu.VMEM((KINDS - 6, moving, width), BF16),
+            pltpu.VMEM((groups, 2 * MODES + 16, width), BF16),
+            pltpu.SemaphoreType.DMA,
         ],
         compiler_params=pltpu.CompilerParams(vmem_limit_bytes=40 * 1024 * 1024),
         name="band_rows",

time: 123 us -> 121 us (0.984)
  no operation moved by 1% of the time
where the time goes in v12:
time: 121 us
  starting transfers between devices  58.2 us (48%)
  waiting for transfers between devices  26.8 us (22%)
  Pallas kernels  25.8 us (21%)
  local copies, waits for them, and re-layouts  4.43 us (4%)
  other arithmetic  4.12 us (3%)
    all_to_all x3, starting transfers between devices, swap(): return lax.all_to_all(blocks, 'dp', split_axis=0, concat_axis=0, tiled=True)  29.5 us
    ppermute x7, starting transfers between devices, pass_on(): left = lax.ppermute(left, 'tensor', [(i, (i - 1) % n) for i in range(n)])  18.9 us
    pallas_call x4, Pallas kernels, products(): pl.pallas_call(products_kernel, grid_spec=pltpu.PrefetchScalarGridSpec(nu...  11.2 us
    ppermute x7, waiting for transfers between devices, pass_on(): right = lax.ppermute(right, 'tensor', [(i, (i + 1) % n) for i in range(n)])  9.4 us
    ppermute x7, waiting for transfers between devices, pass_on(): left = lax.ppermute(left, 'tensor', [(i, (i - 1) % n) for i in range(n)])  6.82 us
    ppermute x4, waiting for transfers between devices, sent_on(): return lax.ppermute(x, 'tensor', [(i, (i + away) % n) for i in range(n)])  5.71 us
    ppermute x4, starting transfers between devices, sent_on(): return lax.ppermute(x, 'tensor', [(i, (i + away) % n) for i in range(n)])  5.54 us
    pallas_call x1, Pallas kernels, per_device(): pl.pallas_call(band_kernel, in_specs=[pl.BlockSpec(memory_space=pltpu.SME...  5.36 us
  transfers between devices with their start and end apart: 21, of which 15 were waited for; matrix products, arithmetic and copies ran while one was open for 5% of the time, Pallas kernels for 13%

profile of v12, /device:TPU:1, one launch (start us, length us, event | category | flops | bytes accessed | tf_op | source)
XLA Modules:
  0.0 120.6 jit_solution(1801886780520107842)
XLA Ops:
  0.6 5.2 %home_rows.1 = (bf16[32,64,512]{2,1,0:T(8,128)(2,1)}, bf16[128,512]{1,0:T(8,128)(2,1)}, f32[16,16,512]{2,1,0:T(8,128)}) custom-call(bf16[4,3,80,512]{3,2,1,0:T(8,128)(2,1)} %bitcast.114, bf16[80,3,2,512]{3,2,1,0:T(2,128)(2,1)} %fir_hbm.1, f32[80,16,512]{2,1,0:T(8,128)} %state_hbm.1, f32[3,3,512]{2,1,0:T(4,128)} %taps.1, f32[16,512]{1,0:T(8,128)} %poles.1, ...), custom_call_target="tpu_custom_call" | custom-call | tf_op jit(solution)/shard_map/home_rows/pallas_call | solution.py:391
  5.8 8.7 %all-to-all-start = ((bf16[32,64,512]{2,1,0:T(8,128)(2,1)}), bf16[32,64,512]{2,1,0:T(8,128)(2,1)S(1)}, u32[]{:S(2)}, u32[]{:S(2)}) async-start(bf16[32,64,512]{2,1,0:T(8,128)(2,1)} %get-tuple-element.88), calls=%async_computation | async-start | bytes 4194304 | tf_op jit(solution)/shard_map/all_to_all | solution.py:334
  14.6 1.1 constant_dynamic-slice_fusion.far_weight
  15.7 0.2 convolution_convert_fusion
  15.9 5.7 %collective-permute-start.1 = (bf16[64,512]{1,0:T(8,128)(2,1)S(1)}, bf16[64,512]{1,0:T(8,128)(2,1)S(1)}, u32[]{:S(2)}, u32[]{:S(2)}) collective-permute-start(bf16[64,512]{1,0:T(8,128)(2,1)S(1)} %get-tuple-element.143), channel_id=1, source_target_pairs={{0,7},{1,0},{2,1},{3,2},{4,3},{5,4},{6,5},{7,6},{8,15},{9,8},{10,9... | collective-permute-start | bytes 196616 | tf_op jit(solution)/shard_map/ppermute | solution.py:340
  21.6 2.9 %ring_products.4 = f32[4,128,512]{2,1,0:T(8,128)S(1)} custom-call(s32[1]{0:T(128)} %bitcast.2.place, bf16[128,512]{1,0:T(8,128)(2,1)S(1)} %copy-done.3, bf16[512,4096]{1,0:T(8,128)(2,1)} %weight.7), custom_call_target="tpu_custom_call" | custom-call | flops 4294967296 | bytes 4194304 | tf_op jit(solution)/shard_map/ring_products/pallas_call | solution.py:239
  24.5 1.0 copy-done
  25.5 1.1 slice_bitcast_fusion.12
  26.8 1.0 fusion.25
  27.8 2.7 %collective-permute-start.3 = (bf16[128,512]{1,0:T(8,128)(2,1)S(1)}, bf16[128,512]{1,0:T(8,128)(2,1)S(1)}, u32[]{:S(2)}, u32[]{:S(2)}) collective-permute-start(bf16[128,512]{1,0:T(8,128)(2,1)S(1)} %get-tuple-element.137), channel_id=1, source_target_pairs={{0,7},{1,0},{2,1},{3,2},{4,3},{5,4},{6,5},{7,6},{8,15},{9,8},{10,9... | collective-permute-start | bytes 393224 | tf_op jit(solution)/shard_map/ppermute | solution.py:340
  30.6 1.9 %collective-permute-done.3 = bf16[128,512]{1,0:T(8,128)(2,1)S(1)} collective-permute-done((bf16[128,512]{1,0:T(8,128)(2,1)S(1)}, bf16[128,512]{1,0:T(8,128)(2,1)S(1)}, u32[]{:S(2)}, u32[]{:S(2)}) %collective-permute-start.3) | collective-permute-done | bytes 131104 | tf_op jit(solution)/shard_map/ppermute | solution.py:340
  32.5 3.4 %collective-permute-done.2 = bf16[128,512]{1,0:T(8,128)(2,1)S(1)} collective-permute-done((bf16[128,512]{1,0:T(8,128)(2,1)S(1)}, bf16[128,512]{1,0:T(8,128)(2,1)S(1)}, u32[]{:S(2)}, u32[]{:S(2)}) %collective-permute-start.2) | collective-permute-done | bytes 131104 | tf_op jit(solution)/shard_map/ppermute | solution.py:339
  35.9 1.1 fusion.13
  37.0 0.2 collective-permute-start.5
  37.2 1.4 %collective-permute-start.4 = (bf16[128,512]{1,0:T(8,128)(2,1)S(1)}, bf16[128,512]{1,0:T(8,128)(2,1)S(1)}, u32[]{:S(2)}, u32[]{:S(2)}) collective-permute-start(bf16[128,512]{1,0:T(8,128)(2,1)S(1)} %get-tuple-element.136), channel_id=1, source_target_pairs={{0,1},{1,2},{2,3},{3,4},{4,5},{5,6},{6,7},{7,0},{8,9},{9,10},{10,1... | collective-permute-start | bytes 393224 | tf_op jit(solution)/shard_map/ppermute | solution.py:339
  38.5 2.6 %ring_products.5 = f32[3,128,512]{2,1,0:T(8,128)S(1)} custom-call(s32[1]{0:T(128)} %bitcast.2.place, bf16[128,512]{1,0:T(8,128)(2,1)S(1)} %copy-done.3, bf16[512,4096]{1,0:T(8,128)(2,1)} %weight.7), custom_call_target="tpu_custom_call" | custom-call | flops 4294967296 | bytes 4194304 | tf_op jit(solution)/shard_map/ring_products/pallas_call | solution.py:239
  41.2 1.0 collective-permute-done.4
  42.4 5.4 %band_rows.1 = (bf16[32,48,512]{2,1,0:T(8,128)(2,1)}, bf16[192,512]{1,0:T(8,128)(2,1)S(1)}, bf16[224,512]{1,0:T(8,128)(2,1)S(1)}, bf16[224,512]{1,0:T(8,128)(2,1)S(1)}) custom-call(s32[3]{0:T(128)S(1)} %and_select_fusion.turns, bf16[32,64,512]{2,1,0:T(8,128)(2,1)S(1)} %all-to-all-done.got, f32[3,3,512]{2,1,0:T(4,128)S(1)} %copy-done.4, ...), custom_call_target="tpu_custom_call" | custom-call | tf_op jit(solution)/shard_map/band_rows/pallas_call | solution.py:437
  47.8 1.7 %collective-permute-start.6 = (bf16[224,512]{1,0:T(8,128)(2,1)S(1)}, bf16[224,512]{1,0:T(8,128)(2,1)S(1)}, u32[]{:S(2)}, u32[]{:S(2)}) collective-permute-start(bf16[224,512]{1,0:T(8,128)(2,1)S(1)} %get-tuple-element.102), channel_id=1, source_target_pairs={{0,1},{1,2},{2,3},{3,4},{4,5},{5,6},{6,7},{7,0},{8,9},{9,10},{10,1... | collective-permute-start | bytes 688136 | tf_op jit(solution)/shard_map/ppermute | solution.py:339
  49.5 4.0 %collective-permute-start.7 = (bf16[224,512]{1,0:T(8,128)(2,1)S(1)}, bf16[224,512]{1,0:T(8,128)(2,1)S(1)}, u32[]{:S(2)}, u32[]{:S(2)}) collective-permute-start(bf16[224,512]{1,0:T(8,128)(2,1)S(1)} %get-tuple-element.103), channel_id=1, source_target_pairs={{0,7},{1,0},{2,1},{3,2},{4,3},{5,4},{6,5},{7,6},{8,15},{9,8},{10,9... | collective-permute-start | bytes 688136 | tf_op jit(solution)/shard_map/ppermute | solution.py:340
  53.5 3.0 %ring_products.6 = f32[4,192,512]{2,1,0:T(8,128)S(1)} custom-call(s32[1]{0:T(128)} %bitcast.2.place, bf16[192,512]{1,0:T(8,128)(2,1)S(1)} %get-tuple-element.109.gated, bf16[512,4096]{1,0:T(8,128)(2,1)} %weight.7), custom_call_target="tpu_custom_call" | custom-call | flops 6442450944 | bytes 4194304 | tf_op jit(solution)/shard_map/ring_products/pallas_call | solution.py:239
  56.6 0.3 collective-permute-done.6
  56.9 2.8 %collective-permute-start.9 = (bf16[192,512]{1,0:T(8,128)(2,1)S(1)}, bf16[192,512]{1,0:T(8,128)(2,1)S(1)}, u32[]{:S(2)}, u32[]{:S(2)}) collective-permute-start(bf16[192,512]{1,0:T(8,128)(2,1)S(1)} %get-tuple-element.129), channel_id=1, source_target_pairs={{0,7},{1,0},{2,1},{3,2},{4,3},{5,4},{6,5},{7,6},{8,15},{9,8},{10,9... | collective-permute-start | bytes 589832 | tf_op jit(solution)/shard_map/ppermute | solution.py:340
  59.8 9.0 %all-to-all-start.1 = ((bf16[32,48,512]{2,1,0:T(8,128)(2,1)}), bf16[32,48,512]{2,1,0:T(8,128)(2,1)}, u32[]{:S(2)}, u32[]{:S(2)}) async-start(bf16[32,48,512]{2,1,0:T(8,128)(2,1)} %get-tuple-element.116), calls=%async_computation.1 | async-start | bytes 3145728 | tf_op jit(solution)/shard_map/all_to_all | solution.py:334
  68.9 3.0 %collective-permute-start.11 = (bf16[192,512]{1,0:T(8,128)(2,1)S(1)}, bf16[192,512]{1,0:T(8,128)(2,1)S(1)}, u32[]{:S(2)}, u32[]{:S(2)}) collective-permute-start(bf16[192,512]{1,0:T(8,128)(2,1)S(1)} %get-tuple-element.127), channel_id=1, source_target_pairs={{0,7},{1,0},{2,1},{3,2},{4,3},{5,4},{6,5},{7,6},{8,15},{9,8},{10,9... | collective-permute-start | bytes 589832 | tf_op jit(solution)/shard_map/ppermute | solution.py:340
  72.0 2.7 %ring_products.7 = f32[3,192,512]{2,1,0:T(8,128)S(1)} custom-call(s32[1]{0:T(128)} %bitcast.2.place, bf16[192,512]{1,0:T(8,128)(2,1)S(1)} %get-tuple-element.109.gated, bf16[512,4096]{1,0:T(8,128)(2,1)} %weight.7), custom_call_target="tpu_custom_call" | custom-call | flops 6442450944 | bytes 4194304 | tf_op jit(solution)/shard_map/ring_products/pallas_call | solution.py:239
  74.6 1.3 %collective-permute-done.11 = bf16[192,512]{1,0:T(8,128)(2,1)S(1)} collective-permute-done((bf16[192,512]{1,0:T(8,128)(2,1)S(1)}, bf16[192,512]{1,0:T(8,128)(2,1)S(1)}, u32[]{:S(2)}, u32[]{:S(2)}) %collective-permute-start.11) | collective-permute-done | bytes 196640 | tf_op jit(solution)/shard_map/ppermute | solution.py:340
  76.0 3.2 %collective-permute-done.10 = bf16[192,512]{1,0:T(8,128)(2,1)S(1)} collective-permute-done((bf16[192,512]{1,0:T(8,128)(2,1)S(1)}, bf16[192,512]{1,0:T(8,128)(2,1)S(1)}, u32[]{:S(2)}, u32[]{:S(2)}) %collective-permute-start.10) | collective-permute-done | bytes 196640 | tf_op jit(solution)/shard_map/ppermute | solution.py:339
  79.3 0.4 collective-permute-start.13
  79.7 1.1 collective-permute-start.12
  80.9 3.6 %collective-permute-done.13 = bf16[192,512]{1,0:T(8,128)(2,1)S(1)} collective-permute-done((bf16[192,512]{1,0:T(8,128)(2,1)S(1)}, bf16[192,512]{1,0:T(8,128)(2,1)S(1)}, u32[]{:S(2)}, u32[]{:S(2)}) %collective-permute-start.13) | collective-permute-done | bytes 196640 | tf_op jit(solution)/shard_map/ppermute | solution.py:340
  84.5 1.6 %collective-permute-done.12 = bf16[192,512]{1,0:T(8,128)(2,1)S(1)} collective-permute-done((bf16[192,512]{1,0:T(8,128)(2,1)S(1)}, bf16[192,512]{1,0:T(8,128)(2,1)S(1)}, u32[]{:S(2)}, u32[]{:S(2)}) %collective-permute-start.12) | collective-permute-done | bytes 196640 | tf_op jit(solution)/shard_map/ppermute | solution.py:339
  86.1 0.2 multiply_reduce_fusion
  86.3 0.3 collective-permute-start.15
  86.6 1.2 collective-permute-start.14
  87.8 1.0 collective-permute-done.15
  88.8 1.5 %collective-permute-done.14 = f32[320]{0:T(512)S(1)} collective-permute-done((f32[320]{0:T(512)S(1)}, f32[320]{0:T(512)S(1)}, u32[]{:S(2)}, u32[]{:S(2)}) %collective-permute-start.14) | collective-permute-done | bytes 1312 | tf_op jit(solution)/shard_map/ppermute | solution.py:360
  90.3 0.7 all-to-all-done.1.back_hbm
  91.0 1.9 %collective-permute-start.17 = (f32[320]{0:T(512)S(1)}, f32[320]{0:T(512)S(1)}, u32[]{:S(2)}, u32[]{:S(2)}) collective-permute-start(f32[320]{0:T(512)S(1)} %get-tuple-element.118), channel_id=1, source_target_pairs={{0,5},{1,6},{2,7},{3,0},{4,1},{5,2},{6,3},{7,4},{8,13},{9,14},{10,... | collective-permute-start | bytes 3848 | tf_op jit(solution)/shard_map/ppermute | solution.py:360
  92.9 2.2 %collective-permute-start.16 = (f32[320]{0:T(512)S(1)}, f32[320]{0:T(512)S(1)}, u32[]{:S(2)}, u32[]{:S(2)}) collective-permute-start(f32[320]{0:T(512)S(1)} %get-tuple-element.117), channel_id=1, source_target_pairs={{0,3},{1,4},{2,5},{3,6},{4,7},{5,0},{6,1},{7,2},{8,11},{9,12},{10,... | collective-permute-start | bytes 3848 | tf_op jit(solution)/shard_map/ppermute | solution.py:360
  95.1 1.0 collective-permute-done.17
  96.1 2.3 %collective-permute-done.16 = f32[320]{0:T(512)S(1)} collective-permute-done((f32[320]{0:T(512)S(1)}, f32[320]{0:T(512)S(1)}, u32[]{:S(2)}, u32[]{:S(2)}) %collective-permute-start.16) | collective-permute-done | bytes 1312 | tf_op jit(solution)/shard_map/ppermute | solution.py:360
  98.7 0.8 copy.18
  99.5 11.8 %all-to-all-start.2 = ((bf16[32,3,2,512]{3,2,1,0:T(2,128)(2,1)}), bf16[32,3,2,512]{3,2,1,0:T(2,128)(2,1)S(1)}, u32[]{:S(2)}, u32[]{:S(2)}) async-start(bf16[32,3,2,512]{3,2,1,0:T(2,128)(2,1)} %bitcast.111), calls=%async_computation.2 | async-start | bytes 393216 | tf_op jit(solution)/shard_map/all_to_all | solution.py:334
  111.3 4.1 %last_rows.1 = (f32[80,16,512]{2,1,0:T(8,128)}, bf16[80,3,2,512]{3,2,1,0:T(2,128)(2,1)}) custom-call(bf16[32,48,512]{2,1,0:T(8,128)(2,1)} %all-to-all-done.1.back_hbm, bf16[4,3,80,512]{3,2,1,0:T(8,128)(2,1)} %bitcast.115, f32[16,16,512]{2,1,0:T(8,128)} %get-tuple-element.122.stay_hbm, s32[3,80]{1,0:T(4,128)} %finished.1), custom_call_target="tpu_custom_call" | custom-call | tf_op jit(solution)/shard_map/last_rows/pallas_call | solution.py:485
  115.5 4.1 %all-to-all-done.2 = bf16[32,3,2,512]{3,2,1,0:T(2,128)(2,1)S(1)} async-done(((bf16[32,3,2,512]{3,2,1,0:T(2,128)(2,1)}), bf16[32,3,2,512]{3,2,1,0:T(2,128)(2,1)S(1)}, u32[]{:S(2)}, u32[]{:S(2)}) %all-to-all-start.2) | async-done | bytes 196640 | tf_op jit(solution)/shard_map/all_to_all | solution.py:334
  119.6 0.1 copy.16
  119.8 0.8 maximum_maximum_fusion
  (50 shorter events, 1.6 us)
Async XLA Ops:
  5.8 9.9 %copy-start.3 = (bf16[128,512]{1,0:T(8,128)(2,1)S(1)}, bf16[128,512]{1,0:T(8,128)(2,1)}, u32[]{:S(2)}) copy-start(bf16[128,512]{1,0:T(8,128)(2,1)} %get-tuple-element.94.gated) | copy-start | bytes 393220
  5.8 36.6 %all-to-all-start = ((bf16[32,64,512]{2,1,0:T(8,128)(2,1)}), bf16[32,64,512]{2,1,0:T(8,128)(2,1)S(1)}, u32[]{:S(2)}, u32[]{:S(2)}) async-start(bf16[32,64,512]{2,1,0:T(8,128)(2,1)} %get-tuple-element.88), calls=%async_computation | async-start | bytes 4194304 | tf_op jit(solution)/shard_map/all_to_all | solution.py:334
  15.9 10.9 %collective-permute-start.1 = (bf16[64,512]{1,0:T(8,128)(2,1)S(1)}, bf16[64,512]{1,0:T(8,128)(2,1)S(1)}, u32[]{:S(2)}, u32[]{:S(2)}) collective-permute-start(bf16[64,512]{1,0:T(8,128)(2,1)S(1)} %get-tuple-element.143), channel_id=1, source_target_pairs={{0,7},{1,0},{2,1},{3,2},{4,3},{5,4},{6,5},{7,6},{8,15},{9,8},{10,9... | collective-permute-start | bytes 196616 | tf_op jit(solution)/shard_map/ppermute | solution.py:340
  21.6 5.2 %collective-permute-start = (bf16[64,512]{1,0:T(8,128)(2,1)S(1)}, bf16[64,512]{1,0:T(8,128)(2,1)S(1)}, u32[]{:S(2)}, u32[]{:S(2)}) collective-permute-start(bf16[64,512]{1,0:T(8,128)(2,1)S(1)} %get-tuple-element.144), channel_id=1, source_target_pairs={{0,1},{1,2},{2,3},{3,4},{4,5},{5,6},{6,7},{7,0},{8,9},{9,10},{10,1... | collective-permute-start | bytes 196616 | tf_op jit(solution)/shard_map/ppermute | solution.py:339
  21.6 5.0 %copy-start.7 = (s32[3,80]{1,0:T(4,128)S(1)}, s32[3,80]{1,0:T(4,128)}, u32[]{:S(2)}) copy-start(s32[3,80]{1,0:T(4,128)} %param.29) | copy-start | bytes 2884
  24.5 1.0 copy-start
  27.8 4.7 %collective-permute-start.3 = (bf16[128,512]{1,0:T(8,128)(2,1)S(1)}, bf16[128,512]{1,0:T(8,128)(2,1)S(1)}, u32[]{:S(2)}, u32[]{:S(2)}) collective-permute-start(bf16[128,512]{1,0:T(8,128)(2,1)S(1)} %get-tuple-element.137), channel_id=1, source_target_pairs={{0,7},{1,0},{2,1},{3,2},{4,3},{5,4},{6,5},{7,6},{8,15},{9,8},{10,9... | collective-permute-start | bytes 393224 | tf_op jit(solution)/shard_map/ppermute | solution.py:340
  30.6 5.3 %collective-permute-start.2 = (bf16[128,512]{1,0:T(8,128)(2,1)S(1)}, bf16[128,512]{1,0:T(8,128)(2,1)S(1)}, u32[]{:S(2)}, u32[]{:S(2)}) collective-permute-start(bf16[128,512]{1,0:T(8,128)(2,1)S(1)} %get-tuple-element.138), channel_id=1, source_target_pairs={{0,1},{1,2},{2,3},{3,4},{4,5},{5,6},{6,7},{7,0},{8,9},{9,10},{10,1... | collective-permute-start | bytes 393224 | tf_op jit(solution)/shard_map/ppermute | solution.py:339
  37.0 4.2 %collective-permute-start.5 = (bf16[128,512]{1,0:T(8,128)(2,1)S(1)}, bf16[128,512]{1,0:T(8,128)(2,1)S(1)}, u32[]{:S(2)}, u32[]{:S(2)}) collective-permute-start(bf16[128,512]{1,0:T(8,128)(2,1)S(1)} %get-tuple-element.135), channel_id=1, source_target_pairs={{0,7},{1,0},{2,1},{3,2},{4,3},{5,4},{6,5},{7,6},{8,15},{9,8},{10,9... | collective-permute-start | bytes 393224 | tf_op jit(solution)/shard_map/ppermute | solution.py:340
  37.2 5.0 %collective-permute-start.4 = (bf16[128,512]{1,0:T(8,128)(2,1)S(1)}, bf16[128,512]{1,0:T(8,128)(2,1)S(1)}, u32[]{:S(2)}, u32[]{:S(2)}) collective-permute-start(bf16[128,512]{1,0:T(8,128)(2,1)S(1)} %get-tuple-element.136), channel_id=1, source_target_pairs={{0,1},{1,2},{2,3},{3,4},{4,5},{5,6},{6,7},{7,0},{8,9},{9,10},{10,1... | collective-permute-start | bytes 393224 | tf_op jit(solution)/shard_map/ppermute | solution.py:339
  41.1 1.3 %copy-start.1 = (f32[16,512]{1,0:T(8,128)S(1)}, f32[16,512]{1,0:T(8,128)}, u32[]{:S(2)}) copy-start(f32[16,512]{1,0:T(8,128)} %poles.1) | copy-start | bytes 98308
  41.1 1.3 %copy-start.2 = (f32[16,512]{1,0:T(8,128)S(1)}, f32[16,512]{1,0:T(8,128)}, u32[]{:S(2)}) copy-start(f32[16,512]{1,0:T(8,128)} %residues.1) | copy-start | bytes 98308
  41.1 1.3 %copy-start.4 = (f32[3,3,512]{2,1,0:T(4,128)S(1)}, f32[3,3,512]{2,1,0:T(4,128)}, u32[]{:S(2)}) copy-start(f32[3,3,512]{2,1,0:T(4,128)} %taps.1) | copy-start | bytes 55300
  41.2 1.3 %copy-start.5 = (f32[512]{0:T(512)S(1)}, f32[512]{0:T(512)}, u32[]{:S(2)}) copy-start(f32[512]{0:T(512)} %param.25) | copy-start | bytes 6148
  47.8 9.1 %collective-permute-start.6 = (bf16[224,512]{1,0:T(8,128)(2,1)S(1)}, bf16[224,512]{1,0:T(8,128)(2,1)S(1)}, u32[]{:S(2)}, u32[]{:S(2)}) collective-permute-start(bf16[224,512]{1,0:T(8,128)(2,1)S(1)} %get-tuple-element.102), channel_id=1, source_target_pairs={{0,1},{1,2},{2,3},{3,4},{4,5},{5,6},{6,7},{7,0},{8,9},{9,10},{10,1... | collective-permute-start | bytes 688136 | tf_op jit(solution)/shard_map/ppermute | solution.py:339
  49.5 7.4 %collective-permute-start.7 = (bf16[224,512]{1,0:T(8,128)(2,1)S(1)}, bf16[224,512]{1,0:T(8,128)(2,1)S(1)}, u32[]{:S(2)}, u32[]{:S(2)}) collective-permute-start(bf16[224,512]{1,0:T(8,128)(2,1)S(1)} %get-tuple-element.103), channel_id=1, source_target_pairs={{0,7},{1,0},{2,1},{3,2},{4,3},{5,4},{6,5},{7,6},{8,15},{9,8},{10,9... | collective-permute-start | bytes 688136 | tf_op jit(solution)/shard_map/ppermute | solution.py:340
  56.9 11.9 %collective-permute-start.9 = (bf16[192,512]{1,0:T(8,128)(2,1)S(1)}, bf16[192,512]{1,0:T(8,128)(2,1)S(1)}, u32[]{:S(2)}, u32[]{:S(2)}) collective-permute-start(bf16[192,512]{1,0:T(8,128)(2,1)S(1)} %get-tuple-element.129), channel_id=1, source_target_pairs={{0,7},{1,0},{2,1},{3,2},{4,3},{5,4},{6,5},{7,6},{8,15},{9,8},{10,9... | collective-permute-start | bytes 589832 | tf_op jit(solution)/shard_map/ppermute | solution.py:340
  59.8 9.0 %collective-permute-start.8 = (bf16[192,512]{1,0:T(8,128)(2,1)S(1)}, bf16[192,512]{1,0:T(8,128)(2,1)S(1)}, u32[]{:S(2)}, u32[]{:S(2)}) collective-permute-start(bf16[192,512]{1,0:T(8,128)(2,1)S(1)} %get-tuple-element.130), channel_id=1, source_target_pairs={{0,1},{1,2},{2,3},{3,4},{4,5},{5,6},{6,7},{7,0},{8,9},{9,10},{10,1... | collective-permute-start | bytes 589832 | tf_op jit(solution)/shard_map/ppermute | solution.py:339
  59.8 31.3 %all-to-all-start.1 = ((bf16[32,48,512]{2,1,0:T(8,128)(2,1)}), bf16[32,48,512]{2,1,0:T(8,128)(2,1)}, u32[]{:S(2)}, u32[]{:S(2)}) async-start(bf16[32,48,512]{2,1,0:T(8,128)(2,1)} %get-tuple-element.116), calls=%async_computation.1 | async-start | bytes 3145728 | tf_op jit(solution)/shard_map/all_to_all | solution.py:334
  68.9 7.0 %collective-permute-start.11 = (bf16[192,512]{1,0:T(8,128)(2,1)S(1)}, bf16[192,512]{1,0:T(8,128)(2,1)S(1)}, u32[]{:S(2)}, u32[]{:S(2)}) collective-permute-start(bf16[192,512]{1,0:T(8,128)(2,1)S(1)} %get-tuple-element.127), channel_id=1, source_target_pairs={{0,7},{1,0},{2,1},{3,2},{4,3},{5,4},{6,5},{7,6},{8,15},{9,8},{10,9... | collective-permute-start | bytes 589832 | tf_op jit(solution)/shard_map/ppermute | solution.py:340
  72.0 7.2 %collective-permute-start.10 = (bf16[192,512]{1,0:T(8,128)(2,1)S(1)}, bf16[192,512]{1,0:T(8,128)(2,1)S(1)}, u32[]{:S(2)}, u32[]{:S(2)}) collective-permute-start(bf16[192,512]{1,0:T(8,128)(2,1)S(1)} %get-tuple-element.128), channel_id=1, source_target_pairs={{0,1},{1,2},{2,3},{3,4},{4,5},{5,6},{6,7},{7,0},{8,9},{9,10},{10,1... | collective-permute-start | bytes 589832 | tf_op jit(solution)/shard_map/ppermute | solution.py:339
  74.6 23.8 %copy-start.6 = (f32[512]{0:T(512)S(1)}, f32[512]{0:T(512)}, u32[]{:S(2)}) copy-start(f32[512]{0:T(512)} %param.27) | copy-start | bytes 6148
  79.3 5.2 %collective-permute-start.13 = (bf16[192,512]{1,0:T(8,128)(2,1)S(1)}, bf16[192,512]{1,0:T(8,128)(2,1)S(1)}, u32[]{:S(2)}, u32[]{:S(2)}) collective-permute-start(bf16[192,512]{1,0:T(8,128)(2,1)S(1)} %get-tuple-element.133), channel_id=1, source_target_pairs={{0,7},{1,0},{2,1},{3,2},{4,3},{5,4},{6,5},{7,6},{8,15},{9,8},{10,9... | collective-permute-start | bytes 589832 | tf_op jit(solution)/shard_map/ppermute | solution.py:340
  79.7 6.4 %collective-permute-start.12 = (bf16[192,512]{1,0:T(8,128)(2,1)S(1)}, bf16[192,512]{1,0:T(8,128)(2,1)S(1)}, u32[]{:S(2)}, u32[]{:S(2)}) collective-permute-start(bf16[192,512]{1,0:T(8,128)(2,1)S(1)} %get-tuple-element.134), channel_id=1, source_target_pairs={{0,1},{1,2},{2,3},{3,4},{4,5},{5,6},{6,7},{7,0},{8,9},{9,10},{10,1... | collective-permute-start | bytes 589832 | tf_op jit(solution)/shard_map/ppermute | solution.py:339
  86.3 2.4 %collective-permute-start.15 = (f32[320]{0:T(512)S(1)}, f32[320]{0:T(512)S(1)}, u32[]{:S(2)}, u32[]{:S(2)}) collective-permute-start(f32[320]{0:T(512)S(1)} %pad_maximum_fusion.1), channel_id=1, source_target_pairs={{0,7},{1,0},{2,1},{3,2},{4,3},{5,4},{6,5},{7,6},{8,15},{9,8},{10,9... | collective-permute-start | bytes 3848 | tf_op jit(solution)/shard_map/ppermute | solution.py:360
  86.6 3.6 %collective-permute-start.14 = (f32[320]{0:T(512)S(1)}, f32[320]{0:T(512)S(1)}, u32[]{:S(2)}, u32[]{:S(2)}) collective-permute-start(f32[320]{0:T(512)S(1)} %pad_maximum_fusion.1), channel_id=1, source_target_pairs={{0,1},{1,2},{2,3},{3,4},{4,5},{5,6},{6,7},{7,0},{8,9},{9,10},{10,1... | collective-permute-start | bytes 3848 | tf_op jit(solution)/shard_map/ppermute | solution.py:360
  91.0 5.0 %collective-permute-start.17 = (f32[320]{0:T(512)S(1)}, f32[320]{0:T(512)S(1)}, u32[]{:S(2)}, u32[]{:S(2)}) collective-permute-start(f32[320]{0:T(512)S(1)} %get-tuple-element.118), channel_id=1, source_target_pairs={{0,5},{1,6},{2,7},{3,0},{4,1},{5,2},{6,3},{7,4},{8,13},{9,14},{10,... | collective-permute-start | bytes 3848 | tf_op jit(solution)/shard_map/ppermute | solution.py:360
  92.9 5.4 %collective-permute-start.16 = (f32[320]{0:T(512)S(1)}, f32[320]{0:T(512)S(1)}, u32[]{:S(2)}, u32[]{:S(2)}) collective-permute-start(f32[320]{0:T(512)S(1)} %get-tuple-element.117), channel_id=1, source_target_pairs={{0,3},{1,4},{2,5},{3,6},{4,7},{5,0},{6,1},{7,2},{8,11},{9,12},{10,... | collective-permute-start | bytes 3848 | tf_op jit(solution)/shard_map/ppermute | solution.py:360
  99.5 20.0 %all-to-all-start.2 = ((bf16[32,3,2,512]{3,2,1,0:T(2,128)(2,1)}), bf16[32,3,2,512]{3,2,1,0:T(2,128)(2,1)S(1)}, u32[]{:S(2)}, u32[]{:S(2)}) async-start(bf16[32,3,2,512]{3,2,1,0:T(2,128)(2,1)} %bitcast.111), calls=%async_computation.2 | async-start | bytes 393216 | tf_op jit(solution)/shard_map/all_to_all | solution.py:334

commit v13 on v12

--- a/solution.py
+++ b/solution.py
@@ -165,7 +165,7 @@
         if t < 2:
             live[t] = wide(dot(turn, kinds[9, :, t * half : (t + 1) * half]), width)
 
-    @pl.loop(0, rows // 8)
+    @pl.loop(0, rows // 8, unroll=2)
     def _(i):
         at = pl.ds(pl.multiple_of(i * 8, 8), 8)
         lag0 = [lags[j, at] for j in range(3)]
@@ -194,7 +194,7 @@
     last = lags[0:3].reshape(3 * rows, width).astype(BF16)
     sent[:, 2 * MODES :] = dot(order, last).reshape(groups, 16, width).astype(BF16)
 
-    @pl.loop(0, groups)
+    @pl.loop(0, groups, unroll=2)
     def _(g):
         final = []
         for side in range(2):

time: 121 us -> 121 us (level)
  no operation moved by 1% of the time
where the time goes in v13:
time: 121 us; the launch traced here: 120 us
  starting transfers between devices  58.2 us (48%)
  waiting for transfers between devices  26.8 us (22%)
  Pallas kernels  25.7 us (21%)
  local copies, waits for them, and re-layouts  4.43 us (4%)
  other arithmetic  4.12 us (3%)
    all_to_all x3, starting transfers between devices, swap(): return lax.all_to_all(blocks, 'dp', split_axis=0, concat_axis=0, tiled=True)  29.5 us
    ppermute x7, starting transfers between devices, pass_on(): left = lax.ppermute(left, 'tensor', [(i, (i - 1) % n) for i in range(n)])  18.9 us
    pallas_call x4, Pallas kernels, products(): pl.pallas_call(products_kernel, grid_spec=pltpu.PrefetchScalarGridSpec(nu...  11.2 us
    ppermute x7, waiting for transfers between devices, pass_on(): right = lax.ppermute(right, 'tensor', [(i, (i + 1) % n) for i in range(n)])  9.4 us
    ppermute x7, waiting for transfers between devices, pass_on(): left = lax.ppermute(left, 'tensor', [(i, (i - 1) % n) for i in range(n)])  6.82 us
    ppermute x4, waiting for transfers between devices, sent_on(): return lax.ppermute(x, 'tensor', [(i, (i + away) % n) for i in range(n)])  5.7 us
    ppermute x4, starting transfers between devices, sent_on(): return lax.ppermute(x, 'tensor', [(i, (i + away) % n) for i in range(n)])  5.53 us
    pallas_call x1, Pallas kernels, per_device(): pl.pallas_call(band_kernel, in_specs=[pl.BlockSpec(memory_space=pltpu.SME...  5.25 us
  transfers between devices with their start and end apart: 21, of which 15 were waited for; matrix products, arithmetic and copies ran while one was open for 5% of the time, Pallas kernels for 13%

profile of v13, /device:TPU:1, one launch (start us, length us, event | category | flops | bytes accessed | tf_op | source)
XLA Modules:
  0.0 120.4 jit_solution(5731633617516289960)
XLA Ops:
  0.6 5.2 %home_rows.1 = (bf16[32,64,512]{2,1,0:T(8,128)(2,1)}, bf16[128,512]{1,0:T(8,128)(2,1)}, f32[16,16,512]{2,1,0:T(8,128)}) custom-call(bf16[4,3,80,512]{3,2,1,0:T(8,128)(2,1)} %bitcast.114, bf16[80,3,2,512]{3,2,1,0:T(2,128)(2,1)} %fir_hbm.1, f32[80,16,512]{2,1,0:T(8,128)} %state_hbm.1, f32[3,3,512]{2,1,0:T(4,128)} %taps.1, f32[16,512]{1,0:T(8,128)} %poles.1, ...), custom_call_target="tpu_custom_call" | custom-call | tf_op jit(solution)/shard_map/home_rows/pallas_call | solution.py:391
  5.8 8.7 %all-to-all-start = ((bf16[32,64,512]{2,1,0:T(8,128)(2,1)}), bf16[32,64,512]{2,1,0:T(8,128)(2,1)S(1)}, u32[]{:S(2)}, u32[]{:S(2)}) async-start(bf16[32,64,512]{2,1,0:T(8,128)(2,1)} %get-tuple-element.88), calls=%async_computation | async-start | bytes 4194304 | tf_op jit(solution)/shard_map/all_to_all | solution.py:334
  14.6 1.1 constant_dynamic-slice_fusion.far_weight
  15.7 0.2 convolution_convert_fusion
  15.9 5.7 %collective-permute-start.1 = (bf16[64,512]{1,0:T(8,128)(2,1)S(1)}, bf16[64,512]{1,0:T(8,128)(2,1)S(1)}, u32[]{:S(2)}, u32[]{:S(2)}) collective-permute-start(bf16[64,512]{1,0:T(8,128)(2,1)S(1)} %get-tuple-element.143), channel_id=1, source_target_pairs={{0,7},{1,0},{2,1},{3,2},{4,3},{5,4},{6,5},{7,6},{8,15},{9,8},{10,9... | collective-permute-start | bytes 196616 | tf_op jit(solution)/shard_map/ppermute | solution.py:340
  21.6 2.9 %ring_products.4 = f32[4,128,512]{2,1,0:T(8,128)S(1)} custom-call(s32[1]{0:T(128)} %bitcast.2.place, bf16[128,512]{1,0:T(8,128)(2,1)S(1)} %copy-done.3, bf16[512,4096]{1,0:T(8,128)(2,1)} %weight.7), custom_call_target="tpu_custom_call" | custom-call | flops 4294967296 | bytes 4194304 | tf_op jit(solution)/shard_map/ring_products/pallas_call | solution.py:239
  24.5 1.0 copy-done
  25.5 1.1 slice_bitcast_fusion.12
  26.8 1.0 fusion.25
  27.8 2.7 %collective-permute-start.3 = (bf16[128,512]{1,0:T(8,128)(2,1)S(1)}, bf16[128,512]{1,0:T(8,128)(2,1)S(1)}, u32[]{:S(2)}, u32[]{:S(2)}) collective-permute-start(bf16[128,512]{1,0:T(8,128)(2,1)S(1)} %get-tuple-element.137), channel_id=1, source_target_pairs={{0,7},{1,0},{2,1},{3,2},{4,3},{5,4},{6,5},{7,6},{8,15},{9,8},{10,9... | collective-permute-start | bytes 393224 | tf_op jit(solution)/shard_map/ppermute | solution.py:340
  30.6 1.9 %collective-permute-done.3 = bf16[128,512]{1,0:T(8,128)(2,1)S(1)} collective-permute-done((bf16[128,512]{1,0:T(8,128)(2,1)S(1)}, bf16[128,512]{1,0:T(8,128)(2,1)S(1)}, u32[]{:S(2)}, u32[]{:S(2)}) %collective-permute-start.3) | collective-permute-done | bytes 131104 | tf_op jit(solution)/shard_map/ppermute | solution.py:340
  32.5 3.4 %collective-permute-done.2 = bf16[128,512]{1,0:T(8,128)(2,1)S(1)} collective-permute-done((bf16[128,512]{1,0:T(8,128)(2,1)S(1)}, bf16[128,512]{1,0:T(8,128)(2,1)S(1)}, u32[]{:S(2)}, u32[]{:S(2)}) %collective-permute-start.2) | collective-permute-done | bytes 131104 | tf_op jit(solution)/shard_map/ppermute | solution.py:339
  35.9 1.1 fusion.13
  37.0 0.2 collective-permute-start.5
  37.2 1.4 %collective-permute-start.4 = (bf16[128,512]{1,0:T(8,128)(2,1)S(1)}, bf16[128,512]{1,0:T(8,128)(2,1)S(1)}, u32[]{:S(2)}, u32[]{:S(2)}) collective-permute-start(bf16[128,512]{1,0:T(8,128)(2,1)S(1)} %get-tuple-element.136), channel_id=1, source_target_pairs={{0,1},{1,2},{2,3},{3,4},{4,5},{5,6},{6,7},{7,0},{8,9},{9,10},{10,1... | collective-permute-start | bytes 393224 | tf_op jit(solution)/shard_map/ppermute | solution.py:339
  38.5 2.6 %ring_products.5 = f32[3,128,512]{2,1,0:T(8,128)S(1)} custom-call(s32[1]{0:T(128)} %bitcast.2.place, bf16[128,512]{1,0:T(8,128)(2,1)S(1)} %copy-done.3, bf16[512,4096]{1,0:T(8,128)(2,1)} %weight.7), custom_call_target="tpu_custom_call" | custom-call | flops 4294967296 | bytes 4194304 | tf_op jit(solution)/shard_map/ring_products/pallas_call | solution.py:239
  41.2 1.0 collective-permute-done.4
  42.4 5.2 %band_rows.1 = (bf16[32,48,512]{2,1,0:T(8,128)(2,1)}, bf16[192,512]{1,0:T(8,128)(2,1)S(1)}, bf16[224,512]{1,0:T(8,128)(2,1)S(1)}, bf16[224,512]{1,0:T(8,128)(2,1)S(1)}) custom-call(s32[3]{0:T(128)S(1)} %and_select_fusion.turns, bf16[32,64,512]{2,1,0:T(8,128)(2,1)S(1)} %all-to-all-done.got, f32[3,3,512]{2,1,0:T(4,128)S(1)} %copy-done.4, ...), custom_call_target="tpu_custom_call" | custom-call | tf_op jit(solution)/shard_map/band_rows/pallas_call | solution.py:437
  47.7 1.7 %collective-permute-start.6 = (bf16[224,512]{1,0:T(8,128)(2,1)S(1)}, bf16[224,512]{1,0:T(8,128)(2,1)S(1)}, u32[]{:S(2)}, u32[]{:S(2)}) collective-permute-start(bf16[224,512]{1,0:T(8,128)(2,1)S(1)} %get-tuple-element.102), channel_id=1, source_target_pairs={{0,1},{1,2},{2,3},{3,4},{4,5},{5,6},{6,7},{7,0},{8,9},{9,10},{10,1... | collective-permute-start | bytes 688136 | tf_op jit(solution)/shard_map/ppermute | solution.py:339
  49.4 4.0 %collective-permute-start.7 = (bf16[224,512]{1,0:T(8,128)(2,1)S(1)}, bf16[224,512]{1,0:T(8,128)(2,1)S(1)}, u32[]{:S(2)}, u32[]{:S(2)}) collective-permute-start(bf16[224,512]{1,0:T(8,128)(2,1)S(1)} %get-tuple-element.103), channel_id=1, source_target_pairs={{0,7},{1,0},{2,1},{3,2},{4,3},{5,4},{6,5},{7,6},{8,15},{9,8},{10,9... | collective-permute-start | bytes 688136 | tf_op jit(solution)/shard_map/ppermute | solution.py:340
  53.4 3.0 %ring_products.6 = f32[4,192,512]{2,1,0:T(8,128)S(1)} custom-call(s32[1]{0:T(128)} %bitcast.2.place, bf16[192,512]{1,0:T(8,128)(2,1)S(1)} %get-tuple-element.109.gated, bf16[512,4096]{1,0:T(8,128)(2,1)} %weight.7), custom_call_target="tpu_custom_call" | custom-call | flops 6442450944 | bytes 4194304 | tf_op jit(solution)/shard_map/ring_products/pallas_call | solution.py:239
  56.5 0.3 collective-permute-done.6
  56.8 2.8 %collective-permute-start.9 = (bf16[192,512]{1,0:T(8,128)(2,1)S(1)}, bf16[192,512]{1,0:T(8,128)(2,1)S(1)}, u32[]{:S(2)}, u32[]{:S(2)}) collective-permute-start(bf16[192,512]{1,0:T(8,128)(2,1)S(1)} %get-tuple-element.129), channel_id=1, source_target_pairs={{0,7},{1,0},{2,1},{3,2},{4,3},{5,4},{6,5},{7,6},{8,15},{9,8},{10,9... | collective-permute-start | bytes 589832 | tf_op jit(solution)/shard_map/ppermute | solution.py:340
  59.6 9.0 %all-to-all-start.1 = ((bf16[32,48,512]{2,1,0:T(8,128)(2,1)}), bf16[32,48,512]{2,1,0:T(8,128)(2,1)}, u32[]{:S(2)}, u32[]{:S(2)}) async-start(bf16[32,48,512]{2,1,0:T(8,128)(2,1)} %get-tuple-element.116), calls=%async_computation.1 | async-start | bytes 3145728 | tf_op jit(solution)/shard_map/all_to_all | solution.py:334
  68.8 3.0 %collective-permute-start.11 = (bf16[192,512]{1,0:T(8,128)(2,1)S(1)}, bf16[192,512]{1,0:T(8,128)(2,1)S(1)}, u32[]{:S(2)}, u32[]{:S(2)}) collective-permute-start(bf16[192,512]{1,0:T(8,128)(2,1)S(1)} %get-tuple-element.127), channel_id=1, source_target_pairs={{0,7},{1,0},{2,1},{3,2},{4,3},{5,4},{6,5},{7,6},{8,15},{9,8},{10,9... | collective-permute-start | bytes 589832 | tf_op jit(solution)/shard_map/ppermute | solution.py:340
  71.9 2.7 %ring_products.7 = f32[3,192,512]{2,1,0:T(8,128)S(1)} custom-call(s32[1]{0:T(128)} %bitcast.2.place, bf16[192,512]{1,0:T(8,128)(2,1)S(1)} %get-tuple-element.109.gated, bf16[512,4096]{1,0:T(8,128)(2,1)} %weight.7), custom_call_target="tpu_custom_call" | custom-call | flops 6442450944 | bytes 4194304 | tf_op jit(solution)/shard_map/ring_products/pallas_call | solution.py:239
  74.5 1.3 %collective-permute-done.11 = bf16[192,512]{1,0:T(8,128)(2,1)S(1)} collective-permute-done((bf16[192,512]{1,0:T(8,128)(2,1)S(1)}, bf16[192,512]{1,0:T(8,128)(2,1)S(1)}, u32[]{:S(2)}, u32[]{:S(2)}) %collective-permute-start.11) | collective-permute-done | bytes 196640 | tf_op jit(solution)/shard_map/ppermute | solution.py:340
  75.8 3.2 %collective-permute-done.10 = bf16[192,512]{1,0:T(8,128)(2,1)S(1)} collective-permute-done((bf16[192,512]{1,0:T(8,128)(2,1)S(1)}, bf16[192,512]{1,0:T(8,128)(2,1)S(1)}, u32[]{:S(2)}, u32[]{:S(2)}) %collective-permute-start.10) | collective-permute-done | bytes 196640 | tf_op jit(solution)/shard_map/ppermute | solution.py:339
  79.2 0.4 collective-permute-start.13
  79.6 1.1 collective-permute-start.12
  80.8 3.6 %collective-permute-done.13 = bf16[192,512]{1,0:T(8,128)(2,1)S(1)} collective-permute-done((bf16[192,512]{1,0:T(8,128)(2,1)S(1)}, bf16[192,512]{1,0:T(8,128)(2,1)S(1)}, u32[]{:S(2)}, u32[]{:S(2)}) %collective-permute-start.13) | collective-permute-done | bytes 196640 | tf_op jit(solution)/shard_map/ppermute | solution.py:340
  84.4 1.6 %collective-permute-done.12 = bf16[192,512]{1,0:T(8,128)(2,1)S(1)} collective-permute-done((bf16[192,512]{1,0:T(8,128)(2,1)S(1)}, bf16[192,512]{1,0:T(8,128)(2,1)S(1)}, u32[]{:S(2)}, u32[]{:S(2)}) %collective-permute-start.12) | collective-permute-done | bytes 196640 | tf_op jit(solution)/shard_map/ppermute | solution.py:339
  86.0 0.2 multiply_reduce_fusion
  86.2 0.3 collective-permute-start.15
  86.5 1.2 collective-permute-start.14
  87.7 1.0 collective-permute-done.15
  88.7 1.5 %collective-permute-done.14 = f32[320]{0:T(512)S(1)} collective-permute-done((f32[320]{0:T(512)S(1)}, f32[320]{0:T(512)S(1)}, u32[]{:S(2)}, u32[]{:S(2)}) %collective-permute-start.14) | collective-permute-done | bytes 1312 | tf_op jit(solution)/shard_map/ppermute | solution.py:360
  90.2 0.7 all-to-all-done.1.back_hbm
  90.9 1.9 %collective-permute-start.17 = (f32[320]{0:T(512)S(1)}, f32[320]{0:T(512)S(1)}, u32[]{:S(2)}, u32[]{:S(2)}) collective-permute-start(f32[320]{0:T(512)S(1)} %get-tuple-element.118), channel_id=1, source_target_pairs={{0,5},{1,6},{2,7},{3,0},{4,1},{5,2},{6,3},{7,4},{8,13},{9,14},{10,... | collective-permute-start | bytes 3848 | tf_op jit(solution)/shard_map/ppermute | solution.py:360
  92.8 2.2 %collective-permute-start.16 = (f32[320]{0:T(512)S(1)}, f32[320]{0:T(512)S(1)}, u32[]{:S(2)}, u32[]{:S(2)}) collective-permute-start(f32[320]{0:T(512)S(1)} %get-tuple-element.117), channel_id=1, source_target_pairs={{0,3},{1,4},{2,5},{3,6},{4,7},{5,0},{6,1},{7,2},{8,11},{9,12},{10,... | collective-permute-start | bytes 3848 | tf_op jit(solution)/shard_map/ppermute | solution.py:360
  95.0 1.0 collective-permute-done.17
  95.9 2.3 %collective-permute-done.16 = f32[320]{0:T(512)S(1)} collective-permute-done((f32[320]{0:T(512)S(1)}, f32[320]{0:T(512)S(1)}, u32[]{:S(2)}, u32[]{:S(2)}) %collective-permute-start.16) | collective-permute-done | bytes 1312 | tf_op jit(solution)/shard_map/ppermute | solution.py:360
  98.6 0.8 copy.18
  99.4 11.8 %all-to-all-start.2 = ((bf16[32,3,2,512]{3,2,1,0:T(2,128)(2,1)}), bf16[32,3,2,512]{3,2,1,0:T(2,128)(2,1)S(1)}, u32[]{:S(2)}, u32[]{:S(2)}) async-start(bf16[32,3,2,512]{3,2,1,0:T(2,128)(2,1)} %bitcast.111), calls=%async_computation.2 | async-start | bytes 393216 | tf_op jit(solution)/shard_map/all_to_all | solution.py:334
  111.2 4.1 %last_rows.1 = (f32[80,16,512]{2,1,0:T(8,128)}, bf16[80,3,2,512]{3,2,1,0:T(2,128)(2,1)}) custom-call(bf16[32,48,512]{2,1,0:T(8,128)(2,1)} %all-to-all-done.1.back_hbm, bf16[4,3,80,512]{3,2,1,0:T(8,128)(2,1)} %bitcast.115, f32[16,16,512]{2,1,0:T(8,128)} %get-tuple-element.122.stay_hbm, s32[3,80]{1,0:T(4,128)} %finished.1), custom_call_target="tpu_custom_call" | custom-call | tf_op jit(solution)/shard_map/last_rows/pallas_call | solution.py:485
  115.4 4.1 %all-to-all-done.2 = bf16[32,3,2,512]{3,2,1,0:T(2,128)(2,1)S(1)} async-done(((bf16[32,3,2,512]{3,2,1,0:T(2,128)(2,1)}), bf16[32,3,2,512]{3,2,1,0:T(2,128)(2,1)S(1)}, u32[]{:S(2)}, u32[]{:S(2)}) %all-to-all-start.2) | async-done | bytes 196640 | tf_op jit(solution)/shard_map/all_to_all | solution.py:334
  119.5 0.1 copy.16
  119.7 0.8 maximum_maximum_fusion
  (50 shorter events, 1.6 us)
Async XLA Ops:
  5.8 9.9 %copy-start.3 = (bf16[128,512]{1,0:T(8,128)(2,1)S(1)}, bf16[128,512]{1,0:T(8,128)(2,1)}, u32[]{:S(2)}) copy-start(bf16[128,512]{1,0:T(8,128)(2,1)} %get-tuple-element.94.gated) | copy-start | bytes 393220
  5.8 36.6 %all-to-all-start = ((bf16[32,64,512]{2,1,0:T(8,128)(2,1)}), bf16[32,64,512]{2,1,0:T(8,128)(2,1)S(1)}, u32[]{:S(2)}, u32[]{:S(2)}) async-start(bf16[32,64,512]{2,1,0:T(8,128)(2,1)} %get-tuple-element.88), calls=%async_computation | async-start | bytes 4194304 | tf_op jit(solution)/shard_map/all_to_all | solution.py:334
  15.9 10.9 %collective-permute-start.1 = (bf16[64,512]{1,0:T(8,128)(2,1)S(1)}, bf16[64,512]{1,0:T(8,128)(2,1)S(1)}, u32[]{:S(2)}, u32[]{:S(2)}) collective-permute-start(bf16[64,512]{1,0:T(8,128)(2,1)S(1)} %get-tuple-element.143), channel_id=1, source_target_pairs={{0,7},{1,0},{2,1},{3,2},{4,3},{5,4},{6,5},{7,6},{8,15},{9,8},{10,9... | collective-permute-start | bytes 196616 | tf_op jit(solution)/shard_map/ppermute | solution.py:340
  21.6 5.2 %collective-permute-start = (bf16[64,512]{1,0:T(8,128)(2,1)S(1)}, bf16[64,512]{1,0:T(8,128)(2,1)S(1)}, u32[]{:S(2)}, u32[]{:S(2)}) collective-permute-start(bf16[64,512]{1,0:T(8,128)(2,1)S(1)} %get-tuple-element.144), channel_id=1, source_target_pairs={{0,1},{1,2},{2,3},{3,4},{4,5},{5,6},{6,7},{7,0},{8,9},{9,10},{10,1... | collective-permute-start | bytes 196616 | tf_op jit(solution)/shard_map/ppermute | solution.py:339
  21.6 5.0 %copy-start.7 = (s32[3,80]{1,0:T(4,128)S(1)}, s32[3,80]{1,0:T(4,128)}, u32[]{:S(2)}) copy-start(s32[3,80]{1,0:T(4,128)} %param.29) | copy-start | bytes 2884
  24.5 1.0 copy-start
  27.8 4.7 %collective-permute-start.3 = (bf16[128,512]{1,0:T(8,128)(2,1)S(1)}, bf16[128,512]{1,0:T(8,128)(2,1)S(1)}, u32[]{:S(2)}, u32[]{:S(2)}) collective-permute-start(bf16[128,512]{1,0:T(8,128)(2,1)S(1)} %get-tuple-element.137), channel_id=1, source_target_pairs={{0,7},{1,0},{2,1},{3,2},{4,3},{5,4},{6,5},{7,6},{8,15},{9,8},{10,9... | collective-permute-start | bytes 393224 | tf_op jit(solution)/shard_map/ppermute | solution.py:340
  30.6 5.3 %collective-permute-start.2 = (bf16[128,512]{1,0:T(8,128)(2,1)S(1)}, bf16[128,512]{1,0:T(8,128)(2,1)S(1)}, u32[]{:S(2)}, u32[]{:S(2)}) collective-permute-start(bf16[128,512]{1,0:T(8,128)(2,1)S(1)} %get-tuple-element.138), channel_id=1, source_target_pairs={{0,1},{1,2},{2,3},{3,4},{4,5},{5,6},{6,7},{7,0},{8,9},{9,10},{10,1... | collective-permute-start | bytes 393224 | tf_op jit(solution)/shard_map/ppermute | solution.py:339
  37.0 4.2 %collective-permute-start.5 = (bf16[128,512]{1,0:T(8,128)(2,1)S(1)}, bf16[128,512]{1,0:T(8,128)(2,1)S(1)}, u32[]{:S(2)}, u32[]{:S(2)}) collective-permute-start(bf16[128,512]{1,0:T(8,128)(2,1)S(1)} %get-tuple-element.135), channel_id=1, source_target_pairs={{0,7},{1,0},{2,1},{3,2},{4,3},{5,4},{6,5},{7,6},{8,15},{9,8},{10,9... | collective-permute-start | bytes 393224 | tf_op jit(solution)/shard_map/ppermute | solution.py:340
  37.2 5.0 %collective-permute-start.4 = (bf16[128,512]{1,0:T(8,128)(2,1)S(1)}, bf16[128,512]{1,0:T(8,128)(2,1)S(1)}, u32[]{:S(2)}, u32[]{:S(2)}) collective-permute-start(bf16[128,512]{1,0:T(8,128)(2,1)S(1)} %get-tuple-element.136), channel_id=1, source_target_pairs={{0,1},{1,2},{2,3},{3,4},{4,5},{5,6},{6,7},{7,0},{8,9},{9,10},{10,1... | collective-permute-start | bytes 393224 | tf_op jit(solution)/shard_map/ppermute | solution.py:339
  41.1 1.3 %copy-start.1 = (f32[16,512]{1,0:T(8,128)S(1)}, f32[16,512]{1,0:T(8,128)}, u32[]{:S(2)}) copy-start(f32[16,512]{1,0:T(8,128)} %poles.1) | copy-start | bytes 98308
  41.1 1.3 %copy-start.2 = (f32[16,512]{1,0:T(8,128)S(1)}, f32[16,512]{1,0:T(8,128)}, u32[]{:S(2)}) copy-start(f32[16,512]{1,0:T(8,128)} %residues.1) | copy-start | bytes 98308
  41.1 1.3 %copy-start.4 = (f32[3,3,512]{2,1,0:T(4,128)S(1)}, f32[3,3,512]{2,1,0:T(4,128)}, u32[]{:S(2)}) copy-start(f32[3,3,512]{2,1,0:T(4,128)} %taps.1) | copy-start | bytes 55300
  41.2 1.3 %copy-start.5 = (f32[512]{0:T(512)S(1)}, f32[512]{0:T(512)}, u32[]{:S(2)}) copy-start(f32[512]{0:T(512)} %param.25) | copy-start | bytes 6148
  47.7 9.1 %collective-permute-start.6 = (bf16[224,512]{1,0:T(8,128)(2,1)S(1)}, bf16[224,512]{1,0:T(8,128)(2,1)S(1)}, u32[]{:S(2)}, u32[]{:S(2)}) collective-permute-start(bf16[224,512]{1,0:T(8,128)(2,1)S(1)} %get-tuple-element.102), channel_id=1, source_target_pairs={{0,1},{1,2},{2,3},{3,4},{4,5},{5,6},{6,7},{7,0},{8,9},{9,10},{10,1... | collective-permute-start | bytes 688136 | tf_op jit(solution)/shard_map/ppermute | solution.py:339
  49.4 7.4 %collective-permute-start.7 = (bf16[224,512]{1,0:T(8,128)(2,1)S(1)}, bf16[224,512]{1,0:T(8,128)(2,1)S(1)}, u32[]{:S(2)}, u32[]{:S(2)}) collective-permute-start(bf16[224,512]{1,0:T(8,128)(2,1)S(1)} %get-tuple-element.103), channel_id=1, source_target_pairs={{0,7},{1,0},{2,1},{3,2},{4,3},{5,4},{6,5},{7,6},{8,15},{9,8},{10,9... | collective-permute-start | bytes 688136 | tf_op jit(solution)/shard_map/ppermute | solution.py:340
  56.8 11.9 %collective-permute-start.9 = (bf16[192,512]{1,0:T(8,128)(2,1)S(1)}, bf16[192,512]{1,0:T(8,128)(2,1)S(1)}, u32[]{:S(2)}, u32[]{:S(2)}) collective-permute-start(bf16[192,512]{1,0:T(8,128)(2,1)S(1)} %get-tuple-element.129), channel_id=1, source_target_pairs={{0,7},{1,0},{2,1},{3,2},{4,3},{5,4},{6,5},{7,6},{8,15},{9,8},{10,9... | collective-permute-start | bytes 589832 | tf_op jit(solution)/shard_map/ppermute | solution.py:340
  59.6 9.0 %collective-permute-start.8 = (bf16[192,512]{1,0:T(8,128)(2,1)S(1)}, bf16[192,512]{1,0:T(8,128)(2,1)S(1)}, u32[]{:S(2)}, u32[]{:S(2)}) collective-permute-start(bf16[192,512]{1,0:T(8,128)(2,1)S(1)} %get-tuple-element.130), channel_id=1, source_target_pairs={{0,1},{1,2},{2,3},{3,4},{4,5},{5,6},{6,7},{7,0},{8,9},{9,10},{10,1... | collective-permute-start | bytes 589832 | tf_op jit(solution)/shard_map/ppermute | solution.py:339
  59.6 31.3 %all-to-all-start.1 = ((bf16[32,48,512]{2,1,0:T(8,128)(2,1)}), bf16[32,48,512]{2,1,0:T(8,128)(2,1)}, u32[]{:S(2)}, u32[]{:S(2)}) async-start(bf16[32,48,512]{2,1,0:T(8,128)(2,1)} %get-tuple-element.116), calls=%async_computation.1 | async-start | bytes 3145728 | tf_op jit(solution)/shard_map/all_to_all | solution.py:334
  68.8 7.0 %collective-permute-start.11 = (bf16[192,512]{1,0:T(8,128)(2,1)S(1)}, bf16[192,512]{1,0:T(8,128)(2,1)S(1)}, u32[]{:S(2)}, u32[]{:S(2)}) collective-permute-start(bf16[192,512]{1,0:T(8,128)(2,1)S(1)} %get-tuple-element.127), channel_id=1, source_target_pairs={{0,7},{1,0},{2,1},{3,2},{4,3},{5,4},{6,5},{7,6},{8,15},{9,8},{10,9... | collective-permute-start | bytes 589832 | tf_op jit(solution)/shard_map/ppermute | solution.py:340
  71.8 7.2 %collective-permute-start.10 = (bf16[192,512]{1,0:T(8,128)(2,1)S(1)}, bf16[192,512]{1,0:T(8,128)(2,1)S(1)}, u32[]{:S(2)}, u32[]{:S(2)}) collective-permute-start(bf16[192,512]{1,0:T(8,128)(2,1)S(1)} %get-tuple-element.128), channel_id=1, source_target_pairs={{0,1},{1,2},{2,3},{3,4},{4,5},{5,6},{6,7},{7,0},{8,9},{9,10},{10,1... | collective-permute-start | bytes 589832 | tf_op jit(solution)/shard_map/ppermute | solution.py:339
  74.5 23.8 %copy-start.6 = (f32[512]{0:T(512)S(1)}, f32[512]{0:T(512)}, u32[]{:S(2)}) copy-start(f32[512]{0:T(512)} %param.27) | copy-start | bytes 6148
  79.2 5.2 %collective-permute-start.13 = (bf16[192,512]{1,0:T(8,128)(2,1)S(1)}, bf16[192,512]{1,0:T(8,128)(2,1)S(1)}, u32[]{:S(2)}, u32[]{:S(2)}) collective-permute-start(bf16[192,512]{1,0:T(8,128)(2,1)S(1)} %get-tuple-element.133), channel_id=1, source_target_pairs={{0,7},{1,0},{2,1},{3,2},{4,3},{5,4},{6,5},{7,6},{8,15},{9,8},{10,9... | collective-permute-start | bytes 589832 | tf_op jit(solution)/shard_map/ppermute | solution.py:340
  79.6 6.4 %collective-permute-start.12 = (bf16[192,512]{1,0:T(8,128)(2,1)S(1)}, bf16[192,512]{1,0:T(8,128)(2,1)S(1)}, u32[]{:S(2)}, u32[]{:S(2)}) collective-permute-start(bf16[192,512]{1,0:T(8,128)(2,1)S(1)} %get-tuple-element.134), channel_id=1, source_target_pairs={{0,1},{1,2},{2,3},{3,4},{4,5},{5,6},{6,7},{7,0},{8,9},{9,10},{10,1... | collective-permute-start | bytes 589832 | tf_op jit(solution)/shard_map/ppermute | solution.py:339
  86.2 2.4 %collective-permute-start.15 = (f32[320]{0:T(512)S(1)}, f32[320]{0:T(512)S(1)}, u32[]{:S(2)}, u32[]{:S(2)}) collective-permute-start(f32[320]{0:T(512)S(1)} %pad_maximum_fusion.1), channel_id=1, source_target_pairs={{0,7},{1,0},{2,1},{3,2},{4,3},{5,4},{6,5},{7,6},{8,15},{9,8},{10,9... | collective-permute-start | bytes 3848 | tf_op jit(solution)/shard_map/ppermute | solution.py:360
  86.5 3.6 %collective-permute-start.14 = (f32[320]{0:T(512)S(1)}, f32[320]{0:T(512)S(1)}, u32[]{:S(2)}, u32[]{:S(2)}) collective-permute-start(f32[320]{0:T(512)S(1)} %pad_maximum_fusion.1), channel_id=1, source_target_pairs={{0,1},{1,2},{2,3},{3,4},{4,5},{5,6},{6,7},{7,0},{8,9},{9,10},{10,1... | collective-permute-start | bytes 3848 | tf_op jit(solution)/shard_map/ppermute | solution.py:360
  90.9 5.0 %collective-permute-start.17 = (f32[320]{0:T(512)S(1)}, f32[320]{0:T(512)S(1)}, u32[]{:S(2)}, u32[]{:S(2)}) collective-permute-start(f32[320]{0:T(512)S(1)} %get-tuple-element.118), channel_id=1, source_target_pairs={{0,5},{1,6},{2,7},{3,0},{4,1},{5,2},{6,3},{7,4},{8,13},{9,14},{10,... | collective-permute-start | bytes 3848 | tf_op jit(solution)/shard_map/ppermute | solution.py:360
  92.8 5.4 %collective-permute-start.16 = (f32[320]{0:T(512)S(1)}, f32[320]{0:T(512)S(1)}, u32[]{:S(2)}, u32[]{:S(2)}) collective-permute-start(f32[320]{0:T(512)S(1)} %get-tuple-element.117), channel_id=1, source_target_pairs={{0,3},{1,4},{2,5},{3,6},{4,7},{5,0},{6,1},{7,2},{8,11},{9,12},{10,... | collective-permute-start | bytes 3848 | tf_op jit(solution)/shard_map/ppermute | solution.py:360
  99.4 20.0 %all-to-all-start.2 = ((bf16[32,3,2,512]{3,2,1,0:T(2,128)(2,1)}), bf16[32,3,2,512]{3,2,1,0:T(2,128)(2,1)S(1)}, u32[]{:S(2)}, u32[]{:S(2)}) async-start(bf16[32,3,2,512]{3,2,1,0:T(2,128)(2,1)} %bitcast.111), calls=%async_computation.2 | async-start | bytes 393216 | tf_op jit(solution)/shard_map/all_to_all | solution.py:334

commit v14 on v13

--- a/solution.py
+++ b/solution.py
@@ -359,10 +359,9 @@
     def sent_on(x, away):
         return lax.ppermute(x, "tensor", [(i, (i + away) % n) for i in range(n)])
 
-    below = squares + sent_on(squares, 1)
-    three = below + sent_on(squares, -1)
-    three, below, back = lax.optimization_barrier((three, below, back))
-    squares = three + (sent_on(three, 3) + sent_on(below, -3))
+    four = squares + (sent_on(squares, 1) + sent_on(squares, -1)) + sent_on(squares, 2)
+    four, back = lax.optimization_barrier((four, back))
+    squares = sent_on(four, 2) + sent_on(four, -2)
     return lax.rsqrt(squares / (n * own[0].shape[1]) + 1e-05)[:, None], back
 
 

time: 121 us -> 120 us (level)
    ppermute x4 -> x5, starting transfers between devices: 5.53 us -> 4.43 us  [sent_on(): return lax.ppermute(x, 'tensor', [(i, (i + away) % n) for i in range(n)])]
    ppermute x4 -> x5, waiting for transfers between devices: 5.7 us -> 6.55 us  [sent_on(): return lax.ppermute(x, 'tensor', [(i, (i + away) % n) for i in range(n)])]
  transfers between devices with their start and end apart: 21 -> 22, of which waited for: 15 -> 14; matrix products, arithmetic and copies ran while one was open for 5% -> 5% of each run, Pallas kernels for 13% -> 13%
where the time goes in v14:
time: 120 us
  starting transfers between devices  57.1 us (48%)
  waiting for transfers between devices  27 us (22%)
  Pallas kernels  25.7 us (21%)
  local copies, waits for them, and re-layouts  4.43 us (4%)
  other arithmetic  4.12 us (3%)
    all_to_all x3, starting transfers between devices, swap(): return lax.all_to_all(blocks, 'dp', split_axis=0, concat_axis=0, tiled=True)  29.6 us
    ppermute x7, starting transfers between devices, pass_on(): left = lax.ppermute(left, 'tensor', [(i, (i - 1) % n) for i in range(n)])  18.9 us
    pallas_call x4, Pallas kernels, products(): pl.pallas_call(products_kernel, grid_spec=pltpu.PrefetchScalarGridSpec(nu...  11.2 us
    ppermute x7, waiting for transfers between devices, pass_on(): right = lax.ppermute(right, 'tensor', [(i, (i + 1) % n) for i in range(n)])  9.4 us
    ppermute x7, waiting for transfers between devices, pass_on(): left = lax.ppermute(left, 'tensor', [(i, (i - 1) % n) for i in range(n)])  6.82 us
    ppermute x5, waiting for transfers between devices, sent_on(): return lax.ppermute(x, 'tensor', [(i, (i + away) % n) for i in range(n)])  6.55 us
    pallas_call x1, Pallas kernels, per_device(): pl.pallas_call(band_kernel, in_specs=[pl.BlockSpec(memory_space=pltpu.SME...  5.25 us
    pallas_call x1, Pallas kernels, per_device(): pl.pallas_call(home_kernel, in_specs=[pl.BlockSpec(memory_space=pl.ANY)]...  5.18 us
  transfers between devices with their start and end apart: 22, of which 14 were waited for; matrix products, arithmetic and copies ran while one was open for 5% of the time, Pallas kernels for 13%

profile of v14, /device:TPU:1, one launch (start us, length us, event | category | flops | bytes accessed | tf_op | source)
XLA Modules:
  0.0 119.5 jit_solution(15845051701377976462)
XLA Ops:
  0.6 5.2 %home_rows.1 = (bf16[32,64,512]{2,1,0:T(8,128)(2,1)}, bf16[128,512]{1,0:T(8,128)(2,1)}, f32[16,16,512]{2,1,0:T(8,128)}) custom-call(bf16[4,3,80,512]{3,2,1,0:T(8,128)(2,1)} %bitcast.114, bf16[80,3,2,512]{3,2,1,0:T(2,128)(2,1)} %fir_hbm.1, f32[80,16,512]{2,1,0:T(8,128)} %state_hbm.1, f32[3,3,512]{2,1,0:T(4,128)} %taps.1, f32[16,512]{1,0:T(8,128)} %poles.1, ...), custom_call_target="tpu_custom_call" | custom-call | tf_op jit(solution)/shard_map/home_rows/pallas_call | solution.py:390
  5.8 8.7 %all-to-all-start = ((bf16[32,64,512]{2,1,0:T(8,128)(2,1)}), bf16[32,64,512]{2,1,0:T(8,128)(2,1)S(1)}, u32[]{:S(2)}, u32[]{:S(2)}) async-start(bf16[32,64,512]{2,1,0:T(8,128)(2,1)} %get-tuple-element.87), calls=%async_computation | async-start | bytes 4194304 | tf_op jit(solution)/shard_map/all_to_all | solution.py:334
  14.6 1.1 constant_dynamic-slice_fusion.far_weight
  15.7 0.2 convolution_convert_fusion
  15.9 5.7 %collective-permute-start.1 = (bf16[64,512]{1,0:T(8,128)(2,1)S(1)}, bf16[64,512]{1,0:T(8,128)(2,1)S(1)}, u32[]{:S(2)}, u32[]{:S(2)}) collective-permute-start(bf16[64,512]{1,0:T(8,128)(2,1)S(1)} %get-tuple-element.139), channel_id=1, source_target_pairs={{0,7},{1,0},{2,1},{3,2},{4,3},{5,4},{6,5},{7,6},{8,15},{9,8},{10,9... | collective-permute-start | bytes 196616 | tf_op jit(solution)/shard_map/ppermute | solution.py:340
  21.6 2.9 %ring_products.4 = f32[4,128,512]{2,1,0:T(8,128)S(1)} custom-call(s32[1]{0:T(128)} %bitcast.2.place, bf16[128,512]{1,0:T(8,128)(2,1)S(1)} %copy-done.3, bf16[512,4096]{1,0:T(8,128)(2,1)} %weight.7), custom_call_target="tpu_custom_call" | custom-call | flops 4294967296 | bytes 4194304 | tf_op jit(solution)/shard_map/ring_products/pallas_call | solution.py:239
  24.5 1.0 copy-done
  25.5 1.1 slice_bitcast_fusion.12
  26.8 1.0 fusion.25
  27.8 2.7 %collective-permute-start.3 = (bf16[128,512]{1,0:T(8,128)(2,1)S(1)}, bf16[128,512]{1,0:T(8,128)(2,1)S(1)}, u32[]{:S(2)}, u32[]{:S(2)}) collective-permute-start(bf16[128,512]{1,0:T(8,128)(2,1)S(1)} %get-tuple-element.133), channel_id=1, source_target_pairs={{0,7},{1,0},{2,1},{3,2},{4,3},{5,4},{6,5},{7,6},{8,15},{9,8},{10,9... | collective-permute-start | bytes 393224 | tf_op jit(solution)/shard_map/ppermute | solution.py:340
  30.6 1.9 %collective-permute-done.3 = bf16[128,512]{1,0:T(8,128)(2,1)S(1)} collective-permute-done((bf16[128,512]{1,0:T(8,128)(2,1)S(1)}, bf16[128,512]{1,0:T(8,128)(2,1)S(1)}, u32[]{:S(2)}, u32[]{:S(2)}) %collective-permute-start.3) | collective-permute-done | bytes 131104 | tf_op jit(solution)/shard_map/ppermute | solution.py:340
  32.5 3.4 %collective-permute-done.2 = bf16[128,512]{1,0:T(8,128)(2,1)S(1)} collective-permute-done((bf16[128,512]{1,0:T(8,128)(2,1)S(1)}, bf16[128,512]{1,0:T(8,128)(2,1)S(1)}, u32[]{:S(2)}, u32[]{:S(2)}) %collective-permute-start.2) | collective-permute-done | bytes 131104 | tf_op jit(solution)/shard_map/ppermute | solution.py:339
  35.9 1.1 fusion.13
  37.0 0.2 collective-permute-start.5
  37.2 1.4 %collective-permute-start.4 = (bf16[128,512]{1,0:T(8,128)(2,1)S(1)}, bf16[128,512]{1,0:T(8,128)(2,1)S(1)}, u32[]{:S(2)}, u32[]{:S(2)}) collective-permute-start(bf16[128,512]{1,0:T(8,128)(2,1)S(1)} %get-tuple-element.132), channel_id=1, source_target_pairs={{0,1},{1,2},{2,3},{3,4},{4,5},{5,6},{6,7},{7,0},{8,9},{9,10},{10,1... | collective-permute-start | bytes 393224 | tf_op jit(solution)/shard_map/ppermute | solution.py:339
  38.5 2.6 %ring_products.5 = f32[3,128,512]{2,1,0:T(8,128)S(1)} custom-call(s32[1]{0:T(128)} %bitcast.2.place, bf16[128,512]{1,0:T(8,128)(2,1)S(1)} %copy-done.3, bf16[512,4096]{1,0:T(8,128)(2,1)} %weight.7), custom_call_target="tpu_custom_call" | custom-call | flops 4294967296 | bytes 4194304 | tf_op jit(solution)/shard_map/ring_products/pallas_call | solution.py:239
  41.2 1.0 collective-permute-done.4
  42.4 5.2 %band_rows.1 = (bf16[32,48,512]{2,1,0:T(8,128)(2,1)}, bf16[192,512]{1,0:T(8,128)(2,1)S(1)}, bf16[224,512]{1,0:T(8,128)(2,1)S(1)}, bf16[224,512]{1,0:T(8,128)(2,1)S(1)}) custom-call(s32[3]{0:T(128)S(1)} %and_select_fusion.turns, bf16[32,64,512]{2,1,0:T(8,128)(2,1)S(1)} %all-to-all-done.got, f32[3,3,512]{2,1,0:T(4,128)S(1)} %copy-done.4, ...), custom_call_target="tpu_custom_call" | custom-call | tf_op jit(solution)/shard_map/band_rows/pallas_call | solution.py:436
  47.7 1.7 %collective-permute-start.6 = (bf16[224,512]{1,0:T(8,128)(2,1)S(1)}, bf16[224,512]{1,0:T(8,128)(2,1)S(1)}, u32[]{:S(2)}, u32[]{:S(2)}) collective-permute-start(bf16[224,512]{1,0:T(8,128)(2,1)S(1)} %get-tuple-element.101), channel_id=1, source_target_pairs={{0,1},{1,2},{2,3},{3,4},{4,5},{5,6},{6,7},{7,0},{8,9},{9,10},{10,1... | collective-permute-start | bytes 688136 | tf_op jit(solution)/shard_map/ppermute | solution.py:339
  49.4 4.0 %collective-permute-start.7 = (bf16[224,512]{1,0:T(8,128)(2,1)S(1)}, bf16[224,512]{1,0:T(8,128)(2,1)S(1)}, u32[]{:S(2)}, u32[]{:S(2)}) collective-permute-start(bf16[224,512]{1,0:T(8,128)(2,1)S(1)} %get-tuple-element.102), channel_id=1, source_target_pairs={{0,7},{1,0},{2,1},{3,2},{4,3},{5,4},{6,5},{7,6},{8,15},{9,8},{10,9... | collective-permute-start | bytes 688136 | tf_op jit(solution)/shard_map/ppermute | solution.py:340
  53.4 3.0 %ring_products.6 = f32[4,192,512]{2,1,0:T(8,128)S(1)} custom-call(s32[1]{0:T(128)} %bitcast.2.place, bf16[192,512]{1,0:T(8,128)(2,1)S(1)} %get-tuple-element.108.gated, bf16[512,4096]{1,0:T(8,128)(2,1)} %weight.7), custom_call_target="tpu_custom_call" | custom-call | flops 6442450944 | bytes 4194304 | tf_op jit(solution)/shard_map/ring_products/pallas_call | solution.py:239
  56.5 0.3 collective-permute-done.6
  56.8 2.8 %collective-permute-start.9 = (bf16[192,512]{1,0:T(8,128)(2,1)S(1)}, bf16[192,512]{1,0:T(8,128)(2,1)S(1)}, u32[]{:S(2)}, u32[]{:S(2)}) collective-permute-start(bf16[192,512]{1,0:T(8,128)(2,1)S(1)} %get-tuple-element.125), channel_id=1, source_target_pairs={{0,7},{1,0},{2,1},{3,2},{4,3},{5,4},{6,5},{7,6},{8,15},{9,8},{10,9... | collective-permute-start | bytes 589832 | tf_op jit(solution)/shard_map/ppermute | solution.py:340
  59.6 9.0 %all-to-all-start.1 = ((bf16[32,48,512]{2,1,0:T(8,128)(2,1)}), bf16[32,48,512]{2,1,0:T(8,128)(2,1)}, u32[]{:S(2)}, u32[]{:S(2)}) async-start(bf16[32,48,512]{2,1,0:T(8,128)(2,1)} %get-tuple-element.115), calls=%async_computation.1 | async-start | bytes 3145728 | tf_op jit(solution)/shard_map/all_to_all | solution.py:334
  68.7 0.1 fusion.3
  68.8 3.0 %collective-permute-start.11 = (bf16[192,512]{1,0:T(8,128)(2,1)S(1)}, bf16[192,512]{1,0:T(8,128)(2,1)S(1)}, u32[]{:S(2)}, u32[]{:S(2)}) collective-permute-start(bf16[192,512]{1,0:T(8,128)(2,1)S(1)} %get-tuple-element.123), channel_id=1, source_target_pairs={{0,7},{1,0},{2,1},{3,2},{4,3},{5,4},{6,5},{7,6},{8,15},{9,8},{10,9... | collective-permute-start | bytes 589832 | tf_op jit(solution)/shard_map/ppermute | solution.py:340
  71.9 2.7 %ring_products.7 = f32[3,192,512]{2,1,0:T(8,128)S(1)} custom-call(s32[1]{0:T(128)} %bitcast.2.place, bf16[192,512]{1,0:T(8,128)(2,1)S(1)} %get-tuple-element.108.gated, bf16[512,4096]{1,0:T(8,128)(2,1)} %weight.7), custom_call_target="tpu_custom_call" | custom-call | flops 6442450944 | bytes 4194304 | tf_op jit(solution)/shard_map/ring_products/pallas_call | solution.py:239
  74.5 1.3 %collective-permute-done.11 = bf16[192,512]{1,0:T(8,128)(2,1)S(1)} collective-permute-done((bf16[192,512]{1,0:T(8,128)(2,1)S(1)}, bf16[192,512]{1,0:T(8,128)(2,1)S(1)}, u32[]{:S(2)}, u32[]{:S(2)}) %collective-permute-start.11) | collective-permute-done | bytes 196640 | tf_op jit(solution)/shard_map/ppermute | solution.py:340
  75.8 3.2 %collective-permute-done.10 = bf16[192,512]{1,0:T(8,128)(2,1)S(1)} collective-permute-done((bf16[192,512]{1,0:T(8,128)(2,1)S(1)}, bf16[192,512]{1,0:T(8,128)(2,1)S(1)}, u32[]{:S(2)}, u32[]{:S(2)}) %collective-permute-start.10) | collective-permute-done | bytes 196640 | tf_op jit(solution)/shard_map/ppermute | solution.py:339
  79.2 0.4 collective-permute-start.13
  79.6 1.1 collective-permute-start.12
  80.7 0.1 multiply_reduce_fusion.1
  80.8 3.6 %collective-permute-done.13 = bf16[192,512]{1,0:T(8,128)(2,1)S(1)} collective-permute-done((bf16[192,512]{1,0:T(8,128)(2,1)S(1)}, bf16[192,512]{1,0:T(8,128)(2,1)S(1)}, u32[]{:S(2)}, u32[]{:S(2)}) %collective-permute-start.13) | collective-permute-done | bytes 196640 | tf_op jit(solution)/shard_map/ppermute | solution.py:340
  84.4 1.6 %collective-permute-done.12 = bf16[192,512]{1,0:T(8,128)(2,1)S(1)} collective-permute-done((bf16[192,512]{1,0:T(8,128)(2,1)S(1)}, bf16[192,512]{1,0:T(8,128)(2,1)S(1)}, u32[]{:S(2)}, u32[]{:S(2)}) %collective-permute-start.12) | collective-permute-done | bytes 196640 | tf_op jit(solution)/shard_map/ppermute | solution.py:339
  86.0 0.2 multiply_reduce_fusion
  86.2 2.0 %collective-permute-start.15 = (f32[320]{0:T(512)S(1)}, f32[320]{0:T(512)S(1)}, u32[]{:S(2)}, u32[]{:S(2)}) collective-permute-start(f32[320]{0:T(512)S(1)} %pad_maximum_fusion.1), channel_id=1, source_target_pairs={{0,7},{1,0},{2,1},{3,2},{4,3},{5,4},{6,5},{7,6},{8,15},{9,8},{10,9... | collective-permute-start | bytes 3848 | tf_op jit(solution)/shard_map/ppermute | solution.py:360
  88.3 2.5 %collective-permute-done.16 = f32[320]{0:T(512)S(1)} collective-permute-done((f32[320]{0:T(512)S(1)}, f32[320]{0:T(512)S(1)}, u32[]{:S(2)}, u32[]{:S(2)}) %collective-permute-start.16) | collective-permute-done | bytes 1312 | tf_op jit(solution)/shard_map/ppermute | solution.py:360
  90.8 1.5 %collective-permute-done.14 = f32[320]{0:T(512)S(1)} collective-permute-done((f32[320]{0:T(512)S(1)}, f32[320]{0:T(512)S(1)}, u32[]{:S(2)}, u32[]{:S(2)}) %collective-permute-start.14) | collective-permute-done | bytes 1312 | tf_op jit(solution)/shard_map/ppermute | solution.py:360
  92.4 0.4 collective-permute-start.18
  92.7 2.0 %collective-permute-start.17 = (f32[320]{0:T(512)S(1)}, f32[320]{0:T(512)S(1)}, u32[]{:S(2)}, u32[]{:S(2)}) collective-permute-start(f32[320]{0:T(512)S(1)} %add_add_fusion), channel_id=1, source_target_pairs={{0,2},{1,3},{2,4},{3,5},{4,6},{5,7},{6,0},{7,1},{8,10},{9,11},{10,... | collective-permute-start | bytes 3848 | tf_op jit(solution)/shard_map/ppermute | solution.py:360
  94.8 1.0 collective-permute-done.18
  95.8 1.5 %collective-permute-done.17 = f32[320]{0:T(512)S(1)} collective-permute-done((f32[320]{0:T(512)S(1)}, f32[320]{0:T(512)S(1)}, u32[]{:S(2)}, u32[]{:S(2)}) %collective-permute-start.17) | collective-permute-done | bytes 1312 | tf_op jit(solution)/shard_map/ppermute | solution.py:360
  97.7 0.8 copy.18
  98.5 11.8 %all-to-all-start.2 = ((bf16[32,3,2,512]{3,2,1,0:T(2,128)(2,1)}), bf16[32,3,2,512]{3,2,1,0:T(2,128)(2,1)S(1)}, u32[]{:S(2)}, u32[]{:S(2)}) async-start(bf16[32,3,2,512]{3,2,1,0:T(2,128)(2,1)} %bitcast.111), calls=%async_computation.2 | async-start | bytes 393216 | tf_op jit(solution)/shard_map/all_to_all | solution.py:334
  110.3 4.1 %last_rows.1 = (f32[80,16,512]{2,1,0:T(8,128)}, bf16[80,3,2,512]{3,2,1,0:T(2,128)(2,1)}) custom-call(bf16[32,48,512]{2,1,0:T(8,128)(2,1)} %all-to-all-done.1.back_hbm, bf16[4,3,80,512]{3,2,1,0:T(8,128)(2,1)} %bitcast.115, f32[16,16,512]{2,1,0:T(8,128)} %get-tuple-element.120.stay_hbm, s32[3,80]{1,0:T(4,128)} %finished.1), custom_call_target="tpu_custom_call" | custom-call | tf_op jit(solution)/shard_map/last_rows/pallas_call | solution.py:484
  114.5 4.1 %all-to-all-done.2 = bf16[32,3,2,512]{3,2,1,0:T(2,128)(2,1)S(1)} async-done(((bf16[32,3,2,512]{3,2,1,0:T(2,128)(2,1)}), bf16[32,3,2,512]{3,2,1,0:T(2,128)(2,1)S(1)}, u32[]{:S(2)}, u32[]{:S(2)}) %all-to-all-start.2) | async-done | bytes 196640 | tf_op jit(solution)/shard_map/all_to_all | solution.py:334
  118.6 0.1 copy.16
  118.8 0.8 maximum_maximum_fusion
  (52 shorter events, 1.4 us)
Async XLA Ops:
  5.8 9.9 %copy-start.3 = (bf16[128,512]{1,0:T(8,128)(2,1)S(1)}, bf16[128,512]{1,0:T(8,128)(2,1)}, u32[]{:S(2)}) copy-start(bf16[128,512]{1,0:T(8,128)(2,1)} %get-tuple-element.93.gated) | copy-start | bytes 393220
  5.8 36.6 %all-to-all-start = ((bf16[32,64,512]{2,1,0:T(8,128)(2,1)}), bf16[32,64,512]{2,1,0:T(8,128)(2,1)S(1)}, u32[]{:S(2)}, u32[]{:S(2)}) async-start(bf16[32,64,512]{2,1,0:T(8,128)(2,1)} %get-tuple-element.87), calls=%async_computation | async-start | bytes 4194304 | tf_op jit(solution)/shard_map/all_to_all | solution.py:334
  15.9 10.9 %collective-permute-start.1 = (bf16[64,512]{1,0:T(8,128)(2,1)S(1)}, bf16[64,512]{1,0:T(8,128)(2,1)S(1)}, u32[]{:S(2)}, u32[]{:S(2)}) collective-permute-start(bf16[64,512]{1,0:T(8,128)(2,1)S(1)} %get-tuple-element.139), channel_id=1, source_target_pairs={{0,7},{1,0},{2,1},{3,2},{4,3},{5,4},{6,5},{7,6},{8,15},{9,8},{10,9... | collective-permute-start | bytes 196616 | tf_op jit(solution)/shard_map/ppermute | solution.py:340
  21.6 5.2 %collective-permute-start = (bf16[64,512]{1,0:T(8,128)(2,1)S(1)}, bf16[64,512]{1,0:T(8,128)(2,1)S(1)}, u32[]{:S(2)}, u32[]{:S(2)}) collective-permute-start(bf16[64,512]{1,0:T(8,128)(2,1)S(1)} %get-tuple-element.140), channel_id=1, source_target_pairs={{0,1},{1,2},{2,3},{3,4},{4,5},{5,6},{6,7},{7,0},{8,9},{9,10},{10,1... | collective-permute-start | bytes 196616 | tf_op jit(solution)/shard_map/ppermute | solution.py:339
  21.6 5.0 %copy-start.7 = (s32[3,80]{1,0:T(4,128)S(1)}, s32[3,80]{1,0:T(4,128)}, u32[]{:S(2)}) copy-start(s32[3,80]{1,0:T(4,128)} %param.29) | copy-start | bytes 2884
  24.5 1.0 copy-start
  27.8 4.7 %collective-permute-start.3 = (bf16[128,512]{1,0:T(8,128)(2,1)S(1)}, bf16[128,512]{1,0:T(8,128)(2,1)S(1)}, u32[]{:S(2)}, u32[]{:S(2)}) collective-permute-start(bf16[128,512]{1,0:T(8,128)(2,1)S(1)} %get-tuple-element.133), channel_id=1, source_target_pairs={{0,7},{1,0},{2,1},{3,2},{4,3},{5,4},{6,5},{7,6},{8,15},{9,8},{10,9... | collective-permute-start | bytes 393224 | tf_op jit(solution)/shard_map/ppermute | solution.py:340
  30.6 5.3 %collective-permute-start.2 = (bf16[128,512]{1,0:T(8,128)(2,1)S(1)}, bf16[128,512]{1,0:T(8,128)(2,1)S(1)}, u32[]{:S(2)}, u32[]{:S(2)}) collective-permute-start(bf16[128,512]{1,0:T(8,128)(2,1)S(1)} %get-tuple-element.134), channel_id=1, source_target_pairs={{0,1},{1,2},{2,3},{3,4},{4,5},{5,6},{6,7},{7,0},{8,9},{9,10},{10,1... | collective-permute-start | bytes 393224 | tf_op jit(solution)/shard_map/ppermute | solution.py:339
  37.0 4.2 %collective-permute-start.5 = (bf16[128,512]{1,0:T(8,128)(2,1)S(1)}, bf16[128,512]{1,0:T(8,128)(2,1)S(1)}, u32[]{:S(2)}, u32[]{:S(2)}) collective-permute-start(bf16[128,512]{1,0:T(8,128)(2,1)S(1)} %get-tuple-element.131), channel_id=1, source_target_pairs={{0,7},{1,0},{2,1},{3,2},{4,3},{5,4},{6,5},{7,6},{8,15},{9,8},{10,9... | collective-permute-start | bytes 393224 | tf_op jit(solution)/shard_map/ppermute | solution.py:340
  37.2 5.0 %collective-permute-start.4 = (bf16[128,512]{1,0:T(8,128)(2,1)S(1)}, bf16[128,512]{1,0:T(8,128)(2,1)S(1)}, u32[]{:S(2)}, u32[]{:S(2)}) collective-permute-start(bf16[128,512]{1,0:T(8,128)(2,1)S(1)} %get-tuple-element.132), channel_id=1, source_target_pairs={{0,1},{1,2},{2,3},{3,4},{4,5},{5,6},{6,7},{7,0},{8,9},{9,10},{10,1... | collective-permute-start | bytes 393224 | tf_op jit(solution)/shard_map/ppermute | solution.py:339
  41.1 1.3 %copy-start.1 = (f32[16,512]{1,0:T(8,128)S(1)}, f32[16,512]{1,0:T(8,128)}, u32[]{:S(2)}) copy-start(f32[16,512]{1,0:T(8,128)} %poles.1) | copy-start | bytes 98308
  41.1 1.3 %copy-start.2 = (f32[16,512]{1,0:T(8,128)S(1)}, f32[16,512]{1,0:T(8,128)}, u32[]{:S(2)}) copy-start(f32[16,512]{1,0:T(8,128)} %residues.1) | copy-start | bytes 98308
  41.1 1.3 %copy-start.4 = (f32[3,3,512]{2,1,0:T(4,128)S(1)}, f32[3,3,512]{2,1,0:T(4,128)}, u32[]{:S(2)}) copy-start(f32[3,3,512]{2,1,0:T(4,128)} %taps.1) | copy-start | bytes 55300
  41.2 1.3 %copy-start.5 = (f32[512]{0:T(512)S(1)}, f32[512]{0:T(512)}, u32[]{:S(2)}) copy-start(f32[512]{0:T(512)} %param.25) | copy-start | bytes 6148
  47.7 9.1 %collective-permute-start.6 = (bf16[224,512]{1,0:T(8,128)(2,1)S(1)}, bf16[224,512]{1,0:T(8,128)(2,1)S(1)}, u32[]{:S(2)}, u32[]{:S(2)}) collective-permute-start(bf16[224,512]{1,0:T(8,128)(2,1)S(1)} %get-tuple-element.101), channel_id=1, source_target_pairs={{0,1},{1,2},{2,3},{3,4},{4,5},{5,6},{6,7},{7,0},{8,9},{9,10},{10,1... | collective-permute-start | bytes 688136 | tf_op jit(solution)/shard_map/ppermute | solution.py:339
  49.4 7.4 %collective-permute-start.7 = (bf16[224,512]{1,0:T(8,128)(2,1)S(1)}, bf16[224,512]{1,0:T(8,128)(2,1)S(1)}, u32[]{:S(2)}, u32[]{:S(2)}) collective-permute-start(bf16[224,512]{1,0:T(8,128)(2,1)S(1)} %get-tuple-element.102), channel_id=1, source_target_pairs={{0,7},{1,0},{2,1},{3,2},{4,3},{5,4},{6,5},{7,6},{8,15},{9,8},{10,9... | collective-permute-start | bytes 688136 | tf_op jit(solution)/shard_map/ppermute | solution.py:340
  56.8 11.9 %collective-permute-start.9 = (bf16[192,512]{1,0:T(8,128)(2,1)S(1)}, bf16[192,512]{1,0:T(8,128)(2,1)S(1)}, u32[]{:S(2)}, u32[]{:S(2)}) collective-permute-start(bf16[192,512]{1,0:T(8,128)(2,1)S(1)} %get-tuple-element.125), channel_id=1, source_target_pairs={{0,7},{1,0},{2,1},{3,2},{4,3},{5,4},{6,5},{7,6},{8,15},{9,8},{10,9... | collective-permute-start | bytes 589832 | tf_op jit(solution)/shard_map/ppermute | solution.py:340
  59.6 9.0 %collective-permute-start.8 = (bf16[192,512]{1,0:T(8,128)(2,1)S(1)}, bf16[192,512]{1,0:T(8,128)(2,1)S(1)}, u32[]{:S(2)}, u32[]{:S(2)}) collective-permute-start(bf16[192,512]{1,0:T(8,128)(2,1)S(1)} %get-tuple-element.126), channel_id=1, source_target_pairs={{0,1},{1,2},{2,3},{3,4},{4,5},{5,6},{6,7},{7,0},{8,9},{9,10},{10,1... | collective-permute-start | bytes 589832 | tf_op jit(solution)/shard_map/ppermute | solution.py:339
  59.6 32.8 %all-to-all-start.1 = ((bf16[32,48,512]{2,1,0:T(8,128)(2,1)}), bf16[32,48,512]{2,1,0:T(8,128)(2,1)}, u32[]{:S(2)}, u32[]{:S(2)}) async-start(bf16[32,48,512]{2,1,0:T(8,128)(2,1)} %get-tuple-element.115), calls=%async_computation.1 | async-start | bytes 3145728 | tf_op jit(solution)/shard_map/all_to_all | solution.py:334
  68.8 7.0 %collective-permute-start.11 = (bf16[192,512]{1,0:T(8,128)(2,1)S(1)}, bf16[192,512]{1,0:T(8,128)(2,1)S(1)}, u32[]{:S(2)}, u32[]{:S(2)}) collective-permute-start(bf16[192,512]{1,0:T(8,128)(2,1)S(1)} %get-tuple-element.123), channel_id=1, source_target_pairs={{0,7},{1,0},{2,1},{3,2},{4,3},{5,4},{6,5},{7,6},{8,15},{9,8},{10,9... | collective-permute-start | bytes 589832 | tf_op jit(solution)/shard_map/ppermute | solution.py:340
  71.8 7.2 %collective-permute-start.10 = (bf16[192,512]{1,0:T(8,128)(2,1)S(1)}, bf16[192,512]{1,0:T(8,128)(2,1)S(1)}, u32[]{:S(2)}, u32[]{:S(2)}) collective-permute-start(bf16[192,512]{1,0:T(8,128)(2,1)S(1)} %get-tuple-element.124), channel_id=1, source_target_pairs={{0,1},{1,2},{2,3},{3,4},{4,5},{5,6},{6,7},{7,0},{8,9},{9,10},{10,1... | collective-permute-start | bytes 589832 | tf_op jit(solution)/shard_map/ppermute | solution.py:339
  74.5 22.9 %copy-start.6 = (f32[512]{0:T(512)S(1)}, f32[512]{0:T(512)}, u32[]{:S(2)}) copy-start(f32[512]{0:T(512)} %param.27) | copy-start | bytes 6148
  79.2 5.2 %collective-permute-start.13 = (bf16[192,512]{1,0:T(8,128)(2,1)S(1)}, bf16[192,512]{1,0:T(8,128)(2,1)S(1)}, u32[]{:S(2)}, u32[]{:S(2)}) collective-permute-start(bf16[192,512]{1,0:T(8,128)(2,1)S(1)} %get-tuple-element.129), channel_id=1, source_target_pairs={{0,7},{1,0},{2,1},{3,2},{4,3},{5,4},{6,5},{7,6},{8,15},{9,8},{10,9... | collective-permute-start | bytes 589832 | tf_op jit(solution)/shard_map/ppermute | solution.py:340
  79.6 6.4 %collective-permute-start.12 = (bf16[192,512]{1,0:T(8,128)(2,1)S(1)}, bf16[192,512]{1,0:T(8,128)(2,1)S(1)}, u32[]{:S(2)}, u32[]{:S(2)}) collective-permute-start(bf16[192,512]{1,0:T(8,128)(2,1)S(1)} %get-tuple-element.130), channel_id=1, source_target_pairs={{0,1},{1,2},{2,3},{3,4},{4,5},{5,6},{6,7},{7,0},{8,9},{9,10},{10,1... | collective-permute-start | bytes 589832 | tf_op jit(solution)/shard_map/ppermute | solution.py:339
  86.2 4.6 %collective-permute-start.16 = (f32[320]{0:T(512)S(1)}, f32[320]{0:T(512)S(1)}, u32[]{:S(2)}, u32[]{:S(2)}) collective-permute-start(f32[320]{0:T(512)S(1)} %pad_maximum_fusion.1), channel_id=1, source_target_pairs={{0,2},{1,3},{2,4},{3,5},{4,6},{5,7},{6,0},{7,1},{8,10},{9,11},{10,... | collective-permute-start | bytes 3848 | tf_op jit(solution)/shard_map/ppermute | solution.py:360
  86.2 4.5 %collective-permute-start.15 = (f32[320]{0:T(512)S(1)}, f32[320]{0:T(512)S(1)}, u32[]{:S(2)}, u32[]{:S(2)}) collective-permute-start(f32[320]{0:T(512)S(1)} %pad_maximum_fusion.1), channel_id=1, source_target_pairs={{0,7},{1,0},{2,1},{3,2},{4,3},{5,4},{6,5},{7,6},{8,15},{9,8},{10,9... | collective-permute-start | bytes 3848 | tf_op jit(solution)/shard_map/ppermute | solution.py:360
  88.3 4.0 %collective-permute-start.14 = (f32[320]{0:T(512)S(1)}, f32[320]{0:T(512)S(1)}, u32[]{:S(2)}, u32[]{:S(2)}) collective-permute-start(f32[320]{0:T(512)S(1)} %pad_maximum_fusion.1), channel_id=1, source_target_pairs={{0,1},{1,2},{2,3},{3,4},{4,5},{5,6},{6,7},{7,0},{8,9},{9,10},{10,1... | collective-permute-start | bytes 3848 | tf_op jit(solution)/shard_map/ppermute | solution.py:360
  92.4 3.4 %collective-permute-start.18 = (f32[320]{0:T(512)S(1)}, f32[320]{0:T(512)S(1)}, u32[]{:S(2)}, u32[]{:S(2)}) collective-permute-start(f32[320]{0:T(512)S(1)} %add_add_fusion), channel_id=1, source_target_pairs={{0,6},{1,7},{2,0},{3,1},{4,2},{5,3},{6,4},{7,5},{8,14},{9,15},{10,... | collective-permute-start | bytes 3848 | tf_op jit(solution)/shard_map/ppermute | solution.py:360
  92.7 4.5 %collective-permute-start.17 = (f32[320]{0:T(512)S(1)}, f32[320]{0:T(512)S(1)}, u32[]{:S(2)}, u32[]{:S(2)}) collective-permute-start(f32[320]{0:T(512)S(1)} %add_add_fusion), channel_id=1, source_target_pairs={{0,2},{1,3},{2,4},{3,5},{4,6},{5,7},{6,0},{7,1},{8,10},{9,11},{10,... | collective-permute-start | bytes 3848 | tf_op jit(solution)/shard_map/ppermute | solution.py:360
  98.5 20.1 %all-to-all-start.2 = ((bf16[32,3,2,512]{3,2,1,0:T(2,128)(2,1)}), bf16[32,3,2,512]{3,2,1,0:T(2,128)(2,1)S(1)}, u32[]{:S(2)}, u32[]{:S(2)}) async-start(bf16[32,3,2,512]{3,2,1,0:T(2,128)(2,1)} %bitcast.111), calls=%async_computation.2 | async-start | bytes 393216 | tf_op jit(solution)/shard_map/all_to_all | solution.py:334
